TPU v7x, 32 devices: a whole 2x2x4 slice. The times are simulated.
32 devices in a mesh: seq: 8 (over z, x), head: 4 (over y, core).
Axes of the slice: x: 2, y: 2, z: 4, core: 2. Of those that a mesh axis runs over, the one named last changes fastest.
Arguments:
- tokens: bfloat16 [4096, 2240], P('seq', 'head'), may hold values from -6 to 6
- norm_gain: bfloat16 [2240], replicated, may hold values from 0.099609375 to 1.8984375
- w_query: bfloat16 [2240, 2048], P(None, 'head'), may hold values from -0.125 to 0.125
- w_key: bfloat16 [2240, 2048], P(None, 'head'), may hold values from -0.125 to 0.125
- w_value: bfloat16 [2240, 2048], P(None, 'head'), may hold values from -0.125 to 0.125
- w_decay: bfloat16 [2240, 16], P(None, 'head'), may hold values from -1 to 1
- w_beta: bfloat16 [2240, 16], P(None, 'head'), may hold values from -0.125 to 0.125
- head_rates: float32 [2, 16], P(None, 'head'), may hold values from -6.5 to 1.5, as said below
- head_gain: bfloat16 [128], replicated, may hold values from 0.099609375 to 1.8984375
- w_out: bfloat16 [2048, 2240], P('head'), may hold values from -0.1875 to 0.1875
- ffn_gain: bfloat16 [2240], replicated, may hold values from 0.099609375 to 1.8984375
- w_up: bfloat16 [2240, 5600], P(None, 'head'), may hold values from -0.125 to 0.125
- conv_taps: bfloat16 [3, 5600], P(None, 'head'), may hold values from -3 to 3
- w_down: bfloat16 [5600, 2240], P('head'), may hold values from -0.109375 to 0.109375
Outputs:
- layer_out: bfloat16 [4096, 2240], P('seq', 'head')
Inputs may be any that keep to these rules, and one draw needn't show every extreme that they name: `head_rates`: row 0 is positive and at most 0.03; row 1 lies in -6.5 to 1.5.
All inputs are finite; a program needn't handle non-finite values.
Results may differ from a plain program's by a relative error of at most 0.02.
Values may be sent and summed in bfloat16 or wider, within the bound.
No kernel may reach another device: no remote copies, remote signals or barrier semaphores. Data moves between devices by JAX's collectives and lax.ppermute only.
A program may use at most 64 MiB of HBM per device.

v0:
```python
import jax
import jax.numpy as jnp
from jax import lax
from jax.sharding import PartitionSpec as P

DK = 128
BLOCK = 128


exact_mode = lax.Precision.HIGHEST
epsilon = 1e-06


def entering(value, axis, join, neutral):
    place = lax.axis_index(axis)
    gathered = jax.tree.map(
        lambda a, kind: lax.all_gather(a.astype(kind), axis), value, (jnp.bfloat16, jnp.bfloat16)
    )
    state = jax.tree.map(lambda a, e: jnp.zeros_like(a) + jnp.asarray(e, a.dtype), value, neutral)

    def one(lap, state):
        return join(
            state,
            jax.tree.map(
                lambda a, own: lax.dynamic_index_in_dim(a, lap, 0, False).astype(own.dtype),
                gathered,
                value,
            ),
        )

    return lax.fori_loop(0, place, one, state)


def with_halo(value, sides, width):
    for axis, dim in sides:
        peers, length = (lax.axis_size(axis), value.shape[dim])
        up = [(i, (i + 1) % peers) for i in range(peers - 1)]
        down = [(j, i) for i, j in up]
        last = lax.slice_in_dim(value, length - width, length, axis=dim)
        initial = lax.slice_in_dim(value, 0, width, axis=dim)
        before = lax.ppermute(last, axis, up)
        after = lax.ppermute(initial, axis, down)
        value = jnp.concatenate([before, value, after], axis=dim)
    return value


def root_scale(matrix, gain_row):
    floating = matrix.astype(jnp.float32)
    inverse = lax.rsqrt(jnp.mean(floating * floating, axis=-1, keepdims=True) + epsilon)
    return floating * inverse * gain_row.astype(jnp.float32)


def unit_rows(matrix):
    return matrix * lax.rsqrt(jnp.sum(matrix * matrix, axis=-1, keepdims=True) + epsilon)


def inverse_apply(lower_part, right_side):
    length = lower_part.shape[-1]
    powered = lower_part
    result = right_side - jnp.einsum(
        "...ij,...jk->...ik", powered, right_side, precision=exact_mode
    )
    for level_index in range((length - 1).bit_length() - 1):
        powered = jnp.einsum("...ij,...jk->...ik", powered, powered, precision=exact_mode)
        result = result + jnp.einsum("...ij,...jk->...ik", powered, result, precision=exact_mode)
    return result


def block_terms(query_rows, key_rows, value_rows, log_decay, strength):
    length = query_rows.shape[-2]
    rows_at = lax.broadcasted_iota(jnp.int32, (length, length), 0)
    cols_at = lax.broadcasted_iota(jnp.int32, (length, length), 1)
    strict = rows_at > cols_at
    inclusive = rows_at >= cols_at
    totals = jnp.cumsum(log_decay, axis=-1)
    spread = totals[..., :, None] - totals[..., None, :]
    decay_strict = jnp.where(strict, jnp.exp(jnp.where(strict, spread, 0.0)), 0.0)
    decay_incl = jnp.where(inclusive, jnp.exp(jnp.where(inclusive, spread, 0.0)), 0.0)
    key_inner = jnp.einsum("...id,...jd->...ij", key_rows, key_rows, precision=exact_mode)
    lower_part = strength[..., :, None] * decay_strict * key_inner
    growth = jnp.exp(totals)
    stacked = jnp.concatenate(
        [strength[..., None] * value_rows, (strength * growth)[..., None] * key_rows], axis=-1
    )
    solved = inverse_apply(lower_part, stacked)
    value_width = value_rows.shape[-1]
    written = solved[..., :value_width]
    erased = solved[..., value_width:]
    scores = decay_incl * jnp.einsum(
        "...id,...jd->...ij", query_rows, key_rows, precision=exact_mode
    )
    query_state = growth[..., None] * query_rows - jnp.einsum(
        "...ij,...jd->...id", scores, erased, precision=exact_mode
    )
    local_out = jnp.einsum("...ij,...jd->...id", scores, written, precision=exact_mode)
    to_end = jnp.exp(totals[..., -1:] - totals)
    faded_keys = to_end[..., None] * key_rows
    identity = jnp.eye(key_rows.shape[-1], dtype=jnp.float32)
    transition = jnp.exp(totals[..., -1])[..., None, None] * identity - jnp.einsum(
        "...ci,...cj->...ij", faded_keys, erased, precision=exact_mode
    )
    offset = jnp.einsum("...ci,...cj->...ij", faded_keys, written, precision=exact_mode)
    return (query_state, local_out, transition, offset)


def into_blocks(matrix, head_count, block_count):
    return matrix.reshape(block_count, BLOCK, head_count, DK).transpose(2, 0, 1, 3)


def gate_blocks(matrix, head_count, block_count):
    return matrix.reshape(block_count, BLOCK, head_count).transpose(2, 0, 1)


def batch_product(left_maps, right_maps):
    return jnp.einsum("hij,hjk->hik", left_maps, right_maps, precision=exact_mode)


def shards(
    tokens,
    norm_gain,
    w_query,
    w_key,
    w_value,
    w_decay,
    w_beta,
    head_rates,
    head_gain,
    w_out,
    ffn_gain,
    w_up,
    conv_taps,
    w_down,
):
    gathered = lax.all_gather(tokens, "head", axis=1, tiled=True)
    normed = root_scale(gathered, norm_gain).astype(jnp.bfloat16)
    token_count = gathered.shape[0]
    local_heads = w_query.shape[1] // DK
    block_count = token_count // BLOCK
    query_all = jnp.dot(normed, w_query, preferred_element_type=jnp.float32).astype(jnp.bfloat16)
    key_all = jnp.dot(normed, w_key, preferred_element_type=jnp.float32).astype(jnp.bfloat16)
    value_all = jnp.dot(normed, w_value, preferred_element_type=jnp.float32).astype(jnp.bfloat16)
    decay_pre = jnp.dot(normed, w_decay, preferred_element_type=jnp.float32)
    log_decay = -head_rates[0] * jax.nn.softplus(decay_pre)
    strength = jax.nn.sigmoid(
        jnp.dot(normed, w_beta, preferred_element_type=jnp.float32) + head_rates[1]
    )
    query_rows = into_blocks(query_all.astype(jnp.float32), local_heads, block_count)
    key_rows = unit_rows(into_blocks(key_all.astype(jnp.float32), local_heads, block_count))
    value_rows = into_blocks(value_all.astype(jnp.float32), local_heads, block_count)
    query_state, local_out, transition, offset = block_terms(
        query_rows,
        key_rows,
        value_rows,
        gate_blocks(log_decay, local_heads, block_count),
        gate_blocks(strength, local_heads, block_count),
    )
    identity_map = jnp.broadcast_to(jnp.eye(DK, dtype=jnp.float32), (local_heads, DK, DK))
    empty_state = jnp.zeros((local_heads, DK, DK), jnp.float32)

    def compose(carried, pieces):
        prior_map, prior_shift = carried
        query_part, local_part, trans_part, offset_part = pieces
        shard_query = jnp.einsum("hcd,hde->hce", query_part, prior_map, precision=exact_mode)
        free_out = (
            jnp.einsum("hcd,hde->hce", query_part, prior_shift, precision=exact_mode) + local_part
        )
        next_carry = (
            batch_product(trans_part, prior_map),
            batch_product(trans_part, prior_shift) + offset_part,
        )
        return (next_carry, (shard_query, free_out))

    block_pieces = (
        jnp.moveaxis(query_state, 1, 0),
        jnp.moveaxis(local_out, 1, 0),
        jnp.moveaxis(transition, 1, 0),
        jnp.moveaxis(offset, 1, 0),
    )
    (shard_map_m, shard_shift), (shard_query, free_out) = lax.scan(
        compose, (identity_map, empty_state), block_pieces
    )

    def combine(earlier, later):
        return (batch_product(later[0], earlier[0]), batch_product(later[0], earlier[1]) + later[1])

    prefix_map, start_state = entering(
        (shard_map_m, shard_shift), "seq", combine, (identity_map, empty_state)
    )
    head_out = (
        jnp.einsum("nhcd,hde->nhce", shard_query, start_state, precision=exact_mode) + free_out
    )
    head_out = head_out.transpose(0, 2, 1, 3).reshape(token_count, local_heads, DK)
    mixed_heads = (
        root_scale(head_out, head_gain).astype(jnp.bfloat16).reshape(token_count, local_heads * DK)
    )
    partial_out = jnp.dot(mixed_heads, w_out, preferred_element_type=jnp.float32)
    attended = lax.psum(partial_out.astype(jnp.bfloat16), "head").astype(jnp.float32)
    middle_all = (gathered.astype(jnp.float32) + attended).astype(jnp.bfloat16)
    feature_share = tokens.shape[1]
    middle_part = lax.dynamic_slice_in_dim(
        middle_all, lax.axis_index("head") * feature_share, feature_share, 1
    )
    hidden_in = root_scale(middle_all, ffn_gain).astype(jnp.bfloat16)
    lifted = jnp.dot(hidden_in, w_up, preferred_element_type=jnp.float32).astype(jnp.bfloat16)
    padded = with_halo(lifted, (("seq", 0),), 1)
    tap_values = conv_taps.astype(jnp.float32)
    convolved = (
        tap_values[0] * padded[:-2] + tap_values[1] * padded[1:-1] + tap_values[2] * padded[2:]
    )
    activated = jax.nn.gelu(convolved, approximate=True).astype(jnp.bfloat16)
    ffn_partial = jnp.dot(activated, w_down, preferred_element_type=jnp.float32)
    ffn_total = lax.psum_scatter(
        ffn_partial.astype(jnp.bfloat16), "head", scatter_dimension=1, tiled=True
    ).astype(jnp.float32)
    return (middle_part.astype(jnp.float32) + ffn_total).astype(jnp.bfloat16)


def solution(mesh):
    placed = (
        P("seq", "head"),
        P(),
        P(None, "head"),
        P(None, "head"),
        P(None, "head"),
        P(None, "head"),
        P(None, "head"),
        P(None, "head"),
        P(),
        P("head", None),
        P(),
        P(None, "head"),
        P(None, "head"),
        P("head", None),
    )
    return jax.shard_map(
        shards, mesh=mesh, in_specs=placed, out_specs=P("seq", "head"), check_vma=False
    )
```

profile of v0, /device:TPU:16, one launch (start us, length us, event | category | flops | bytes accessed | tf_op | source)
XLA Modules:
  0.0 373.6 jit_solution(1059472438420650146)
XLA Ops:
  8.8 24.9 %all-gather.6.cloned.1.call-done = bf16[512,2240]{0,1:T(8,128)(2,1)} async-done(((bf16[512,560]{0,1:T(8,128)(2,1)}), bf16[512,2240]{0,1:T(8,128)(2,1)}) %all-gather.6.cloned.1.call-update) | async-done | bytes 2293776 | tf_op jit(solution)/shard_map/all_gather | solution.py:134
  33.7 2.3 fusion.29
  36.1 4.2 %fusion.62 = f32[512,512]{1,0:T(8,128)} fusion(bf16[2240,512]{1,0:T(8,128)(2,1)} %param.21, bf16[512,2240]{0,1:T(8,128)(2,1)S(1)} %copy-done.2, f32[2240]{0:T(1024)S(1)} %convert_element_type.104, f32[512]{0:T(512)S(1)} %add_rsqrt_fusion.3), kind=kOutput, calls=%fused_computation.93 | convolution fusion | flops 1179516928 | bytes 5647104 | tf_op jit(solution)/shard_map/dot_general | solution.py:140
  42.2 2.3 fusion.94
  44.5 1.7 reduce_window_sum.11
  46.4 2.3 fusion.66
  48.8 4.8 %fusion.61 = f32[512,512]{1,0:T(8,128)} fusion(bf16[2240,512]{1,0:T(8,128)(2,1)} %param.22, bf16[512,2240]{0,1:T(8,128)(2,1)} %all-gather.6.cloned.1.call-done, f32[2240]{0:T(1024)S(1)} %convert_element_type.104, f32[512]{0:T(512)S(1)} %add_rsqrt_fusion.3), kind=kOutput, calls=%fused_computation.91 | convolution fusion | flops 1179516928 | bytes 5647104 | tf_op jit(solution)/shard_map/dot_general | solution.py:141
  53.6 2.5 reshape.101
  56.8 2.6 convolution_multiply_fusion.1
  62.1 2.1 convolution_subtract_fusion
  64.2 1.9 fusion.112
  67.5 2.2 convolution_add_fusion.5
  70.9 1.9 fusion.115
  74.0 2.2 convolution_add_fusion.4
  76.2 2.2 fusion.119
  78.4 3.2 fusion.118
  81.6 2.6 convolution_convert_fusion.3
  84.2 2.0 reshape.97
  86.2 4.7 %convolution_add_fusion.3 = f32[4,4,128,256]{3,2,1,0:T(8,128)S(1)} fusion(f32[4,4,128,128]{3,2,1,0:T(8,128)} %fusion.119, f32[4,4,128,256]{3,2,1,0:T(8,128)} %copy-done.1, f32[4,4,128,256]{3,2,1,0:T(8,128)} %fusion.118), kind=kOutput, calls=%fused_computation.58 | convolution fusion | flops 806354944 | bytes 7340032 | tf_op jit(solution)/shard_map/...ij,...jk->...ik/dot_general | solution.py:65
  92.3 2.2 convolution_bitcast_fusion.2
  94.5 2.4 fusion.57
  96.8 3.4 convolution_bitcast_fusion.4
  100.3 3.5 fusion.58
  103.8 35.3 %while.30 = (s32[]{:T(128)}, f32[4,128,128]{2,1,0:T(8,128)S(1)}, f32[4,128,128]{2,1,0:T(8,128)}, f32[4,4,128,128]{3,2,0,1:T(8,128)}, f32[4,4,128,128]{2,3,0,1:T(...) while((s32[]{:T(128)}, f32[4,128,128]{2,1,0:T(8,128)S(1)}, ...), condition=%wide.region_4.5_spmd.clone, body=%wide.region_3.4_spmd.clone.sunk | while | flops 402915328 | bytes 5771384 | solution.py:179
  107.0 2.1 convolution_add_fusion.10
  109.2 2.1 fusion.180
  115.8 2.1 convolution_add_fusion.10
  118.0 2.1 fusion.180
  124.7 2.1 convolution_add_fusion.10
  126.8 2.0 fusion.180
  133.5 2.1 convolution_add_fusion.10
  135.6 2.1 fusion.180
  139.8 1.6 convert_element_type.110
  141.5 36.8 %all-gather.8.cloned.1.call-done = bf16[32,128,128]{2,1,0:T(8,128)(2,1)} async-done(((bf16[4,128,128]{2,1,0:T(8,128)(2,1)}), bf16[32,128,128]{2,1,0:T(8,128)(2,1)}) %all-gather.8.cloned.1.call-update) | async-done | bytes 1048592 | tf_op jit(solution)/shard_map/all_gather | solution.py:17
  178.3 41.1 %all-gather.10.cloned.1.call-done = bf16[32,128,128]{2,1,0:T(8,128)(2,1)} async-done(((bf16[4,128,128]{2,1,0:T(8,128)(2,1)}), bf16[32,128,128]{2,1,0:T(8,128)(2,1)}) %all-gather.10.cloned.1.call-update) | async-done | bytes 1048592 | tf_op jit(solution)/shard_map/all_gather | solution.py:17
  219.4 5.7 %while.29 = (s32[]{:T(128)}, f32[4,128,128]{2,1,0:T(8,128)S(1)}, s32[]{:T(128)}, bf16[8,4,128,128]{3,2,1,0:T(8,128)(2,1)}, bf16[8,4,128,128]{3,2,1,0:T(8,128)(2,1)}, /*index=5*/s32[]{:T(128)}, s32[]{:T(128)}, s32[]{:T(128)}) while((s32[]{:T(128)}, f32[4,128,128]{2,1,0:T(8,128)S(1)}, s32[]{:T(128)}, bf16[8,4,128,128]{3,2,1,0:T(8,128)(2,1)}, ...), condition=%wide.region_6.7_spmd, body=%wide.region_5.6_spmd.sunk | while | flops 100794368 | bytes 1311863 | solution.py:31
  225.1 3.6 multiply_reduce_fusion
  232.8 2.8 convolution_convert_fusion.1
  236.4 58.5 %all-reduce.2.cloned.1.call-done = bf16[512,2240]{0,1:T(8,128)(2,1)} async-done(((bf16[512,2240]{0,1:T(8,128)(2,1)}), bf16[512,2240]{0,1:T(8,128)(2,1)}) %all-reduce.2.cloned.1.call-update) | async-done | bytes 2293776 | tf_op jit(solution)/shard_map/psum | solution.py:197
  294.8 3.4 fusion.26
  298.3 7.5 %convolution_convert_fusion.2 = bf16[512,1400]{0,1:T(8,128)(2,1)S(1)} fusion(bf16[2240,1400]{1,0:T(8,128)(2,1)} %param.29, bf16[512,2240]{0,1:T(8,128)(2,1)S(1)} %get-tuple-element.193, f32[2240]{0:T(1024)S(1)} %convert_element_type.119, f32[512]{0:T(512)S(1)} %add_rsqrt_fusion.2), kind=kOutput, calls=%fused_computation.46 | convolution fusion | flops 3216568320 | bytes 10010368 | tf_op jit(solution)/shard_map/dot_general | solution.py:204
  306.0 3.4 collective-permute-start
  309.4 3.5 collective-permute-start.1
  313.0 11.6 %collective-permute-done = bf16[1,1400]{0,1:T(8,128)(2,1)S(1)} collective-permute-done((bf16[1,1400]{0,1:T(8,128)(2,1)S(1)}, bf16[1,1400]{0,1:T(8,128)(2,1)S(1)}, u32[]{:S(2)}, u32[]{:S(2)}) %collective-permute-start) | collective-permute-done | bytes 2832 | tf_op jit(solution)/shard_map/ppermute | solution.py:41
  324.6 1.9 collective-permute-done.1
  326.5 6.1 %convolution_convert_fusion = bf16[512,2240]{0,1:T(8,128)(2,1)} fusion(bf16[1400,2240]{0,1:T(8,128)(2,1)S(1)} %bitcast.191, bf16[512,1400]{0,1:T(8,128)(2,1)S(1)} %convolution_convert_fusion.2, bf16[1,1400]{0,1:T(8,128)(2,1)S(1)} %collective-permute-done.1, bf16[1,1400]{0,1:T(8,128)(2,1)S(1)} %collective-permute-done, f32[1400]{0:T(1024)S(1)} %get-tuple-element.162, ...), kind=kOutput, calls=%fused_computation.43 | convolution fusion | flops 3228897280 | bytes 10021760 | tf_op jit(solution)/shard_map/dot_general | solution.py:211
  332.6 32.1 %reduce-scatter.2.cloned.1.call-done = bf16[512,560]{0,1:T(8,128)(2,1)} async-done(((bf16[512,2240]{0,1:T(8,128)(2,1)}), bf16[512,560]{0,1:T(8,128)(2,1)}) %reduce-scatter.2.cloned.1.call-update) | async-done | bytes 573456 | tf_op jit(solution)/shard_map/reduce_scatter | solution.py:212
  364.7 2.2 add_convert_fusion
  (111 shorter events, 42.1 us)
Async XLA Ops:
  6.5 226.2 %copy-start = (bf16[512,2240]{0,1:T(8,128)(2,1)S(1)}, bf16[512,2240]{0,1:T(8,128)(2,1)}, u32[]{:S(2)}) copy-start(bf16[512,2240]{0,1:T(8,128)(2,1)} %param.27) | copy-start | bytes 6881284
  6.5 27.2 %all-gather.6.cloned.1.call-start = ((), (), s32[]{:S(2)}) async-start(), calls=%async_computation.1 | async-start | bytes 2867200 | tf_op jit(solution)/shard_map/all_gather | solution.py:134
  7.3 171.1 %all-gather.8.cloned.1.call-start = ((), (), s32[]{:S(2)}) async-start(), calls=%async_computation.4 | async-start | bytes 1179648 | tf_op jit(solution)/shard_map/all_gather | solution.py:17
  33.7 2.4 copy-start.2
  40.2 1.9 copy-start.10
  42.2 4.3 %copy-start.11 = (bf16[2240,4]{0,1:T(4,128)(2,1)S(1)}, bf16[2240,4]{0,1:T(4,128)(2,1)}, u32[]{:S(2)}) copy-start(bf16[2240,4]{0,1:T(4,128)(2,1)} %param.24) | copy-start | bytes 53764
  56.2 3.2 copy-start.4
  76.2 5.5 %copy-start.1 = (f32[4,4,128,256]{3,2,1,0:T(8,128)}, f32[4,4,128,256]{3,2,1,0:T(8,128)S(1)}, u32[]{:S(2)}) copy-start(f32[4,4,128,256]{3,2,1,0:T(8,128)S(1)} %convolution_add_fusion.4) | copy-start | bytes 6291460
  78.4 3.2 copy-start.3
  78.4 3.2 copy-start.9
  86.2 4.7 %copy-start.6 = (bf16[4,128,4,128]{3,2,1,0:T(4,128)(2,1)S(1)}, bf16[4,128,4,128]{3,2,1,0:T(4,128)(2,1)}, u32[]{:S(2)}) copy-start(bf16[4,128,4,128]{3,2,1,0:T(4,128)(2,1)} %reshape.97) | copy-start | bytes 1572868
  103.8 37.7 %copy-start.12 = (bf16[128]{0:T(256)(128)(2,1)S(1)}, bf16[128]{0:T(256)(128)(2,1)}, u32[]{:S(2)}) copy-start(bf16[128]{0:T(256)(128)(2,1)} %param.26) | copy-start | bytes 772
  139.7 79.6 %all-gather.10.cloned.1.call-start = ((), (), s32[]{:S(2)}) async-start(), calls=%async_computation.5 | async-start | bytes 1179648 | tf_op jit(solution)/shard_map/all_gather | solution.py:17
  141.4 153.4 %all-reduce.2.cloned.1.call-start = ((), (), s32[]{:S(2)}) async-start(), calls=%async_computation.2 | async-start | bytes 4587520 | tf_op jit(solution)/shard_map/psum | solution.py:197
  235.6 0.7 copy-start.8
  235.6 0.7 copy-start.7
  235.7 129.1 %reduce-scatter.2.cloned.1.call-start = ((), (), s32[]{:S(2)}) async-start(), calls=%async_computation.3 | async-start | bytes 2867200 | tf_op jit(solution)/shard_map/reduce_scatter | solution.py:212
  294.8 31.7 %slice-start = ((s8[6307840]{0:T(1024)(128)(4,1)}), s8[4194304]{0:T(1024)(128)(4,1)S(1)}, s32[]{:S(2)}) async-start(s8[6307840]{0:T(1024)(128)(4,1)} %bitcast.190), calls=%async_computation.6 | async-start | bytes 8388608
  298.2 7.6 %copy-start.5 = (bf16[512,2240]{0,1:T(8,128)(2,1)}, bf16[512,2240]{0,1:T(8,128)(2,1)S(1)}, u32[]{:S(2)}) copy-start(bf16[512,2240]{0,1:T(8,128)(2,1)S(1)} %get-tuple-element.193) | copy-start | bytes 6881284
  298.3 28.3 %slice-start.1 = ((s8[6307840]{0:T(1024)(128)(4,1)}), s8[2113536]{0:T(1024)(128)(4,1)S(1)}, s32[]{:S(2)}) async-start(s8[6307840]{0:T(1024)(128)(4,1)} %bitcast.190), calls=%async_computation.7 | async-start | bytes 4227072
  306.0 18.6 %collective-permute-start = (bf16[1,1400]{0,1:T(8,128)(2,1)S(1)}, bf16[1,1400]{0,1:T(8,128)(2,1)S(1)}, u32[]{:S(2)}, u32[]{:S(2)}) collective-permute-start(bf16[1,1400]{0,1:T(8,128)(2,1)S(1)} %get-tuple-element.194), channel_id=1, source_target_pairs={{0,4},{4,8},{8,12},{12,16},{16,20},{20,24},{24,28},{1,5},{5,9},{9,... | collective-permute-start | bytes 8408 | tf_op jit(solution)/shard_map/ppermute | solution.py:41
  309.4 17.1 %collective-permute-start.1 = (bf16[1,1400]{0,1:T(8,128)(2,1)S(1)}, bf16[1,1400]{0,1:T(8,128)(2,1)S(1)}, u32[]{:S(2)}, u32[]{:S(2)}) collective-permute-start(bf16[1,1400]{0,1:T(8,128)(2,1)S(1)} %get-tuple-element.195), channel_id=1, source_target_pairs={{4,0},{8,4},{12,8},{16,12},{20,16},{24,20},{28,24},{5,1},{9,5},{13... | collective-permute-start | bytes 8408 | tf_op jit(solution)/shard_map/ppermute | solution.py:42
Sparse Core Ops, SparseCore 0:
  8.9 24.7 all-gather.5
  139.9 38.4 all-gather.7
  180.4 38.8 all-gather.9
  235.8 59.0 all-reduce.1
  332.7 31.9 reduce-scatter.1
where the time goes:
time: 379 us; the launch traced here: 374 us
  waiting for transfers between devices  208 us (55%)
  matrix products  111 us (29%)
  local copies, waits for them, and re-layouts  18.7 us (5%)
  other arithmetic  14.9 us (4%)
  between operations  13.7 us (4%)
  starting transfers between devices  7.08 us (2%)
    all_gather x2, waiting for transfers between devices, entering(): lax.all_gather(a.astype(kind), axis)  77.9 us
    psum x1, waiting for transfers between devices, shards(): lax.psum(partial_out.astype(jnp.bfloat16), 'head').astype(jnp.float32)  58.5 us
    reduce_scatter x1, waiting for transfers between devices, shards(): lax.psum_scatter(ffn_partial.astype(jnp.bfloat16), 'head', scatter_dimens...  32.1 us
    all_gather x1, waiting for transfers between devices, shards(): gathered = lax.all_gather(tokens, 'head', axis=1, tiled=True)  24.9 us
    dot_general x12, matrix products, batch_product(): jnp.einsum('hij,hjk->hik', left_maps, right_maps, precision=exact_mode)  18.8 us
    dot_general x6, matrix products, inverse_apply(): jnp.einsum('...ij,...jk->...ik', powered, result, precision=exact_mode)  16.2 us
    ppermute x1, waiting for transfers between devices, with_halo(): before = lax.ppermute(last, axis, up)  11.6 us
    dot_general x4, matrix products, compose(): jnp.einsum('hcd,hde->hce', query_part, prior_map, precision=exact_mode)  8.26 us
  transfers between devices with their start and end apart: 7, of which 7 were waited for; matrix products, arithmetic and copies ran while one was open for 1% of the time, Pallas kernels for 0%

commit v1 on v0

v1 whole, which is shorter than its diff:
```python
import functools

import jax
import jax.numpy as jnp
from jax import lax
from jax.experimental import pallas as pl
from jax.experimental.pallas import tpu as pltpu
from jax.sharding import PartitionSpec as P

DK = 128
BLOCK = 128
epsilon = 1e-06
f32 = jnp.float32
bf16 = jnp.bfloat16
LIMIT = 56 * 1024 * 1024

VM = pl.BlockSpec(memory_space=pltpu.VMEM)
SM = pl.BlockSpec(memory_space=pltpu.SMEM)
ANY = pl.BlockSpec(memory_space=pl.ANY)


def params():
    return pltpu.CompilerParams(vmem_limit_bytes=LIMIT)


def dot(a, b):
    return jnp.dot(a, b, preferred_element_type=f32)


def dot_nt(a, b):
    return lax.dot_general(a, b, (((1,), (1,)), ((), ())), preferred_element_type=f32)


def dot_tn(a, b):
    return lax.dot_general(a, b, (((0,), (0,)), ((), ())), preferred_element_type=f32)


def iotas(shape):
    return lax.broadcasted_iota(jnp.int32, shape, 0), lax.broadcasted_iota(jnp.int32, shape, 1)


def maps_kernel(n, width, heads, order, *refs):
    pieces = refs[:n]
    gain, rates, weights, normed, keys, erased, entry, maps, totals = refs[n : n + 9]
    held, raw_k, raw_v, total_b, beta_b, total_t, sem = refs[n + 9 :]
    count, part = pieces[0].shape
    blocks = count // BLOCK
    inner = heads * DK
    copies = [
        pltpu.make_async_copy(
            weights.at[pl.ds(pl.multiple_of(order[p] * width, 128), width)],
            held.at[pl.ds(p * width, width)],
            sem.at[p],
        )
        for p in range(n)
    ]
    for copy in copies:
        copy.start()
    tail = (part // 128) * 128
    for p in range(n):
        if tail < width:
            normed[:, p * width + tail : (p + 1) * width] = jnp.zeros((count, width - tail), bf16)

    @pl.loop(0, count // 32)
    def _(r):
        rows = pl.ds(pl.multiple_of(r * 32, 32), 32)
        values = [ref[rows, :].astype(f32) for ref in pieces]
        square = sum(jnp.sum(v * v, axis=1, keepdims=True) for v in values)
        inverse = lax.rsqrt(square / (n * part) + epsilon)
        for p, v in enumerate(values):
            scale = gain[pl.ds(order[p], 1), :][:, :part]
            normed[rows, p * width : p * width + part] = (v * inverse * scale).astype(bf16)

    for copy in copies:
        copy.wait()

    pre = dot(normed[...], held[:, 2 * inner : 2 * inner + 128])
    soft = jnp.maximum(pre, 0.0) + jnp.log1p(jnp.exp(-jnp.abs(pre)))
    decay = -rates[0:1, :] * soft
    beta = jax.nn.sigmoid(pre + rates[1:2, :])
    row_at, col_at = iotas((BLOCK, BLOCK))
    lower = (row_at >= col_at).astype(f32)
    for c in range(blocks):
        part_total = jnp.dot(
            lower,
            decay[c * BLOCK : (c + 1) * BLOCK],
            precision=lax.Precision.HIGHEST,
            preferred_element_type=f32,
        )
        totals[c * BLOCK : (c + 1) * BLOCK, :] = part_total
        total_t[c] = part_total.T
    for h in range(heads):
        total_b[h] = jnp.broadcast_to(totals[:, h : h + 1], (count, DK))
        beta_b[h] = jnp.broadcast_to(beta[:, heads + h : heads + h + 1], (count, DK))

    @pl.loop(0, inner // 256)
    def _(t):
        cols = pl.ds(pl.multiple_of(t * 256, 256), 256)
        raw_k[:, cols] = dot(normed[...], held[:, cols]).astype(bf16)
        more = pl.ds(pl.multiple_of(inner + t * 256, 256), 256)
        raw_v[:, cols] = dot(normed[...], held[:, more]).astype(bf16)

    xor = jnp.where(row_at > col_at, row_at ^ col_at, 0)
    eye = jnp.where(row_at == col_at, 1.0, 0.0)

    @pl.loop(0, heads)
    def _(h):
        cols = pl.ds(pl.multiple_of(h * DK, DK), DK)
        wide = pl.ds(pl.multiple_of(h * 2 * DK, 2 * DK), 2 * DK)
        raw = raw_k[:, cols].astype(f32)
        unit = raw * lax.rsqrt(jnp.sum(raw * raw, axis=1, keepdims=True) + epsilon)
        keys[:, cols] = unit.astype(bf16)
        rows = [slice(c * BLOCK, (c + 1) * BLOCK) for c in range(blocks)]
        lows, solved = [], []
        for c in range(blocks):
            k = keys[rows[c], cols]
            t_col = total_b[h, rows[c], :]
            t_row = total_t[c, pl.ds(h, 1), :]
            fade = jnp.exp(jnp.minimum(t_col - t_row, 0.0))
            low = jnp.where(xor > 0, beta_b[h, rows[c], :] * fade * dot_nt(k, k), 0.0)
            lows.append(low)
            solved.append(eye - jnp.where(xor == 1, low, 0.0))
        size = 2
        while size < BLOCK:
            mask = (xor >= size) & (xor < 2 * size)
            first = []
            for c in range(blocks):
                link = jnp.where(mask, lows[c], 0.0).astype(bf16)
                first.append(dot(link, solved[c].astype(bf16)).astype(bf16))
            solved = [
                solved[c] - dot(solved[c].astype(bf16), first[c]) for c in range(blocks)
            ]
            size *= 2
        state = None
        grown = []
        for c in range(blocks):
            k = keys[rows[c], cols].astype(f32)
            t_col = total_b[h, rows[c], :]
            b_col = beta_b[h, rows[c], :]
            right = jnp.concatenate(
                [
                    (b_col * jnp.exp(t_col) * k).astype(bf16),
                    (b_col * raw_v[rows[c], cols].astype(f32)).astype(bf16),
                ],
                axis=1,
            )
            both = dot(solved[c].astype(bf16), right).astype(bf16)
            erased[rows[c], wide] = both
            t_end = t_col[BLOCK - 1 : BLOCK, :]
            faded = (jnp.exp(t_end - t_col) * k).astype(bf16)
            grown.append((jnp.exp(t_end), dot_tn(faded, both)))
        for c in range(blocks):
            end, product = grown[c]
            erase, write = product[:, :DK], product[:, DK:]
            if c == 0:
                state = jnp.concatenate([end * eye - erase, write], axis=1)
            else:
                step = dot(erase.astype(bf16), state.astype(bf16))
                state = (
                    jnp.concatenate([end, end], axis=1) * state
                    - step
                    + jnp.concatenate([jnp.zeros_like(write), write], axis=1)
                )
            if c < blocks - 1:
                entry[c, :, wide] = state.astype(bf16)
        maps[h] = state.astype(bf16)


def block_maps(order, pieces, gain, rates, weights, heads, width):
    n = len(pieces)
    count = pieces[0].shape[0]
    blocks = count // BLOCK
    inner = heads * DK
    return pl.pallas_call(
        functools.partial(maps_kernel, n, width, heads),
        out_shape=(
            jax.ShapeDtypeStruct((count, n * width), bf16),
            jax.ShapeDtypeStruct((count, inner), bf16),
            jax.ShapeDtypeStruct((count, 2 * inner), bf16),
            jax.ShapeDtypeStruct((blocks - 1, DK, 2 * inner), bf16),
            jax.ShapeDtypeStruct((heads, DK, 2 * DK), bf16),
            jax.ShapeDtypeStruct((count, 128), f32),
        ),
        in_specs=[SM] + [VM] * (n + 2) + [ANY],
        out_specs=[VM] * 6,
        scratch_shapes=[
            pltpu.VMEM((n * width, 2 * inner + 128), bf16),
            pltpu.VMEM((count, inner), bf16),
            pltpu.VMEM((count, inner), bf16),
            pltpu.VMEM((heads, count, DK), f32),
            pltpu.VMEM((heads, count, DK), f32),
            pltpu.VMEM((blocks, BLOCK, 128), f32),
            pltpu.SemaphoreType.DMA((n,)),
        ],
        compiler_params=params(),
        cost_estimate=pl.CostEstimate(
            flops=8 * 10**9, bytes_accessed=12 * 10**6, transcendentals=10**6
        ),
        name="block_maps",
    )(order, *pieces, gain, rates, weights)


def query_kernel(n, width, order, normed, weights, query, held, sem):
    copies = [
        pltpu.make_async_copy(
            weights.at[pl.ds(pl.multiple_of(order[p] * width, 128), width)],
            held.at[pl.ds(p * width, width)],
            sem.at[p],
        )
        for p in range(n)
    ]
    for copy in copies:
        copy.start()
    for copy in copies:
        copy.wait()

    @pl.loop(0, query.shape[1] // 256)
    def _(t):
        cols = pl.ds(pl.multiple_of(t * 256, 256), 256)
        query[:, cols] = dot(normed[...], held[:, cols]).astype(bf16)


def queries(order, normed, weights, width):
    n = normed.shape[1] // width
    return pl.pallas_call(
        functools.partial(query_kernel, n, width),
        out_shape=jax.ShapeDtypeStruct((normed.shape[0], weights.shape[1]), bf16),
        in_specs=[SM, VM, ANY],
        out_specs=VM,
        scratch_shapes=[pltpu.VMEM(weights.shape, bf16), pltpu.SemaphoreType.DMA((n,))],
        compiler_params=params(),
        cost_estimate=pl.CostEstimate(
            flops=2 * 10**9, bytes_accessed=6 * 10**6, transcendentals=0
        ),
        name="queries",
    )(order, normed, weights)


def outputs_kernel(heads, query, keys, erased, entry, totals, after, shard_query, free, total_t):
    count = query.shape[0]
    blocks = count // BLOCK
    row_at, col_at = iotas((BLOCK, BLOCK))
    for c in range(blocks):
        total_t[c] = totals[c * BLOCK : (c + 1) * BLOCK, :].T
    for h in range(heads):
        cols = slice(h * DK, (h + 1) * DK)
        wide = slice(h * 2 * DK, (h + 1) * 2 * DK)
        for c in range(blocks):
            rows = slice(c * BLOCK, (c + 1) * BLOCK)
            t_col = jnp.broadcast_to(totals[rows, h : h + 1], (BLOCK, BLOCK))
            t_row = total_t[c, h : h + 1, :]
            fade = jnp.where(row_at >= col_at, jnp.exp(jnp.minimum(t_col - t_row, 0.0)), 0.0)
            q = query[rows, cols]
            scores = (fade * dot_nt(q, keys[rows, cols])).astype(bf16)
            both = dot(scores, erased[rows, wide])
            reach = jnp.exp(t_col) * q.astype(f32) - both[:, :DK]
            local = both[:, DK:]
            if c > 0:
                product = dot(reach.astype(bf16), entry[c - 1, :, wide])
                reach = product[:, :DK]
                local = local + product[:, DK:]
            shard_query[rows, cols] = reach.astype(bf16)
            free[rows, cols] = local


def block_outputs(query, keys, erased, entry, totals, after, heads):
    count = query.shape[0]
    return pl.pallas_call(
        functools.partial(outputs_kernel, heads),
        out_shape=(
            jax.ShapeDtypeStruct(query.shape, bf16),
            jax.ShapeDtypeStruct(query.shape, f32),
        ),
        in_specs=[VM] * 5 + [ANY],
        out_specs=[VM] * 2,
        scratch_shapes=[pltpu.VMEM((count // BLOCK, BLOCK, 128), f32)],
        compiler_params=params(),
        cost_estimate=pl.CostEstimate(
            flops=3 * 10**9, bytes_accessed=4 * 10**6, transcendentals=10**6
        ),
        name="block_outputs",
    )(query, keys, erased, entry, totals, after)


def pair_kernel(place, own, other, pair, first, done):
    even = place[0] == 0
    for h in range(own.shape[0]):
        mine, theirs = own[h], other[h]
        early = jnp.where(even, mine, theirs)
        late = jnp.where(even, theirs, mine)
        product = dot(late[:, :DK], early)
        shift = late[:, DK:].astype(f32)
        pair[h] = (product + jnp.concatenate([jnp.zeros_like(shift), shift], axis=1)).astype(bf16)
        first[h] = early
    done[...] = jnp.zeros_like(done)


def pair_maps(place, own, other):
    return pl.pallas_call(
        pair_kernel,
        out_shape=(
            jax.ShapeDtypeStruct(own.shape, bf16),
            jax.ShapeDtypeStruct(own.shape, bf16),
            jax.ShapeDtypeStruct((8, 128), f32),
        ),
        in_specs=[SM, VM, VM],
        out_specs=[VM] * 3,
        compiler_params=params(),
        name="pair_maps",
    )(place, own, other)


def apply_map(whole, state):
    high = state.astype(bf16)
    low = (state - high.astype(f32)).astype(bf16)
    product = dot(whole[:, :DK], jnp.concatenate([high, low], axis=1))
    return product[:, :DK] + product[:, DK:] + whole[:, DK:].astype(f32)


def start_kernel(steps, place, first, *refs):
    pairs, (keep, give) = refs[:steps], refs[steps:]
    even = place[0] == 0
    for h in range(first.shape[0]):
        state = pairs[0][h][:, DK:].astype(f32)
        for pair in pairs[1:]:
            state = apply_map(pair[h], state)
        later = apply_map(first[h], state)
        keep[h] = jnp.where(even, state, later).astype(bf16)
        give[h] = jnp.where(even, later, state).astype(bf16)


def start_states(place, first, pairs):
    heads = first.shape[0]
    shape = jax.ShapeDtypeStruct((heads, DK, DK), bf16)
    return pl.pallas_call(
        functools.partial(start_kernel, len(pairs)),
        out_shape=(shape, shape),
        in_specs=[SM] + [VM] * (1 + len(pairs)),
        out_specs=[VM] * 2,
        compiler_params=params(),
        name="start_states",
    )(place, first, *pairs)


def mixer_kernel(heads, units, place, own, other, shard_query, free, gain, weights, give, keep, mixed, held, sem):
    copy = pltpu.make_async_copy(weights, held, sem)
    copy.start()
    even = place[0] == 0
    core = place[1]
    half = heads // 2
    for u, unit in enumerate(units):
        rows = slice(unit * BLOCK, (unit + 1) * BLOCK)
        for h in range(heads):
            cols = slice(h * DK, (h + 1) * DK)
            if h < half:
                state = jnp.where(even, own[h], other[h])
            else:
                state = jnp.where(even, other[h - half], own[h - half])
            out = dot(shard_query[rows, cols], state) + free[rows, cols]
            scale = lax.rsqrt(jnp.mean(out * out, axis=1, keepdims=True) + epsilon)
            mixed[u * BLOCK : (u + 1) * BLOCK, cols] = (
                out * scale * gain[...].astype(f32)
            ).astype(bf16)
    copy.wait()
    give_rows = pl.ds(pl.multiple_of((1 - core) * BLOCK, BLOCK), BLOCK)
    keep_rows = pl.ds(pl.multiple_of(core * BLOCK, BLOCK), BLOCK)
    give[...] = dot(mixed[give_rows, :], held[...]).astype(bf16)
    keep[...] = dot(mixed[keep_rows, :], held[...]).astype(bf16)


def mixer_out(place, own, other, shard_query, free, gain, weights, heads, units):
    shape = jax.ShapeDtypeStruct((BLOCK, weights.shape[1]), bf16)
    return pl.pallas_call(
        functools.partial(mixer_kernel, heads, units),
        out_shape=(shape, shape),
        in_specs=[SM] + [VM] * 5 + [ANY],
        out_specs=[VM] * 2,
        scratch_shapes=[
            pltpu.VMEM((2 * BLOCK, heads * DK), bf16),
            pltpu.VMEM(weights.shape, bf16),
            pltpu.SemaphoreType.DMA,
        ],
        compiler_params=params(),
        cost_estimate=pl.CostEstimate(
            flops=10**9, bytes_accessed=5 * 10**6, transcendentals=0
        ),
        name="mixer_out",
    )(place, own, other, shard_query, free, gain, weights)


def up_kernel(place, own, other, gain, weights, lifted, normed, held, sem):
    copy = pltpu.make_async_copy(weights, held, sem)
    copy.start()
    core = place[1]
    for u, ref in enumerate((own, other)):
        slot = core if u == 0 else 1 - core

        @pl.loop(0, BLOCK // 32)
        def _(r):
            rows = pl.ds(pl.multiple_of(r * 32, 32), 32)
            value = ref[rows, :].astype(f32)
            inverse = lax.rsqrt(jnp.mean(value * value, axis=1, keepdims=True) + epsilon)
            target = pl.ds(pl.multiple_of(slot * BLOCK + r * 32, 32), 32)
            normed[target, :] = (value * inverse * gain[...].astype(f32)).astype(bf16)

    copy.wait()
    lifted[...] = dot(normed[...], held[...]).astype(bf16)


def up_project(place, own, other, gain, weights):
    return pl.pallas_call(
        up_kernel,
        out_shape=jax.ShapeDtypeStruct((2 * BLOCK, weights.shape[1]), bf16),
        in_specs=[SM, VM, VM, VM, ANY],
        out_specs=VM,
        scratch_shapes=[
            pltpu.VMEM((2 * BLOCK, weights.shape[0]), bf16),
            pltpu.VMEM(weights.shape, bf16),
            pltpu.SemaphoreType.DMA,
        ],
        compiler_params=params(),
        cost_estimate=pl.CostEstimate(
            flops=2 * 10**9, bytes_accessed=8 * 10**6, transcendentals=0
        ),
        name="up_project",
    )(place, own, other, gain, weights)


def gelu_of(x):
    inner = 0.7978845608028654 * (x + 0.044715 * (x * x * x))
    return 0.5 * x * (1.0 + jnp.tanh(inner))


def down_kernel(n_out, order, outer, inside, before, after, taps, weights, *refs):
    outs = refs[:n_out]
    act, padded, held, sem = refs[n_out:]
    copies = [
        pltpu.make_async_copy(weights.at[order[p]], held.at[p], sem.at[p]) for p in range(n_out)
    ]
    for copy in copies:
        copy.start()
    count = act.shape[0]
    padded[7:8, :] = before[...].astype(f32)
    padded[8 : 8 + BLOCK, :] = outer[0:BLOCK, :].astype(f32)
    padded[8 + BLOCK : 8 + count - BLOCK, :] = inside[...].astype(f32)
    padded[8 + count - BLOCK : 8 + count, :] = outer[BLOCK:, :].astype(f32)
    padded[8 + count : 9 + count, :] = after[...].astype(f32)

    @pl.loop(0, count // 32)
    def _(r):
        base = pl.multiple_of(r * 32, 32)
        window = padded[pl.ds(base, 48), :]
        value = (
            taps[0:1, :] * window[7:39, :]
            + taps[1:2, :] * window[8:40, :]
            + taps[2:3, :] * window[9:41, :]
        )
        act[pl.ds(base, 32), :] = gelu_of(value).astype(bf16)

    for p in range(n_out):
        copies[p].wait()
        outs[p][...] = dot(act[...], held[p]).astype(bf16)


def down_project(order, outer, inside, before, after, taps, weights, n_out):
    hidden, part = weights.shape[1:]
    count = outer.shape[0] + inside.shape[0]
    shape = jax.ShapeDtypeStruct((count, part), bf16)
    results = pl.pallas_call(
        functools.partial(down_kernel, n_out),
        out_shape=[shape] * n_out + [jax.ShapeDtypeStruct((count, hidden), bf16)],
        in_specs=[SM] + [VM] * 5 + [ANY],
        out_specs=[VM] * (n_out + 1),
        scratch_shapes=[
            pltpu.VMEM((count + 16, hidden), f32),
            pltpu.VMEM((n_out, hidden, part), bf16),
            pltpu.SemaphoreType.DMA((n_out,)),
        ],
        compiler_params=params(),
        cost_estimate=pl.CostEstimate(
            flops=3 * 10**9, bytes_accessed=8 * 10**6, transcendentals=10**6
        ),
        name="down_project",
    )(order, outer, inside, before, after, taps, weights)
    return results[:n_out], results[n_out]


def rest_kernel(n_out, order, act, weights, *refs):
    outs = refs[:n_out]
    held, sem = refs[n_out:]
    copies = [
        pltpu.make_async_copy(weights.at[order[p]], held.at[p], sem.at[p]) for p in range(n_out)
    ]
    for copy in copies:
        copy.start()
    for p in range(n_out):
        copies[p].wait()
        outs[p][...] = dot(act[...], held[p]).astype(bf16)


def rest_project(order, act, weights, n_out):
    hidden, part = weights.shape[1:]
    shape = jax.ShapeDtypeStruct((act.shape[0], part), bf16)
    return pl.pallas_call(
        functools.partial(rest_kernel, n_out),
        out_shape=[shape] * n_out,
        in_specs=[SM, VM, ANY],
        out_specs=[VM] * n_out,
        scratch_shapes=[
            pltpu.VMEM((n_out, hidden, part), bf16),
            pltpu.SemaphoreType.DMA((n_out,)),
        ],
        compiler_params=params(),
        cost_estimate=pl.CostEstimate(
            flops=2 * 10**9, bytes_accessed=6 * 10**6, transcendentals=0
        ),
        name="rest_project",
    )(order, act, weights)


def core_swap(value, n):
    return lax.ppermute(value, "head", [(i, i ^ 1) for i in range(n)])


def y_shift(value, n, step):
    return lax.ppermute(value, "head", [(i, (i + 2 * step) % n) for i in range(n)])


def pair_swap(value, n):
    return lax.ppermute(value, "seq", [(i, i ^ 1) for i in range(n)])


def later(value, n, step):
    return lax.ppermute(value, "seq", [(i, i + 2 * step) for i in range(n - 2 * step)])


def widened(matrix, n, part, width):
    cols = matrix.shape[1]
    return jnp.pad(matrix.reshape(n, part, cols), ((0, 0), (0, width - part), (0, 0))).reshape(
        n * width, cols
    )


def shards(
    tokens,
    norm_gain,
    w_query,
    w_key,
    w_value,
    w_decay,
    w_beta,
    head_rates,
    head_gain,
    w_out,
    ffn_gain,
    w_up,
    conv_taps,
    w_down,
):
    n = lax.axis_size("head")
    seqs = lax.axis_size("seq")
    me = lax.axis_index("head")
    at = lax.axis_index("seq")
    core = me % 2
    parity = at % 2
    ys = n // 2
    count, part = tokens.shape
    heads = w_query.shape[1] // DK
    half = heads // 2
    hidden = w_up.shape[1]
    width = -(-part // 128) * 128
    features = n * part

    along = [tokens] + [y_shift(tokens, n, d) for d in range(1, ys)]
    pieces, order = [], []
    for d, piece in enumerate(along):
        from_here = (me + n - 2 * d) % n
        pieces += [piece, core_swap(piece, n)]
        order += [from_here, from_here ^ 1]
    order = jnp.stack(order).astype(jnp.int32)

    gates = jnp.concatenate([w_decay, w_beta], axis=1)
    gates = jnp.pad(gates, ((0, 0), (0, 128 - 2 * heads)))
    w_kvg = widened(jnp.concatenate([w_key, w_value, gates], axis=1), n, part, width)
    w_q = widened(w_query, n, part, width)
    gain_rows = jnp.pad(
        norm_gain.astype(f32).reshape(n, part), ((0, 0), (0, width - part))
    )
    empty = jnp.zeros((heads,), f32)
    fill = jnp.zeros((128 - 2 * heads,), f32)
    rates = jnp.stack(
        [
            jnp.concatenate([head_rates[0], empty, fill]),
            jnp.concatenate([empty, head_rates[1], fill]),
        ]
    )
    rates = jnp.pad(rates, ((0, 6), (0, 0)))
    w_parts = w_down.reshape(hidden, n, part).transpose(1, 0, 2)

    normed, keys, erased, entry, maps, totals = block_maps(
        order, pieces, gain_rows, rates, w_kvg, heads, width
    )

    place = jnp.stack([parity, core]).astype(jnp.int32)
    own_maps = lax.dynamic_slice_in_dim(maps, parity * half, half, 0)
    sent_maps = lax.dynamic_slice_in_dim(maps, (1 - parity) * half, half, 0)
    other_maps = pair_swap(sent_maps, seqs)
    query = queries(order, normed, w_q, width)
    pair, first, done = pair_maps(place, own_maps, other_maps)
    pairs = [later(pair, seqs, d) for d in range(seqs // 2 - 1, 0, -1)]
    shard_query, free = block_outputs(query, keys, erased, entry, totals, done, heads)
    kept_state, given_state = start_states(place, first, pairs)
    other_state = pair_swap(given_state, seqs)

    by_place = [None] * n
    whole = jnp.zeros((count, n, part), bf16)
    for j in range(n):
        block = pieces[0]
        for p in range(1, n):
            block = jnp.where(order[p] == j, pieces[p], block)
        by_place[j] = block
    whole = jnp.concatenate(by_place, axis=1)

    blocks = count // BLOCK
    head_scale = head_gain.reshape(1, DK)
    ffn_scale = ffn_gain.reshape(1, features)
    lifted = []
    middles = [None] * blocks
    for units in ((0, 3), (1, 2)):
        give, keep = mixer_out(
            place, kept_state, other_state, shard_query, free, head_scale, w_out, heads, units
        )
        arrived = core_swap(give, n)
        chip = (keep.astype(f32) + arrived.astype(f32)).astype(bf16)
        row = jnp.where(core == 0, units[0], units[1]) * BLOCK
        total = lax.dynamic_slice_in_dim(whole, row, BLOCK, 0).astype(f32) + chip.astype(f32)
        for d in range(1, ys):
            total = total + y_shift(chip, n, d).astype(f32)
        mid_own = total.astype(bf16)
        mid_other = core_swap(mid_own, n)
        lifted.append(up_project(place, mid_own, mid_other, ffn_scale, w_up))
        middles[units[0]] = jnp.where(core == 0, mid_own, mid_other)
        middles[units[1]] = jnp.where(core == 0, mid_other, mid_own)
    outer, inside = lifted

    up = [(i, i + 1) for i in range(seqs - 1)]
    down = [(i + 1, i) for i in range(seqs - 1)]
    before = lax.ppermute(outer[2 * BLOCK - 1 : 2 * BLOCK], "seq", up)
    after = lax.ppermute(outer[0:1], "seq", down)

    target, order_far = [], []
    for d in range(1, ys):
        there = (me + 2 * d) % n
        order_far += [there ^ 1, there]
    order_far = jnp.stack(order_far).astype(jnp.int32)
    order_near = jnp.stack([me ^ 1, me]).astype(jnp.int32)
    taps = conv_taps.astype(f32)
    far, act = down_project(
        order_far, outer, inside, before, after, taps, w_parts, 2 * (ys - 1)
    )
    near_give, near_keep = rest_project(order_near, act, w_parts, 2)
    total = near_keep.astype(f32)
    for d in range(1, ys):
        chip = (
            far[2 * d - 1].astype(f32) + core_swap(far[2 * d - 2], n).astype(f32)
        ).astype(bf16)
        total = total + y_shift(chip, n, d).astype(f32)
    total = total + core_swap(near_give, n).astype(f32)
    middle = jnp.concatenate(middles, axis=0)
    middle_part = lax.dynamic_slice_in_dim(middle, me * part, part, 1)
    return (middle_part.astype(f32) + total).astype(bf16)


def solution(mesh):
    placed = (
        P("seq", "head"),
        P(),
        P(None, "head"),
        P(None, "head"),
        P(None, "head"),
        P(None, "head"),
        P(None, "head"),
        P(None, "head"),
        P(),
        P("head", None),
        P(),
        P(None, "head"),
        P(None, "head"),
        P("head", None),
    )
    return jax.shard_map(
        shards, mesh=mesh, in_specs=placed, out_specs=P("seq", "head"), check_vma=False
    )
```

time: 379 us -> 214 us (0.56); the launches traced: 374 us -> 213 us
  waiting for transfers between devices: 208 us -> 38.9 us
  matrix products: 111 us -> 0 us
  Pallas kernels: 0 us -> 76.9 us
  local copies, waits for them, and re-layouts: 18.7 us -> 53.6 us
  starting transfers between devices: 7.08 us -> 22.1 us
  between operations: 13.7 us -> 0.4 us
  other arithmetic: 14.9 us -> 20.7 us
    dot_general x48 -> x0, matrix products: 111 us -> none  [the longest x12 18.8 us: batch_product(): jnp.einsum('hij,hjk->hik', left_maps, right_maps, precision=exact_mode)]
    all_gather x3 -> x0, waiting for transfers between devices: 103 us -> none  [the longest x2 77.9 us: entering(): lax.all_gather(a.astype(kind), axis)]
    pallas_call x0 -> x11, Pallas kernels: none -> 76.9 us  [the longest x1 21.8 us: block_maps(): pl.pallas_call(functools.partial(maps_kernel, n, width, heads), out_shape...]
    psum x1 -> x0, waiting for transfers between devices: 58.5 us -> none  [shards(): lax.psum(partial_out.astype(jnp.bfloat16), 'head').astype(jnp.float32)]
    reduce_scatter x1 -> x0, waiting for transfers between devices: 32.1 us -> none  [shards(): lax.psum_scatter(ffn_partial.astype(jnp.bfloat16), 'head', scatter_dimens...]
    ppermute x2 -> x19, waiting for transfers between devices: 13.5 us -> 38.9 us  [the longest x4 33 us: y_shift(): lax.ppermute(value, 'head', [(i, (i + 2 * step) % n) for i in range(n)])]
    ppermute x2 -> x19, starting transfers between devices: 6.91 us -> 22.1 us  [the longest x3 6.25 us: later(): lax.ppermute(value, 'seq', [(i, i + 2 * step) for i in range(n - 2 * step)])]
    ppermute x0 -> x12, local copies, waits for them, and re-layouts: none -> 10.5 us  [the longest x8 6.5 us: core_swap(): return lax.ppermute(value, 'head', [(i, i ^ 1) for i in range(n)])]
  transfers between devices with their start and end apart: 7 -> 19, of which waited for: 7 -> 6; matrix products, arithmetic and copies ran while one was open for 1% -> 28% of each run, Pallas kernels for 0% -> 17%
where the time goes in v1:
time: 214 us; the launch traced here: 213 us
  Pallas kernels  76.9 us (36%)
  local copies, waits for them, and re-layouts  53.6 us (25%)
  waiting for transfers between devices  38.9 us (18%)
  starting transfers between devices  22.1 us (10%)
  other arithmetic  20.7 us (10%)
    ppermute x4, waiting for transfers between devices, y_shift(): lax.ppermute(value, 'head', [(i, (i + 2 * step) % n) for i in range(n)])  33 us
    pallas_call x1, Pallas kernels, block_maps(): pl.pallas_call(functools.partial(maps_kernel, n, width, heads), out_shape...  21.8 us
    pallas_call x2, Pallas kernels, up_project(): pl.pallas_call(up_kernel, out_shape=jax.ShapeDtypeStruct((2 * BLOCK, weig...  13.9 us
    reshape x1, local copies, waits for them, and re-layouts, shards(): w_parts = w_down.reshape(hidden, n, part).transpose(1, 0, 2)  9.77 us
    pallas_call x2, Pallas kernels, mixer_out(): pl.pallas_call(functools.partial(mixer_kernel, heads, units), out_shape=(...  9.5 us
    pallas_call x1, Pallas kernels, down_project(): pl.pallas_call(functools.partial(down_kernel, n_out), out_shape=[shape] *...  9.17 us
    unnamed x45, local copies, waits for them, and re-layouts  8.28 us
    pad x2, local copies, waits for them, and re-layouts, widened(): jnp.pad(matrix.reshape(n, part, cols), ((0, 0), (0, width - part), (0, 0)))  7.14 us
  transfers between devices with their start and end apart: 19, of which 6 were waited for; matrix products, arithmetic and copies ran while one was open for 28% of the time, Pallas kernels for 17%

profile of v1, /device:TPU:16, one launch (start us, length us, event | category | flops | bytes accessed | tf_op | source)
XLA Modules:
  0.0 212.6 jit_solution(12903254129157988641)
XLA Ops:
  0.0 1.5 collective-permute-start
  2.6 5.5 %fusion.1 = bf16[2240,1152]{1,0:T(8,128)(2,1)} fusion(bf16[2240,8]{1,0:T(8,128)(2,1)S(1)} %copy.85, bf16[2240,512]{1,0:T(8,128)(2,1)} %param.18, bf16[2240,512]{1,0:T(8,128)(2,1)} %param.17), kind=kLoop, calls=%fused_computation.2 | loop fusion | flops 20643840 | bytes 9784320 | tf_op jit(solution)/shard_map/concatenate | solution.py:584
  8.1 6.8 %collective-permute-done = bf16[512,560]{0,1:T(8,128)(2,1)S(1)} collective-permute-done((bf16[512,560]{0,1:T(8,128)(2,1)}, bf16[512,560]{0,1:T(8,128)(2,1)S(1)}, u32[]{:S(2)}, u32[]{:S(2)}) %collective-permute-start) | collective-permute-done | bytes 573472 | tf_op jit(solution)/shard_map/ppermute | solution.py:526
  15.6 1.1 copy.39.refs_0_
  16.8 5.4 %pad.26 = bf16[4,640,1152]{2,1,0:T(8,128)(2,1)} pad(bf16[4,560,1152]{2,1,0:T(8,128)(2,1)} %bitcast.25, bf16[]{:T(256)} %constant.60.clone.1), padding=0_0x0_80x0_0 | pad | bytes 11059202 | tf_op jit(solution)/shard_map/jit(_pad)/pad | solution.py:539
  23.5 1.1 copy.40.refs_2_
  24.6 1.1 copy.38.refs_1_
  25.7 1.1 copy.41.refs_3_
  26.8 21.8 %block_maps.1 = (bf16[512,2560]{1,0:T(8,128)(2,1)}, bf16[512,512]{1,0:T(8,128)(2,1)}, bf16[512,1024]{1,0:T(8,128)(2,1)}, bf16[3,128,1024]{2,1,0:T(8,128)(2,1)}, ...) custom-call(s32[4]{0:T(128)} %pad_add_fusion.1.order, bf16[512,560]{1,0:T(8,128)(2,1)} %copy.39.refs_0_, ...), custom_call_target="tpu_custom_call" | custom-call | flops 8000000000 | bytes 12000000 | tf_op jit(solution)/shard_map/block_maps/pallas_call | solution.py:174
  48.6 1.6 constant_dynamic-slice_fusion
  50.3 1.5 collective-permute-start.3
  51.7 1.7 pad.27
  53.4 4.3 %copy.59.weights = bf16[512,2240]{1,0:T(8,128)(2,1)} copy(bf16[512,2240]{0,1:T(8,128)(2,1)} %param.23) | data formatting | bytes 4587520 | tf_op args[9]
  59.0 1.8 pair_maps.1
  61.5 1.3 collective-permute-start.5
  62.8 4.3 %collective-permute-start.6 = (bf16[2,128,256]{2,1,0:T(8,128)(2,1)}, bf16[2,128,256]{2,1,0:T(8,128)(2,1)S(1)}, u32[]{:S(2)}, u32[]{:S(2)}) collective-permute-start(bf16[2,128,256]{2,1,0:T(8,128)(2,1)} %get-tuple-element.29), channel_id=1, source_target_pairs={{0,8},{4,12},{8,16},{12,20},{16,24},{20,28},{1,9},{5,13},{9,17},{1... | collective-permute-start | bytes 393224 | tf_op jit(solution)/shard_map/ppermute | solution.py:534
  67.1 6.0 %queries.1.query = bf16[512,512]{1,0:T(8,128)(2,1)} custom-call(s32[4]{0:T(128)} %pad_add_fusion.1.order, bf16[512,2560]{1,0:T(8,128)(2,1)} %get-tuple-element.32.normed, bf16[2560,512]{1,0:T(8,128)(2,1)} %bitcast.28), custom_call_target="tpu_custom_call" | custom-call | flops 2000000000 | bytes 6000000 | tf_op jit(solution)/shard_map/queries/pallas_call | solution.py:225
  74.0 4.9 %collective-permute-done.6.refs_2_ = bf16[2,128,256]{2,1,0:T(8,128)(2,1)S(1)} collective-permute-done((bf16[2,128,256]{2,1,0:T(8,128)(2,1)}, bf16[2,128,256]{2,1,0:T(8,128)(2,1)S(1)}, u32[]{:S(2)}, u32[]{:S(2)}) %collective-permute-start.6) | collective-permute-done | bytes 131104 | tf_op jit(solution)/shard_map/ppermute | solution.py:534
  79.5 2.4 %start_states.1 = (bf16[2,128,128]{2,1,0:T(8,128)(2,1)}, bf16[2,128,128]{2,1,0:T(8,128)(2,1)}) custom-call(s32[2]{0:T(128)} %pad_add_fusion.place, bf16[2,128,256]{2,1,0:T(8,128)(2,1)} %get-tuple-element.28.first, bf16[2,128,256]{2,1,0:T(8,128)(2,1)} %copy-done.11, bf16[2,128,256]{2,1,0:T(8,128)(2,1)} %copy-done.12, bf16[2,128,256]{2,1,0:T(8,128)(2,1)} %copy-done.13), custom_call_target="tpu_custom_call" | custom-call | tf_op jit(solution)/shard_map/start_states/pallas_call | solution.py:335
  82.5 5.4 %block_outputs.1 = (bf16[512,512]{1,0:T(8,128)(2,1)}, f32[512,512]{1,0:T(8,128)}) custom-call(bf16[512,512]{1,0:T(8,128)(2,1)} %queries.1.query, bf16[512,512]{1,0:T(8,128)(2,1)} %get-tuple-element.33.keys, bf16[512,1024]{1,0:T(8,128)(2,1)} %get-tuple-element.34.erased, bf16[3,128,1024]{2,1,0:T(8,128)(2,1)} %get-tuple-element.35.entry, ...), custom_call_target="tpu_custom_call" | custom-call | flops 3000000000 | bytes 4000000 | tf_op jit(solution)/shard_map/block_outputs/pallas_call | solution.py:268
  88.5 4.7 %mixer_out.2 = (bf16[128,2240]{1,0:T(8,128)(2,1)}, bf16[128,2240]{1,0:T(8,128)(2,1)}) custom-call(s32[2]{0:T(128)} %pad_add_fusion.place, bf16[2,128,128]{2,1,0:T(8,128)(2,1)} %get-tuple-element.30.own, bf16[2,128,128]{2,1,0:T(8,128)(2,1)} %copy-done.10, bf16[512,512]{1,0:T(8,128)(2,1)} %get-tuple-element.38.shard_query, f32[512,512]{1,0:T(8,128)} %get-tuple-element.39.free, ...), custom_call_target="tpu_custom_call" | custom-call | flops 1000000000 | bytes 5000000 | tf_op jit(solution)/shard_map/mixer_out/pallas_call | solution.py:373
  93.2 1.4 copy.60
  94.7 4.8 %mixer_out.3 = (bf16[128,2240]{1,0:T(8,128)(2,1)}, bf16[128,2240]{1,0:T(8,128)(2,1)}) custom-call(s32[2]{0:T(128)} %pad_add_fusion.place, bf16[2,128,128]{2,1,0:T(8,128)(2,1)} %get-tuple-element.30.own, bf16[2,128,128]{2,1,0:T(8,128)(2,1)} %copy-done.10, bf16[512,512]{1,0:T(8,128)(2,1)} %get-tuple-element.38.shard_query, f32[512,512]{1,0:T(8,128)} %get-tuple-element.39.free, ...), custom_call_target="tpu_custom_call" | custom-call | flops 1000000000 | bytes 5000000 | tf_op jit(solution)/shard_map/mixer_out/pallas_call | solution.py:373
  99.5 1.4 copy.67
  102.8 1.5 collective-permute-start.9
  106.3 3.0 %select_select_fusion = (bf16[512,560]{1,0:T(8,128)(2,1)S(1)}, bf16[512,560]{1,0:T(8,128)(2,1)S(1)}, bf16[512,560]{1,0:T(8,128)(2,1)S(1)}, bf16[512,560]{1,0:T(8,128)(2,1)}) fusion(bf16[512,560]{1,0:T(8,128)(2,1)} %copy.41.refs_3_, bf16[512,560]{1,0:T(8,128)(2,1)} %copy.40.refs_2_, bf16[512,560]{1,0:T(8,128)(2,1)} %copy.38.refs_1_, ...), kind=kLoop, calls=%fused_computation.16 | loop fusion | flops 3440640 | bytes 4587532 | tf_op jit(solution)/shard_map/jit(_where)/select_n | solution.py:620
  109.3 4.6 %concatenate.18 = bf16[512,2240]{1,0:T(8,128)(2,1)} concatenate(bf16[512,560]{1,0:T(8,128)(2,1)} %get-tuple-element.52, bf16[512,560]{1,0:T(8,128)(2,1)S(1)} %get-tuple-element.51, bf16[512,560]{1,0:T(8,128)(2,1)S(1)} %get-tuple-element.50, bf16[512,560]{1,0:T(8,128)(2,1)S(1)} %get-tuple-element.49), dimensions={1} | concatenate | bytes 4587520 | tf_op jit(solution)/shard_map/concatenate | solution.py:622
  113.9 5.1 %collective-permute-done.9 = bf16[128,2240]{0,1:T(8,128)(2,1)} collective-permute-done((bf16[128,2240]{0,1:T(8,128)(2,1)}, bf16[128,2240]{0,1:T(8,128)(2,1)}, u32[]{:S(2)}, u32[]{:S(2)}) %collective-permute-start.9) | collective-permute-done | bytes 573472 | tf_op jit(solution)/shard_map/ppermute | solution.py:526
  119.0 1.3 copy.63
  120.3 10.1 %collective-permute-done.12 = bf16[128,2240]{0,1:T(8,128)(2,1)} collective-permute-done((bf16[128,2240]{0,1:T(8,128)(2,1)}, bf16[128,2240]{0,1:T(8,128)(2,1)}, u32[]{:S(2)}, u32[]{:S(2)}) %collective-permute-start.12) | collective-permute-done | bytes 573472 | tf_op jit(solution)/shard_map/ppermute | solution.py:526
  130.4 1.3 copy.70
  131.7 1.7 add_convert_fusion.2
  134.4 9.8 %copy.77 = bf16[1400,4,560]{2,0,1:T(8,128)(2,1)} copy(bf16[1400,4,560]{0,2,1:T(8,128)(2,1)} %bitcast.26) | data formatting | bytes 12544000 | tf_op jit(solution)/shard_map/reshape | solution.py:598
  147.0 1.1 copy.65.other
  148.1 6.9 %up_project.2.outer = bf16[256,1400]{1,0:T(8,128)(2,1)} custom-call(s32[2]{0:T(128)} %pad_add_fusion.place, bf16[128,2240]{1,0:T(8,128)(2,1)} %copy-done, bf16[128,2240]{1,0:T(8,128)(2,1)} %copy.65.other, bf16[1,2240]{1,0:T(2,128)(2,1)} %reshape.31.gain, bf16[2240,1400]{1,0:T(8,128)(2,1)} %weights.5), custom_call_target="tpu_custom_call" | custom-call | flops 2000000000 | bytes 8000000 | tf_op jit(solution)/shard_map/up_project/pallas_call | solution.py:411
  155.8 3.4 %collective-permute-start.14 = (bf16[1,1400]{1,0:T(2,128)(2,1)S(1)}, bf16[1,1400]{1,0:T(2,128)(2,1)S(1)}, u32[]{:S(2)}, u32[]{:S(2)}) collective-permute-start(bf16[1,1400]{1,0:T(2,128)(2,1)S(1)} %get-tuple-element.60), channel_id=1, source_target_pairs={{0,4},{4,8},{8,12},{12,16},{16,20},{20,24},{24,28},{1,5},{5,9},{9,... | collective-permute-start | bytes 8408 | tf_op jit(solution)/shard_map/ppermute | solution.py:648
  159.2 3.6 %collective-permute-start.15 = (bf16[1,1400]{1,0:T(2,128)(2,1)S(1)}, bf16[1,1400]{1,0:T(2,128)(2,1)S(1)}, u32[]{:S(2)}, u32[]{:S(2)}) collective-permute-start(bf16[1,1400]{1,0:T(2,128)(2,1)S(1)} %get-tuple-element.59), channel_id=1, source_target_pairs={{4,0},{8,4},{12,8},{16,12},{20,16},{24,20},{28,24},{5,1},{9,5},{13... | collective-permute-start | bytes 8408 | tf_op jit(solution)/shard_map/ppermute | solution.py:649
  163.9 6.9 %up_project.3.inside = bf16[256,1400]{1,0:T(8,128)(2,1)} custom-call(s32[2]{0:T(128)} %pad_add_fusion.place, bf16[128,2240]{1,0:T(8,128)(2,1)} %copy-done.2, bf16[128,2240]{1,0:T(8,128)(2,1)} %copy.72.other, bf16[1,2240]{1,0:T(2,128)(2,1)} %reshape.31.gain, bf16[2240,1400]{1,0:T(8,128)(2,1)} %weights.5), custom_call_target="tpu_custom_call" | custom-call | flops 2000000000 | bytes 8000000 | tf_op jit(solution)/shard_map/up_project/pallas_call | solution.py:411
  171.4 9.2 %down_project.1 = (bf16[512,560]{1,0:T(8,128)(2,1)}, bf16[512,560]{1,0:T(8,128)(2,1)}, bf16[512,1400]{1,0:T(8,128)(2,1)}) custom-call(s32[2]{0:T(128)} %pad_add_fusion.3.order, bf16[256,1400]{1,0:T(8,128)(2,1)} %up_project.2.outer, bf16[256,1400]{1,0:T(8,128)(2,1)} %up_project.3.inside, bf16[1,1400]{1,0:T(2,128)(2,1)} %copy-done.19, ...), custom_call_target="tpu_custom_call" | custom-call | flops 3000000000 | bytes 8000000 | tf_op jit(solution)/shard_map/down_project/pallas_call | solution.py:469
  180.6 1.3 copy.78
  182.9 7.0 %rest_project.1 = (bf16[512,560]{1,0:T(8,128)(2,1)}, bf16[512,560]{1,0:T(8,128)(2,1)}) custom-call(s32[2]{0:T(128)} %pad_add_fusion.2.order, bf16[512,1400]{1,0:T(8,128)(2,1)} %get-tuple-element.44.act, bf16[4,1400,560]{2,1,0:T(8,128)(2,1)} %bitcast.24), custom_call_target="tpu_custom_call" | custom-call | flops 2000000000 | bytes 6000000 | tf_op jit(solution)/shard_map/rest_project/pallas_call | solution.py:504
  190.0 2.1 copy.82
  192.9 1.2 add_convert_fusion.1
  194.3 1.6 collective-permute-start.17
  195.9 1.1 broadcast_select_fusion
  197.0 1.4 copy.83
  198.4 11.0 %collective-permute-done.17 = bf16[512,560]{0,1:T(8,128)(2,1)S(1)} collective-permute-done((bf16[512,560]{0,1:T(8,128)(2,1)S(1)}, bf16[512,560]{0,1:T(8,128)(2,1)S(1)}, u32[]{:S(2)}, u32[]{:S(2)}) %collective-permute-start.17) | collective-permute-done | bytes 573472 | tf_op jit(solution)/shard_map/ppermute | solution.py:526
  209.7 1.9 add_convert_fusion
  (97 shorter events, 21.3 us)
Async XLA Ops:
  0.0 14.9 %collective-permute-start = (bf16[512,560]{0,1:T(8,128)(2,1)}, bf16[512,560]{0,1:T(8,128)(2,1)S(1)}, u32[]{:S(2)}, u32[]{:S(2)}) collective-permute-start(bf16[512,560]{0,1:T(8,128)(2,1)} %param.14), channel_id=1, source_target_pairs={{0,2},{1,3},{2,0},{3,1},{4,6},{5,7},{6,4},{7,5},{8,10},{9,11},{10,... | collective-permute-start | bytes 1720328 | tf_op jit(solution)/shard_map/ppermute | solution.py:526
  1.5 23.1 %collective-permute-start.2 = (bf16[512,560]{0,1:T(8,128)(2,1)}, bf16[512,560]{0,1:T(8,128)(2,1)S(1)}, u32[]{:S(2)}, u32[]{:S(2)}) collective-permute-start(bf16[512,560]{0,1:T(8,128)(2,1)} %param.14), channel_id=1, source_target_pairs={{0,1},{1,0},{2,3},{3,2},{4,5},{5,4},{6,7},{7,6},{8,9},{9,8},{10,11... | collective-permute-start | bytes 1720328 | tf_op jit(solution)/shard_map/ppermute | solution.py:522
  2.6 13.0 %copy-start.9 = (bf16[512,560]{0,1:T(8,128)(2,1)S(1)}, bf16[512,560]{0,1:T(8,128)(2,1)}, u32[]{:S(2)}) copy-start(bf16[512,560]{0,1:T(8,128)(2,1)} %param.14) | copy-start | bytes 1720324
  2.6 14.1 %copy-start.16 = (bf16[2240]{0:T(1024)(128)(2,1)S(1)}, bf16[2240]{0:T(1024)(128)(2,1)}, u32[]{:S(2)}) copy-start(bf16[2240]{0:T(1024)(128)(2,1)} %param.15) | copy-start | bytes 13444
  14.9 10.8 %collective-permute-start.1 = (bf16[512,560]{0,1:T(8,128)(2,1)S(1)}, bf16[512,560]{0,1:T(8,128)(2,1)S(1)}, u32[]{:S(2)}, u32[]{:S(2)}) collective-permute-start(bf16[512,560]{0,1:T(8,128)(2,1)S(1)} %collective-permute-done), channel_id=1, source_target_pairs={{0,1},{1,0},{2,3},{3,2},{4,5},{5,4},{6,7},{7,6},{8,9},{9,8},{10,11... | collective-permute-start | bytes 1720328 | tf_op jit(solution)/shard_map/ppermute | solution.py:522
  16.8 5.4 %copy-start.18 = (f32[2,4]{1,0:T(2,128)S(1)}, f32[2,4]{1,0:T(2,128)}, u32[]{:S(2)}) copy-start(f32[2,4]{1,0:T(2,128)} %param.21) | copy-start | bytes 100
  26.8 25.0 %copy-start.6 = (bf16[2240,512]{1,0:T(8,128)(2,1)S(1)}, bf16[2240,512]{1,0:T(8,128)(2,1)}, u32[]{:S(2)}) copy-start(bf16[2240,512]{1,0:T(8,128)(2,1)} %param.16) | copy-start | bytes 6881284
  50.3 8.1 %collective-permute-start.3 = (bf16[2,128,256]{2,1,0:T(8,128)(2,1)S(1)}, bf16[2,128,256]{2,1,0:T(8,128)(2,1)S(1)}, u32[]{:S(2)}, u32[]{:S(2)}) collective-permute-start(bf16[2,128,256]{2,1,0:T(8,128)(2,1)S(1)} %get-tuple-element.61), channel_id=1, source_target_pairs={{0,4},{4,0},{8,12},{12,8},{16,20},{20,16},{24,28},{28,24},{1,5},{5... | collective-permute-start | bytes 393224 | tf_op jit(solution)/shard_map/ppermute | solution.py:530
  58.4 0.7 copy-start.14
  60.8 12.2 %collective-permute-start.4 = (bf16[2,128,256]{2,1,0:T(8,128)(2,1)}, bf16[2,128,256]{2,1,0:T(8,128)(2,1)S(1)}, u32[]{:S(2)}, u32[]{:S(2)}) collective-permute-start(bf16[2,128,256]{2,1,0:T(8,128)(2,1)} %get-tuple-element.29), channel_id=1, source_target_pairs={{0,24},{4,28},{1,25},{5,29},{2,26},{6,30},{3,27},{7,31}} | collective-permute-start | bytes 393224 | tf_op jit(solution)/shard_map/ppermute | solution.py:534
  61.5 12.5 %collective-permute-start.5 = (bf16[2,128,256]{2,1,0:T(8,128)(2,1)}, bf16[2,128,256]{2,1,0:T(8,128)(2,1)S(1)}, u32[]{:S(2)}, u32[]{:S(2)}) collective-permute-start(bf16[2,128,256]{2,1,0:T(8,128)(2,1)} %get-tuple-element.29), channel_id=1, source_target_pairs={{0,16},{4,20},{8,24},{12,28},{1,17},{5,21},{9,25},{13,29},{2,18},{... | collective-permute-start | bytes 393224 | tf_op jit(solution)/shard_map/ppermute | solution.py:534
  62.8 16.1 %collective-permute-start.6 = (bf16[2,128,256]{2,1,0:T(8,128)(2,1)}, bf16[2,128,256]{2,1,0:T(8,128)(2,1)S(1)}, u32[]{:S(2)}, u32[]{:S(2)}) collective-permute-start(bf16[2,128,256]{2,1,0:T(8,128)(2,1)} %get-tuple-element.29), channel_id=1, source_target_pairs={{0,8},{4,12},{8,16},{12,20},{16,24},{20,28},{1,9},{5,13},{9,17},{1... | collective-permute-start | bytes 393224 | tf_op jit(solution)/shard_map/ppermute | solution.py:534
  73.1 5.8 %copy-start.11 = (bf16[2,128,256]{2,1,0:T(8,128)(2,1)}, bf16[2,128,256]{2,1,0:T(8,128)(2,1)S(1)}, u32[]{:S(2)}) copy-start(bf16[2,128,256]{2,1,0:T(8,128)(2,1)S(1)} %collective-permute-done.4.refs_0_) | copy-start | bytes 393220
  74.0 4.9 %copy-start.12 = (bf16[2,128,256]{2,1,0:T(8,128)(2,1)}, bf16[2,128,256]{2,1,0:T(8,128)(2,1)S(1)}, u32[]{:S(2)}) copy-start(bf16[2,128,256]{2,1,0:T(8,128)(2,1)S(1)} %collective-permute-done.5.refs_1_) | copy-start | bytes 393220
  78.9 0.6 copy-start.13
  82.0 5.9 %collective-permute-start.7 = (bf16[2,128,128]{2,1,0:T(8,128)(2,1)}, bf16[2,128,128]{2,1,0:T(8,128)(2,1)S(1)}, u32[]{:S(2)}, u32[]{:S(2)}) collective-permute-start(bf16[2,128,128]{2,1,0:T(8,128)(2,1)} %get-tuple-element.31), channel_id=1, source_target_pairs={{0,4},{4,0},{8,12},{12,8},{16,20},{20,16},{24,28},{28,24},{1,5},{5... | collective-permute-start | bytes 196616 | tf_op jit(solution)/shard_map/ppermute | solution.py:530
  87.9 0.6 copy-start.10
  94.6 7.0 %copy-start.8 = (bf16[128,2240]{1,0:T(8,128)(2,1)S(1)}, bf16[128,2240]{1,0:T(8,128)(2,1)}, u32[]{:S(2)}) copy-start(bf16[128,2240]{1,0:T(8,128)(2,1)} %get-tuple-element.40) | copy-start | bytes 1720324
  94.6 6.7 %collective-permute-start.8 = (bf16[128,2240]{0,1:T(8,128)(2,1)S(1)}, bf16[128,2240]{0,1:T(8,128)(2,1)S(1)}, u32[]{:S(2)}, u32[]{:S(2)}) collective-permute-start(bf16[128,2240]{0,1:T(8,128)(2,1)S(1)} %copy.60), channel_id=1, source_target_pairs={{0,1},{1,0},{2,3},{3,2},{4,5},{5,4},{6,7},{7,6},{8,9},{9,8},{10,11... | collective-permute-start | bytes 1720328 | tf_op jit(solution)/shard_map/ppermute | solution.py:522
  100.8 3.5 %collective-permute-start.11 = (bf16[128,2240]{0,1:T(8,128)(2,1)S(1)}, bf16[128,2240]{0,1:T(8,128)(2,1)S(1)}, u32[]{:S(2)}, u32[]{:S(2)}) collective-permute-start(bf16[128,2240]{0,1:T(8,128)(2,1)S(1)} %copy.67), channel_id=1, source_target_pairs={{0,1},{1,0},{2,3},{3,2},{4,5},{5,4},{6,7},{7,6},{8,9},{9,8},{10,11... | collective-permute-start | bytes 1720328 | tf_op jit(solution)/shard_map/ppermute | solution.py:522
  101.6 3.0 %copy-start.7 = (bf16[128,2240]{1,0:T(8,128)(2,1)S(1)}, bf16[128,2240]{1,0:T(8,128)(2,1)}, u32[]{:S(2)}) copy-start(bf16[128,2240]{1,0:T(8,128)(2,1)} %get-tuple-element.42) | copy-start | bytes 1720324
  102.8 16.1 %collective-permute-start.9 = (bf16[128,2240]{0,1:T(8,128)(2,1)}, bf16[128,2240]{0,1:T(8,128)(2,1)}, u32[]{:S(2)}, u32[]{:S(2)}) collective-permute-start(bf16[128,2240]{0,1:T(8,128)(2,1)} %copy.62), channel_id=1, source_target_pairs={{0,2},{1,3},{2,0},{3,1},{4,6},{5,7},{6,4},{7,5},{8,10},{9,11},{10,... | collective-permute-start | bytes 1720328 | tf_op jit(solution)/shard_map/ppermute | solution.py:526
  105.8 24.6 %collective-permute-start.12 = (bf16[128,2240]{0,1:T(8,128)(2,1)}, bf16[128,2240]{0,1:T(8,128)(2,1)}, u32[]{:S(2)}, u32[]{:S(2)}) collective-permute-start(bf16[128,2240]{0,1:T(8,128)(2,1)} %copy.69), channel_id=1, source_target_pairs={{0,2},{1,3},{2,0},{3,1},{4,6},{5,7},{6,4},{7,5},{8,10},{9,11},{10,... | collective-permute-start | bytes 1720328 | tf_op jit(solution)/shard_map/ppermute | solution.py:526
  131.7 2.1 copy-start.17
  133.4 10.8 %copy-start = (bf16[128,2240]{1,0:T(8,128)(2,1)}, bf16[128,2240]{1,0:T(8,128)(2,1)S(1)}, u32[]{:S(2)}) copy-start(bf16[128,2240]{1,0:T(8,128)(2,1)S(1)} %get-tuple-element.54.own) | copy-start | bytes 1720324
  133.4 12.7 %copy-start.2 = (bf16[128,2240]{1,0:T(8,128)(2,1)}, bf16[128,2240]{1,0:T(8,128)(2,1)S(1)}, u32[]{:S(2)}) copy-start(bf16[128,2240]{1,0:T(8,128)(2,1)S(1)} %get-tuple-element.53.own) | copy-start | bytes 1720324
  133.7 13.3 %collective-permute-start.10 = (bf16[128,2240]{0,1:T(8,128)(2,1)S(1)}, bf16[128,2240]{0,1:T(8,128)(2,1)S(1)}, u32[]{:S(2)}, u32[]{:S(2)}) collective-permute-start(bf16[128,2240]{0,1:T(8,128)(2,1)S(1)} %copy.64), channel_id=1, source_target_pairs={{0,1},{1,0},{2,3},{3,2},{4,5},{5,4},{6,7},{7,6},{8,9},{9,8},{10,11... | collective-permute-start | bytes 1720328 | tf_op jit(solution)/shard_map/ppermute | solution.py:522
  134.4 9.8 %copy-start.15 = (bf16[3,1400]{1,0:T(4,128)(2,1)S(1)}, bf16[3,1400]{1,0:T(4,128)(2,1)}, u32[]{:S(2)}) copy-start(bf16[3,1400]{1,0:T(4,128)(2,1)} %param.26) | copy-start | bytes 25204
  146.4 16.3 %collective-permute-start.13 = (bf16[128,2240]{0,1:T(8,128)(2,1)S(1)}, bf16[128,2240]{0,1:T(8,128)(2,1)S(1)}, u32[]{:S(2)}, u32[]{:S(2)}) collective-permute-start(bf16[128,2240]{0,1:T(8,128)(2,1)S(1)} %copy.71), channel_id=1, source_target_pairs={{0,1},{1,0},{2,3},{3,2},{4,5},{5,4},{6,7},{7,6},{8,9},{9,8},{10,11... | collective-permute-start | bytes 1720328 | tf_op jit(solution)/shard_map/ppermute | solution.py:522
  155.8 15.0 %collective-permute-start.14 = (bf16[1,1400]{1,0:T(2,128)(2,1)S(1)}, bf16[1,1400]{1,0:T(2,128)(2,1)S(1)}, u32[]{:S(2)}, u32[]{:S(2)}) collective-permute-start(bf16[1,1400]{1,0:T(2,128)(2,1)S(1)} %get-tuple-element.60), channel_id=1, source_target_pairs={{0,4},{4,8},{8,12},{12,16},{16,20},{20,24},{24,28},{1,5},{5,9},{9,... | collective-permute-start | bytes 8408 | tf_op jit(solution)/shard_map/ppermute | solution.py:648
  159.2 11.6 %collective-permute-start.15 = (bf16[1,1400]{1,0:T(2,128)(2,1)S(1)}, bf16[1,1400]{1,0:T(2,128)(2,1)S(1)}, u32[]{:S(2)}, u32[]{:S(2)}) collective-permute-start(bf16[1,1400]{1,0:T(2,128)(2,1)S(1)} %get-tuple-element.59), channel_id=1, source_target_pairs={{4,0},{8,4},{12,8},{16,12},{20,16},{24,20},{28,24},{5,1},{9,5},{13... | collective-permute-start | bytes 8408 | tf_op jit(solution)/shard_map/ppermute | solution.py:649
  170.8 0.6 copy-start.19
  170.8 0.6 copy-start.20
  171.4 10.6 %copy-start.3 = (bf16[128,2240]{1,0:T(8,128)(2,1)S(1)}, bf16[128,2240]{1,0:T(8,128)(2,1)}, u32[]{:S(2)}) copy-start(bf16[128,2240]{1,0:T(8,128)(2,1)} %copy-done.2) | copy-start | bytes 1720324
  171.4 10.6 %copy-start.5 = (bf16[128,2240]{1,0:T(8,128)(2,1)S(1)}, bf16[128,2240]{1,0:T(8,128)(2,1)}, u32[]{:S(2)}) copy-start(bf16[128,2240]{1,0:T(8,128)(2,1)} %copy.72.other) | copy-start | bytes 1720324
  181.9 10.6 %collective-permute-start.16 = (bf16[512,560]{0,1:T(8,128)(2,1)S(1)}, bf16[512,560]{0,1:T(8,128)(2,1)S(1)}, u32[]{:S(2)}, u32[]{:S(2)}) collective-permute-start(bf16[512,560]{0,1:T(8,128)(2,1)S(1)} %copy.78), channel_id=1, source_target_pairs={{0,1},{1,0},{2,3},{3,2},{4,5},{5,4},{6,7},{7,6},{8,9},{9,8},{10,11... | collective-permute-start | bytes 1720328 | tf_op jit(solution)/shard_map/ppermute | solution.py:522
  192.1 3.9 %copy-start.1 = (bf16[128,2240]{1,0:T(8,128)(2,1)S(1)}, bf16[128,2240]{1,0:T(8,128)(2,1)}, u32[]{:S(2)}) copy-start(bf16[128,2240]{1,0:T(8,128)(2,1)} %copy-done) | copy-start | bytes 1720324
  192.1 3.9 %copy-start.4 = (bf16[128,2240]{1,0:T(8,128)(2,1)S(1)}, bf16[128,2240]{1,0:T(8,128)(2,1)}, u32[]{:S(2)}) copy-start(bf16[128,2240]{1,0:T(8,128)(2,1)} %copy.65.other) | copy-start | bytes 1720324
  192.1 5.0 %collective-permute-start.18 = (bf16[512,560]{0,1:T(8,128)(2,1)}, bf16[512,560]{0,1:T(8,128)(2,1)}, u32[]{:S(2)}, u32[]{:S(2)}) collective-permute-start(bf16[512,560]{0,1:T(8,128)(2,1)} %copy.82), channel_id=1, source_target_pairs={{0,1},{1,0},{2,3},{3,2},{4,5},{5,4},{6,7},{7,6},{8,9},{9,8},{10,11... | collective-permute-start | bytes 1720328 | tf_op jit(solution)/shard_map/ppermute | solution.py:522
  194.3 15.0 %collective-permute-start.17 = (bf16[512,560]{0,1:T(8,128)(2,1)S(1)}, bf16[512,560]{0,1:T(8,128)(2,1)S(1)}, u32[]{:S(2)}, u32[]{:S(2)}) collective-permute-start(bf16[512,560]{0,1:T(8,128)(2,1)S(1)} %copy.80), channel_id=1, source_target_pairs={{0,2},{1,3},{2,0},{3,1},{4,6},{5,7},{6,4},{7,5},{8,10},{9,11},{10,... | collective-permute-start | bytes 1720328 | tf_op jit(solution)/shard_map/ppermute | solution.py:526

commit v2 on v1

v2 whole, which is shorter than its diff:
```python
import functools

import jax
import jax.numpy as jnp
from jax import lax
from jax.experimental import pallas as pl
from jax.experimental.pallas import tpu as pltpu
from jax.sharding import PartitionSpec as P

DK = 128
BLOCK = 128
epsilon = 1e-06
f32 = jnp.float32
bf16 = jnp.bfloat16

VM = pl.BlockSpec(memory_space=pltpu.VMEM)
SM = pl.BlockSpec(memory_space=pltpu.SMEM)
ANY = pl.BlockSpec(memory_space=pl.ANY)


def params(mebibytes):
    return pltpu.CompilerParams(vmem_limit_bytes=mebibytes * 1024 * 1024)


def cost(flops, moved):
    return pl.CostEstimate(flops=flops, bytes_accessed=moved, transcendentals=0)


def shape_of(shape, dtype=bf16):
    return jax.ShapeDtypeStruct(shape, dtype)


def dot(a, b):
    return jnp.dot(a, b, preferred_element_type=f32)


def dot_nt(a, b):
    return lax.dot_general(a, b, (((1,), (1,)), ((), ())), preferred_element_type=f32)


def dot_tn(a, b):
    return lax.dot_general(a, b, (((0,), (0,)), ((), ())), preferred_element_type=f32)


def iotas(shape):
    return lax.broadcasted_iota(jnp.int32, shape, 0), lax.broadcasted_iota(jnp.int32, shape, 1)


def column_of(row, lanes=128):
    return jnp.broadcast_to(row, (lanes, row.shape[1])).T


def square_sums(ref, features):
    tokens = ref.shape[1]

    def step(r, total):
        value = ref[pl.ds(pl.multiple_of(r * 32, 32), 32), :].astype(f32)
        value = value * value
        return total + (value[0:8] + value[8:16]) + (value[16:24] + value[24:32])

    total = lax.fori_loop(0, features // 32, step, jnp.zeros((8, tokens), f32))
    return jnp.sum(total, axis=0, keepdims=True)


def scaled_rows(ref, features, inverse, gain, target):
    full = features // 128

    def one(start, size):
        value = ref[pl.ds(start, size), :].astype(f32)
        scale = column_of(gain[:, pl.ds(start, size)].astype(f32))
        scale = jnp.concatenate([scale] * (value.shape[1] // 128), axis=1)
        target[:, pl.ds(start, size)] = (value * inverse * scale).astype(bf16).T

    @pl.loop(0, full)
    def _(f):
        one(pl.multiple_of(f * 128, 128), 128)

    if features % 128:
        one(full * 128, features % 128)


def maps_kernel(n, heads, slots, meta, *refs):
    pieces = refs[:n]
    gain, rates, gates, w_key, w_value = refs[n : n + 5]
    outs = refs[n + 5 : n + 13]
    normed, keys, erased, entry, own, sent, totals, part_a = outs[:8]
    part_b = refs[n + 13]
    whole, held_k, held_v, raw_k, raw_v, rows_at_head, total_b, beta_b, sem = refs[n + 14 :]
    features, count = whole.shape
    part = pieces[0].shape[0]
    blocks = count // BLOCK
    inner = heads * DK
    parity = meta[slots]
    copies = [
        pltpu.make_async_copy(
            pieces[p],
            whole.at[pl.ds(pl.multiple_of(meta[p] * part, 16), part)],
            sem.at[p],
        )
        for p in range(n)
    ]
    for copy in copies:
        copy.start()
    copy_k = pltpu.make_async_copy(w_key, held_k, sem.at[n])
    copy_v = pltpu.make_async_copy(w_value, held_v, sem.at[n + 1])
    copy_k.start()
    copy_v.start()
    for copy in copies:
        copy.wait()

    inverse = lax.rsqrt(square_sums(whole, features) / features + epsilon)
    scaled_rows(whole, features, inverse, gain, normed)

    part_a[:, :BLOCK] = whole[:, :BLOCK]
    part_a[:, BLOCK:] = whole[:, count - BLOCK :]
    part_b[...] = whole[:, BLOCK : count - BLOCK]

    pre = dot_nt(gates[...], normed[...])
    soft = jnp.maximum(pre, 0.0) + jnp.log1p(jnp.exp(-jnp.abs(pre)))
    rate = jnp.concatenate([rates[...]] * (count // 128), axis=1)
    decay = -rate * soft
    beta = jax.nn.sigmoid(pre + rate)
    row_at, col_at = iotas((BLOCK, BLOCK))
    upper = (row_at <= col_at).astype(f32)
    rows_at_head[...] = jnp.zeros_like(rows_at_head)
    for c in range(blocks):
        tokens = slice(c * BLOCK, (c + 1) * BLOCK)
        total = jnp.dot(
            decay[:, tokens], upper, precision=lax.Precision.HIGHEST, preferred_element_type=f32
        )
        totals[c] = total
        rows_at_head[0:16, :] = total
        rows_at_head[16:32, :] = beta[:, tokens]
        columns = rows_at_head[...].T
        for h in range(heads):
            total_b[h, tokens, :] = jnp.broadcast_to(columns[:, h : h + 1], (BLOCK, DK))
            at = 16 + heads + h
            beta_b[h, tokens, :] = jnp.broadcast_to(columns[:, at : at + 1], (BLOCK, DK))

    copy_k.wait()
    copy_v.wait()

    @pl.loop(0, inner // 256)
    def _(t):
        cols = pl.ds(pl.multiple_of(t * 256, 256), 256)
        raw_k[:, cols] = dot(normed[...], held_k[:, cols]).astype(bf16)
        raw_v[:, cols] = dot(normed[...], held_v[:, cols]).astype(bf16)

    xor = jnp.where(row_at > col_at, row_at ^ col_at, 0)
    eye = jnp.where(row_at == col_at, 1.0, 0.0)
    group = 2 if heads % 2 == 0 else 1

    @pl.loop(0, heads // group)
    def _(at):
        lows, solved = [], []
        chains = []
        for g in range(group):
            h = at * group + g
            cols = pl.ds(pl.multiple_of(h * DK, DK), DK)
            wide = pl.ds(pl.multiple_of(h * 2 * DK, 2 * DK), 2 * DK)
            raw = raw_k[:, cols].astype(f32)
            unit = raw * lax.rsqrt(jnp.sum(raw * raw, axis=1, keepdims=True) + epsilon)
            keys[:, cols] = unit.astype(bf16)
            for c in range(blocks):
                chains.append((h, cols, wide, c, slice(c * BLOCK, (c + 1) * BLOCK)))
        for h, cols, wide, c, rows in chains:
            k = keys[rows, cols]
            fade = jnp.exp(jnp.minimum(total_b[h, rows, :] - totals[c, pl.ds(h, 1), :], 0.0))
            low = jnp.where(xor > 0, beta_b[h, rows, :] * fade * dot_nt(k, k), 0.0)
            lows.append(low)
            solved.append(eye - jnp.where(xor == 1, low, 0.0))
        size = 2
        while size < BLOCK:
            mask = (xor >= size) & (xor < 2 * size)
            first = []
            for i in range(len(chains)):
                link = jnp.where(mask, lows[i], 0.0).astype(bf16)
                first.append(dot(link, solved[i].astype(bf16)).astype(bf16))
            solved = [
                solved[i] - dot(solved[i].astype(bf16), first[i]) for i in range(len(chains))
            ]
            size *= 2
        grown = []
        for i, (h, cols, wide, c, rows) in enumerate(chains):
            k = keys[rows, cols].astype(f32)
            t_col = total_b[h, rows, :]
            b_col = beta_b[h, rows, :]
            right = jnp.concatenate(
                [
                    (b_col * jnp.exp(t_col) * k).astype(bf16),
                    (b_col * raw_v[rows, cols].astype(f32)).astype(bf16),
                ],
                axis=1,
            )
            both = dot(solved[i].astype(bf16), right).astype(bf16)
            erased[rows, wide] = both
            t_end = t_col[BLOCK - 1 : BLOCK, :]
            faded = (jnp.exp(t_end - t_col) * k).astype(bf16)
            grown.append((jnp.exp(t_end), dot_tn(faded, both)))
        states = [None] * group
        for c in range(blocks):
            for g in range(group):
                h, cols, wide = chains[g * blocks][:3]
                end, product = grown[g * blocks + c]
                erase, write = product[:, :DK], product[:, DK:]
                if c == 0:
                    state = jnp.concatenate([end * eye - erase, write], axis=1)
                else:
                    step = dot(erase.astype(bf16), states[g].astype(bf16))
                    state = (
                        jnp.concatenate([end, end], axis=1) * states[g]
                        - step
                        + jnp.concatenate([jnp.zeros_like(write), write], axis=1)
                    )
                if c < blocks - 1:
                    entry[c, :, wide] = state.astype(bf16)
                states[g] = state
        for g in range(group):
            h = at * group + g
            half = heads // 2
            mine = (h >= half) == (parity == 1)
            slot = lax.rem(h, half)

            @pl.when(mine)
            def _():
                own[slot] = states[g].astype(bf16)

            @pl.when(jnp.logical_not(mine))
            def _():
                sent[slot] = states[g].astype(bf16)


def block_maps(meta, slots, pieces, gain, rates, gates, w_key, w_value):
    n = len(pieces)
    count = pieces[0].shape[1]
    features, inner = w_key.shape
    heads = inner // DK
    blocks = count // BLOCK
    middle = count - 2 * BLOCK
    return pl.pallas_call(
        functools.partial(maps_kernel, n, heads, slots),
        out_shape=(
            shape_of((count, features)),
            shape_of((count, inner)),
            shape_of((count, 2 * inner)),
            shape_of((blocks - 1, DK, 2 * inner)),
            shape_of((heads // 2, DK, 2 * DK)),
            shape_of((heads // 2, DK, 2 * DK)),
            shape_of((blocks, 16, 128), f32),
            shape_of((features, 2 * BLOCK)),
            shape_of((features, middle)),
        ),
        in_specs=[SM] + [ANY] * n + [VM] * 3 + [ANY] * 2,
        out_specs=[VM] * 9,
        scratch_shapes=[
            pltpu.VMEM((features, count), bf16),
            pltpu.VMEM(w_key.shape, bf16),
            pltpu.VMEM(w_value.shape, bf16),
            pltpu.VMEM((count, inner), bf16),
            pltpu.VMEM((count, inner), bf16),
            pltpu.VMEM((128, BLOCK), f32),
            pltpu.VMEM((heads, count, DK), f32),
            pltpu.VMEM((heads, count, DK), f32),
            pltpu.SemaphoreType.DMA((n + 2,)),
        ],
        compiler_params=params(28),
        cost_estimate=cost(10 * 10**9, 14 * 10**6),
        name="block_maps",
    )(meta, *pieces, gain, rates, gates, w_key, w_value)


def query_kernel(normed, weights, query, done, held, sem):
    copy = pltpu.make_async_copy(weights, held, sem)
    copy.start()
    done[...] = jnp.zeros_like(done)
    copy.wait()

    @pl.loop(0, query.shape[1] // 256)
    def _(t):
        cols = pl.ds(pl.multiple_of(t * 256, 256), 256)
        query[:, cols] = dot(normed[...], held[:, cols]).astype(bf16)


def queries(normed, weights):
    return pl.pallas_call(
        query_kernel,
        out_shape=(shape_of((normed.shape[0], weights.shape[1])), shape_of((8, 128), f32)),
        in_specs=[VM, ANY],
        out_specs=[VM] * 2,
        scratch_shapes=[pltpu.VMEM(weights.shape, bf16), pltpu.SemaphoreType.DMA],
        compiler_params=params(16),
        cost_estimate=cost(2 * 10**9, 6 * 10**6),
        name="queries",
    )(normed, weights)


def outputs_kernel(heads, query, keys, erased, entry, totals, after, shard_query, free, done, rows_at_head):
    count = query.shape[0]
    blocks = count // BLOCK
    row_at, col_at = iotas((BLOCK, BLOCK))
    done[...] = jnp.zeros_like(done)
    rows_at_head[...] = jnp.zeros_like(rows_at_head)
    for c in range(blocks):
        rows = slice(c * BLOCK, (c + 1) * BLOCK)
        rows_at_head[0:16, :] = totals[c]
        columns = rows_at_head[...].T
        for h in range(heads):
            cols = slice(h * DK, (h + 1) * DK)
            wide = slice(h * 2 * DK, (h + 1) * 2 * DK)
            t_col = jnp.broadcast_to(columns[:, h : h + 1], (BLOCK, BLOCK))
            t_row = totals[c, h : h + 1, :]
            fade = jnp.where(row_at >= col_at, jnp.exp(jnp.minimum(t_col - t_row, 0.0)), 0.0)
            q = query[rows, cols]
            scores = (fade * dot_nt(q, keys[rows, cols])).astype(bf16)
            both = dot(scores, erased[rows, wide])
            reach = jnp.exp(t_col) * q.astype(f32) - both[:, :DK]
            local = both[:, DK:]
            if c > 0:
                product = dot(reach.astype(bf16), entry[c - 1, :, wide])
                reach = product[:, :DK]
                local = local + product[:, DK:]
            shard_query[rows, cols] = reach.astype(bf16)
            free[rows, cols] = local


def block_outputs(query, keys, erased, entry, totals, after):
    heads = query.shape[1] // DK
    return pl.pallas_call(
        functools.partial(outputs_kernel, heads),
        out_shape=(shape_of(query.shape), shape_of(query.shape, f32), shape_of((8, 128), f32)),
        in_specs=[VM] * 5 + [ANY],
        out_specs=[VM] * 3,
        scratch_shapes=[pltpu.VMEM((128, BLOCK), f32)],
        compiler_params=params(16),
        cost_estimate=cost(3 * 10**9, 4 * 10**6),
        name="block_outputs",
    )(query, keys, erased, entry, totals, after)


def pair_kernel(slots, meta, own, other, after, pair, first, done):
    even = meta[slots] == 0
    for h in range(own.shape[0]):
        mine, theirs = own[h], other[h]
        early = jnp.where(even, mine, theirs)
        late = jnp.where(even, theirs, mine)
        product = dot(late[:, :DK], early)
        shift = late[:, DK:].astype(f32)
        pair[h] = (product + jnp.concatenate([jnp.zeros_like(shift), shift], axis=1)).astype(bf16)
        first[h] = early
    done[...] = jnp.zeros_like(done)


def pair_maps(meta, slots, own, other, after):
    return pl.pallas_call(
        functools.partial(pair_kernel, slots),
        out_shape=(shape_of(own.shape), shape_of(own.shape), shape_of((8, 128), f32)),
        in_specs=[SM, VM, VM, ANY],
        out_specs=[VM] * 3,
        compiler_params=params(8),
        name="pair_maps",
    )(meta, own, other, after)


def apply_map(whole, state):
    high = state.astype(bf16)
    low = (state - high.astype(f32)).astype(bf16)
    product = dot(whole[:, :DK], jnp.concatenate([high, low], axis=1))
    return product[:, :DK] + product[:, DK:] + whole[:, DK:].astype(f32)


def start_kernel(slots, steps, meta, first, *refs):
    pairs, (after, keep, give) = refs[:steps], refs[steps:]
    even = meta[slots] == 0
    for h in range(first.shape[0]):
        state = pairs[0][h][:, DK:].astype(f32)
        for pair in pairs[1:]:
            state = apply_map(pair[h], state)
        later = apply_map(first[h], state)
        keep[h] = jnp.where(even, state, later).astype(bf16)
        give[h] = jnp.where(even, later, state).astype(bf16)


def start_states(meta, slots, first, pairs, after):
    heads = first.shape[0]
    shape = shape_of((heads, DK, DK))
    return pl.pallas_call(
        functools.partial(start_kernel, slots, len(pairs)),
        out_shape=(shape, shape),
        in_specs=[SM] + [VM] * (1 + len(pairs)) + [ANY],
        out_specs=[VM] * 2,
        compiler_params=params(8),
        name="start_states",
    )(meta, first, *pairs, after)


def mixed_kernel(heads, slots, meta, own, other, shard_query, free, gain, mixed_a, mixed_b):
    even = meta[slots] == 0
    half = heads // 2
    blocks = shard_query.shape[0] // BLOCK
    for h in range(heads):
        cols = slice(h * DK, (h + 1) * DK)
        if h < half:
            state = jnp.where(even, own[h], other[h])
        else:
            state = jnp.where(even, other[h - half], own[h - half])
        for unit in range(blocks):
            rows = slice(unit * BLOCK, (unit + 1) * BLOCK)
            out = dot(shard_query[rows, cols], state) + free[rows, cols]
            scale = lax.rsqrt(jnp.mean(out * out, axis=1, keepdims=True) + epsilon)
            value = (out * scale * gain[...].astype(f32)).astype(bf16)
            if unit == 0:
                mixed_a[:BLOCK, cols] = value
            elif unit == blocks - 1:
                mixed_a[BLOCK:, cols] = value
            else:
                mixed_b[(unit - 1) * BLOCK : unit * BLOCK, cols] = value


def mixed_heads(meta, slots, own, other, shard_query, free, gain):
    count, inner = shard_query.shape
    return pl.pallas_call(
        functools.partial(mixed_kernel, inner // DK, slots),
        out_shape=(shape_of((2 * BLOCK, inner)), shape_of((count - 2 * BLOCK, inner))),
        in_specs=[SM] + [VM] * 5,
        out_specs=[VM] * 2,
        compiler_params=params(12),
        cost_estimate=cost(10**9, 3 * 10**6),
        name="mixed_heads",
    )(meta, own, other, shard_query, free, gain)


def attend_kernel(slots, meta, own, other, weights, other_weights, chip):
    rows = pl.ds(pl.multiple_of(meta[slots + 1] * chip.shape[0], 16), chip.shape[0])
    total = dot_nt(weights[rows, :], own[...]) + dot_nt(other_weights[...], other[...])
    chip[...] = total.astype(bf16)


def attend(meta, slots, own, other, weights, other_weights):
    return pl.pallas_call(
        functools.partial(attend_kernel, slots),
        out_shape=shape_of((other_weights.shape[0], own.shape[0])),
        in_specs=[SM] + [VM] * 4,
        out_specs=VM,
        compiler_params=params(16),
        cost_estimate=cost(10**9, 5 * 10**6),
        name="attend",
    )(meta, own, other, weights, other_weights)


def up_kernel(slots, adds, meta, *refs):
    tokens = refs[0]
    own, other = refs[1 : 1 + adds], refs[1 + adds : 1 + 2 * adds]
    gain, weights, lifted, middle_part, first, last, middle, hidden, held, sem = refs[1 + 2 * adds :]
    copy = pltpu.make_async_copy(weights, held, sem)
    copy.start()
    core, me = meta[slots + 1], meta[slots + 2]
    features = middle.shape[0]
    half = features // 2
    step = 32
    for side, parts in ((core, own), (1 - core, other)):

        @pl.loop(0, half // step)
        def _(r):
            rows = pl.ds(pl.multiple_of(r * step, step), step)
            target = pl.ds(pl.multiple_of(side * half + r * step, 32), step)
            total = tokens[target, :].astype(f32)
            for ref in parts:
                total = total + ref[rows, :].astype(f32)
            middle[target, :] = total.astype(bf16).astype(f32)

    inverse = lax.rsqrt(square_sums(middle, features) / features + epsilon)
    scaled_rows(middle, features, inverse, gain, hidden)
    part = middle_part.shape[0]
    middle_part[...] = middle[pl.ds(pl.multiple_of(me * part, 8), part), :]
    copy.wait()
    lifted[...] = dot(hidden[...], held[...]).astype(bf16)
    count = lifted.shape[0]
    first[...] = lifted[0:1, :]
    last[...] = lifted[count - 1 : count, :]


def up_project(meta, slots, tokens, own, other, gain, weights, part):
    features, hidden = weights.shape
    count = tokens.shape[1]
    return pl.pallas_call(
        functools.partial(up_kernel, slots, len(own)),
        out_shape=(
            shape_of((count, hidden)),
            shape_of((part, count), f32),
            shape_of((1, hidden)),
            shape_of((1, hidden)),
        ),
        in_specs=[SM] + [VM] * (2 + 2 * len(own)) + [ANY],
        out_specs=[VM] * 4,
        scratch_shapes=[
            pltpu.VMEM((features, count), f32),
            pltpu.VMEM((count, features), bf16),
            pltpu.VMEM(weights.shape, bf16),
            pltpu.SemaphoreType.DMA,
        ],
        compiler_params=params(24),
        cost_estimate=cost(2 * 10**9, 8 * 10**6),
        name="up_project",
    )(meta, tokens, *own, *other, gain, weights)


def gelu_of(x):
    inner = 0.7978845608028654 * (x + 0.044715 * (x * x * x))
    return 0.5 * x * (1.0 + jnp.tanh(inner))


def down_kernel(n_out, at, meta, outer, inside, before, after, taps, weights, *refs):
    outs = refs[:n_out]
    act, padded, held, sem = refs[n_out:]
    copies = [
        pltpu.make_async_copy(weights.at[meta[at + p]], held.at[p], sem.at[p])
        for p in range(n_out)
    ]
    for copy in copies:
        copy.start()
    count = act.shape[0]
    padded[7:8, :] = before[...].astype(f32)
    padded[8 : 8 + BLOCK, :] = outer[0:BLOCK, :].astype(f32)
    padded[8 + BLOCK : 8 + count - BLOCK, :] = inside[...].astype(f32)
    padded[8 + count - BLOCK : 8 + count, :] = outer[BLOCK:, :].astype(f32)
    padded[8 + count : 9 + count, :] = after[...].astype(f32)

    @pl.loop(0, count // 32)
    def _(r):
        base = pl.multiple_of(r * 32, 32)
        window = padded[pl.ds(base, 48), :]
        value = (
            taps[0:1, :] * window[7:39, :]
            + taps[1:2, :] * window[8:40, :]
            + taps[2:3, :] * window[9:41, :]
        )
        act[pl.ds(base, 32), :] = gelu_of(value).astype(bf16)

    for p in range(n_out):
        copies[p].wait()
        outs[p][...] = dot_nt(held[p], act[...]).astype(bf16)


def down_project(meta, at, outer, inside, before, after, taps, weights, n_out):
    part, hidden = weights.shape[1:]
    count = outer.shape[0] + inside.shape[0]
    results = pl.pallas_call(
        functools.partial(down_kernel, n_out, at),
        out_shape=[shape_of((part, count))] * n_out + [shape_of((count, hidden))],
        in_specs=[SM] + [VM] * 5 + [ANY],
        out_specs=[VM] * (n_out + 1),
        scratch_shapes=[
            pltpu.VMEM((count + 16, hidden), f32),
            pltpu.VMEM((n_out, part, hidden), bf16),
            pltpu.SemaphoreType.DMA((n_out,)),
        ],
        compiler_params=params(24),
        cost_estimate=cost(4 * 10**9, 8 * 10**6),
        name="down_project",
    )(meta, outer, inside, before, after, taps, weights)
    return results[:n_out], results[n_out]


def rest_kernel(at, meta, act, middle_a, middle_b, weights, give, base, held, sem):
    copies = [
        pltpu.make_async_copy(weights.at[meta[at + p]], held.at[p], sem.at[p]) for p in range(2)
    ]
    for copy in copies:
        copy.start()
    count = act.shape[0]
    copies[0].wait()
    give[...] = dot_nt(held[0], act[...]).astype(bf16)
    copies[1].wait()
    kept = dot_nt(held[1], act[...]).astype(bf16).astype(f32)
    base[:, :BLOCK] = kept[:, :BLOCK] + middle_a[:, :BLOCK]
    base[:, BLOCK : count - BLOCK] = kept[:, BLOCK : count - BLOCK] + middle_b[...]
    base[:, count - BLOCK :] = kept[:, count - BLOCK :] + middle_a[:, BLOCK:]


def rest_project(meta, at, act, middle_a, middle_b, weights):
    part, hidden = weights.shape[1:]
    count = act.shape[0]
    return pl.pallas_call(
        functools.partial(rest_kernel, at),
        out_shape=(shape_of((part, count)), shape_of((part, count), f32)),
        in_specs=[SM] + [VM] * 3 + [ANY],
        out_specs=[VM] * 2,
        scratch_shapes=[
            pltpu.VMEM((2, part, hidden), bf16),
            pltpu.SemaphoreType.DMA((2,)),
        ],
        compiler_params=params(20),
        cost_estimate=cost(2 * 10**9, 6 * 10**6),
        name="rest_project",
    )(meta, act, middle_a, middle_b, weights)


def core_swap(value, n):
    return lax.ppermute(value, "head", [(i, i ^ 1) for i in range(n)])


def y_shift(value, n, step):
    return lax.ppermute(value, "head", [(i, (i + 2 * step) % n) for i in range(n)])


def pair_swap(value, n):
    return lax.ppermute(value, "seq", [(i, i ^ 1) for i in range(n)])


def later(value, n, step):
    return lax.ppermute(value, "seq", [(i, i + 2 * step) for i in range(n - 2 * step)])


def shards(
    tokens,
    norm_gain,
    w_query,
    w_key,
    w_value,
    w_decay,
    w_beta,
    head_rates,
    head_gain,
    w_out,
    ffn_gain,
    w_up,
    conv_taps,
    w_down,
):
    n = lax.axis_size("head")
    seqs = lax.axis_size("seq")
    me = lax.axis_index("head")
    at = lax.axis_index("seq")
    core = me % 2
    parity = at % 2
    ys = n // 2
    count, part = tokens.shape
    heads = w_query.shape[1] // DK
    hidden = w_up.shape[1]
    features = n * part

    mine = tokens.T
    along = [mine] + [y_shift(mine, n, d) for d in range(1, ys)]
    pieces, order = [], []
    for d, piece in enumerate(along):
        from_here = (me + n - 2 * d) % n
        pieces += [piece, core_swap(piece, n)]
        order += [from_here, from_here ^ 1]
    if part % 16:
        by_place = []
        for j in range(n):
            block = pieces[0]
            for p in range(1, n):
                block = jnp.where(order[p] == j, pieces[p], block)
            by_place.append(block)
        pieces, order = [jnp.concatenate(by_place, axis=0)], [jnp.zeros_like(me)]
    slots = len(order)
    far_order = []
    for d in range(1, ys):
        there = (me + 2 * d) % n
        far_order += [there ^ 1, there]
    near_order = [me ^ 1, me]
    meta = jnp.stack(order + [parity, core, me] + far_order + near_order).astype(jnp.int32)
    far_at = slots + 3
    near_at = far_at + len(far_order)

    w_out_t = w_out.T
    other_w_out = core_swap(
        lax.dynamic_slice_in_dim(w_out_t, (1 - core) * (features // 2), features // 2, 0), n
    )

    gates = jnp.concatenate([w_decay.T, w_beta.T], axis=0)
    gates = jnp.pad(gates, ((0, 16 - 2 * heads), (0, 0)))
    rates = jnp.pad(head_rates.reshape(2 * heads, 1), ((0, 16 - 2 * heads), (0, 0)))
    rates = jnp.broadcast_to(rates, (16, 128))
    taps = conv_taps.astype(f32)

    normed, keys, erased, entry, own_maps, sent_maps, totals, tokens_a, tokens_b = block_maps(
        meta, slots, pieces, norm_gain.reshape(1, features), rates, gates, w_key, w_value
    )

    other_maps = pair_swap(sent_maps, seqs)
    query, query_done = queries(normed, w_query)
    pair, first, done = pair_maps(meta, slots, own_maps, other_maps, query_done)
    pairs = [later(pair, seqs, d) for d in range(seqs // 2 - 1, 0, -1)]
    shard_query, free, out_done = block_outputs(query, keys, erased, entry, totals, done)
    kept_state, given_state = start_states(meta, slots, first, pairs, out_done)
    other_state = pair_swap(given_state, seqs)

    mixed = mixed_heads(
        meta, slots, kept_state, other_state, shard_query, free, head_gain.reshape(1, DK)
    )
    ups = []
    for own_mixed, own_tokens in zip(mixed, (tokens_a, tokens_b)):
        chip = attend(meta, slots, own_mixed, core_swap(own_mixed, n), w_out_t, other_w_out)
        own = [chip] + [y_shift(chip, n, d) for d in range(1, ys)]
        other = [core_swap(value, n) for value in own]
        ups.append(
            up_project(
                meta,
                slots,
                own_tokens,
                own,
                other,
                ffn_gain.reshape(1, features),
                w_up,
                part,
            )
        )
    (outer, middle_a, first_row, last_row), (inside, middle_b, _, _) = ups
    before = lax.ppermute(last_row, "seq", [(i, i + 1) for i in range(seqs - 1)])
    after = lax.ppermute(first_row, "seq", [(i + 1, i) for i in range(seqs - 1)])

    w_parts = w_down.T.reshape(n, part, hidden)
    far, act = down_project(
        meta, far_at, outer, inside, before, after, taps, w_parts, len(far_order)
    )
    near_give, total = rest_project(meta, near_at, act, middle_a, middle_b, w_parts)
    for d in range(1, ys):
        chip = (
            far[2 * d - 1].astype(f32) + core_swap(far[2 * d - 2], n).astype(f32)
        ).astype(bf16)
        total = total + y_shift(chip, n, d).astype(f32)
    total = total + core_swap(near_give, n).astype(f32)
    return total.astype(bf16).T


def solution(mesh):
    placed = (
        P("seq", "head"),
        P(),
        P(None, "head"),
        P(None, "head"),
        P(None, "head"),
        P(None, "head"),
        P(None, "head"),
        P(None, "head"),
        P(),
        P("head", None),
        P(),
        P(None, "head"),
        P(None, "head"),
        P("head", None),
    )
    return jax.shard_map(
        shards, mesh=mesh, in_specs=placed, out_specs=P("seq", "head"), check_vma=False
    )
```

time: 214 us -> 148 us (0.69)
  local copies, waits for them, and re-layouts: 53.6 us -> 5.42 us
  waiting for transfers between devices: 38.9 us -> 63.6 us
  Pallas kernels: 76.9 us -> 53.1 us
  other arithmetic: 20.7 us -> 1.25 us
    pallas_call x11 -> x12, Pallas kernels: 76.9 us -> 53.1 us  [the longest x1 18.1 us: block_maps(): pl.pallas_call(functools.partial(maps_kernel, n, heads, slots), out_shape...]
    ppermute x4, waiting for transfers between devices: 33 us -> 50.2 us  [y_shift(): lax.ppermute(value, 'head', [(i, (i + 2 * step) % n) for i in range(n)])]
    ppermute x12 -> x0, local copies, waits for them, and re-layouts: 10.5 us -> none  [the longest x8 6.5 us: core_swap(): return lax.ppermute(value, 'head', [(i, i ^ 1) for i in range(n)])]
    reshape x3, local copies, waits for them, and re-layouts: 10.5 us -> 0.1 us  [the longest x1 0.08 us: shards(): head_rates.reshape(2 * heads, 1)]
    pad x2 -> x0, local copies, waits for them, and re-layouts: 7.14 us -> none  [widened(): jnp.pad(matrix.reshape(n, part, cols), ((0, 0), (0, width - part), (0, 0)))]
    concatenate x2 -> x1, other arithmetic: 6.24 us -> 0.03 us  [shards(): gates = jnp.concatenate([w_decay.T, w_beta.T], axis=0)]
    pallas_call x4 -> x0, local copies, waits for them, and re-layouts: 6.19 us -> none  [the longest x2 2.76 us: mixer_out(): pl.pallas_call(functools.partial(mixer_kernel, heads, units), out_shape=(...]
    unnamed x45 -> x32, local copies, waits for them, and re-layouts: 8.28 us -> 2.78 us
  transfers between devices with their start and end apart: 19 -> 22, of which waited for: 6 -> 9; matrix products, arithmetic and copies ran while one was open for 28% -> 2% of each run, Pallas kernels for 17% -> 32%
where the time goes in v2:
time: 148 us; the launch traced here: 147 us
  waiting for transfers between devices  63.6 us (43%)
  Pallas kernels  53.1 us (36%)
  starting transfers between devices  23.6 us (16%)
  local copies, waits for them, and re-layouts  5.42 us (4%)
    ppermute x4, waiting for transfers between devices, y_shift(): lax.ppermute(value, 'head', [(i, (i + 2 * step) % n) for i in range(n)])  50.2 us
    pallas_call x1, Pallas kernels, block_maps(): pl.pallas_call(functools.partial(maps_kernel, n, heads, slots), out_shape...  18.1 us
    pallas_call x2, Pallas kernels, up_project(): pl.pallas_call(functools.partial(up_kernel, slots, len(own)), out_shape=(...  15.5 us
    ppermute x3, waiting for transfers between devices, later(): lax.ppermute(value, 'seq', [(i, i + 2 * step) for i in range(n - 2 * step)])  7.64 us
    ppermute x3, starting transfers between devices, later(): lax.ppermute(value, 'seq', [(i, i + 2 * step) for i in range(n - 2 * step)])  6.25 us
    pallas_call x1, Pallas kernels, down_project(): pl.pallas_call(functools.partial(down_kernel, n_out, at), out_shape=[shap...  6.01 us
    ppermute x4, starting transfers between devices, y_shift(): lax.ppermute(value, 'head', [(i, (i + 2 * step) % n) for i in range(n)])  5.25 us
    ppermute x2, waiting for transfers between devices, pair_swap(): return lax.ppermute(value, 'seq', [(i, i ^ 1) for i in range(n)])  4.67 us
  transfers between devices with their start and end apart: 22, of which 9 were waited for; matrix products, arithmetic and copies ran while one was open for 2% of the time, Pallas kernels for 32%

profile of v2, /device:TPU:16, one launch (start us, length us, event | category | flops | bytes accessed | tf_op | source)
XLA Modules:
  0.0 147.3 jit_solution(17578305738519655259)
XLA Ops:
  0.0 1.5 %collective-permute-start.1 = (bf16[560,512]{1,0:T(8,128)(2,1)}, bf16[560,512]{1,0:T(8,128)(2,1)}, u32[]{:S(2)}, u32[]{:S(2)}) collective-permute-start(bf16[560,512]{1,0:T(8,128)(2,1)} %bitcast.30), channel_id=1, source_target_pairs={{0,2},{1,3},{2,0},{3,1},{4,6},{5,7},{6,4},{7,5},{8,10},{9,11},{10,... | collective-permute-start | bytes 1720328 | tf_op jit(solution)/shard_map/ppermute | solution.py:603
  1.6 13.5 %collective-permute-done.1.refs_2_ = bf16[560,512]{1,0:T(8,128)(2,1)} collective-permute-done((bf16[560,512]{1,0:T(8,128)(2,1)}, bf16[560,512]{1,0:T(8,128)(2,1)}, u32[]{:S(2)}, u32[]{:S(2)}) %collective-permute-start.1) | collective-permute-done | bytes 573472 | tf_op jit(solution)/shard_map/ppermute | solution.py:603
  15.0 2.4 %dynamic-slice_bitcast_fusion = bf16[1120,512]{1,0:T(8,128)(2,1)} fusion(bf16[512,2240]{0,1:T(8,128)(2,1)} %param.23, s32[]{:T(128)S(6)} %select_n.28), kind=kLoop, calls=%fused_computation.2 | loop fusion | bytes 2293764 | tf_op jit(solution)/shard_map/dynamic_slice | solution.py:669
  17.4 0.5 collective-permute-start.9
  17.9 0.1 reshape.17
  18.0 0.1 stack.38.meta
  18.2 0.1 broadcast_in_dim.8.refs_5_
  18.3 1.6 %copy-done.2 = bf16[2240,512]{1,0:T(8,128)(2,1)S(1)} copy-done((bf16[2240,512]{1,0:T(8,128)(2,1)S(1)}, bf16[2240,512]{1,0:T(8,128)(2,1)}, u32[]{:S(2)}) %copy-start.2) | copy-done | bytes 2293784
  19.9 1.1 copy-done.4
  21.0 18.1 %block_maps.1 = (bf16[512,2240]{1,0:T(8,128)(2,1)S(1)}, bf16[512,512]{1,0:T(8,128)(2,1)S(1)}, bf16[512,1024]{1,0:T(8,128)(2,1)S(1)}, bf16[3,128,1024]{2,1,0:T(8,...) custom-call(s32[11]{0:T(128)S(1)} %stack.38.meta, ...), custom_call_target="tpu_custom_call" | custom-call | flops 10000000000 | bytes 14000000 | tf_op jit(solution)/shard_map/block_maps/pallas_call | solution.py:240
  39.0 1.6 %collective-permute-start.3 = (bf16[2,128,256]{2,1,0:T(8,128)(2,1)S(1)}, bf16[2,128,256]{2,1,0:T(8,128)(2,1)S(1)}, u32[]{:S(2)}, u32[]{:S(2)}) collective-permute-start(bf16[2,128,256]{2,1,0:T(8,128)(2,1)S(1)} %get-tuple-element.39), channel_id=1, source_target_pairs={{0,4},{4,0},{8,12},{12,8},{16,20},{20,16},{24,28},{28,24},{1,5},{5... | collective-permute-start | bytes 393224 | tf_op jit(solution)/shard_map/ppermute | solution.py:607
  40.6 2.0 %queries.1 = (bf16[512,512]{1,0:T(8,128)(2,1)S(1)}, f32[8,128]{1,0:T(8,128)S(1)}) custom-call(bf16[512,2240]{1,0:T(8,128)(2,1)S(1)} %get-tuple-element.40.normed, bf16[2240,512]{1,0:T(8,128)(2,1)S(1)} %copy-done.3), custom_call_target="tpu_custom_call" | custom-call | flops 2000000000 | bytes 6000000 | tf_op jit(solution)/shard_map/queries/pallas_call | solution.py:285
  42.6 1.9 %collective-permute-done.3.other = bf16[2,128,256]{2,1,0:T(8,128)(2,1)S(1)} collective-permute-done((bf16[2,128,256]{2,1,0:T(8,128)(2,1)S(1)}, bf16[2,128,256]{2,1,0:T(8,128)(2,1)S(1)}, u32[]{:S(2)}, u32[]{:S(2)}) %collective-permute-start.3) | collective-permute-done | bytes 131104 | tf_op jit(solution)/shard_map/ppermute | solution.py:607
  44.5 0.7 pair_maps.1
  45.2 0.7 collective-permute-start.4
  45.9 1.3 collective-permute-start.5
  47.2 4.3 %collective-permute-start.6 = (bf16[2,128,256]{2,1,0:T(8,128)(2,1)S(1)}, bf16[2,128,256]{2,1,0:T(8,128)(2,1)S(1)}, u32[]{:S(2)}, u32[]{:S(2)}) collective-permute-start(bf16[2,128,256]{2,1,0:T(8,128)(2,1)S(1)} %get-tuple-element.43), channel_id=1, source_target_pairs={{0,8},{4,12},{8,16},{12,20},{16,24},{20,28},{1,9},{5,13},{9,17},{1... | collective-permute-start | bytes 393224 | tf_op jit(solution)/shard_map/ppermute | solution.py:611
  51.5 2.8 %block_outputs.1 = (bf16[512,512]{1,0:T(8,128)(2,1)S(1)}, f32[512,512]{1,0:T(8,128)S(1)}, f32[8,128]{1,0:T(8,128)S(1)}) custom-call(bf16[512,512]{1,0:T(8,128)(2,1)S(1)} %get-tuple-element.44.query, bf16[512,512]{1,0:T(8,128)(2,1)S(1)} %get-tuple-element.45.keys, bf16[512,1024]{1,0:T(8,128)(2,1)S(1)} %get-tuple-element.46.erased, ...), custom_call_target="tpu_custom_call" | custom-call | flops 3000000000 | bytes 4000000 | tf_op jit(solution)/shard_map/block_outputs/pallas_call | solution.py:328
  54.4 3.5 %collective-permute-done.5.refs_1_ = bf16[2,128,256]{2,1,0:T(8,128)(2,1)S(1)} collective-permute-done((bf16[2,128,256]{2,1,0:T(8,128)(2,1)S(1)}, bf16[2,128,256]{2,1,0:T(8,128)(2,1)S(1)}, u32[]{:S(2)}, u32[]{:S(2)}) %collective-permute-start.5) | collective-permute-done | bytes 131104 | tf_op jit(solution)/shard_map/ppermute | solution.py:611
  57.9 4.2 %collective-permute-done.6.refs_2_ = bf16[2,128,256]{2,1,0:T(8,128)(2,1)S(1)} collective-permute-done((bf16[2,128,256]{2,1,0:T(8,128)(2,1)S(1)}, bf16[2,128,256]{2,1,0:T(8,128)(2,1)S(1)}, u32[]{:S(2)}, u32[]{:S(2)}) %collective-permute-start.6) | collective-permute-done | bytes 131104 | tf_op jit(solution)/shard_map/ppermute | solution.py:611
  62.0 1.2 start_states.1
  63.2 1.6 %collective-permute-start.7 = (bf16[2,128,128]{2,1,0:T(8,128)(2,1)S(1)}, bf16[2,128,128]{2,1,0:T(8,128)(2,1)S(1)}, u32[]{:S(2)}, u32[]{:S(2)}) collective-permute-start(bf16[2,128,128]{2,1,0:T(8,128)(2,1)S(1)} %get-tuple-element.52), channel_id=1, source_target_pairs={{0,4},{4,0},{8,12},{12,8},{16,20},{20,16},{24,28},{28,24},{1,5},{5... | collective-permute-start | bytes 196616 | tf_op jit(solution)/shard_map/ppermute | solution.py:607
  64.8 2.8 %collective-permute-done.7.other = bf16[2,128,128]{2,1,0:T(8,128)(2,1)S(1)} collective-permute-done((bf16[2,128,128]{2,1,0:T(8,128)(2,1)S(1)}, bf16[2,128,128]{2,1,0:T(8,128)(2,1)S(1)}, u32[]{:S(2)}, u32[]{:S(2)}) %collective-permute-start.7) | collective-permute-done | bytes 65568 | tf_op jit(solution)/shard_map/ppermute | solution.py:607
  67.6 1.1 mixed_heads.1
  68.7 0.1 collective-permute-start.8
  68.7 0.5 collective-permute-start.13
  69.2 1.0 collective-permute-done.8.other
  70.3 1.3 attend.2.refs_1_
  71.6 1.6 %collective-permute-start.10 = (bf16[1120,256]{1,0:T(8,128)(2,1)S(1)}, bf16[1120,256]{1,0:T(8,128)(2,1)S(1)}, u32[]{:S(2)}, u32[]{:S(2)}) collective-permute-start(bf16[1120,256]{1,0:T(8,128)(2,1)S(1)} %attend.2.refs_1_), channel_id=1, source_target_pairs={{0,2},{1,3},{2,0},{3,1},{4,6},{5,7},{6,4},{7,5},{8,10},{9,11},{10,... | collective-permute-start | bytes 1720328 | tf_op jit(solution)/shard_map/ppermute | solution.py:603
  73.2 1.3 attend.3.refs_1_
  74.5 0.6 collective-permute-start.14
  75.1 12.4 %collective-permute-done.10.refs_2_ = bf16[1120,256]{1,0:T(8,128)(2,1)S(1)} collective-permute-done((bf16[1120,256]{1,0:T(8,128)(2,1)S(1)}, bf16[1120,256]{1,0:T(8,128)(2,1)S(1)}, u32[]{:S(2)}, u32[]{:S(2)}) %collective-permute-start.10) | collective-permute-done | bytes 573472 | tf_op jit(solution)/shard_map/ppermute | solution.py:603
  87.5 0.5 collective-permute-start.15
  88.0 11.0 %collective-permute-done.14.refs_2_ = bf16[1120,256]{1,0:T(8,128)(2,1)S(1)} collective-permute-done((bf16[1120,256]{1,0:T(8,128)(2,1)S(1)}, bf16[1120,256]{1,0:T(8,128)(2,1)S(1)}, u32[]{:S(2)}, u32[]{:S(2)}) %collective-permute-start.14) | collective-permute-done | bytes 573472 | tf_op jit(solution)/shard_map/ppermute | solution.py:603
  99.1 0.0 slice-start.2
  99.1 7.5 %up_project.2 = (bf16[256,1400]{1,0:T(8,128)(2,1)S(1)}, f32[560,256]{1,0:T(8,128)S(1)}, bf16[1,1400]{1,0:T(2,128)(2,1)S(1)}, bf16[1,1400]{1,0:T(2,128)(2,1)S(1)}) custom-call(s32[11]{0:T(128)S(1)} %stack.38.meta, bf16[2240,256]{1,0:T(8,128)(2,1)S(1)} %get-tuple-element.37.refs_0_, bf16[1120,256]{1,0:T(8,128)(2,1)S(1)} %attend.2.refs_1_, ...), custom_call_target="tpu_custom_call" | custom-call | flops 2000000000 | bytes 8000000 | tf_op jit(solution)/shard_map/up_project/pallas_call | solution.py:485
  106.6 3.4 %collective-permute-start.17 = (bf16[1,1400]{1,0:T(2,128)(2,1)S(1)}, bf16[1,1400]{1,0:T(2,128)(2,1)S(1)}, u32[]{:S(2)}, u32[]{:S(2)}) collective-permute-start(bf16[1,1400]{1,0:T(2,128)(2,1)S(1)} %get-tuple-element.60), channel_id=1, source_target_pairs={{0,4},{4,8},{8,12},{12,16},{16,20},{20,24},{24,28},{1,5},{5,9},{9,... | collective-permute-start | bytes 8408 | tf_op jit(solution)/shard_map/ppermute | solution.py:711
  110.0 3.3 %collective-permute-start.18 = (bf16[1,1400]{1,0:T(2,128)(2,1)S(1)}, bf16[1,1400]{1,0:T(2,128)(2,1)S(1)}, u32[]{:S(2)}, u32[]{:S(2)}) collective-permute-start(bf16[1,1400]{1,0:T(2,128)(2,1)S(1)} %get-tuple-element.61), channel_id=1, source_target_pairs={{4,0},{8,4},{12,8},{16,12},{20,16},{24,20},{28,24},{5,1},{9,5},{13... | collective-permute-start | bytes 8408 | tf_op jit(solution)/shard_map/ppermute | solution.py:712
  113.4 0.0 slice-start.3
  113.4 8.1 %up_project.3 = (bf16[256,1400]{1,0:T(8,128)(2,1)S(1)}, f32[560,256]{1,0:T(8,128)S(1)}, bf16[1,1400]{1,0:T(2,128)(2,1)}, bf16[1,1400]{1,0:T(2,128)(2,1)}) custom-call(s32[11]{0:T(128)S(1)} %stack.38.meta, bf16[2240,256]{1,0:T(8,128)(2,1)S(1)} %get-tuple-element.57.refs_0_, bf16[1120,256]{1,0:T(8,128)(2,1)S(1)} %attend.3.refs_1_, ...), custom_call_target="tpu_custom_call" | custom-call | flops 2000000000 | bytes 8000000 | tf_op jit(solution)/shard_map/up_project/pallas_call | solution.py:485
  121.5 6.0 %down_project.1 = (bf16[560,512]{1,0:T(8,128)(2,1)S(1)}, bf16[560,512]{1,0:T(8,128)(2,1)S(1)}, bf16[512,1400]{1,0:T(8,128)(2,1)S(1)}) custom-call(s32[11]{0:T(128)S(1)} %stack.38.meta, bf16[256,1400]{1,0:T(8,128)(2,1)S(1)} %get-tuple-element.56.outer, bf16[256,1400]{1,0:T(8,128)(2,1)S(1)} %get-tuple-element.59.inside, ...), custom_call_target="tpu_custom_call" | custom-call | flops 4000000000 | bytes 8000000 | tf_op jit(solution)/shard_map/down_project/pallas_call | solution.py:547
  127.5 0.1 collective-permute-start.19
  127.6 3.0 %rest_project.1 = (bf16[560,512]{1,0:T(8,128)(2,1)S(1)}, f32[560,512]{1,0:T(8,128)S(1)}) custom-call(s32[11]{0:T(128)S(1)} %stack.38.meta, bf16[512,1400]{1,0:T(8,128)(2,1)S(1)} %get-tuple-element.62.act, f32[560,256]{1,0:T(8,128)S(1)} %get-tuple-element.63.middle_a, f32[560,256]{1,0:T(8,128)S(1)} %get-tuple-element.64.middle_b, ...), custom_call_target="tpu_custom_call" | custom-call | flops 2000000000 | bytes 6000000 | tf_op jit(solution)/shard_map/rest_project/pallas_call | solution.py:583
  130.6 0.6 collective-permute-start.21
  131.2 0.2 add_convert_fusion.1
  131.3 1.6 %collective-permute-start.20 = (bf16[560,512]{1,0:T(8,128)(2,1)S(1)}, bf16[560,512]{1,0:T(8,128)(2,1)S(1)}, u32[]{:S(2)}, u32[]{:S(2)}) collective-permute-start(bf16[560,512]{1,0:T(8,128)(2,1)S(1)} %add_convert_fusion.1), channel_id=1, source_target_pairs={{0,2},{1,3},{2,0},{3,1},{4,6},{5,7},{6,4},{7,5},{8,10},{9,11},{10,... | collective-permute-start | bytes 1720328 | tf_op jit(solution)/shard_map/ppermute | solution.py:603
  132.9 13.4 %collective-permute-done.20 = bf16[560,512]{1,0:T(8,128)(2,1)S(1)} collective-permute-done((bf16[560,512]{1,0:T(8,128)(2,1)S(1)}, bf16[560,512]{1,0:T(8,128)(2,1)S(1)}, u32[]{:S(2)}, u32[]{:S(2)}) %collective-permute-start.20) | collective-permute-done | bytes 573472 | tf_op jit(solution)/shard_map/ppermute | solution.py:603
  146.3 1.1 fusion
  (53 shorter events, 0.2 us)
Async XLA Ops:
  0.0 15.0 %collective-permute-start.1 = (bf16[560,512]{1,0:T(8,128)(2,1)}, bf16[560,512]{1,0:T(8,128)(2,1)}, u32[]{:S(2)}, u32[]{:S(2)}) collective-permute-start(bf16[560,512]{1,0:T(8,128)(2,1)} %bitcast.30), channel_id=1, source_target_pairs={{0,2},{1,3},{2,0},{3,1},{4,6},{5,7},{6,4},{7,5},{8,10},{9,11},{10,... | collective-permute-start | bytes 1720328 | tf_op jit(solution)/shard_map/ppermute | solution.py:603
  1.5 16.7 %collective-permute-start = (bf16[560,512]{1,0:T(8,128)(2,1)}, bf16[560,512]{1,0:T(8,128)(2,1)}, u32[]{:S(2)}, u32[]{:S(2)}) collective-permute-start(bf16[560,512]{1,0:T(8,128)(2,1)} %bitcast.31), channel_id=1, source_target_pairs={{0,1},{1,0},{2,3},{3,2},{4,5},{5,4},{6,7},{7,6},{8,9},{9,8},{10,11... | collective-permute-start | bytes 1720328 | tf_op jit(solution)/shard_map/ppermute | solution.py:599
  1.5 16.4 %copy-start.11 = (f32[2,4]{1,0:T(2,128)S(1)}, f32[2,4]{1,0:T(2,128)}, u32[]{:S(2)}) copy-start(f32[2,4]{1,0:T(2,128)} %param.21) | copy-start | bytes 100
  1.5 16.5 %copy-start.9 = (bf16[2240]{0:T(1024)(128)(2,1)S(1)}, bf16[2240]{0:T(1024)(128)(2,1)}, u32[]{:S(2)}) copy-start(bf16[2240]{0:T(1024)(128)(2,1)} %param.15) | copy-start | bytes 13444
  1.5 16.6 %copy-start.6 = (bf16[2240,4]{0,1:T(4,128)(2,1)S(1)}, bf16[2240,4]{0,1:T(4,128)(2,1)}, u32[]{:S(2)}) copy-start(bf16[2240,4]{0,1:T(4,128)(2,1)} %param.20) | copy-start | bytes 53764
  1.5 16.6 %copy-start.7 = (bf16[2240,4]{0,1:T(4,128)(2,1)S(1)}, bf16[2240,4]{0,1:T(4,128)(2,1)}, u32[]{:S(2)}) copy-start(bf16[2240,4]{0,1:T(4,128)(2,1)} %param.19) | copy-start | bytes 53764
  1.5 16.7 %copy-start.1 = (bf16[2240,512]{1,0:T(8,128)(2,1)S(1)}, bf16[2240,512]{1,0:T(8,128)(2,1)}, u32[]{:S(2)}) copy-start(bf16[2240,512]{1,0:T(8,128)(2,1)} %refs_7_.1) | copy-start | bytes 6881284
  15.0 3.2 %collective-permute-start.2 = (bf16[560,512]{1,0:T(8,128)(2,1)}, bf16[560,512]{1,0:T(8,128)(2,1)}, u32[]{:S(2)}, u32[]{:S(2)}) collective-permute-start(bf16[560,512]{1,0:T(8,128)(2,1)} %collective-permute-done.1.refs_2_), channel_id=1, source_target_pairs={{0,1},{1,0},{2,3},{3,2},{4,5},{5,4},{6,7},{7,6},{8,9},{9,8},{10,11... | collective-permute-start | bytes 1720328 | tf_op jit(solution)/shard_map/ppermute | solution.py:599
  17.4 51.8 %collective-permute-start.9 = (bf16[1120,512]{1,0:T(8,128)(2,1)}, bf16[1120,512]{1,0:T(8,128)(2,1)S(1)}, u32[]{:S(2)}, u32[]{:S(2)}) collective-permute-start(bf16[1120,512]{1,0:T(8,128)(2,1)} %dynamic-slice_bitcast_fusion), channel_id=1, source_target_pairs={{0,1},{1,0},{2,3},{3,2},{4,5},{5,4},{6,7},{7,6},{8,9},{9,8},{10,11... | collective-permute-start | bytes 3440648 | tf_op jit(solution)/shard_map/ppermute | solution.py:599
  18.3 1.6 %copy-start.2 = (bf16[2240,512]{1,0:T(8,128)(2,1)S(1)}, bf16[2240,512]{1,0:T(8,128)(2,1)}, u32[]{:S(2)}) copy-start(bf16[2240,512]{1,0:T(8,128)(2,1)} %refs_8_.1) | copy-start | bytes 6881284
  19.9 1.1 copy-start.4
  21.0 19.6 %copy-start.3 = (bf16[2240,512]{1,0:T(8,128)(2,1)S(1)}, bf16[2240,512]{1,0:T(8,128)(2,1)}, u32[]{:S(2)}) copy-start(bf16[2240,512]{1,0:T(8,128)(2,1)} %weights.1) | copy-start | bytes 6881284
  39.0 5.5 %collective-permute-start.3 = (bf16[2,128,256]{2,1,0:T(8,128)(2,1)S(1)}, bf16[2,128,256]{2,1,0:T(8,128)(2,1)S(1)}, u32[]{:S(2)}, u32[]{:S(2)}) collective-permute-start(bf16[2,128,256]{2,1,0:T(8,128)(2,1)S(1)} %get-tuple-element.39), channel_id=1, source_target_pairs={{0,4},{4,0},{8,12},{12,8},{16,20},{20,16},{24,28},{28,24},{1,5},{5... | collective-permute-start | bytes 393224 | tf_op jit(solution)/shard_map/ppermute | solution.py:607
  45.2 9.1 %collective-permute-start.4 = (bf16[2,128,256]{2,1,0:T(8,128)(2,1)S(1)}, bf16[2,128,256]{2,1,0:T(8,128)(2,1)S(1)}, u32[]{:S(2)}, u32[]{:S(2)}) collective-permute-start(bf16[2,128,256]{2,1,0:T(8,128)(2,1)S(1)} %get-tuple-element.43), channel_id=1, source_target_pairs={{0,24},{4,28},{1,25},{5,29},{2,26},{6,30},{3,27},{7,31}} | collective-permute-start | bytes 393224 | tf_op jit(solution)/shard_map/ppermute | solution.py:611
  45.9 11.9 %collective-permute-start.5 = (bf16[2,128,256]{2,1,0:T(8,128)(2,1)S(1)}, bf16[2,128,256]{2,1,0:T(8,128)(2,1)S(1)}, u32[]{:S(2)}, u32[]{:S(2)}) collective-permute-start(bf16[2,128,256]{2,1,0:T(8,128)(2,1)S(1)} %get-tuple-element.43), channel_id=1, source_target_pairs={{0,16},{4,20},{8,24},{12,28},{1,17},{5,21},{9,25},{13,29},{2,18},{... | collective-permute-start | bytes 393224 | tf_op jit(solution)/shard_map/ppermute | solution.py:611
  47.2 14.8 %collective-permute-start.6 = (bf16[2,128,256]{2,1,0:T(8,128)(2,1)S(1)}, bf16[2,128,256]{2,1,0:T(8,128)(2,1)S(1)}, u32[]{:S(2)}, u32[]{:S(2)}) collective-permute-start(bf16[2,128,256]{2,1,0:T(8,128)(2,1)S(1)} %get-tuple-element.43), channel_id=1, source_target_pairs={{0,8},{4,12},{8,16},{12,20},{16,24},{20,28},{1,9},{5,13},{9,17},{1... | collective-permute-start | bytes 393224 | tf_op jit(solution)/shard_map/ppermute | solution.py:611
  51.5 16.1 %copy-start.5 = (bf16[128]{0:T(256)(128)(2,1)S(1)}, bf16[128]{0:T(256)(128)(2,1)}, u32[]{:S(2)}) copy-start(bf16[128]{0:T(256)(128)(2,1)} %param.22) | copy-start | bytes 772
  51.5 18.7 %copy-start = (bf16[512,2240]{0,1:T(8,128)(2,1)S(1)}, bf16[512,2240]{0,1:T(8,128)(2,1)}, u32[]{:S(2)}) copy-start(bf16[512,2240]{0,1:T(8,128)(2,1)} %param.23) | copy-start | bytes 6881284
  63.2 4.3 %collective-permute-start.7 = (bf16[2,128,128]{2,1,0:T(8,128)(2,1)S(1)}, bf16[2,128,128]{2,1,0:T(8,128)(2,1)S(1)}, u32[]{:S(2)}, u32[]{:S(2)}) collective-permute-start(bf16[2,128,128]{2,1,0:T(8,128)(2,1)S(1)} %get-tuple-element.52), channel_id=1, source_target_pairs={{0,4},{4,0},{8,12},{12,8},{16,20},{20,16},{24,28},{28,24},{1,5},{5... | collective-permute-start | bytes 196616 | tf_op jit(solution)/shard_map/ppermute | solution.py:607
  67.6 31.5 %slice-start = ((s8[6307840]{0:T(1024)(128)(4,1)}), s8[4194304]{0:T(1024)(128)(4,1)S(1)}, s32[]{:S(2)}) async-start(s8[6307840]{0:T(1024)(128)(4,1)} %bitcast.22), calls=%async_computation | async-start | bytes 8388608
  68.7 1.6 %collective-permute-start.8 = (bf16[256,512]{1,0:T(8,128)(2,1)S(1)}, bf16[256,512]{1,0:T(8,128)(2,1)S(1)}, u32[]{:S(2)}, u32[]{:S(2)}) collective-permute-start(bf16[256,512]{1,0:T(8,128)(2,1)S(1)} %get-tuple-element.55.own), channel_id=1, source_target_pairs={{0,1},{1,0},{2,3},{3,2},{4,5},{5,4},{6,7},{7,6},{8,9},{9,8},{10,11... | collective-permute-start | bytes 786440 | tf_op jit(solution)/shard_map/ppermute | solution.py:599
  68.7 4.5 %collective-permute-start.13 = (bf16[256,512]{1,0:T(8,128)(2,1)S(1)}, bf16[256,512]{1,0:T(8,128)(2,1)S(1)}, u32[]{:S(2)}, u32[]{:S(2)}) collective-permute-start(bf16[256,512]{1,0:T(8,128)(2,1)S(1)} %get-tuple-element.58.own), channel_id=1, source_target_pairs={{0,1},{1,0},{2,3},{3,2},{4,5},{5,4},{6,7},{7,6},{8,9},{9,8},{10,11... | collective-permute-start | bytes 786440 | tf_op jit(solution)/shard_map/ppermute | solution.py:599
  70.3 28.8 %slice-start.1 = ((s8[6307840]{0:T(1024)(128)(4,1)}), s8[2113536]{0:T(1024)(128)(4,1)S(1)}, s32[]{:S(2)}) async-start(s8[6307840]{0:T(1024)(128)(4,1)} %bitcast.22), calls=%async_computation.1 | async-start | bytes 4227072
  71.6 27.4 %copy-start.10 = (bf16[2240]{0:T(1024)(128)(2,1)S(1)}, bf16[2240]{0:T(1024)(128)(2,1)}, u32[]{:S(2)}) copy-start(bf16[2240]{0:T(1024)(128)(2,1)} %param.24) | copy-start | bytes 13444
  71.6 27.4 %copy-start.8 = (bf16[3,1400]{1,0:T(4,128)(2,1)S(1)}, bf16[3,1400]{1,0:T(4,128)(2,1)}, u32[]{:S(2)}) copy-start(bf16[3,1400]{1,0:T(4,128)(2,1)} %param.26) | copy-start | bytes 25204
  71.6 15.9 %collective-permute-start.10 = (bf16[1120,256]{1,0:T(8,128)(2,1)S(1)}, bf16[1120,256]{1,0:T(8,128)(2,1)S(1)}, u32[]{:S(2)}, u32[]{:S(2)}) collective-permute-start(bf16[1120,256]{1,0:T(8,128)(2,1)S(1)} %attend.2.refs_1_), channel_id=1, source_target_pairs={{0,2},{1,3},{2,0},{3,1},{4,6},{5,7},{6,4},{7,5},{8,10},{9,11},{10,... | collective-permute-start | bytes 1720328 | tf_op jit(solution)/shard_map/ppermute | solution.py:603
  74.5 24.5 %collective-permute-start.14 = (bf16[1120,256]{1,0:T(8,128)(2,1)S(1)}, bf16[1120,256]{1,0:T(8,128)(2,1)S(1)}, u32[]{:S(2)}, u32[]{:S(2)}) collective-permute-start(bf16[1120,256]{1,0:T(8,128)(2,1)S(1)} %attend.3.refs_1_), channel_id=1, source_target_pairs={{0,2},{1,3},{2,0},{3,1},{4,6},{5,7},{6,4},{7,5},{8,10},{9,11},{10,... | collective-permute-start | bytes 1720328 | tf_op jit(solution)/shard_map/ppermute | solution.py:603
  75.1 23.9 %collective-permute-start.11 = (bf16[1120,256]{1,0:T(8,128)(2,1)S(1)}, bf16[1120,256]{1,0:T(8,128)(2,1)S(1)}, u32[]{:S(2)}, u32[]{:S(2)}) collective-permute-start(bf16[1120,256]{1,0:T(8,128)(2,1)S(1)} %attend.2.refs_1_), channel_id=1, source_target_pairs={{0,1},{1,0},{2,3},{3,2},{4,5},{5,4},{6,7},{7,6},{8,9},{9,8},{10,11... | collective-permute-start | bytes 1720328 | tf_op jit(solution)/shard_map/ppermute | solution.py:599
  87.5 11.5 %collective-permute-start.12 = (bf16[1120,256]{1,0:T(8,128)(2,1)S(1)}, bf16[1120,256]{1,0:T(8,128)(2,1)S(1)}, u32[]{:S(2)}, u32[]{:S(2)}) collective-permute-start(bf16[1120,256]{1,0:T(8,128)(2,1)S(1)} %collective-permute-done.10.refs_2_), channel_id=1, source_target_pairs={{0,1},{1,0},{2,3},{3,2},{4,5},{5,4},{6,7},{7,6},{8,9},{9,8},{10,11... | collective-permute-start | bytes 1720328 | tf_op jit(solution)/shard_map/ppermute | solution.py:599
  87.5 25.8 %collective-permute-start.15 = (bf16[1120,256]{1,0:T(8,128)(2,1)S(1)}, bf16[1120,256]{1,0:T(8,128)(2,1)S(1)}, u32[]{:S(2)}, u32[]{:S(2)}) collective-permute-start(bf16[1120,256]{1,0:T(8,128)(2,1)S(1)} %attend.3.refs_1_), channel_id=1, source_target_pairs={{0,1},{1,0},{2,3},{3,2},{4,5},{5,4},{6,7},{7,6},{8,9},{9,8},{10,11... | collective-permute-start | bytes 1720328 | tf_op jit(solution)/shard_map/ppermute | solution.py:599
  99.0 14.4 %collective-permute-start.16 = (bf16[1120,256]{1,0:T(8,128)(2,1)S(1)}, bf16[1120,256]{1,0:T(8,128)(2,1)S(1)}, u32[]{:S(2)}, u32[]{:S(2)}) collective-permute-start(bf16[1120,256]{1,0:T(8,128)(2,1)S(1)} %collective-permute-done.14.refs_2_), channel_id=1, source_target_pairs={{0,1},{1,0},{2,3},{3,2},{4,5},{5,4},{6,7},{7,6},{8,9},{9,8},{10,11... | collective-permute-start | bytes 1720328 | tf_op jit(solution)/shard_map/ppermute | solution.py:599
  99.1 22.4 %slice-start.2 = ((s8[6307840]{0:T(1024)(128)(4,1)}), s8[4194304]{0:T(1024)(128)(4,1)S(1)}, s32[]{:S(2)}) async-start(s8[6307840]{0:T(1024)(128)(4,1)} %bitcast.26), calls=%async_computation.2 | async-start | bytes 8388608
  106.6 14.9 %collective-permute-start.17 = (bf16[1,1400]{1,0:T(2,128)(2,1)S(1)}, bf16[1,1400]{1,0:T(2,128)(2,1)S(1)}, u32[]{:S(2)}, u32[]{:S(2)}) collective-permute-start(bf16[1,1400]{1,0:T(2,128)(2,1)S(1)} %get-tuple-element.60), channel_id=1, source_target_pairs={{0,4},{4,8},{8,12},{12,16},{16,20},{20,24},{24,28},{1,5},{5,9},{9,... | collective-permute-start | bytes 8408 | tf_op jit(solution)/shard_map/ppermute | solution.py:711
  110.0 11.5 %collective-permute-start.18 = (bf16[1,1400]{1,0:T(2,128)(2,1)S(1)}, bf16[1,1400]{1,0:T(2,128)(2,1)S(1)}, u32[]{:S(2)}, u32[]{:S(2)}) collective-permute-start(bf16[1,1400]{1,0:T(2,128)(2,1)S(1)} %get-tuple-element.61), channel_id=1, source_target_pairs={{4,0},{8,4},{12,8},{16,12},{20,16},{24,20},{28,24},{5,1},{9,5},{13... | collective-permute-start | bytes 8408 | tf_op jit(solution)/shard_map/ppermute | solution.py:712
  113.4 8.1 %slice-start.3 = ((s8[6307840]{0:T(1024)(128)(4,1)}), s8[2113536]{0:T(1024)(128)(4,1)S(1)}, s32[]{:S(2)}) async-start(s8[6307840]{0:T(1024)(128)(4,1)} %bitcast.26), calls=%async_computation.3 | async-start | bytes 4227072
  127.5 3.6 %collective-permute-start.19 = (bf16[560,512]{1,0:T(8,128)(2,1)S(1)}, bf16[560,512]{1,0:T(8,128)(2,1)S(1)}, u32[]{:S(2)}, u32[]{:S(2)}) collective-permute-start(bf16[560,512]{1,0:T(8,128)(2,1)S(1)} %get-tuple-element.67), channel_id=1, source_target_pairs={{0,1},{1,0},{2,3},{3,2},{4,5},{5,4},{6,7},{7,6},{8,9},{9,8},{10,11... | collective-permute-start | bytes 1720328 | tf_op jit(solution)/shard_map/ppermute | solution.py:599
  130.6 2.3 %collective-permute-start.21 = (bf16[560,512]{1,0:T(8,128)(2,1)S(1)}, bf16[560,512]{1,0:T(8,128)(2,1)S(1)}, u32[]{:S(2)}, u32[]{:S(2)}) collective-permute-start(bf16[560,512]{1,0:T(8,128)(2,1)S(1)} %get-tuple-element.68), channel_id=1, source_target_pairs={{0,1},{1,0},{2,3},{3,2},{4,5},{5,4},{6,7},{7,6},{8,9},{9,8},{10,11... | collective-permute-start | bytes 1720328 | tf_op jit(solution)/shard_map/ppermute | solution.py:599
  131.3 15.0 %collective-permute-start.20 = (bf16[560,512]{1,0:T(8,128)(2,1)S(1)}, bf16[560,512]{1,0:T(8,128)(2,1)S(1)}, u32[]{:S(2)}, u32[]{:S(2)}) collective-permute-start(bf16[560,512]{1,0:T(8,128)(2,1)S(1)} %add_convert_fusion.1), channel_id=1, source_target_pairs={{0,2},{1,3},{2,0},{3,1},{4,6},{5,7},{6,4},{7,5},{8,10},{9,11},{10,... | collective-permute-start | bytes 1720328 | tf_op jit(solution)/shard_map/ppermute | solution.py:603

commit v3 on v2

v3 whole, which is shorter than its diff:
```python
import functools

import jax
import jax.numpy as jnp
from jax import lax
from jax.experimental import pallas as pl
from jax.experimental.pallas import tpu as pltpu
from jax.sharding import PartitionSpec as P

DK = 128
BLOCK = 128
epsilon = 1e-06
f32 = jnp.float32
bf16 = jnp.bfloat16

PARITY, CORE, ME, CHIP = 0, 1, 2, 3

VM = pl.BlockSpec(memory_space=pltpu.VMEM)
SM = pl.BlockSpec(memory_space=pltpu.SMEM)
ANY = pl.BlockSpec(memory_space=pl.ANY)


def params(mebibytes):
    return pltpu.CompilerParams(vmem_limit_bytes=mebibytes * 1024 * 1024)


def cost(flops, moved):
    return pl.CostEstimate(flops=flops, bytes_accessed=moved, transcendentals=0)


def shape_of(shape, dtype=bf16):
    return jax.ShapeDtypeStruct(shape, dtype)


def dot(a, b):
    return jnp.dot(a, b, preferred_element_type=f32)


def dot_nt(a, b):
    return lax.dot_general(a, b, (((1,), (1,)), ((), ())), preferred_element_type=f32)


def dot_tn(a, b):
    return lax.dot_general(a, b, (((0,), (0,)), ((), ())), preferred_element_type=f32)


def iotas(shape):
    return lax.broadcasted_iota(jnp.int32, shape, 0), lax.broadcasted_iota(jnp.int32, shape, 1)


def column_of(row, lanes=128):
    return jnp.broadcast_to(row, (lanes, row.shape[1])).T


def scale_pass(source, gain_at, target):
    features, tokens = source.shape
    squares = jnp.zeros((8, tokens), f32)
    for start in range(0, features, 128):
        size = min(128, features - start)
        value = source[start : start + size, :].astype(f32)
        scale = column_of(gain_at(start, size))
        scale = jnp.concatenate([scale] * (tokens // 128), axis=1)
        target[:, start : start + size] = (value * scale).astype(bf16).T
        value = value * value
        for r in range(0, size, 8):
            squares = squares + value[r : r + 8]
    return squares


def inverse_of(squares, features):
    return lax.rsqrt(jnp.sum(squares, axis=0, keepdims=True) / features + epsilon)


def fill_columns(row, target):
    for start in range(0, row.shape[1], 128):
        target[start : start + 128, :] = column_of(row[:, start : start + 128])


def doubled(tile):
    return jnp.concatenate([tile, tile], axis=1)


def slots_of(meta, n):
    return [meta[CORE], 1 - meta[CORE]] if n == 2 else [0]


def load_pair(meta, pieces, whole, sem):
    part = pieces[0].shape[0]
    copies = [
        pltpu.make_async_copy(
            piece, whole.at[pl.ds(pl.multiple_of(slot * part, 16), part)], sem.at[p]
        )
        for p, (piece, slot) in enumerate(zip(pieces, slots_of(meta, len(pieces))))
    ]
    for copy in copies:
        copy.start()
    for copy in copies:
        copy.wait()


def held_rows(meta, at, weights, held, sem):
    span = held.shape[1]
    rows = pl.ds(pl.multiple_of(meta[at] * span, 16), span)
    copies = [
        pltpu.make_async_copy(ref.at[rows], held.at[i], sem.at[i]) for i, ref in enumerate(weights)
    ]
    for copy in copies:
        copy.start()
    return copies


def early_kernel(count_in, at, meta, *refs):
    first = at == CHIP
    pieces = refs[:count_in]
    gain, gates, w_key, w_value, w_query, w_down = refs[count_in : count_in + 6]
    refs = refs[count_in + 6 :]
    before, refs = (None, refs) if first else (refs[:5], refs[5:])
    acc_k, acc_v, acc_q, acc_g, squares = refs[:5]
    partner_w, whole, scaled, held, held_sem, sem = refs[5:] if first else (None, *refs[5:])
    rows_copies = held_rows(meta, at, (w_key, w_value, w_query), held, held_sem)
    copies = [
        pltpu.make_async_copy(
            w_down.at[2 * y + 1 - meta[CORE]], partner_w.at[y], sem.at[count_in + y]
        )
        for y in range(partner_w.shape[0] if first else 0)
    ]
    for copy in copies:
        copy.start()
    load_pair(meta, pieces, whole, sem)
    sums = scale_pass(whole, lambda at, size: gain[:, at : at + size], scaled)
    gate = dot_nt(gates[...], scaled[...])
    squares[...] = sums if first else before[4][...] + sums
    acc_g[...] = gate if first else before[3][...] + gate
    for i, out in enumerate((acc_k, acc_v, acc_q)):
        rows_copies[i].wait()
        product = dot(scaled[...], held[i])
        out[...] = product if first else before[i][...] + product
    for copy in copies:
        copy.wait()


def early_project(meta, at, pieces, gain, gates, w_key, w_value, w_query, w_down, before):
    first = before is None
    blocks, part, hidden = w_down.shape
    ys = blocks // 2
    span = gain.shape[1]
    count = pieces[0].shape[1]
    inner = w_key.shape[1]
    return pl.pallas_call(
        functools.partial(early_kernel, len(pieces), at),
        out_shape=[shape_of((count, inner), f32)] * 3
        + [shape_of((16, count), f32), shape_of((8, count), f32)]
        + [shape_of((ys, part, hidden))] * first,
        in_specs=[SM] + [ANY] * len(pieces) + [VM] * 2 + [ANY] * 4 + [VM] * (0 if first else 5),
        out_specs=[VM] * (5 + first),
        scratch_shapes=[
            pltpu.VMEM((span, count), bf16),
            pltpu.VMEM((count, span), bf16),
            pltpu.VMEM((3, span, inner), bf16),
            pltpu.SemaphoreType.DMA((3,)),
            pltpu.SemaphoreType.DMA((len(pieces) + ys,)),
        ],
        compiler_params=params(24),
        cost_estimate=cost(3 * 10**9, 8 * 10**6),
        name="early_project",
    )(meta, *pieces, gain, gates, w_key, w_value, w_query, w_down, *(before or ()))


def maps_kernel(n, heads, at, meta, *refs):
    pieces = refs[:n]
    gain, rates, gates, w_key, w_value, acc_k, acc_v, acc_g, squares = refs[n : n + 9]
    scaled, scale_b, keys, erased, entry, own, sent, totals = refs[n + 9 : n + 17]
    whole, raw_k, raw_v, rows_at_head, total_b, beta_b, held, held_sem, sem = refs[n + 17 :]
    span, count = whole.shape
    blocks = count // BLOCK
    inner = heads * DK
    features = w_key.shape[0]
    parity = meta[PARITY]
    rows_copies = held_rows(meta, at, (w_key, w_value), held, held_sem)
    load_pair(meta, pieces, whole, sem)
    sums = scale_pass(whole, lambda at, size: gain[:, at : at + size], scaled)
    inverse = inverse_of(sums + squares[...], features)
    fill_columns(inverse, scale_b)

    pre = (acc_g[...] + dot_nt(gates[...], scaled[...])) * inverse
    soft = jnp.maximum(pre, 0.0) + jnp.log1p(jnp.exp(-jnp.abs(pre)))
    rate = jnp.concatenate([rates[...]] * (count // 128), axis=1)
    decay = -rate * soft
    beta = jax.nn.sigmoid(pre + rate)
    row_at, col_at = iotas((BLOCK, BLOCK))
    upper = (row_at <= col_at).astype(f32)
    rows_at_head[...] = jnp.zeros_like(rows_at_head)
    for c in range(blocks):
        tokens = slice(c * BLOCK, (c + 1) * BLOCK)
        total = jnp.dot(
            decay[:, tokens], upper, precision=lax.Precision.HIGHEST, preferred_element_type=f32
        )
        totals[c] = total
        rows_at_head[0:16, :] = total
        rows_at_head[16:32, :] = beta[:, tokens]
        columns = rows_at_head[...].T
        for h in range(heads):
            total_b[h, tokens, :] = jnp.broadcast_to(columns[:, h : h + 1], (BLOCK, DK))
            lane = 16 + heads + h
            beta_b[h, tokens, :] = jnp.broadcast_to(columns[:, lane : lane + 1], (BLOCK, DK))

    for copy in rows_copies:
        copy.wait()
    for start in range(0, inner, 256):
        cols = slice(start, start + 256)
        scale = doubled(scale_b[...])
        raw_k[:, cols] = ((acc_k[:, cols] + dot(scaled[...], held[0, :, cols])) * scale).astype(bf16)
        raw_v[:, cols] = ((acc_v[:, cols] + dot(scaled[...], held[1, :, cols])) * scale).astype(bf16)

    xor = jnp.where(row_at > col_at, row_at ^ col_at, 0)
    eye = jnp.where(row_at == col_at, 1.0, 0.0)
    group = 2 if heads % 2 == 0 else 1

    @pl.loop(0, heads // group)
    def _(batch):
        lows, solved = [], []
        chains = []
        for g in range(group):
            h = batch * group + g
            cols = pl.ds(pl.multiple_of(h * DK, DK), DK)
            wide = pl.ds(pl.multiple_of(h * 2 * DK, 2 * DK), 2 * DK)
            raw = raw_k[:, cols].astype(f32)
            unit = raw * lax.rsqrt(jnp.sum(raw * raw, axis=1, keepdims=True) + epsilon)
            keys[:, cols] = unit.astype(bf16)
            for c in range(blocks):
                chains.append((h, cols, wide, c, slice(c * BLOCK, (c + 1) * BLOCK)))
        for h, cols, wide, c, rows in chains:
            k = keys[rows, cols]
            fade = jnp.exp(jnp.minimum(total_b[h, rows, :] - totals[c, pl.ds(h, 1), :], 0.0))
            low = jnp.where(xor > 0, beta_b[h, rows, :] * fade * dot_nt(k, k), 0.0)
            lows.append(low)
            solved.append(eye - jnp.where(xor == 1, low, 0.0))
        size = 2
        while size < BLOCK:
            mask = (xor >= size) & (xor < 2 * size)
            first = []
            for i in range(len(chains)):
                link = jnp.where(mask, lows[i], 0.0).astype(bf16)
                first.append(dot(link, solved[i].astype(bf16)).astype(bf16))
            solved = [
                solved[i] - dot(solved[i].astype(bf16), first[i]) for i in range(len(chains))
            ]
            size *= 2
        grown = []
        for i, (h, cols, wide, c, rows) in enumerate(chains):
            k = keys[rows, cols].astype(f32)
            t_col = total_b[h, rows, :]
            b_col = beta_b[h, rows, :]
            right = jnp.concatenate(
                [
                    (b_col * jnp.exp(t_col) * k).astype(bf16),
                    (b_col * raw_v[rows, cols].astype(f32)).astype(bf16),
                ],
                axis=1,
            )
            both = dot(solved[i].astype(bf16), right).astype(bf16)
            erased[rows, wide] = both
            t_end = t_col[BLOCK - 1 : BLOCK, :]
            faded = (jnp.exp(t_end - t_col) * k).astype(bf16)
            grown.append((jnp.exp(t_end), dot_tn(faded, both)))
        states = [None] * group
        for c in range(blocks):
            for g in range(group):
                h, cols, wide = chains[g * blocks][:3]
                end, product = grown[g * blocks + c]
                erase, write = product[:, :DK], product[:, DK:]
                if c == 0:
                    state = jnp.concatenate([end * eye - erase, write], axis=1)
                else:
                    step = dot(erase.astype(bf16), states[g].astype(bf16))
                    state = (
                        jnp.concatenate([end, end], axis=1) * states[g]
                        - step
                        + jnp.concatenate([jnp.zeros_like(write), write], axis=1)
                    )
                if c < blocks - 1:
                    entry[c, :, wide] = state.astype(bf16)
                states[g] = state
        for g in range(group):
            h = batch * group + g
            half = heads // 2
            mine = (h >= half) == (parity == 1)
            slot = lax.rem(h, half)

            @pl.when(mine)
            def _():
                own[slot] = states[g].astype(bf16)

            @pl.when(jnp.logical_not(mine))
            def _():
                sent[slot] = states[g].astype(bf16)


def block_maps(meta, at, pieces, gain, rates, gates, w_key, w_value, early):
    n = len(pieces)
    acc_k, acc_v, acc_q, acc_g, squares = early
    count = pieces[0].shape[1]
    span = gain.shape[1]
    inner = w_key.shape[1]
    heads = inner // DK
    blocks = count // BLOCK
    return pl.pallas_call(
        functools.partial(maps_kernel, n, heads, at),
        out_shape=(
            shape_of((count, span)),
            shape_of((count, DK), f32),
            shape_of((count, inner)),
            shape_of((count, 2 * inner)),
            shape_of((blocks - 1, DK, 2 * inner)),
            shape_of((heads // 2, DK, 2 * DK)),
            shape_of((heads // 2, DK, 2 * DK)),
            shape_of((blocks, 16, 128), f32),
        ),
        in_specs=[SM] + [ANY] * n + [VM] * 3 + [ANY] * 2 + [VM] * 4,
        out_specs=[VM] * 8,
        scratch_shapes=[
            pltpu.VMEM((span, count), bf16),
            pltpu.VMEM((count, inner), bf16),
            pltpu.VMEM((count, inner), bf16),
            pltpu.VMEM((128, BLOCK), f32),
            pltpu.VMEM((heads, count, DK), f32),
            pltpu.VMEM((heads, count, DK), f32),
            pltpu.VMEM((2, span, inner), bf16),
            pltpu.SemaphoreType.DMA((2,)),
            pltpu.SemaphoreType.DMA((n,)),
        ],
        compiler_params=params(24),
        cost_estimate=cost(10 * 10**9, 14 * 10**6),
        name="block_maps",
    )(meta, *pieces, gain, rates, gates, w_key, w_value, acc_k, acc_v, acc_g, squares)


def query_kernel(n, ys, meta, scaled, scale_b, weights, acc, *refs):
    pieces, (query, tokens_a, tokens_b, done, held, sem) = refs[: n * ys], refs[n * ys :]
    (copy,) = held_rows(meta, CHIP + ys - 1, (weights,), held, sem)
    span = scaled.shape[1]
    part, count = pieces[0].shape
    for d in range(ys):
        for p, slot in enumerate(slots_of(meta, n)):
            piece = pieces[d * n + p]
            base = meta[CHIP + d] * span + slot * part
            step = part // 7

            @pl.loop(0, 7)
            def _(r):
                rows = pl.ds(pl.multiple_of(r * step, 8), step)
                target = pl.ds(pl.multiple_of(base + r * step, 8), step)
                tokens_a[target, :BLOCK] = piece[rows, :BLOCK]
                tokens_a[target, BLOCK:] = piece[rows, count - BLOCK :]
                tokens_b[target, :] = piece[rows, BLOCK : count - BLOCK]

    done[...] = jnp.zeros_like(done)
    copy.wait()
    for start in range(0, query.shape[1], 256):
        cols = slice(start, start + 256)
        product = acc[:, cols] + dot(scaled[...], held[0, :, cols])
        query[:, cols] = (product * doubled(scale_b[...])).astype(bf16)


def queries(meta, ys, scaled, scale_b, weights, acc, pieces):
    n = len(pieces) // ys
    features = weights.shape[0]
    count = acc.shape[0]
    return pl.pallas_call(
        functools.partial(query_kernel, n, ys),
        out_shape=(
            shape_of(acc.shape),
            shape_of((features, 2 * BLOCK)),
            shape_of((features, count - 2 * BLOCK)),
            shape_of((8, 128), f32),
        ),
        in_specs=[SM] + [VM] * 2 + [ANY] + [VM] * (1 + len(pieces)),
        out_specs=[VM] * 4,
        scratch_shapes=[
            pltpu.VMEM((1, scaled.shape[1], acc.shape[1]), bf16),
            pltpu.SemaphoreType.DMA((1,)),
        ],
        compiler_params=params(16),
        cost_estimate=cost(10**9, 8 * 10**6),
        name="queries",
    )(meta, scaled, scale_b, weights, acc, *pieces)


def outputs_kernel(heads, query, keys, erased, entry, totals, after, shard_query, free, done, rows_at_head):
    count = query.shape[0]
    blocks = count // BLOCK
    row_at, col_at = iotas((BLOCK, BLOCK))
    done[...] = jnp.zeros_like(done)
    rows_at_head[...] = jnp.zeros_like(rows_at_head)
    for c in range(blocks):
        rows = slice(c * BLOCK, (c + 1) * BLOCK)
        rows_at_head[0:16, :] = totals[c]
        columns = rows_at_head[...].T
        for h in range(heads):
            cols = slice(h * DK, (h + 1) * DK)
            wide = slice(h * 2 * DK, (h + 1) * 2 * DK)
            t_col = jnp.broadcast_to(columns[:, h : h + 1], (BLOCK, BLOCK))
            t_row = totals[c, h : h + 1, :]
            fade = jnp.where(row_at >= col_at, jnp.exp(jnp.minimum(t_col - t_row, 0.0)), 0.0)
            q = query[rows, cols]
            scores = (fade * dot_nt(q, keys[rows, cols])).astype(bf16)
            both = dot(scores, erased[rows, wide])
            reach = jnp.exp(t_col) * q.astype(f32) - both[:, :DK]
            local = both[:, DK:]
            if c > 0:
                product = dot(reach.astype(bf16), entry[c - 1, :, wide])
                reach = product[:, :DK]
                local = local + product[:, DK:]
            shard_query[rows, cols] = reach.astype(bf16)
            free[rows, cols] = local


def block_outputs(query, keys, erased, entry, totals, after):
    heads = query.shape[1] // DK
    return pl.pallas_call(
        functools.partial(outputs_kernel, heads),
        out_shape=(shape_of(query.shape), shape_of(query.shape, f32), shape_of((8, 128), f32)),
        in_specs=[VM] * 5 + [ANY],
        out_specs=[VM] * 3,
        scratch_shapes=[pltpu.VMEM((128, BLOCK), f32)],
        compiler_params=params(16),
        cost_estimate=cost(3 * 10**9, 4 * 10**6),
        name="block_outputs",
    )(query, keys, erased, entry, totals, after)


def pair_kernel(meta, own, other, after, pair, first, done):
    even = meta[PARITY] == 0
    for h in range(own.shape[0]):
        mine, theirs = own[h], other[h]
        early = jnp.where(even, mine, theirs)
        late = jnp.where(even, theirs, mine)
        product = dot(late[:, :DK], early)
        shift = late[:, DK:].astype(f32)
        pair[h] = (product + jnp.concatenate([jnp.zeros_like(shift), shift], axis=1)).astype(bf16)
        first[h] = early
    done[...] = jnp.zeros_like(done)


def pair_maps(meta, own, other, after):
    return pl.pallas_call(
        pair_kernel,
        out_shape=(shape_of(own.shape), shape_of(own.shape), shape_of((8, 128), f32)),
        in_specs=[SM, VM, VM, ANY],
        out_specs=[VM] * 3,
        compiler_params=params(8),
        name="pair_maps",
    )(meta, own, other, after)


def apply_map(whole, state):
    high = state.astype(bf16)
    low = (state - high.astype(f32)).astype(bf16)
    product = dot(whole[:, :DK], jnp.concatenate([high, low], axis=1))
    return product[:, :DK] + product[:, DK:] + whole[:, DK:].astype(f32)


def start_kernel(steps, meta, first, *refs):
    pairs, (after, keep, give) = refs[:steps], refs[steps:]
    even = meta[PARITY] == 0
    for h in range(first.shape[0]):
        state = pairs[0][h][:, DK:].astype(f32)
        for pair in pairs[1:]:
            state = apply_map(pair[h], state)
        later = apply_map(first[h], state)
        keep[h] = jnp.where(even, state, later).astype(bf16)
        give[h] = jnp.where(even, later, state).astype(bf16)


def start_states(meta, first, pairs, after):
    heads = first.shape[0]
    shape = shape_of((heads, DK, DK))
    return pl.pallas_call(
        functools.partial(start_kernel, len(pairs)),
        out_shape=(shape, shape),
        in_specs=[SM] + [VM] * (1 + len(pairs)) + [ANY],
        out_specs=[VM] * 2,
        compiler_params=params(8),
        name="start_states",
    )(meta, first, *pairs, after)


def mixed_kernel(heads, meta, own, other, shard_query, free, gain, mixed_a, mixed_b):
    even = meta[PARITY] == 0
    half = heads // 2
    blocks = shard_query.shape[0] // BLOCK
    for h in range(heads):
        cols = slice(h * DK, (h + 1) * DK)
        if h < half:
            state = jnp.where(even, own[h], other[h])
        else:
            state = jnp.where(even, other[h - half], own[h - half])
        for unit in range(blocks):
            rows = slice(unit * BLOCK, (unit + 1) * BLOCK)
            out = dot(shard_query[rows, cols], state) + free[rows, cols]
            scale = lax.rsqrt(jnp.mean(out * out, axis=1, keepdims=True) + epsilon)
            value = (out * scale * gain[...].astype(f32)).astype(bf16)
            if unit == 0:
                mixed_a[:BLOCK, cols] = value
            elif unit == blocks - 1:
                mixed_a[BLOCK:, cols] = value
            else:
                mixed_b[(unit - 1) * BLOCK : unit * BLOCK, cols] = value


def mixed_heads(meta, own, other, shard_query, free, gain):
    count, inner = shard_query.shape
    return pl.pallas_call(
        functools.partial(mixed_kernel, inner // DK),
        out_shape=(shape_of((2 * BLOCK, inner)), shape_of((count - 2 * BLOCK, inner))),
        in_specs=[SM] + [VM] * 5,
        out_specs=[VM] * 2,
        compiler_params=params(12),
        cost_estimate=cost(10**9, 3 * 10**6),
        name="mixed_heads",
    )(meta, own, other, shard_query, free, gain)


def attend_kernel(meta, own, other, weights, other_weights, chip):
    rows = pl.ds(pl.multiple_of(meta[CORE] * chip.shape[0], 16), chip.shape[0])
    total = dot_nt(weights[rows, :], own[...]) + dot_nt(other_weights[rows, :], other[...])
    chip[...] = total.astype(bf16)


def attend(meta, own, other, weights, other_weights):
    return pl.pallas_call(
        attend_kernel,
        out_shape=shape_of((weights.shape[0] // 2, own.shape[0])),
        in_specs=[SM] + [VM] * 4,
        out_specs=VM,
        compiler_params=params(16),
        cost_estimate=cost(10**9, 5 * 10**6),
        name="attend",
    )(meta, own, other, weights, other_weights)


def up_kernel(adds, meta, tokens, *refs):
    own, other = refs[:adds], refs[adds : 2 * adds]
    gain, weights, lifted, middle_part, first, last, middle, hidden, scale_b = refs[2 * adds :]
    features, count = middle.shape
    half = features // 2
    step = 160
    for side, parts in ((meta[CORE], own), (1 - meta[CORE], other)):

        @pl.loop(0, half // step)
        def _(r):
            rows = pl.ds(pl.multiple_of(r * step, 32), step)
            target = pl.ds(pl.multiple_of(side * half + r * step, 32), step)
            total = tokens[target, :].astype(f32)
            for ref in parts:
                total = total + ref[rows, :].astype(f32)
            middle[target, :] = total.astype(bf16).astype(f32)

    squares = scale_pass(middle, lambda at, size: gain[:, at : at + size], hidden)
    fill_columns(inverse_of(squares, features), scale_b)
    part = middle_part.shape[0]
    middle_part[...] = middle[pl.ds(pl.multiple_of(meta[ME] * part, 8), part), :]
    width = lifted.shape[1]
    for start in range(0, width, 256):
        size = min(256, width - start)
        cols = slice(start, start + size)
        scale = doubled(scale_b[...])[:, :size]
        lifted[:, cols] = (dot(hidden[...], weights[:, cols]) * scale).astype(bf16)
    first[...] = lifted[0:1, :]
    last[...] = lifted[count - 1 : count, :]


def up_project(meta, tokens, own, other, gain, weights, part):
    features, hidden = weights.shape
    count = tokens.shape[1]
    return pl.pallas_call(
        functools.partial(up_kernel, len(own)),
        out_shape=(
            shape_of((count, hidden)),
            shape_of((part, count), f32),
            shape_of((1, hidden)),
            shape_of((1, hidden)),
        ),
        in_specs=[SM] + [VM] * (3 + 2 * len(own)),
        out_specs=[VM] * 4,
        scratch_shapes=[
            pltpu.VMEM((features, count), f32),
            pltpu.VMEM((count, features), bf16),
            pltpu.VMEM((count, DK), f32),
        ],
        compiler_params=params(20),
        cost_estimate=cost(2 * 10**9, 8 * 10**6),
        name="up_project",
    )(meta, tokens, *own, *other, gain, weights)


def gelu_of(x):
    inner = 0.7978845608028654 * (x + 0.044715 * (x * x * x))
    return 0.5 * x * (1.0 + jnp.tanh(inner))


def act_kernel(late, meta, outer, inside, before, after, taps, act_t, padded, act):
    count = act.shape[0]
    if late:
        padded[7:8, :] = inside[BLOCK - 1 : BLOCK, :].astype(f32)
        padded[8 : 8 + BLOCK, :] = inside[BLOCK:, :].astype(f32)
        padded[8 + BLOCK : 8 + count, :] = outer[BLOCK:, :].astype(f32)
        padded[8 + count : 9 + count, :] = after[...].astype(f32)
    else:
        padded[7:8, :] = before[...].astype(f32)
        padded[8 : 8 + BLOCK, :] = outer[:BLOCK, :].astype(f32)
        padded[8 + BLOCK : 8 + count, :] = inside[:BLOCK, :].astype(f32)
        padded[8 + count : 9 + count, :] = inside[BLOCK : BLOCK + 1, :].astype(f32)

    @pl.loop(0, count // 32)
    def _(r):
        base = pl.multiple_of(r * 32, 32)
        window = padded[pl.ds(base, 48), :]
        value = (
            taps[0:1, :] * window[7:39, :]
            + taps[1:2, :] * window[8:40, :]
            + taps[2:3, :] * window[9:41, :]
        )
        act[pl.ds(base, 32), :] = gelu_of(value).astype(bf16)

    act_t[...] = act[...].T


def activate(meta, outer, inside, before, after, taps, late):
    hidden = outer.shape[1]
    count = (outer.shape[0] + inside.shape[0]) // 2
    return pl.pallas_call(
        functools.partial(act_kernel, late),
        out_shape=shape_of((hidden, count)),
        in_specs=[SM] + [VM] * 5,
        out_specs=VM,
        scratch_shapes=[pltpu.VMEM((count + 16, hidden), f32), pltpu.VMEM((count, hidden), bf16)],
        compiler_params=params(12),
        cost_estimate=cost(10**9, 2 * 10**6),
        name="activate",
    )(meta, outer, inside, before, after, taps)


def far_kernel(ys, meta, own, other, weights, other_weights, *outs):
    for i, out in enumerate(outs):
        chip = meta[CHIP + ys + i]
        block = 2 * chip + meta[CORE]
        total = dot(weights[block], own[...]) + dot(other_weights[chip], other[...])
        out[...] = total.astype(bf16)


def far_project(meta, ys, own, other, weights, other_weights):
    part = weights.shape[1]
    return pl.pallas_call(
        functools.partial(far_kernel, ys),
        out_shape=[shape_of((part, own.shape[1]))] * (ys - 1),
        in_specs=[SM] + [VM] * 4,
        out_specs=[VM] * (ys - 1),
        compiler_params=params(16),
        cost_estimate=cost(10**9, 4 * 10**6),
        name="far_project",
    )(meta, own, other, weights, other_weights)


def near_kernel(meta, own_a, other_a, own_b, other_b, middle_a, middle_b, weights, other_weights, after, base):
    size = own_a.shape[1]
    middle = (
        jnp.concatenate([middle_a[:, :BLOCK], middle_b[:, :BLOCK]], axis=1),
        jnp.concatenate([middle_b[:, BLOCK:], middle_a[:, BLOCK:]], axis=1),
    )
    for i, (own, other) in enumerate(((own_a, other_a), (own_b, other_b))):
        total = dot(weights[meta[ME]], own[...])
        total = total + dot(other_weights[meta[CHIP]], other[...])
        base[:, i * size : (i + 1) * size] = total + middle[i]


def near_project(meta, own, other, middle_a, middle_b, weights, other_weights, after):
    part = weights.shape[1]
    return pl.pallas_call(
        near_kernel,
        out_shape=shape_of((part, 2 * own[0].shape[1]), f32),
        in_specs=[SM] + [VM] * 8 + [ANY],
        out_specs=VM,
        compiler_params=params(20),
        cost_estimate=cost(2 * 10**9, 6 * 10**6),
        name="near_project",
    )(meta, own[0], other[0], own[1], other[1], middle_a, middle_b, weights, other_weights, after)


def core_swap(value, n):
    return lax.ppermute(value, "head", [(i, i ^ 1) for i in range(n)])


def y_shift(value, n, step):
    return lax.ppermute(value, "head", [(i, (i + 2 * step) % n) for i in range(n)])


def pair_swap(value, n):
    return lax.ppermute(value, "seq", [(i, i ^ 1) for i in range(n)])


def later(value, n, step):
    return lax.ppermute(value, "seq", [(i, i + 2 * step) for i in range(n - 2 * step)])


def shards(
    tokens,
    norm_gain,
    w_query,
    w_key,
    w_value,
    w_decay,
    w_beta,
    head_rates,
    head_gain,
    w_out,
    ffn_gain,
    w_up,
    conv_taps,
    w_down,
):
    n = lax.axis_size("head")
    seqs = lax.axis_size("seq")
    me = lax.axis_index("head")
    at = lax.axis_index("seq")
    core = me % 2
    parity = at % 2
    ys = n // 2
    count, part = tokens.shape
    heads = w_query.shape[1] // DK
    hidden = w_up.shape[1]
    features = n * part

    mine = tokens.T
    shifted = [mine] + [y_shift(mine, n, d) for d in range(1, ys)]

    def group_of(piece):
        partner = core_swap(piece, n)
        if part % 16:
            first = jnp.where(core == 0, piece, partner)
            second = jnp.where(core == 0, partner, piece)
            return [jnp.concatenate([first, second], axis=0)]
        return [piece, partner]

    groups = [group_of(mine)]
    chip = me // 2
    here = [parity, core, me]
    sources = [(chip + ys - d) % ys for d in range(ys)]
    targets = [(chip + d) % ys for d in range(1, ys)]
    meta = jnp.stack(here + sources + targets).astype(jnp.int32)

    w_out_t = w_out.T
    w_parts = w_down.T.reshape(n, part, hidden)

    gates = jnp.concatenate([w_decay.T, w_beta.T], axis=0)
    gates = jnp.pad(gates, ((0, 16 - 2 * heads), (0, 0)))
    gates = gates.reshape(16, ys, 2 * part).transpose(1, 0, 2)
    rates = jnp.pad(head_rates.reshape(2 * heads, 1), ((0, 16 - 2 * heads), (0, 0)))
    rates = jnp.broadcast_to(rates, (16, 128))
    gain = norm_gain.astype(f32).reshape(ys, 1, 2 * part)

    def ours(rows, d):
        return lax.dynamic_index_in_dim(rows, sources[d], 0, False)

    ffn_scale = ffn_gain.astype(f32).reshape(1, features)
    taps = conv_taps.astype(f32)

    early = None
    for d in range(ys - 1):
        early = early_project(
            meta, CHIP + d, groups[d], ours(gain, d), ours(gates, d), w_key, w_value, w_query, w_parts, early
        )
        if d == 0:
            sent_w_down, early = early[5], early[:5]
        piece, _ = lax.optimization_barrier((shifted[d + 1], early[4]))
        groups.append(group_of(piece))
    scaled, scale_b, keys, erased, entry, own_maps, sent_maps, totals = block_maps(
        meta, CHIP + ys - 1, groups[-1], ours(gain, -1), rates, ours(gates, -1), w_key, w_value, early
    )

    sent_w_out, sent_w_down, _ = lax.optimization_barrier((w_out_t, sent_w_down, groups[-1][-1]))
    other_w_out, other_w_down = core_swap(sent_w_out, n), core_swap(sent_w_down, n)
    acc_query, other_w_out, other_w_down = lax.optimization_barrier(
        (early[2], other_w_out, other_w_down)
    )

    other_maps = pair_swap(sent_maps, seqs)
    query, tokens_a, tokens_b, query_done = queries(
        meta, ys, scaled, scale_b, w_query, acc_query, sum(groups, [])
    )
    pair, first, done = pair_maps(meta, own_maps, other_maps, query_done)
    pairs = [later(pair, seqs, d) for d in range(seqs // 2 - 1, 0, -1)]
    shard_query, free, out_done = block_outputs(query, keys, erased, entry, totals, done)
    kept_state, given_state = start_states(meta, first, pairs, out_done)
    other_state = pair_swap(given_state, seqs)

    mixed = mixed_heads(meta, kept_state, other_state, shard_query, free, head_gain.reshape(1, DK))
    sums = []
    for own_mixed in mixed:
        summed = attend(meta, own_mixed, core_swap(own_mixed, n), w_out_t, other_w_out)
        sums.append([summed] + [y_shift(summed, n, d) for d in range(1, ys)])
    ups = []
    for own, own_tokens in zip(sums, (tokens_a, tokens_b)):
        ahead = ups[0][2] if ups else sums[1][0]
        own = own[:1] + list(lax.optimization_barrier((tuple(own[1:]), ahead))[0])
        other = [core_swap(value, n) for value in own]
        ups.append(up_project(meta, own_tokens, own, other, ffn_scale, w_up, part))
    (outer, middle_a, first_row, last_row), (inside, middle_b, _, _) = ups
    before = lax.ppermute(last_row, "seq", [(i, i + 1) for i in range(seqs - 1)])
    after = lax.ppermute(first_row, "seq", [(i + 1, i) for i in range(seqs - 1)])

    acts = [activate(meta, outer, inside, before, after, taps, late) for late in (False, True)]
    partner_acts = [core_swap(act, n) for act in acts]
    fars = [
        far_project(meta, ys, act, partner, w_parts, other_w_down)
        for act, partner in zip(acts, partner_acts)
    ]
    total = near_project(
        meta, acts, partner_acts, middle_a, middle_b, w_parts, other_w_down, fars[1][0]
    )
    for d in range(1, ys):
        halves = [y_shift(far[d - 1], n, d) for far in fars]
        total = total + jnp.concatenate(halves, axis=1).astype(f32)
    return total.astype(bf16).T


def solution(mesh):
    placed = (
        P("seq", "head"),
        P(),
        P(None, "head"),
        P(None, "head"),
        P(None, "head"),
        P(None, "head"),
        P(None, "head"),
        P(None, "head"),
        P(),
        P("head", None),
        P(),
        P(None, "head"),
        P(None, "head"),
        P("head", None),
    )
    return jax.shard_map(
        shards, mesh=mesh, in_specs=placed, out_specs=P("seq", "head"), check_vma=False
    )
```

time: 148 us -> 145 us (0.980)
  waiting for transfers between devices: 63.6 us -> 45.5 us
  local copies, waits for them, and re-layouts: 5.42 us -> 22 us
  Pallas kernels: 53.1 us -> 51.5 us
    ppermute x4 -> x5, waiting for transfers between devices: 50.2 us -> 28 us  [y_shift(): lax.ppermute(value, 'head', [(i, (i + 2 * step) % n) for i in range(n)])]
    unnamed x32 -> x60, local copies, waits for them, and re-layouts: 2.78 us -> 20.6 us
    ppermute x11 -> x12, waiting for transfers between devices: 1.05 us -> 4.72 us  [core_swap(): return lax.ppermute(value, 'head', [(i, i ^ 1) for i in range(n)])]
    dynamic_slice x1 -> x0, local copies, waits for them, and re-layouts: 2.38 us -> none  [shards(): lax.dynamic_slice_in_dim(w_out_t, (1 - core) * (features // 2), features...]
    pallas_call x11 -> x15, Pallas kernels: 50.2 us -> 48.6 us  [the longest x1 12.2 us: block_maps(): pl.pallas_call(functools.partial(maps_kernel, n, heads, at), out_shape=(s...]
    ppermute x4 -> x5, starting transfers between devices: 5.25 us -> 4.83 us  [y_shift(): lax.ppermute(value, 'head', [(i, (i + 2 * step) % n) for i in range(n)])]
  transfers between devices with their start and end apart: 22 -> 24, of which waited for: 9 -> 12; matrix products, arithmetic and copies ran while one was open for 2% -> 1% of each run, Pallas kernels for 32% -> 30%
where the time goes in v3:
time: 145 us; the launch traced here: 144 us
  Pallas kernels  51.5 us (36%)
  waiting for transfers between devices  45.5 us (31%)
  starting transfers between devices  22.4 us (15%)
  local copies, waits for them, and re-layouts  22 us (15%)
  other arithmetic  1.78 us (1%)
    ppermute x5, waiting for transfers between devices, y_shift(): lax.ppermute(value, 'head', [(i, (i + 2 * step) % n) for i in range(n)])  28 us
    unnamed x60, local copies, waits for them, and re-layouts  20.6 us
    pallas_call x1, Pallas kernels, block_maps(): pl.pallas_call(functools.partial(maps_kernel, n, heads, at), out_shape=(s...  12.2 us
    pallas_call x2, Pallas kernels, up_project(): pl.pallas_call(functools.partial(up_kernel, len(own)), out_shape=(shape_o...  8.31 us
    ppermute x3, waiting for transfers between devices, later(): lax.ppermute(value, 'seq', [(i, i + 2 * step) for i in range(n - 2 * step)])  7.83 us
    pallas_call x1, Pallas kernels, early_project(): pl.pallas_call(functools.partial(early_kernel, len(pieces), at), out_shap...  6.74 us
    pallas_call x2, Pallas kernels, attend(): pl.pallas_call(attend_kernel, out_shape=shape_of((weights.shape[0] // 2,...  6.27 us
    ppermute x3, starting transfers between devices, later(): lax.ppermute(value, 'seq', [(i, i + 2 * step) for i in range(n - 2 * step)])  6.26 us
  transfers between devices with their start and end apart: 24, of which 12 were waited for; matrix products, arithmetic and copies ran while one was open for 1% of the time, Pallas kernels for 30%

profile of v3, /device:TPU:16, one launch (start us, length us, event | category | flops | bytes accessed | tf_op | source)
XLA Modules:
  0.0 143.6 jit_solution(7152641447616603751)
XLA Ops:
  0.0 1.6 %collective-permute-start = (bf16[560,512]{1,0:T(8,128)(2,1)}, bf16[560,512]{1,0:T(8,128)(2,1)S(1)}, u32[]{:S(2)}, u32[]{:S(2)}) collective-permute-start(bf16[560,512]{1,0:T(8,128)(2,1)} %bitcast.36), channel_id=1, source_target_pairs={{0,2},{1,3},{2,0},{3,1},{4,6},{5,7},{6,4},{7,5},{8,10},{9,11},{10,... | collective-permute-start | bytes 1720328 | tf_op jit(solution)/shard_map/ppermute | solution.py:695
  3.7 3.0 %copy-done = bf16[1400,2240]{0,1:T(8,128)(2,1)S(1)} copy-done((bf16[1400,2240]{0,1:T(8,128)(2,1)S(1)}, bf16[1400,2240]{0,1:T(8,128)(2,1)}, u32[]{:S(2)}) %copy-start) | copy-done | bytes 6272024
  6.6 1.6 %copy-done.1 = bf16[2240,512]{1,0:T(8,128)(2,1)S(1)} copy-done((bf16[2240,512]{1,0:T(8,128)(2,1)S(1)}, bf16[2240,512]{1,0:T(8,128)(2,1)}, u32[]{:S(2)}) %copy-start.1) | copy-done | bytes 2293784
  8.3 1.6 %copy-done.3 = bf16[2240,512]{1,0:T(8,128)(2,1)S(1)} copy-done((bf16[2240,512]{1,0:T(8,128)(2,1)S(1)}, bf16[2240,512]{1,0:T(8,128)(2,1)}, u32[]{:S(2)}) %copy-start.3) | copy-done | bytes 2293784
  9.9 1.6 %copy-done.5 = bf16[2240,512]{1,0:T(8,128)(2,1)S(1)} copy-done((bf16[2240,512]{1,0:T(8,128)(2,1)S(1)}, bf16[2240,512]{1,0:T(8,128)(2,1)}, u32[]{:S(2)}) %copy-start.5) | copy-done | bytes 2293784
  11.6 6.7 %early_project.1 = (f32[512,512]{1,0:T(8,128)S(1)}, f32[512,512]{1,0:T(8,128)S(1)}, f32[512,512]{1,0:T(8,128)S(1)}, f32[16,512]{1,0:T(8,128)S(1)}, f32[8,512]{1,0:T(8,128)S(1)}, /*index=5*/bf16[2,560,1400]{2,1,0:T(8,128)(2,1)}) custom-call(s32[6]{0:T(128)S(1)} %stack.24.meta, bf16[560,512]{1,0:T(8,128)(2,1)S(1)} %bitcast.37, ...), custom_call_target="tpu_custom_call" | custom-call | flops 3000000000 | bytes 8000000 | tf_op jit(solution)/shard_map/early_project/pallas_call | solution.py:149
  19.3 1.0 copy-done.17
  20.4 1.1 copy-done.19
  22.4 1.0 collective-permute-done.2.refs_1_.refs_3_
  25.0 1.6 %copy-done.4 = bf16[2240,512]{1,0:T(8,128)(2,1)S(1)} copy-done((bf16[2240,512]{1,0:T(8,128)(2,1)S(1)}, bf16[2240,512]{1,0:T(8,128)(2,1)}, u32[]{:S(2)}) %copy-start.4) | copy-done | bytes 2293784
  26.6 1.6 %copy-done.6 = bf16[2240,512]{1,0:T(8,128)(2,1)S(1)} copy-done((bf16[2240,512]{1,0:T(8,128)(2,1)S(1)}, bf16[2240,512]{1,0:T(8,128)(2,1)}, u32[]{:S(2)}) %copy-start.6) | copy-done | bytes 2293784
  28.3 1.1 copy-done.14
  29.3 1.1 copy-done.16
  30.4 1.2 copy-done.18
  31.6 1.2 copy-done.20
  32.8 12.2 %block_maps.1 = (bf16[512,1120]{1,0:T(8,128)(2,1)S(1)}, f32[512,128]{1,0:T(8,128)S(1)}, bf16[512,512]{1,0:T(8,128)(2,1)S(1)}, bf16[512,1024]{1,0:T(8,128)(2,1)S(...) custom-call(s32[6]{0:T(128)S(1)} %stack.24.meta, ...), custom_call_target="tpu_custom_call" | custom-call | flops 10000000000 | bytes 14000000 | tf_op jit(solution)/shard_map/block_maps/pallas_call | solution.py:307
  45.0 1.5 %collective-permute-start.5 = (bf16[2,128,256]{2,1,0:T(8,128)(2,1)S(1)}, bf16[2,128,256]{2,1,0:T(8,128)(2,1)S(1)}, u32[]{:S(2)}, u32[]{:S(2)}) collective-permute-start(bf16[2,128,256]{2,1,0:T(8,128)(2,1)S(1)} %get-tuple-element.61), channel_id=1, source_target_pairs={{0,4},{4,0},{8,12},{12,8},{16,20},{20,16},{24,28},{28,24},{1,5},{5... | collective-permute-start | bytes 393224 | tf_op jit(solution)/shard_map/ppermute | solution.py:699
  46.6 1.9 %queries.1 = (bf16[512,512]{1,0:T(8,128)(2,1)S(1)}, bf16[2240,256]{1,0:T(8,128)(2,1)S(1)}, bf16[2240,256]{1,0:T(8,128)(2,1)S(1)}, f32[8,128]{1,0:T(8,128)S(1)}) custom-call(s32[6]{0:T(128)S(1)} %stack.24.meta, bf16[512,1120]{1,0:T(8,128)(2,1)S(1)} %get-tuple-element.52.scaled, f32[512,128]{1,0:T(8,128)S(1)} %get-tuple-element.53.scale_b, ...), custom_call_target="tpu_custom_call" | custom-call | flops 1000000000 | bytes 8000000 | tf_op jit(solution)/shard_map/queries/pallas_call | solution.py:369
  48.5 2.2 %collective-permute-done.5.other = bf16[2,128,256]{2,1,0:T(8,128)(2,1)S(1)} collective-permute-done((bf16[2,128,256]{2,1,0:T(8,128)(2,1)S(1)}, bf16[2,128,256]{2,1,0:T(8,128)(2,1)S(1)}, u32[]{:S(2)}, u32[]{:S(2)}) %collective-permute-start.5) | collective-permute-done | bytes 131104 | tf_op jit(solution)/shard_map/ppermute | solution.py:699
  52.1 1.3 collective-permute-start.7
  53.4 4.3 %collective-permute-start.8 = (bf16[2,128,256]{2,1,0:T(8,128)(2,1)S(1)}, bf16[2,128,256]{2,1,0:T(8,128)(2,1)S(1)}, u32[]{:S(2)}, u32[]{:S(2)}) collective-permute-start(bf16[2,128,256]{2,1,0:T(8,128)(2,1)S(1)} %get-tuple-element.64), channel_id=1, source_target_pairs={{0,8},{4,12},{8,16},{12,20},{16,24},{20,28},{1,9},{5,13},{9,17},{1... | collective-permute-start | bytes 393224 | tf_op jit(solution)/shard_map/ppermute | solution.py:703
  57.7 2.8 %block_outputs.1 = (bf16[512,512]{1,0:T(8,128)(2,1)S(1)}, f32[512,512]{1,0:T(8,128)S(1)}, f32[8,128]{1,0:T(8,128)S(1)}) custom-call(bf16[512,512]{1,0:T(8,128)(2,1)S(1)} %get-tuple-element.65.query, bf16[512,512]{1,0:T(8,128)(2,1)S(1)} %get-tuple-element.66.keys, bf16[512,1024]{1,0:T(8,128)(2,1)S(1)} %get-tuple-element.67.erased, ...), custom_call_target="tpu_custom_call" | custom-call | flops 3000000000 | bytes 4000000 | tf_op jit(solution)/shard_map/block_outputs/pallas_call | solution.py:420
  60.5 3.7 %collective-permute-done.7.refs_1_ = bf16[2,128,256]{2,1,0:T(8,128)(2,1)S(1)} collective-permute-done((bf16[2,128,256]{2,1,0:T(8,128)(2,1)S(1)}, bf16[2,128,256]{2,1,0:T(8,128)(2,1)S(1)}, u32[]{:S(2)}, u32[]{:S(2)}) %collective-permute-start.7) | collective-permute-done | bytes 131104 | tf_op jit(solution)/shard_map/ppermute | solution.py:703
  64.2 4.2 %collective-permute-done.8.refs_2_ = bf16[2,128,256]{2,1,0:T(8,128)(2,1)S(1)} collective-permute-done((bf16[2,128,256]{2,1,0:T(8,128)(2,1)S(1)}, bf16[2,128,256]{2,1,0:T(8,128)(2,1)S(1)}, u32[]{:S(2)}, u32[]{:S(2)}) %collective-permute-start.8) | collective-permute-done | bytes 131104 | tf_op jit(solution)/shard_map/ppermute | solution.py:703
  68.4 1.2 start_states.1
  69.6 1.5 %collective-permute-start.9 = (bf16[2,128,128]{2,1,0:T(8,128)(2,1)S(1)}, bf16[2,128,128]{2,1,0:T(8,128)(2,1)S(1)}, u32[]{:S(2)}, u32[]{:S(2)}) collective-permute-start(bf16[2,128,128]{2,1,0:T(8,128)(2,1)S(1)} %get-tuple-element.73), channel_id=1, source_target_pairs={{0,4},{4,0},{8,12},{12,8},{16,20},{20,16},{24,28},{28,24},{1,5},{5... | collective-permute-start | bytes 196616 | tf_op jit(solution)/shard_map/ppermute | solution.py:699
  71.1 2.8 %collective-permute-done.9.other = bf16[2,128,128]{2,1,0:T(8,128)(2,1)S(1)} collective-permute-done((bf16[2,128,128]{2,1,0:T(8,128)(2,1)S(1)}, bf16[2,128,128]{2,1,0:T(8,128)(2,1)S(1)}, u32[]{:S(2)}, u32[]{:S(2)}) %collective-permute-start.9) | collective-permute-done | bytes 65568 | tf_op jit(solution)/shard_map/ppermute | solution.py:699
  73.9 1.1 mixed_heads.1
  75.1 1.5 %collective-permute-done.10.other = bf16[256,512]{1,0:T(8,128)(2,1)S(1)} collective-permute-done((bf16[256,512]{1,0:T(8,128)(2,1)S(1)}, bf16[256,512]{1,0:T(8,128)(2,1)S(1)}, u32[]{:S(2)}, u32[]{:S(2)}) %collective-permute-start.10) | collective-permute-done | bytes 262176 | tf_op jit(solution)/shard_map/ppermute | solution.py:691
  76.6 3.1 %attend.2.refs_0_ = bf16[1120,256]{1,0:T(8,128)(2,1)S(1)} custom-call(s32[6]{0:T(128)S(1)} %stack.24.meta, bf16[256,512]{1,0:T(8,128)(2,1)S(1)} %get-tuple-element.76.own, bf16[256,512]{1,0:T(8,128)(2,1)S(1)} %collective-permute-done.10.other, bf16[2240,512]{1,0:T(8,128)(2,1)} %bitcast.15.weights, bf16[2240,512]{1,0:T(8,128)(2,1)} %collective-permute-done.3.other_weights), custom_call_target="tpu_custom_call" | custom-call | flops 1000000000 | bytes 5000000 | tf_op jit(solution)/shard_map/attend/pallas_call | solution.py:531
  80.8 1.0 collective-permute-done.12.other
  81.9 3.1 %attend.3.refs_0_ = bf16[1120,256]{1,0:T(8,128)(2,1)S(1)} custom-call(s32[6]{0:T(128)S(1)} %stack.24.meta, bf16[256,512]{1,0:T(8,128)(2,1)S(1)} %get-tuple-element.78.own, bf16[256,512]{1,0:T(8,128)(2,1)S(1)} %collective-permute-done.12.other, bf16[2240,512]{1,0:T(8,128)(2,1)} %bitcast.15.weights, bf16[2240,512]{1,0:T(8,128)(2,1)} %collective-permute-done.3.other_weights), custom_call_target="tpu_custom_call" | custom-call | flops 1000000000 | bytes 5000000 | tf_op jit(solution)/shard_map/attend/pallas_call | solution.py:531
  85.0 9.8 %collective-permute-done.11.refs_1_ = bf16[1120,256]{1,0:T(8,128)(2,1)S(1)} collective-permute-done((bf16[1120,256]{1,0:T(8,128)(2,1)S(1)}, bf16[1120,256]{1,0:T(8,128)(2,1)S(1)}, u32[]{:S(2)}, u32[]{:S(2)}) %collective-permute-start.11) | collective-permute-done | bytes 573472 | tf_op jit(solution)/shard_map/ppermute | solution.py:695
  95.7 1.1 collective-permute-done.14.refs_3_
  96.8 3.9 %up_project.2 = (bf16[256,1400]{1,0:T(8,128)(2,1)S(1)}, f32[560,256]{1,0:T(8,128)S(1)}, bf16[1,1400]{1,0:T(2,128)(2,1)S(1)}, bf16[1,1400]{1,0:T(2,128)(2,1)S(1)}) custom-call(s32[6]{0:T(128)S(1)} %stack.24.meta, bf16[2240,256]{1,0:T(8,128)(2,1)S(1)} %get-tuple-element.59.tokens, bf16[1120,256]{1,0:T(8,128)(2,1)S(1)} %attend.2.refs_0_, ...), custom_call_target="tpu_custom_call" | custom-call | flops 2000000000 | bytes 8000000 | tf_op jit(solution)/shard_map/up_project/pallas_call | solution.py:576
  100.7 9.5 %collective-permute-done.15.refs_1_ = bf16[1120,256]{1,0:T(8,128)(2,1)S(1)} collective-permute-done((bf16[1120,256]{1,0:T(8,128)(2,1)S(1)}, bf16[1120,256]{1,0:T(8,128)(2,1)S(1)}, u32[]{:S(2)}, u32[]{:S(2)}) %collective-permute-start.15) | collective-permute-done | bytes 573472 | tf_op jit(solution)/shard_map/ppermute | solution.py:695
  110.2 2.4 %collective-permute-start.19 = (bf16[1,1400]{1,0:T(2,128)(2,1)S(1)}, bf16[1,1400]{1,0:T(2,128)(2,1)S(1)}, u32[]{:S(2)}, u32[]{:S(2)}) collective-permute-start(bf16[1,1400]{1,0:T(2,128)(2,1)S(1)} %get-tuple-element.82), channel_id=1, source_target_pairs={{4,0},{8,4},{12,8},{16,12},{20,16},{24,20},{28,24},{5,1},{9,5},{13... | collective-permute-start | bytes 8408 | tf_op jit(solution)/shard_map/ppermute | solution.py:810
  112.6 3.7 %collective-permute-start.18 = (bf16[1,1400]{1,0:T(2,128)(2,1)S(1)}, bf16[1,1400]{1,0:T(2,128)(2,1)S(1)}, u32[]{:S(2)}, u32[]{:S(2)}) collective-permute-start(bf16[1,1400]{1,0:T(2,128)(2,1)S(1)} %get-tuple-element.85), channel_id=1, source_target_pairs={{0,4},{4,8},{8,12},{12,16},{16,20},{20,24},{24,28},{1,5},{5,9},{9,... | collective-permute-start | bytes 8408 | tf_op jit(solution)/shard_map/ppermute | solution.py:809
  116.3 4.4 %up_project.3 = (bf16[256,1400]{1,0:T(8,128)(2,1)S(1)}, f32[560,256]{1,0:T(8,128)S(1)}, bf16[1,1400]{1,0:T(2,128)(2,1)}, bf16[1,1400]{1,0:T(2,128)(2,1)}) custom-call(s32[6]{0:T(128)S(1)} %stack.24.meta, bf16[2240,256]{1,0:T(8,128)(2,1)S(1)} %get-tuple-element.81.tokens, bf16[1120,256]{1,0:T(8,128)(2,1)S(1)} %attend.3.refs_0_, ...), custom_call_target="tpu_custom_call" | custom-call | flops 2000000000 | bytes 8000000 | tf_op jit(solution)/shard_map/up_project/pallas_call | solution.py:576
  120.8 2.3 %activate.2.own_a.own = bf16[1400,256]{1,0:T(8,128)(2,1)S(1)} custom-call(s32[6]{0:T(128)S(1)} %stack.24.meta, bf16[256,1400]{1,0:T(8,128)(2,1)S(1)} %get-tuple-element.80.outer, bf16[256,1400]{1,0:T(8,128)(2,1)S(1)} %get-tuple-element.84.inside, bf16[1,1400]{1,0:T(2,128)(2,1)S(1)} %collective-permute-done.18.before, ...), custom_call_target="tpu_custom_call" | custom-call | flops 1000000000 | bytes 2000000 | tf_op jit(solution)/shard_map/activate/pallas_call | solution.py:632
  123.2 2.3 %activate.3.own.own_b = bf16[1400,256]{1,0:T(8,128)(2,1)S(1)} custom-call(s32[6]{0:T(128)S(1)} %stack.24.meta, bf16[256,1400]{1,0:T(8,128)(2,1)S(1)} %get-tuple-element.80.outer, bf16[256,1400]{1,0:T(8,128)(2,1)S(1)} %get-tuple-element.84.inside, bf16[1,1400]{1,0:T(2,128)(2,1)S(1)} %collective-permute-done.18.before, ...), custom_call_target="tpu_custom_call" | custom-call | flops 1000000000 | bytes 2000000 | tf_op jit(solution)/shard_map/activate/pallas_call | solution.py:632
  126.1 1.6 %far_project.3 = bf16[560,256]{1,0:T(8,128)(2,1)S(1)} custom-call(s32[6]{0:T(128)S(1)} %stack.24.meta, bf16[1400,256]{1,0:T(8,128)(2,1)S(1)} %activate.2.own_a.own, bf16[1400,256]{1,0:T(8,128)(2,1)S(1)} %collective-permute-done.20.other_a.other, bf16[4,560,1400]{2,1,0:T(8,128)(2,1)S(1)} %bitcast.30, ...), custom_call_target="tpu_custom_call" | custom-call | flops 1000000000 | bytes 4000000 | tf_op jit(solution)/shard_map/far_project/pallas_call | solution.py:654
  128.3 1.6 %far_project.2.after = bf16[560,256]{1,0:T(8,128)(2,1)S(1)} custom-call(s32[6]{0:T(128)S(1)} %stack.24.meta, bf16[1400,256]{1,0:T(8,128)(2,1)S(1)} %activate.3.own.own_b, bf16[1400,256]{1,0:T(8,128)(2,1)S(1)} %collective-permute-done.21.other.other_b, bf16[4,560,1400]{2,1,0:T(8,128)(2,1)S(1)} %bitcast.31, ...), custom_call_target="tpu_custom_call" | custom-call | flops 1000000000 | bytes 4000000 | tf_op jit(solution)/shard_map/far_project/pallas_call | solution.py:654
  129.9 1.6 %collective-permute-start.23 = (bf16[560,256]{1,0:T(8,128)(2,1)S(1)}, bf16[560,256]{1,0:T(8,128)(2,1)S(1)}, u32[]{:S(2)}, u32[]{:S(2)}) collective-permute-start(bf16[560,256]{1,0:T(8,128)(2,1)S(1)} %far_project.2.after), channel_id=1, source_target_pairs={{0,2},{1,3},{2,0},{3,1},{4,6},{5,7},{6,4},{7,5},{8,10},{9,11},{10,... | collective-permute-start | bytes 860168 | tf_op jit(solution)/shard_map/ppermute | solution.py:695
  131.4 2.5 %near_project.1 = f32[560,512]{1,0:T(8,128)S(1)} custom-call(s32[6]{0:T(128)S(1)} %stack.24.meta, bf16[1400,256]{1,0:T(8,128)(2,1)S(1)} %activate.2.own_a.own, bf16[1400,256]{1,0:T(8,128)(2,1)S(1)} %collective-permute-done.20.other_a.other, bf16[1400,256]{1,0:T(8,128)(2,1)S(1)} %activate.3.own.own_b, ...), custom_call_target="tpu_custom_call" | custom-call | flops 2000000000 | bytes 6000000 | tf_op jit(solution)/shard_map/near_project/pallas_call | solution.py:679
  133.9 3.5 %collective-permute-done.22 = bf16[560,256]{1,0:T(8,128)(2,1)S(1)} collective-permute-done((bf16[560,256]{1,0:T(8,128)(2,1)S(1)}, bf16[560,256]{1,0:T(8,128)(2,1)S(1)}, u32[]{:S(2)}, u32[]{:S(2)}) %collective-permute-start.22) | collective-permute-done | bytes 286752 | tf_op jit(solution)/shard_map/ppermute | solution.py:695
  137.4 5.2 %collective-permute-done.23 = bf16[560,256]{1,0:T(8,128)(2,1)S(1)} collective-permute-done((bf16[560,256]{1,0:T(8,128)(2,1)S(1)}, bf16[560,256]{1,0:T(8,128)(2,1)S(1)}, u32[]{:S(2)}, u32[]{:S(2)}) %collective-permute-start.23) | collective-permute-done | bytes 286752 | tf_op jit(solution)/shard_map/ppermute | solution.py:695
  142.6 1.0 fusion
  (90 shorter events, 10.2 us)
Async XLA Ops:
  0.0 3.6 %copy-start.7 = (bf16[512,560]{0,1:T(8,128)(2,1)S(1)}, bf16[512,560]{0,1:T(8,128)(2,1)}, u32[]{:S(2)}) copy-start(bf16[512,560]{0,1:T(8,128)(2,1)} %param.14) | copy-start | bytes 1720324
  0.0 3.6 %collective-permute-start.1 = (bf16[560,512]{1,0:T(8,128)(2,1)}, bf16[560,512]{1,0:T(8,128)(2,1)S(1)}, u32[]{:S(2)}, u32[]{:S(2)}) collective-permute-start(bf16[560,512]{1,0:T(8,128)(2,1)} %bitcast.35), channel_id=1, source_target_pairs={{0,1},{1,0},{2,3},{3,2},{4,5},{5,4},{6,7},{7,6},{8,9},{9,8},{10,11... | collective-permute-start | bytes 1720328 | tf_op jit(solution)/shard_map/ppermute | solution.py:691
  0.0 21.4 %collective-permute-start = (bf16[560,512]{1,0:T(8,128)(2,1)}, bf16[560,512]{1,0:T(8,128)(2,1)S(1)}, u32[]{:S(2)}, u32[]{:S(2)}) collective-permute-start(bf16[560,512]{1,0:T(8,128)(2,1)} %bitcast.36), channel_id=1, source_target_pairs={{0,2},{1,3},{2,0},{3,1},{4,6},{5,7},{6,4},{7,5},{8,10},{9,11},{10,... | collective-permute-start | bytes 1720328 | tf_op jit(solution)/shard_map/ppermute | solution.py:695
  3.6 14.7 %copy-start.9 = (bf16[560,512]{1,0:T(8,128)(2,1)}, bf16[560,512]{1,0:T(8,128)(2,1)S(1)}, u32[]{:S(2)}) copy-start(bf16[560,512]{1,0:T(8,128)(2,1)S(1)} %collective-permute-done.1.refs_1_) | copy-start | bytes 1720324
  3.6 3.0 %copy-start = (bf16[1400,2240]{0,1:T(8,128)(2,1)S(1)}, bf16[1400,2240]{0,1:T(8,128)(2,1)}, u32[]{:S(2)}) copy-start(bf16[1400,2240]{0,1:T(8,128)(2,1)} %param.27) | copy-start | bytes 18816004
  6.6 1.6 %copy-start.1 = (bf16[2240,512]{1,0:T(8,128)(2,1)S(1)}, bf16[2240,512]{1,0:T(8,128)(2,1)}, u32[]{:S(2)}) copy-start(bf16[2240,512]{1,0:T(8,128)(2,1)} %weights.1) | copy-start | bytes 6881284
  8.3 1.6 %copy-start.3 = (bf16[2240,512]{1,0:T(8,128)(2,1)S(1)}, bf16[2240,512]{1,0:T(8,128)(2,1)}, u32[]{:S(2)}) copy-start(bf16[2240,512]{1,0:T(8,128)(2,1)} %refs_5_.5) | copy-start | bytes 6881284
  9.9 1.6 %copy-start.5 = (bf16[2240,512]{1,0:T(8,128)(2,1)S(1)}, bf16[2240,512]{1,0:T(8,128)(2,1)}, u32[]{:S(2)}) copy-start(bf16[2240,512]{1,0:T(8,128)(2,1)} %refs_6_.3) | copy-start | bytes 6881284
  11.6 13.2 %copy-start.24 = (f32[2,4]{1,0:T(2,128)S(1)}, f32[2,4]{1,0:T(2,128)}, u32[]{:S(2)}) copy-start(f32[2,4]{1,0:T(2,128)} %param.21) | copy-start | bytes 100
  20.4 1.1 copy-start.19
  21.4 2.0 %collective-permute-start.2 = (bf16[560,512]{1,0:T(8,128)(2,1)S(1)}, bf16[560,512]{1,0:T(8,128)(2,1)S(1)}, u32[]{:S(2)}, u32[]{:S(2)}) collective-permute-start(bf16[560,512]{1,0:T(8,128)(2,1)S(1)} %collective-permute-done.refs_0_.refs_2_), channel_id=1, source_target_pairs={{0,1},{1,0},{2,3},{3,2},{4,5},{5,4},{6,7},{7,6},{8,9},{9,8},{10,11... | collective-permute-start | bytes 1720328 | tf_op jit(solution)/shard_map/ppermute | solution.py:691
  24.3 22.3 %collective-permute-start.4 = (bf16[2,560,1400]{2,1,0:T(8,128)(2,1)}, bf16[2,560,1400]{2,1,0:T(8,128)(2,1)S(1)}, u32[]{:S(2)}, u32[]{:S(2)}) collective-permute-start(bf16[2,560,1400]{2,1,0:T(8,128)(2,1)} %get-tuple-element.57), channel_id=1, source_target_pairs={{0,1},{1,0},{2,3},{3,2},{4,5},{5,4},{6,7},{7,6},{8,9},{9,8},{10,11... | collective-permute-start | bytes 9408008 | tf_op jit(solution)/shard_map/ppermute | solution.py:691
  24.4 22.1 %collective-permute-start.3 = (bf16[2240,512]{1,0:T(8,128)(2,1)}, bf16[2240,512]{1,0:T(8,128)(2,1)}, u32[]{:S(2)}, u32[]{:S(2)}) collective-permute-start(bf16[2240,512]{1,0:T(8,128)(2,1)} %bitcast.15.weights), channel_id=1, source_target_pairs={{0,1},{1,0},{2,3},{3,2},{4,5},{5,4},{6,7},{7,6},{8,9},{9,8},{10,11... | collective-permute-start | bytes 6881288 | tf_op jit(solution)/shard_map/ppermute | solution.py:691
  25.0 1.6 %copy-start.4 = (bf16[2240,512]{1,0:T(8,128)(2,1)S(1)}, bf16[2240,512]{1,0:T(8,128)(2,1)}, u32[]{:S(2)}) copy-start(bf16[2240,512]{1,0:T(8,128)(2,1)} %refs_5_.5) | copy-start | bytes 6881284
  26.6 1.6 %copy-start.6 = (bf16[2240,512]{1,0:T(8,128)(2,1)S(1)}, bf16[2240,512]{1,0:T(8,128)(2,1)}, u32[]{:S(2)}) copy-start(bf16[2240,512]{1,0:T(8,128)(2,1)} %refs_6_.3) | copy-start | bytes 6881284
  28.3 1.1 copy-start.14
  30.4 1.2 copy-start.18
  31.6 1.2 copy-start.20
  32.8 13.8 %copy-start.2 = (bf16[2240,512]{1,0:T(8,128)(2,1)S(1)}, bf16[2240,512]{1,0:T(8,128)(2,1)}, u32[]{:S(2)}) copy-start(bf16[2240,512]{1,0:T(8,128)(2,1)} %weights.1) | copy-start | bytes 6881284
  32.8 13.8 %copy-start.8 = (bf16[512,560]{0,1:T(8,128)(2,1)S(1)}, bf16[512,560]{0,1:T(8,128)(2,1)}, u32[]{:S(2)}) copy-start(bf16[512,560]{0,1:T(8,128)(2,1)} %param.14) | copy-start | bytes 1720324
  32.8 13.8 %copy-start.10 = (bf16[560,512]{1,0:T(8,128)(2,1)S(1)}, bf16[560,512]{1,0:T(8,128)(2,1)}, u32[]{:S(2)}) copy-start(bf16[560,512]{1,0:T(8,128)(2,1)} %copy-done.9) | copy-start | bytes 1720324
  32.8 13.8 %copy-start.12 = (f32[512,512]{1,0:T(8,128)S(1)}, f32[512,512]{1,0:T(8,128)}, u32[]{:S(2)}) copy-start(f32[512,512]{1,0:T(8,128)} %copy-done.11) | copy-start | bytes 3145732
  45.0 5.6 %collective-permute-start.5 = (bf16[2,128,256]{2,1,0:T(8,128)(2,1)S(1)}, bf16[2,128,256]{2,1,0:T(8,128)(2,1)S(1)}, u32[]{:S(2)}, u32[]{:S(2)}) collective-permute-start(bf16[2,128,256]{2,1,0:T(8,128)(2,1)S(1)} %get-tuple-element.61), channel_id=1, source_target_pairs={{0,4},{4,0},{8,12},{12,8},{16,20},{20,16},{24,28},{28,24},{1,5},{5... | collective-permute-start | bytes 393224 | tf_op jit(solution)/shard_map/ppermute | solution.py:699
  51.4 9.1 %collective-permute-start.6 = (bf16[2,128,256]{2,1,0:T(8,128)(2,1)S(1)}, bf16[2,128,256]{2,1,0:T(8,128)(2,1)S(1)}, u32[]{:S(2)}, u32[]{:S(2)}) collective-permute-start(bf16[2,128,256]{2,1,0:T(8,128)(2,1)S(1)} %get-tuple-element.64), channel_id=1, source_target_pairs={{0,24},{4,28},{1,25},{5,29},{2,26},{6,30},{3,27},{7,31}} | collective-permute-start | bytes 393224 | tf_op jit(solution)/shard_map/ppermute | solution.py:703
  52.1 12.1 %collective-permute-start.7 = (bf16[2,128,256]{2,1,0:T(8,128)(2,1)S(1)}, bf16[2,128,256]{2,1,0:T(8,128)(2,1)S(1)}, u32[]{:S(2)}, u32[]{:S(2)}) collective-permute-start(bf16[2,128,256]{2,1,0:T(8,128)(2,1)S(1)} %get-tuple-element.64), channel_id=1, source_target_pairs={{0,16},{4,20},{8,24},{12,28},{1,17},{5,21},{9,25},{13,29},{2,18},{... | collective-permute-start | bytes 393224 | tf_op jit(solution)/shard_map/ppermute | solution.py:703
  53.4 15.0 %collective-permute-start.8 = (bf16[2,128,256]{2,1,0:T(8,128)(2,1)S(1)}, bf16[2,128,256]{2,1,0:T(8,128)(2,1)S(1)}, u32[]{:S(2)}, u32[]{:S(2)}) collective-permute-start(bf16[2,128,256]{2,1,0:T(8,128)(2,1)S(1)} %get-tuple-element.64), channel_id=1, source_target_pairs={{0,8},{4,12},{8,16},{12,20},{16,24},{20,28},{1,9},{5,13},{9,17},{1... | collective-permute-start | bytes 393224 | tf_op jit(solution)/shard_map/ppermute | solution.py:703
  57.7 16.2 %copy-start.21 = (bf16[128]{0:T(256)(128)(2,1)S(1)}, bf16[128]{0:T(256)(128)(2,1)}, u32[]{:S(2)}) copy-start(bf16[128]{0:T(256)(128)(2,1)} %param.22) | copy-start | bytes 772
  69.6 4.3 %collective-permute-start.9 = (bf16[2,128,128]{2,1,0:T(8,128)(2,1)S(1)}, bf16[2,128,128]{2,1,0:T(8,128)(2,1)S(1)}, u32[]{:S(2)}, u32[]{:S(2)}) collective-permute-start(bf16[2,128,128]{2,1,0:T(8,128)(2,1)S(1)} %get-tuple-element.73), channel_id=1, source_target_pairs={{0,4},{4,0},{8,12},{12,8},{16,20},{20,16},{24,28},{28,24},{1,5},{5... | collective-permute-start | bytes 196616 | tf_op jit(solution)/shard_map/ppermute | solution.py:699
  73.9 22.9 %slice-start.2 = ((s8[6307840]{0:T(1024)(128)(4,1)}), s8[4194304]{0:T(1024)(128)(4,1)S(1)}, s32[]{:S(2)}) async-start(s8[6307840]{0:T(1024)(128)(4,1)} %bitcast.33), calls=%async_computation.2 | async-start | bytes 8388608
  75.0 21.8 %slice-start.3 = ((s8[6307840]{0:T(1024)(128)(4,1)}), s8[2113536]{0:T(1024)(128)(4,1)S(1)}, s32[]{:S(2)}) async-start(s8[6307840]{0:T(1024)(128)(4,1)} %bitcast.33), calls=%async_computation.3 | async-start | bytes 4227072
  75.0 1.6 %collective-permute-start.10 = (bf16[256,512]{1,0:T(8,128)(2,1)S(1)}, bf16[256,512]{1,0:T(8,128)(2,1)S(1)}, u32[]{:S(2)}, u32[]{:S(2)}) collective-permute-start(bf16[256,512]{1,0:T(8,128)(2,1)S(1)} %get-tuple-element.76.own), channel_id=1, source_target_pairs={{0,1},{1,0},{2,3},{3,2},{4,5},{5,4},{6,7},{7,6},{8,9},{9,8},{10,11... | collective-permute-start | bytes 786440 | tf_op jit(solution)/shard_map/ppermute | solution.py:691
  79.7 15.1 %collective-permute-start.11 = (bf16[1120,256]{1,0:T(8,128)(2,1)S(1)}, bf16[1120,256]{1,0:T(8,128)(2,1)S(1)}, u32[]{:S(2)}, u32[]{:S(2)}) collective-permute-start(bf16[1120,256]{1,0:T(8,128)(2,1)S(1)} %attend.2.refs_0_), channel_id=1, source_target_pairs={{0,2},{1,3},{2,0},{3,1},{4,6},{5,7},{6,4},{7,5},{8,10},{9,11},{10,... | collective-permute-start | bytes 1720328 | tf_op jit(solution)/shard_map/ppermute | solution.py:695
  80.3 15.0 %copy-start.23 = (bf16[2240]{0:T(1024)(128)(2,1)S(1)}, bf16[2240]{0:T(1024)(128)(2,1)}, u32[]{:S(2)}) copy-start(bf16[2240]{0:T(1024)(128)(2,1)} %param.24) | copy-start | bytes 13444
  80.3 1.5 %collective-permute-start.12 = (bf16[256,512]{1,0:T(8,128)(2,1)S(1)}, bf16[256,512]{1,0:T(8,128)(2,1)S(1)}, u32[]{:S(2)}, u32[]{:S(2)}) collective-permute-start(bf16[256,512]{1,0:T(8,128)(2,1)S(1)} %get-tuple-element.78.own), channel_id=1, source_target_pairs={{0,1},{1,0},{2,3},{3,2},{4,5},{5,4},{6,7},{7,6},{8,9},{9,8},{10,11... | collective-permute-start | bytes 786440 | tf_op jit(solution)/shard_map/ppermute | solution.py:691
  80.3 15.3 %collective-permute-start.13 = (bf16[1120,256]{1,0:T(8,128)(2,1)S(1)}, bf16[1120,256]{1,0:T(8,128)(2,1)S(1)}, u32[]{:S(2)}, u32[]{:S(2)}) collective-permute-start(bf16[1120,256]{1,0:T(8,128)(2,1)S(1)} %attend.2.refs_0_), channel_id=1, source_target_pairs={{0,1},{1,0},{2,3},{3,2},{4,5},{5,4},{6,7},{7,6},{8,9},{9,8},{10,11... | collective-permute-start | bytes 1720328 | tf_op jit(solution)/shard_map/ppermute | solution.py:691
  94.8 2.0 %collective-permute-start.14 = (bf16[1120,256]{1,0:T(8,128)(2,1)S(1)}, bf16[1120,256]{1,0:T(8,128)(2,1)S(1)}, u32[]{:S(2)}, u32[]{:S(2)}) collective-permute-start(bf16[1120,256]{1,0:T(8,128)(2,1)S(1)} %collective-permute-done.11.refs_1_), channel_id=1, source_target_pairs={{0,1},{1,0},{2,3},{3,2},{4,5},{5,4},{6,7},{7,6},{8,9},{9,8},{10,11... | collective-permute-start | bytes 1720328 | tf_op jit(solution)/shard_map/ppermute | solution.py:691
  94.8 15.4 %collective-permute-start.15 = (bf16[1120,256]{1,0:T(8,128)(2,1)S(1)}, bf16[1120,256]{1,0:T(8,128)(2,1)S(1)}, u32[]{:S(2)}, u32[]{:S(2)}) collective-permute-start(bf16[1120,256]{1,0:T(8,128)(2,1)S(1)} %attend.3.refs_0_), channel_id=1, source_target_pairs={{0,2},{1,3},{2,0},{3,1},{4,6},{5,7},{6,4},{7,5},{8,10},{9,11},{10,... | collective-permute-start | bytes 1720328 | tf_op jit(solution)/shard_map/ppermute | solution.py:695
  95.4 21.0 %collective-permute-start.16 = (bf16[1120,256]{1,0:T(8,128)(2,1)S(1)}, bf16[1120,256]{1,0:T(8,128)(2,1)S(1)}, u32[]{:S(2)}, u32[]{:S(2)}) collective-permute-start(bf16[1120,256]{1,0:T(8,128)(2,1)S(1)} %attend.3.refs_0_), channel_id=1, source_target_pairs={{0,1},{1,0},{2,3},{3,2},{4,5},{5,4},{6,7},{7,6},{8,9},{9,8},{10,11... | collective-permute-start | bytes 1720328 | tf_op jit(solution)/shard_map/ppermute | solution.py:691
  96.8 13.4 %copy-start.22 = (bf16[3,1400]{1,0:T(4,128)(2,1)S(1)}, bf16[3,1400]{1,0:T(4,128)(2,1)}, u32[]{:S(2)}) copy-start(bf16[3,1400]{1,0:T(4,128)(2,1)} %param.26) | copy-start | bytes 25204
  96.8 29.2 %slice-start = ((s8[6307840]{0:T(1024)(128)(4,1)}), s8[4194304]{0:T(1024)(128)(4,1)S(1)}, s32[]{:S(2)}) async-start(s8[6307840]{0:T(1024)(128)(4,1)} %bitcast.28), calls=%async_computation | async-start | bytes 8388608
  110.2 6.1 %collective-permute-start.17 = (bf16[1120,256]{1,0:T(8,128)(2,1)S(1)}, bf16[1120,256]{1,0:T(8,128)(2,1)S(1)}, u32[]{:S(2)}, u32[]{:S(2)}) collective-permute-start(bf16[1120,256]{1,0:T(8,128)(2,1)S(1)} %collective-permute-done.15.refs_1_), channel_id=1, source_target_pairs={{0,1},{1,0},{2,3},{3,2},{4,5},{5,4},{6,7},{7,6},{8,9},{9,8},{10,11... | collective-permute-start | bytes 1720328 | tf_op jit(solution)/shard_map/ppermute | solution.py:691
  110.2 10.6 %collective-permute-start.19 = (bf16[1,1400]{1,0:T(2,128)(2,1)S(1)}, bf16[1,1400]{1,0:T(2,128)(2,1)S(1)}, u32[]{:S(2)}, u32[]{:S(2)}) collective-permute-start(bf16[1,1400]{1,0:T(2,128)(2,1)S(1)} %get-tuple-element.82), channel_id=1, source_target_pairs={{4,0},{8,4},{12,8},{16,12},{20,16},{24,20},{28,24},{5,1},{9,5},{13... | collective-permute-start | bytes 8408 | tf_op jit(solution)/shard_map/ppermute | solution.py:810
  112.6 8.2 %collective-permute-start.18 = (bf16[1,1400]{1,0:T(2,128)(2,1)S(1)}, bf16[1,1400]{1,0:T(2,128)(2,1)S(1)}, u32[]{:S(2)}, u32[]{:S(2)}) collective-permute-start(bf16[1,1400]{1,0:T(2,128)(2,1)S(1)} %get-tuple-element.85), channel_id=1, source_target_pairs={{0,4},{4,8},{8,12},{12,16},{16,20},{20,24},{24,28},{1,5},{5,9},{9,... | collective-permute-start | bytes 8408 | tf_op jit(solution)/shard_map/ppermute | solution.py:809
  116.3 9.7 %slice-start.1 = ((s8[6307840]{0:T(1024)(128)(4,1)}), s8[2113536]{0:T(1024)(128)(4,1)S(1)}, s32[]{:S(2)}) async-start(s8[6307840]{0:T(1024)(128)(4,1)} %bitcast.28), calls=%async_computation.1 | async-start | bytes 4227072
  123.1 2.9 %collective-permute-start.20 = (bf16[1400,256]{1,0:T(8,128)(2,1)S(1)}, bf16[1400,256]{1,0:T(8,128)(2,1)S(1)}, u32[]{:S(2)}, u32[]{:S(2)}) collective-permute-start(bf16[1400,256]{1,0:T(8,128)(2,1)S(1)} %activate.2.own_a.own), channel_id=1, source_target_pairs={{0,1},{1,0},{2,3},{3,2},{4,5},{5,4},{6,7},{7,6},{8,9},{9,8},{10,11... | collective-permute-start | bytes 2150408 | tf_op jit(solution)/shard_map/ppermute | solution.py:691
  125.5 2.8 %collective-permute-start.21 = (bf16[1400,256]{1,0:T(8,128)(2,1)S(1)}, bf16[1400,256]{1,0:T(8,128)(2,1)S(1)}, u32[]{:S(2)}, u32[]{:S(2)}) collective-permute-start(bf16[1400,256]{1,0:T(8,128)(2,1)S(1)} %activate.3.own.own_b), channel_id=1, source_target_pairs={{0,1},{1,0},{2,3},{3,2},{4,5},{5,4},{6,7},{7,6},{8,9},{9,8},{10,11... | collective-permute-start | bytes 2150408 | tf_op jit(solution)/shard_map/ppermute | solution.py:691
  127.7 9.8 %collective-permute-start.22 = (bf16[560,256]{1,0:T(8,128)(2,1)S(1)}, bf16[560,256]{1,0:T(8,128)(2,1)S(1)}, u32[]{:S(2)}, u32[]{:S(2)}) collective-permute-start(bf16[560,256]{1,0:T(8,128)(2,1)S(1)} %far_project.3), channel_id=1, source_target_pairs={{0,2},{1,3},{2,0},{3,1},{4,6},{5,7},{6,4},{7,5},{8,10},{9,11},{10,... | collective-permute-start | bytes 860168 | tf_op jit(solution)/shard_map/ppermute | solution.py:695
  129.9 12.8 %collective-permute-start.23 = (bf16[560,256]{1,0:T(8,128)(2,1)S(1)}, bf16[560,256]{1,0:T(8,128)(2,1)S(1)}, u32[]{:S(2)}, u32[]{:S(2)}) collective-permute-start(bf16[560,256]{1,0:T(8,128)(2,1)S(1)} %far_project.2.after), channel_id=1, source_target_pairs={{0,2},{1,3},{2,0},{3,1},{4,6},{5,7},{6,4},{7,5},{8,10},{9,11},{10,... | collective-permute-start | bytes 860168 | tf_op jit(solution)/shard_map/ppermute | solution.py:695
  (5 other events, 4.8 us)

commit v4 on v3

--- a/solution.py
+++ b/solution.py
@@ -152,7 +152,7 @@
         + [shape_of((16, count), f32), shape_of((8, count), f32)]
         + [shape_of((ys, part, hidden))] * first,
         in_specs=[SM] + [ANY] * len(pieces) + [VM] * 2 + [ANY] * 4 + [VM] * (0 if first else 5),
-        out_specs=[VM] * (5 + first),
+        out_specs=[VM] * 5 + [ANY] * first,
         scratch_shapes=[
             pltpu.VMEM((span, count), bf16),
             pltpu.VMEM((count, span), bf16),
@@ -160,7 +160,7 @@
             pltpu.SemaphoreType.DMA((3,)),
             pltpu.SemaphoreType.DMA((len(pieces) + ys,)),
         ],
-        compiler_params=params(24),
+        compiler_params=params(54),
         cost_estimate=cost(3 * 10**9, 8 * 10**6),
         name="early_project",
     )(meta, *pieces, gain, gates, w_key, w_value, w_query, w_down, *(before or ()))
@@ -170,13 +170,20 @@
     pieces = refs[:n]
     gain, rates, gates, w_key, w_value, acc_k, acc_v, acc_g, squares = refs[n : n + 9]
     scaled, scale_b, keys, erased, entry, own, sent, totals = refs[n + 9 : n + 17]
-    whole, raw_k, raw_v, rows_at_head, total_b, beta_b, held, held_sem, sem = refs[n + 17 :]
+    whole, raw_k, raw_v, rows_at_head, total_b, beta_b, held, held_sem, acc, acc_sem, sem = refs[
+        n + 17 :
+    ]
     span, count = whole.shape
     blocks = count // BLOCK
     inner = heads * DK
     features = w_key.shape[0]
     parity = meta[PARITY]
     rows_copies = held_rows(meta, at, (w_key, w_value), held, held_sem)
+    rows_copies += [
+        pltpu.make_async_copy(ref, acc.at[i], acc_sem.at[i]) for i, ref in enumerate((acc_k, acc_v))
+    ]
+    for copy in rows_copies[2:]:
+        copy.start()
     load_pair(meta, pieces, whole, sem)
     sums = scale_pass(whole, lambda at, size: gain[:, at : at + size], scaled)
     inverse = inverse_of(sums + squares[...], features)
@@ -209,8 +216,8 @@
     for start in range(0, inner, 256):
         cols = slice(start, start + 256)
         scale = doubled(scale_b[...])
-        raw_k[:, cols] = ((acc_k[:, cols] + dot(scaled[...], held[0, :, cols])) * scale).astype(bf16)
-        raw_v[:, cols] = ((acc_v[:, cols] + dot(scaled[...], held[1, :, cols])) * scale).astype(bf16)
+        raw_k[:, cols] = ((acc[0, :, cols] + dot(scaled[...], held[0, :, cols])) * scale).astype(bf16)
+        raw_v[:, cols] = ((acc[1, :, cols] + dot(scaled[...], held[1, :, cols])) * scale).astype(bf16)
 
     xor = jnp.where(row_at > col_at, row_at ^ col_at, 0)
     eye = jnp.where(row_at == col_at, 1.0, 0.0)
@@ -316,7 +323,7 @@
             shape_of((heads // 2, DK, 2 * DK)),
             shape_of((blocks, 16, 128), f32),
         ),
-        in_specs=[SM] + [ANY] * n + [VM] * 3 + [ANY] * 2 + [VM] * 4,
+        in_specs=[SM] + [ANY] * n + [VM] * 3 + [ANY] * 4 + [VM] * 2,
         out_specs=[VM] * 8,
         scratch_shapes=[
             pltpu.VMEM((span, count), bf16),
@@ -327,9 +334,11 @@
             pltpu.VMEM((heads, count, DK), f32),
             pltpu.VMEM((2, span, inner), bf16),
             pltpu.SemaphoreType.DMA((2,)),
+            pltpu.VMEM((2, count, inner), f32),
+            pltpu.SemaphoreType.DMA((2,)),
             pltpu.SemaphoreType.DMA((n,)),
         ],
-        compiler_params=params(24),
+        compiler_params=params(54),
         cost_estimate=cost(10 * 10**9, 14 * 10**6),
         name="block_maps",
     )(meta, *pieces, gain, rates, gates, w_key, w_value, acc_k, acc_v, acc_g, squares)
@@ -380,7 +389,7 @@
             pltpu.VMEM((1, scaled.shape[1], acc.shape[1]), bf16),
             pltpu.SemaphoreType.DMA((1,)),
         ],
-        compiler_params=params(16),
+        compiler_params=params(12),
         cost_estimate=cost(10**9, 8 * 10**6),
         name="queries",
     )(meta, scaled, scale_b, weights, acc, *pieces)
@@ -423,7 +432,7 @@
         in_specs=[VM] * 5 + [ANY],
         out_specs=[VM] * 3,
         scratch_shapes=[pltpu.VMEM((128, BLOCK), f32)],
-        compiler_params=params(16),
+        compiler_params=params(8),
         cost_estimate=cost(3 * 10**9, 4 * 10**6),
         name="block_outputs",
     )(query, keys, erased, entry, totals, after)
@@ -448,7 +457,7 @@
         out_shape=(shape_of(own.shape), shape_of(own.shape), shape_of((8, 128), f32)),
         in_specs=[SM, VM, VM, ANY],
         out_specs=[VM] * 3,
-        compiler_params=params(8),
+        compiler_params=params(4),
         name="pair_maps",
     )(meta, own, other, after)
 
@@ -480,7 +489,7 @@
         out_shape=(shape, shape),
         in_specs=[SM] + [VM] * (1 + len(pairs)) + [ANY],
         out_specs=[VM] * 2,
-        compiler_params=params(8),
+        compiler_params=params(4),
         name="start_states",
     )(meta, first, *pairs, after)
 
@@ -515,7 +524,7 @@
         out_shape=(shape_of((2 * BLOCK, inner)), shape_of((count - 2 * BLOCK, inner))),
         in_specs=[SM] + [VM] * 5,
         out_specs=[VM] * 2,
-        compiler_params=params(12),
+        compiler_params=params(6),
         cost_estimate=cost(10**9, 3 * 10**6),
         name="mixed_heads",
     )(meta, own, other, shard_query, free, gain)
@@ -533,7 +542,7 @@
         out_shape=shape_of((weights.shape[0] // 2, own.shape[0])),
         in_specs=[SM] + [VM] * 4,
         out_specs=VM,
-        compiler_params=params(16),
+        compiler_params=params(10),
         cost_estimate=cost(10**9, 5 * 10**6),
         name="attend",
     )(meta, own, other, weights, other_weights)
@@ -588,7 +597,7 @@
             pltpu.VMEM((count, features), bf16),
             pltpu.VMEM((count, DK), f32),
         ],
-        compiler_params=params(20),
+        compiler_params=params(16),
         cost_estimate=cost(2 * 10**9, 8 * 10**6),
         name="up_project",
     )(meta, tokens, *own, *other, gain, weights)
@@ -635,7 +644,7 @@
         in_specs=[SM] + [VM] * 5,
         out_specs=VM,
         scratch_shapes=[pltpu.VMEM((count + 16, hidden), f32), pltpu.VMEM((count, hidden), bf16)],
-        compiler_params=params(12),
+        compiler_params=params(8),
         cost_estimate=cost(10**9, 2 * 10**6),
         name="activate",
     )(meta, outer, inside, before, after, taps)
@@ -656,7 +665,7 @@
         out_shape=[shape_of((part, own.shape[1]))] * (ys - 1),
         in_specs=[SM] + [VM] * 4,
         out_specs=[VM] * (ys - 1),
-        compiler_params=params(16),
+        compiler_params=params(8),
         cost_estimate=cost(10**9, 4 * 10**6),
         name="far_project",
     )(meta, own, other, weights, other_weights)
@@ -681,7 +690,7 @@
         out_shape=shape_of((part, 2 * own[0].shape[1]), f32),
         in_specs=[SM] + [VM] * 8 + [ANY],
         out_specs=VM,
-        compiler_params=params(20),
+        compiler_params=params(10),
         cost_estimate=cost(2 * 10**9, 6 * 10**6),
         name="near_project",
     )(meta, own[0], other[0], own[1], other[1], middle_a, middle_b, weights, other_weights, after)

time: 145 us -> 228 us (1.57)
  Pallas kernels: 51.5 us -> 149 us
  local copies, waits for them, and re-layouts: 22 us -> 8.36 us
    pallas_call x1, Pallas kernels: 6.74 us -> 99.2 us  [early_project(): pl.pallas_call(functools.partial(early_kernel, len(pieces), at), out_shap...]
    unnamed x60 -> x52, local copies, waits for them, and re-layouts: 20.6 us -> 5.24 us
    pallas_call x1, Pallas kernels: 12.2 us -> 17 us  [block_maps(): pl.pallas_call(functools.partial(maps_kernel, n, heads, at), out_shape=(s...]
  transfers between devices with their start and end apart: 24 -> 24, of which waited for: 12 -> 12; matrix products, arithmetic and copies ran while one was open for 1% -> 2% of each run, Pallas kernels for 30% -> 62%
where the time goes in v4:
time: 228 us; the launch traced here: 227 us
  Pallas kernels  149 us (65%)
  waiting for transfers between devices  45.2 us (20%)
  starting transfers between devices  22.1 us (10%)
  local copies, waits for them, and re-layouts  8.36 us (4%)
    pallas_call x1, Pallas kernels, early_project(): pl.pallas_call(functools.partial(early_kernel, len(pieces), at), out_shap...  99.2 us
    ppermute x5, waiting for transfers between devices, y_shift(): lax.ppermute(value, 'head', [(i, (i + 2 * step) % n) for i in range(n)])  28.1 us
    pallas_call x1, Pallas kernels, block_maps(): pl.pallas_call(functools.partial(maps_kernel, n, heads, at), out_shape=(s...  17 us
    ppermute x3, waiting for transfers between devices, later(): lax.ppermute(value, 'seq', [(i, i + 2 * step) for i in range(n - 2 * step)])  8.25 us
    pallas_call x2, Pallas kernels, up_project(): pl.pallas_call(functools.partial(up_kernel, len(own)), out_shape=(shape_o...  8.17 us
    pallas_call x2, Pallas kernels, attend(): pl.pallas_call(attend_kernel, out_shape=shape_of((weights.shape[0] // 2,...  6.28 us
    ppermute x3, starting transfers between devices, later(): lax.ppermute(value, 'seq', [(i, i + 2 * step) for i in range(n - 2 * step)])  6.25 us
    ppermute x12, waiting for transfers between devices, core_swap(): return lax.ppermute(value, 'head', [(i, i ^ 1) for i in range(n)])  5.48 us
  transfers between devices with their start and end apart: 24, of which 12 were waited for; matrix products, arithmetic and copies ran while one was open for 2% of the time, Pallas kernels for 62%

profile of v4, /device:TPU:16, one launch (start us, length us, event | category | flops | bytes accessed | tf_op | source)
XLA Modules:
  0.0 226.6 jit_solution(8863518834200544237)
XLA Ops:
  0.0 1.5 collective-permute-start
  1.5 0.8 fusion.3
  2.7 0.6 copy.22
  3.3 0.8 reshape.36
  4.1 0.7 stack.24.meta
  4.8 0.6 dynamic-slice_bitcast_fusion
  5.4 0.8 copy-done.2
  6.2 99.2 %early_project.1 = (f32[512,512]{1,0:T(8,128)}, f32[512,512]{1,0:T(8,128)}, f32[512,512]{1,0:T(8,128)}, f32[16,512]{1,0:T(8,128)}, f32[8,512]{1,0:T(8,128)}, /*index=5*/bf16[2,560,1400]{2,1,0:T(8,128)(2,1)}) custom-call(s32[6]{0:T(128)} %stack.24.meta, bf16[560,512]{1,0:T(8,128)(2,1)} %bitcast.37, bf16[560,512]{1,0:T(8,128)(2,1)} %copy-done.2, ...), custom_call_target="tpu_custom_call" | custom-call | flops 3000000000 | bytes 8000000 | tf_op jit(solution)/shard_map/early_project/pallas_call | solution.py:149
  105.8 1.8 collective-permute-done.2.refs_1_.refs_3_
  107.5 0.8 copy-done.8
  108.9 0.6 copy.21
  109.6 0.7 broadcast_in_dim.8.refs_3_
  110.3 17.0 %block_maps.1 = (bf16[512,1120]{1,0:T(8,128)(2,1)}, f32[512,128]{1,0:T(8,128)}, bf16[512,512]{1,0:T(8,128)(2,1)}, bf16[512,1024]{1,0:T(8,128)(2,1)}, bf16[3,128,...) custom-call(s32[6]{0:T(128)} %stack.24.meta, ...), custom_call_target="tpu_custom_call" | custom-call | flops 10000000000 | bytes 14000000 | tf_op jit(solution)/shard_map/block_maps/pallas_call | solution.py:314
  127.3 1.6 collective-permute-start.5
  128.9 1.3 copy-done.4
  130.2 0.9 copy-done.10
  131.2 1.9 queries.1
  133.2 0.7 pair_maps.1
  133.9 0.7 collective-permute-start.6
  134.6 1.3 collective-permute-start.7
  135.9 4.3 %collective-permute-start.8 = (bf16[2,128,256]{2,1,0:T(8,128)(2,1)S(1)}, bf16[2,128,256]{2,1,0:T(8,128)(2,1)S(1)}, u32[]{:S(2)}, u32[]{:S(2)}) collective-permute-start(bf16[2,128,256]{2,1,0:T(8,128)(2,1)S(1)} %get-tuple-element.64), channel_id=1, source_target_pairs={{0,8},{4,12},{8,16},{12,20},{16,24},{20,28},{1,9},{5,13},{9,17},{1... | collective-permute-start | bytes 393224 | tf_op jit(solution)/shard_map/ppermute | solution.py:712
  140.3 2.8 %block_outputs.1 = (bf16[512,512]{1,0:T(8,128)(2,1)S(1)}, f32[512,512]{1,0:T(8,128)S(1)}, f32[8,128]{1,0:T(8,128)S(1)}) custom-call(bf16[512,512]{1,0:T(8,128)(2,1)S(1)} %get-tuple-element.65.query, bf16[512,512]{1,0:T(8,128)(2,1)S(1)} %copy-done.16, bf16[512,1024]{1,0:T(8,128)(2,1)S(1)} %copy-done.14, bf16[3,128,1024]{2,1,0:T(8,128)(2,1)S(1)} %copy-done.15, ...), custom_call_target="tpu_custom_call" | custom-call | flops 3000000000 | bytes 4000000 | tf_op jit(solution)/shard_map/block_outputs/pallas_call | solution.py:429
  143.1 3.9 %collective-permute-done.7.refs_1_ = bf16[2,128,256]{2,1,0:T(8,128)(2,1)S(1)} collective-permute-done((bf16[2,128,256]{2,1,0:T(8,128)(2,1)S(1)}, bf16[2,128,256]{2,1,0:T(8,128)(2,1)S(1)}, u32[]{:S(2)}, u32[]{:S(2)}) %collective-permute-start.7) | collective-permute-done | bytes 131104 | tf_op jit(solution)/shard_map/ppermute | solution.py:712
  147.0 4.4 %collective-permute-done.8.refs_2_ = bf16[2,128,256]{2,1,0:T(8,128)(2,1)S(1)} collective-permute-done((bf16[2,128,256]{2,1,0:T(8,128)(2,1)S(1)}, bf16[2,128,256]{2,1,0:T(8,128)(2,1)S(1)}, u32[]{:S(2)}, u32[]{:S(2)}) %collective-permute-start.8) | collective-permute-done | bytes 131104 | tf_op jit(solution)/shard_map/ppermute | solution.py:712
  151.4 1.2 start_states.1
  152.6 1.2 collective-permute-start.9
  153.7 3.2 %collective-permute-done.9.other = bf16[2,128,128]{2,1,0:T(8,128)(2,1)S(1)} collective-permute-done((bf16[2,128,128]{2,1,0:T(8,128)(2,1)S(1)}, bf16[2,128,128]{2,1,0:T(8,128)(2,1)S(1)}, u32[]{:S(2)}, u32[]{:S(2)}) %collective-permute-start.9) | collective-permute-done | bytes 65568 | tf_op jit(solution)/shard_map/ppermute | solution.py:708
  156.9 1.1 mixed_heads.1
  158.1 1.5 collective-permute-done.10.other
  159.6 3.1 %attend.2.refs_0_ = bf16[1120,256]{1,0:T(8,128)(2,1)S(1)} custom-call(s32[6]{0:T(128)S(1)} %copy-done.12, bf16[256,512]{1,0:T(8,128)(2,1)S(1)} %get-tuple-element.76.own, bf16[256,512]{1,0:T(8,128)(2,1)S(1)} %collective-permute-done.10.other, bf16[2240,512]{1,0:T(8,128)(2,1)} %bitcast.15.weights, bf16[2240,512]{1,0:T(8,128)(2,1)} %collective-permute-done.3.other_weights), custom_call_target="tpu_custom_call" | custom-call | flops 1000000000 | bytes 5000000 | tf_op jit(solution)/shard_map/attend/pallas_call | solution.py:540
  163.8 1.0 collective-permute-done.12.other
  164.9 3.1 %attend.3.refs_0_ = bf16[1120,256]{1,0:T(8,128)(2,1)S(1)} custom-call(s32[6]{0:T(128)S(1)} %copy-done.12, bf16[256,512]{1,0:T(8,128)(2,1)S(1)} %get-tuple-element.78.own, bf16[256,512]{1,0:T(8,128)(2,1)S(1)} %collective-permute-done.12.other, bf16[2240,512]{1,0:T(8,128)(2,1)} %bitcast.15.weights, bf16[2240,512]{1,0:T(8,128)(2,1)} %collective-permute-done.3.other_weights), custom_call_target="tpu_custom_call" | custom-call | flops 1000000000 | bytes 5000000 | tf_op jit(solution)/shard_map/attend/pallas_call | solution.py:540
  168.0 9.8 %collective-permute-done.11.refs_1_ = bf16[1120,256]{1,0:T(8,128)(2,1)S(1)} collective-permute-done((bf16[1120,256]{1,0:T(8,128)(2,1)S(1)}, bf16[1120,256]{1,0:T(8,128)(2,1)S(1)}, u32[]{:S(2)}, u32[]{:S(2)}) %collective-permute-start.11) | collective-permute-done | bytes 573472 | tf_op jit(solution)/shard_map/ppermute | solution.py:704
  178.7 1.2 collective-permute-done.14.refs_3_
  179.9 3.8 %up_project.2 = (bf16[256,1400]{1,0:T(8,128)(2,1)S(1)}, f32[560,256]{1,0:T(8,128)S(1)}, bf16[1,1400]{1,0:T(2,128)(2,1)S(1)}, bf16[1,1400]{1,0:T(2,128)(2,1)S(1)}) custom-call(s32[6]{0:T(128)S(1)} %copy-done.12, bf16[2240,256]{1,0:T(8,128)(2,1)S(1)} %get-tuple-element.59.tokens, bf16[1120,256]{1,0:T(8,128)(2,1)S(1)} %attend.2.refs_0_, ...), custom_call_target="tpu_custom_call" | custom-call | flops 2000000000 | bytes 8000000 | tf_op jit(solution)/shard_map/up_project/pallas_call | solution.py:585
  183.7 9.6 %collective-permute-done.15.refs_1_ = bf16[1120,256]{1,0:T(8,128)(2,1)S(1)} collective-permute-done((bf16[1120,256]{1,0:T(8,128)(2,1)S(1)}, bf16[1120,256]{1,0:T(8,128)(2,1)S(1)}, u32[]{:S(2)}, u32[]{:S(2)}) %collective-permute-start.15) | collective-permute-done | bytes 573472 | tf_op jit(solution)/shard_map/ppermute | solution.py:704
  193.3 2.0 collective-permute-start.19
  195.2 4.1 %collective-permute-start.18 = (bf16[1,1400]{1,0:T(2,128)(2,1)S(1)}, bf16[1,1400]{1,0:T(2,128)(2,1)S(1)}, u32[]{:S(2)}, u32[]{:S(2)}) collective-permute-start(bf16[1,1400]{1,0:T(2,128)(2,1)S(1)} %get-tuple-element.85), channel_id=1, source_target_pairs={{0,4},{4,8},{8,12},{12,16},{16,20},{20,24},{24,28},{1,5},{5,9},{9,... | collective-permute-start | bytes 8408 | tf_op jit(solution)/shard_map/ppermute | solution.py:818
  199.4 4.4 %up_project.3 = (bf16[256,1400]{1,0:T(8,128)(2,1)S(1)}, f32[560,256]{1,0:T(8,128)S(1)}, bf16[1,1400]{1,0:T(2,128)(2,1)}, bf16[1,1400]{1,0:T(2,128)(2,1)}) custom-call(s32[6]{0:T(128)S(1)} %copy-done.12, bf16[2240,256]{1,0:T(8,128)(2,1)S(1)} %get-tuple-element.81.tokens, bf16[1120,256]{1,0:T(8,128)(2,1)S(1)} %attend.3.refs_0_, ...), custom_call_target="tpu_custom_call" | custom-call | flops 2000000000 | bytes 8000000 | tf_op jit(solution)/shard_map/up_project/pallas_call | solution.py:585
  203.7 2.3 %activate.2.own_a.own = bf16[1400,256]{1,0:T(8,128)(2,1)S(1)} custom-call(s32[6]{0:T(128)S(1)} %copy-done.12, bf16[256,1400]{1,0:T(8,128)(2,1)S(1)} %get-tuple-element.80.outer, bf16[256,1400]{1,0:T(8,128)(2,1)S(1)} %get-tuple-element.84.inside, bf16[1,1400]{1,0:T(2,128)(2,1)S(1)} %collective-permute-done.18.before, ...), custom_call_target="tpu_custom_call" | custom-call | flops 1000000000 | bytes 2000000 | tf_op jit(solution)/shard_map/activate/pallas_call | solution.py:641
  206.1 2.3 %activate.3.own.own_b = bf16[1400,256]{1,0:T(8,128)(2,1)S(1)} custom-call(s32[6]{0:T(128)S(1)} %copy-done.12, bf16[256,1400]{1,0:T(8,128)(2,1)S(1)} %get-tuple-element.80.outer, bf16[256,1400]{1,0:T(8,128)(2,1)S(1)} %get-tuple-element.84.inside, bf16[1,1400]{1,0:T(2,128)(2,1)S(1)} %collective-permute-done.18.before, ...), custom_call_target="tpu_custom_call" | custom-call | flops 1000000000 | bytes 2000000 | tf_op jit(solution)/shard_map/activate/pallas_call | solution.py:641
  209.0 1.6 far_project.3
  211.2 1.6 far_project.2.after
  212.8 1.6 collective-permute-start.23
  214.4 2.5 %near_project.1 = f32[560,512]{1,0:T(8,128)S(1)} custom-call(s32[6]{0:T(128)S(1)} %copy-done.12, bf16[1400,256]{1,0:T(8,128)(2,1)S(1)} %activate.2.own_a.own, bf16[1400,256]{1,0:T(8,128)(2,1)S(1)} %collective-permute-done.20.other_a.other, bf16[1400,256]{1,0:T(8,128)(2,1)S(1)} %activate.3.own.own_b, ...), custom_call_target="tpu_custom_call" | custom-call | flops 2000000000 | bytes 6000000 | tf_op jit(solution)/shard_map/near_project/pallas_call | solution.py:688
  216.9 3.5 %collective-permute-done.22 = bf16[560,256]{1,0:T(8,128)(2,1)S(1)} collective-permute-done((bf16[560,256]{1,0:T(8,128)(2,1)S(1)}, bf16[560,256]{1,0:T(8,128)(2,1)S(1)}, u32[]{:S(2)}, u32[]{:S(2)}) %collective-permute-start.22) | collective-permute-done | bytes 286752 | tf_op jit(solution)/shard_map/ppermute | solution.py:704
  220.4 5.2 %collective-permute-done.23 = bf16[560,256]{1,0:T(8,128)(2,1)S(1)} collective-permute-done((bf16[560,256]{1,0:T(8,128)(2,1)S(1)}, bf16[560,256]{1,0:T(8,128)(2,1)S(1)}, u32[]{:S(2)}, u32[]{:S(2)}) %collective-permute-start.23) | collective-permute-done | bytes 286752 | tf_op jit(solution)/shard_map/ppermute | solution.py:704
  225.6 1.0 fusion
  (82 shorter events, 4.7 us)
Async XLA Ops:
  0.0 5.4 %collective-permute-start.1 = (bf16[560,512]{1,0:T(8,128)(2,1)}, bf16[560,512]{1,0:T(8,128)(2,1)S(1)}, u32[]{:S(2)}, u32[]{:S(2)}) collective-permute-start(bf16[560,512]{1,0:T(8,128)(2,1)} %bitcast.35), channel_id=1, source_target_pairs={{0,1},{1,0},{2,3},{3,2},{4,5},{5,4},{6,7},{7,6},{8,9},{9,8},{10,11... | collective-permute-start | bytes 1720328 | tf_op jit(solution)/shard_map/ppermute | solution.py:700
  0.0 105.4 %collective-permute-start = (bf16[560,512]{1,0:T(8,128)(2,1)}, bf16[560,512]{1,0:T(8,128)(2,1)S(1)}, u32[]{:S(2)}, u32[]{:S(2)}) collective-permute-start(bf16[560,512]{1,0:T(8,128)(2,1)} %bitcast.36), channel_id=1, source_target_pairs={{0,2},{1,3},{2,0},{3,1},{4,6},{5,7},{6,4},{7,5},{8,10},{9,11},{10,... | collective-permute-start | bytes 1720328 | tf_op jit(solution)/shard_map/ppermute | solution.py:704
  6.2 103.3 %copy-start.20 = (f32[2,4]{1,0:T(2,128)S(1)}, f32[2,4]{1,0:T(2,128)}, u32[]{:S(2)}) copy-start(f32[2,4]{1,0:T(2,128)} %param.21) | copy-start | bytes 100
  105.4 2.1 copy-start.6
  105.5 2.0 collective-permute-start.2
  107.5 0.9 copy-start.8
  108.4 20.5 %collective-permute-start.4 = (bf16[2,560,1400]{2,1,0:T(8,128)(2,1)}, bf16[2,560,1400]{2,1,0:T(8,128)(2,1)S(1)}, u32[]{:S(2)}, u32[]{:S(2)}) collective-permute-start(bf16[2,560,1400]{2,1,0:T(8,128)(2,1)} %get-tuple-element.57), channel_id=1, source_target_pairs={{0,1},{1,0},{2,3},{3,2},{4,5},{5,4},{6,7},{7,6},{8,9},{9,8},{10,11... | collective-permute-start | bytes 9408008 | tf_op jit(solution)/shard_map/ppermute | solution.py:700
  108.6 20.3 %collective-permute-start.3 = (bf16[2240,512]{1,0:T(8,128)(2,1)}, bf16[2240,512]{1,0:T(8,128)(2,1)}, u32[]{:S(2)}, u32[]{:S(2)}) collective-permute-start(bf16[2240,512]{1,0:T(8,128)(2,1)} %bitcast.15.weights), channel_id=1, source_target_pairs={{0,1},{1,0},{2,3},{3,2},{4,5},{5,4},{6,7},{7,6},{8,9},{9,8},{10,11... | collective-permute-start | bytes 6881288 | tf_op jit(solution)/shard_map/ppermute | solution.py:700
  110.2 18.6 %copy-start = (bf16[2240,512]{1,0:T(8,128)(2,1)S(1)}, bf16[2240,512]{1,0:T(8,128)(2,1)}, u32[]{:S(2)}) copy-start(bf16[2240,512]{1,0:T(8,128)(2,1)} %weights.1) | copy-start | bytes 6881284
  110.2 18.6 %copy-start.1 = (bf16[512,560]{0,1:T(8,128)(2,1)S(1)}, bf16[512,560]{0,1:T(8,128)(2,1)}, u32[]{:S(2)}) copy-start(bf16[512,560]{0,1:T(8,128)(2,1)} %param.14) | copy-start | bytes 1720324
  110.2 18.6 %copy-start.3 = (bf16[560,512]{1,0:T(8,128)(2,1)S(1)}, bf16[560,512]{1,0:T(8,128)(2,1)}, u32[]{:S(2)}) copy-start(bf16[560,512]{1,0:T(8,128)(2,1)} %copy-done.2) | copy-start | bytes 1720324
  110.2 18.6 %copy-start.5 = (f32[512,512]{1,0:T(8,128)S(1)}, f32[512,512]{1,0:T(8,128)}, u32[]{:S(2)}) copy-start(f32[512,512]{1,0:T(8,128)} %get-tuple-element.58.acc) | copy-start | bytes 3145732
  110.2 18.6 %copy-start.7 = (bf16[560,512]{1,0:T(8,128)(2,1)S(1)}, bf16[560,512]{1,0:T(8,128)(2,1)}, u32[]{:S(2)}) copy-start(bf16[560,512]{1,0:T(8,128)(2,1)} %copy-done.6) | copy-start | bytes 1720324
  110.3 18.6 %copy-start.9 = (bf16[560,512]{1,0:T(8,128)(2,1)S(1)}, bf16[560,512]{1,0:T(8,128)(2,1)}, u32[]{:S(2)}) copy-start(bf16[560,512]{1,0:T(8,128)(2,1)} %copy-done.8) | copy-start | bytes 1720324
  110.3 18.6 %copy-start.12 = (s32[6]{0:T(128)S(1)}, s32[6]{0:T(128)}, u32[]{:S(2)}) copy-start(s32[6]{0:T(128)} %stack.24.meta) | copy-start | bytes 76
  127.3 5.9 %collective-permute-start.5 = (bf16[2,128,256]{2,1,0:T(8,128)(2,1)}, bf16[2,128,256]{2,1,0:T(8,128)(2,1)S(1)}, u32[]{:S(2)}, u32[]{:S(2)}) collective-permute-start(bf16[2,128,256]{2,1,0:T(8,128)(2,1)} %get-tuple-element.61), channel_id=1, source_target_pairs={{0,4},{4,0},{8,12},{12,8},{16,20},{20,16},{24,28},{28,24},{1,5},{5... | collective-permute-start | bytes 393224 | tf_op jit(solution)/shard_map/ppermute | solution.py:708
  128.9 1.3 copy-start.4
  130.2 0.9 copy-start.10
  131.1 2.1 copy-start.11
  131.1 9.1 %copy-start.14 = (bf16[512,1024]{1,0:T(8,128)(2,1)S(1)}, bf16[512,1024]{1,0:T(8,128)(2,1)}, u32[]{:S(2)}) copy-start(bf16[512,1024]{1,0:T(8,128)(2,1)} %get-tuple-element.67.erased) | copy-start | bytes 3145732
  131.2 9.1 %copy-start.15 = (bf16[3,128,1024]{2,1,0:T(8,128)(2,1)S(1)}, bf16[3,128,1024]{2,1,0:T(8,128)(2,1)}, u32[]{:S(2)}) copy-start(bf16[3,128,1024]{2,1,0:T(8,128)(2,1)} %get-tuple-element.68.entry) | copy-start | bytes 2359300
  131.2 9.1 %copy-start.16 = (bf16[512,512]{1,0:T(8,128)(2,1)S(1)}, bf16[512,512]{1,0:T(8,128)(2,1)}, u32[]{:S(2)}) copy-start(bf16[512,512]{1,0:T(8,128)(2,1)} %get-tuple-element.66.keys) | copy-start | bytes 1572868
  131.2 9.1 %copy-start.17 = (f32[4,16,128]{2,1,0:T(8,128)S(1)}, f32[4,16,128]{2,1,0:T(8,128)}, u32[]{:S(2)}) copy-start(f32[4,16,128]{2,1,0:T(8,128)} %get-tuple-element.69.totals) | copy-start | bytes 98308
  133.9 9.2 %collective-permute-start.6 = (bf16[2,128,256]{2,1,0:T(8,128)(2,1)S(1)}, bf16[2,128,256]{2,1,0:T(8,128)(2,1)S(1)}, u32[]{:S(2)}, u32[]{:S(2)}) collective-permute-start(bf16[2,128,256]{2,1,0:T(8,128)(2,1)S(1)} %get-tuple-element.64), channel_id=1, source_target_pairs={{0,24},{4,28},{1,25},{5,29},{2,26},{6,30},{3,27},{7,31}} | collective-permute-start | bytes 393224 | tf_op jit(solution)/shard_map/ppermute | solution.py:712
  134.6 12.4 %collective-permute-start.7 = (bf16[2,128,256]{2,1,0:T(8,128)(2,1)S(1)}, bf16[2,128,256]{2,1,0:T(8,128)(2,1)S(1)}, u32[]{:S(2)}, u32[]{:S(2)}) collective-permute-start(bf16[2,128,256]{2,1,0:T(8,128)(2,1)S(1)} %get-tuple-element.64), channel_id=1, source_target_pairs={{0,16},{4,20},{8,24},{12,28},{1,17},{5,21},{9,25},{13,29},{2,18},{... | collective-permute-start | bytes 393224 | tf_op jit(solution)/shard_map/ppermute | solution.py:712
  135.9 15.5 %collective-permute-start.8 = (bf16[2,128,256]{2,1,0:T(8,128)(2,1)S(1)}, bf16[2,128,256]{2,1,0:T(8,128)(2,1)S(1)}, u32[]{:S(2)}, u32[]{:S(2)}) collective-permute-start(bf16[2,128,256]{2,1,0:T(8,128)(2,1)S(1)} %get-tuple-element.64), channel_id=1, source_target_pairs={{0,8},{4,12},{8,16},{12,20},{16,24},{20,28},{1,9},{5,13},{9,17},{1... | collective-permute-start | bytes 393224 | tf_op jit(solution)/shard_map/ppermute | solution.py:712
  140.2 16.7 %copy-start.13 = (bf16[128]{0:T(256)(128)(2,1)S(1)}, bf16[128]{0:T(256)(128)(2,1)}, u32[]{:S(2)}) copy-start(bf16[128]{0:T(256)(128)(2,1)} %param.22) | copy-start | bytes 772
  152.6 4.3 %collective-permute-start.9 = (bf16[2,128,128]{2,1,0:T(8,128)(2,1)S(1)}, bf16[2,128,128]{2,1,0:T(8,128)(2,1)S(1)}, u32[]{:S(2)}, u32[]{:S(2)}) collective-permute-start(bf16[2,128,128]{2,1,0:T(8,128)(2,1)S(1)} %get-tuple-element.73), channel_id=1, source_target_pairs={{0,4},{4,0},{8,12},{12,8},{16,20},{20,16},{24,28},{28,24},{1,5},{5... | collective-permute-start | bytes 196616 | tf_op jit(solution)/shard_map/ppermute | solution.py:708
  156.9 22.9 %slice-start.2 = ((s8[6307840]{0:T(1024)(128)(4,1)}), s8[4194304]{0:T(1024)(128)(4,1)S(1)}, s32[]{:S(2)}) async-start(s8[6307840]{0:T(1024)(128)(4,1)} %bitcast.33), calls=%async_computation.2 | async-start | bytes 8388608
  158.0 21.8 %slice-start.3 = ((s8[6307840]{0:T(1024)(128)(4,1)}), s8[2113536]{0:T(1024)(128)(4,1)S(1)}, s32[]{:S(2)}) async-start(s8[6307840]{0:T(1024)(128)(4,1)} %bitcast.33), calls=%async_computation.3 | async-start | bytes 4227072
  158.0 1.6 collective-permute-start.10
  162.8 15.1 %collective-permute-start.11 = (bf16[1120,256]{1,0:T(8,128)(2,1)S(1)}, bf16[1120,256]{1,0:T(8,128)(2,1)S(1)}, u32[]{:S(2)}, u32[]{:S(2)}) collective-permute-start(bf16[1120,256]{1,0:T(8,128)(2,1)S(1)} %attend.2.refs_0_), channel_id=1, source_target_pairs={{0,2},{1,3},{2,0},{3,1},{4,6},{5,7},{6,4},{7,5},{8,10},{9,11},{10,... | collective-permute-start | bytes 1720328 | tf_op jit(solution)/shard_map/ppermute | solution.py:704
  163.3 15.0 %copy-start.19 = (bf16[2240]{0:T(1024)(128)(2,1)S(1)}, bf16[2240]{0:T(1024)(128)(2,1)}, u32[]{:S(2)}) copy-start(bf16[2240]{0:T(1024)(128)(2,1)} %param.24) | copy-start | bytes 13444
  163.3 1.5 collective-permute-start.12
  163.3 15.3 %collective-permute-start.13 = (bf16[1120,256]{1,0:T(8,128)(2,1)S(1)}, bf16[1120,256]{1,0:T(8,128)(2,1)S(1)}, u32[]{:S(2)}, u32[]{:S(2)}) collective-permute-start(bf16[1120,256]{1,0:T(8,128)(2,1)S(1)} %attend.2.refs_0_), channel_id=1, source_target_pairs={{0,1},{1,0},{2,3},{3,2},{4,5},{5,4},{6,7},{7,6},{8,9},{9,8},{10,11... | collective-permute-start | bytes 1720328 | tf_op jit(solution)/shard_map/ppermute | solution.py:700
  177.8 2.0 collective-permute-start.14
  177.9 15.4 %collective-permute-start.15 = (bf16[1120,256]{1,0:T(8,128)(2,1)S(1)}, bf16[1120,256]{1,0:T(8,128)(2,1)S(1)}, u32[]{:S(2)}, u32[]{:S(2)}) collective-permute-start(bf16[1120,256]{1,0:T(8,128)(2,1)S(1)} %attend.3.refs_0_), channel_id=1, source_target_pairs={{0,2},{1,3},{2,0},{3,1},{4,6},{5,7},{6,4},{7,5},{8,10},{9,11},{10,... | collective-permute-start | bytes 1720328 | tf_op jit(solution)/shard_map/ppermute | solution.py:704
  178.4 21.0 %collective-permute-start.16 = (bf16[1120,256]{1,0:T(8,128)(2,1)S(1)}, bf16[1120,256]{1,0:T(8,128)(2,1)S(1)}, u32[]{:S(2)}, u32[]{:S(2)}) collective-permute-start(bf16[1120,256]{1,0:T(8,128)(2,1)S(1)} %attend.3.refs_0_), channel_id=1, source_target_pairs={{0,1},{1,0},{2,3},{3,2},{4,5},{5,4},{6,7},{7,6},{8,9},{9,8},{10,11... | collective-permute-start | bytes 1720328 | tf_op jit(solution)/shard_map/ppermute | solution.py:700
  179.8 13.4 %copy-start.18 = (bf16[3,1400]{1,0:T(4,128)(2,1)S(1)}, bf16[3,1400]{1,0:T(4,128)(2,1)}, u32[]{:S(2)}) copy-start(bf16[3,1400]{1,0:T(4,128)(2,1)} %param.26) | copy-start | bytes 25204
  179.8 29.1 %slice-start = ((s8[6307840]{0:T(1024)(128)(4,1)}), s8[4194304]{0:T(1024)(128)(4,1)S(1)}, s32[]{:S(2)}) async-start(s8[6307840]{0:T(1024)(128)(4,1)} %bitcast.28), calls=%async_computation | async-start | bytes 8388608
  193.2 6.1 %collective-permute-start.17 = (bf16[1120,256]{1,0:T(8,128)(2,1)S(1)}, bf16[1120,256]{1,0:T(8,128)(2,1)S(1)}, u32[]{:S(2)}, u32[]{:S(2)}) collective-permute-start(bf16[1120,256]{1,0:T(8,128)(2,1)S(1)} %collective-permute-done.15.refs_1_), channel_id=1, source_target_pairs={{0,1},{1,0},{2,3},{3,2},{4,5},{5,4},{6,7},{7,6},{8,9},{9,8},{10,11... | collective-permute-start | bytes 1720328 | tf_op jit(solution)/shard_map/ppermute | solution.py:700
  193.3 10.5 %collective-permute-start.19 = (bf16[1,1400]{1,0:T(2,128)(2,1)S(1)}, bf16[1,1400]{1,0:T(2,128)(2,1)S(1)}, u32[]{:S(2)}, u32[]{:S(2)}) collective-permute-start(bf16[1,1400]{1,0:T(2,128)(2,1)S(1)} %get-tuple-element.82), channel_id=1, source_target_pairs={{4,0},{8,4},{12,8},{16,12},{20,16},{24,20},{28,24},{5,1},{9,5},{13... | collective-permute-start | bytes 8408 | tf_op jit(solution)/shard_map/ppermute | solution.py:819
  195.2 8.5 %collective-permute-start.18 = (bf16[1,1400]{1,0:T(2,128)(2,1)S(1)}, bf16[1,1400]{1,0:T(2,128)(2,1)S(1)}, u32[]{:S(2)}, u32[]{:S(2)}) collective-permute-start(bf16[1,1400]{1,0:T(2,128)(2,1)S(1)} %get-tuple-element.85), channel_id=1, source_target_pairs={{0,4},{4,8},{8,12},{12,16},{16,20},{20,24},{24,28},{1,5},{5,9},{9,... | collective-permute-start | bytes 8408 | tf_op jit(solution)/shard_map/ppermute | solution.py:818
  199.4 9.6 %slice-start.1 = ((s8[6307840]{0:T(1024)(128)(4,1)}), s8[2113536]{0:T(1024)(128)(4,1)S(1)}, s32[]{:S(2)}) async-start(s8[6307840]{0:T(1024)(128)(4,1)} %bitcast.28), calls=%async_computation.1 | async-start | bytes 4227072
  206.0 2.9 %collective-permute-start.20 = (bf16[1400,256]{1,0:T(8,128)(2,1)S(1)}, bf16[1400,256]{1,0:T(8,128)(2,1)S(1)}, u32[]{:S(2)}, u32[]{:S(2)}) collective-permute-start(bf16[1400,256]{1,0:T(8,128)(2,1)S(1)} %activate.2.own_a.own), channel_id=1, source_target_pairs={{0,1},{1,0},{2,3},{3,2},{4,5},{5,4},{6,7},{7,6},{8,9},{9,8},{10,11... | collective-permute-start | bytes 2150408 | tf_op jit(solution)/shard_map/ppermute | solution.py:700
  208.4 2.8 %collective-permute-start.21 = (bf16[1400,256]{1,0:T(8,128)(2,1)S(1)}, bf16[1400,256]{1,0:T(8,128)(2,1)S(1)}, u32[]{:S(2)}, u32[]{:S(2)}) collective-permute-start(bf16[1400,256]{1,0:T(8,128)(2,1)S(1)} %activate.3.own.own_b), channel_id=1, source_target_pairs={{0,1},{1,0},{2,3},{3,2},{4,5},{5,4},{6,7},{7,6},{8,9},{9,8},{10,11... | collective-permute-start | bytes 2150408 | tf_op jit(solution)/shard_map/ppermute | solution.py:700
  210.6 9.8 %collective-permute-start.22 = (bf16[560,256]{1,0:T(8,128)(2,1)S(1)}, bf16[560,256]{1,0:T(8,128)(2,1)S(1)}, u32[]{:S(2)}, u32[]{:S(2)}) collective-permute-start(bf16[560,256]{1,0:T(8,128)(2,1)S(1)} %far_project.3), channel_id=1, source_target_pairs={{0,2},{1,3},{2,0},{3,1},{4,6},{5,7},{6,4},{7,5},{8,10},{9,11},{10,... | collective-permute-start | bytes 860168 | tf_op jit(solution)/shard_map/ppermute | solution.py:704
  212.8 12.8 %collective-permute-start.23 = (bf16[560,256]{1,0:T(8,128)(2,1)S(1)}, bf16[560,256]{1,0:T(8,128)(2,1)S(1)}, u32[]{:S(2)}, u32[]{:S(2)}) collective-permute-start(bf16[560,256]{1,0:T(8,128)(2,1)S(1)} %far_project.2.after), channel_id=1, source_target_pairs={{0,2},{1,3},{2,0},{3,1},{4,6},{5,7},{6,4},{7,5},{8,10},{9,11},{10,... | collective-permute-start | bytes 860168 | tf_op jit(solution)/shard_map/ppermute | solution.py:704
  (1 other events, 0.8 us)

commit v5 on v4

--- a/solution.py
+++ b/solution.py
@@ -152,7 +152,7 @@
         + [shape_of((16, count), f32), shape_of((8, count), f32)]
         + [shape_of((ys, part, hidden))] * first,
         in_specs=[SM] + [ANY] * len(pieces) + [VM] * 2 + [ANY] * 4 + [VM] * (0 if first else 5),
-        out_specs=[VM] * 5 + [ANY] * first,
+        out_specs=[VM] * (5 + first),
         scratch_shapes=[
             pltpu.VMEM((span, count), bf16),
             pltpu.VMEM((count, span), bf16),
@@ -160,7 +160,7 @@
             pltpu.SemaphoreType.DMA((3,)),
             pltpu.SemaphoreType.DMA((len(pieces) + ys,)),
         ],
-        compiler_params=params(54),
+        compiler_params=params(48),
         cost_estimate=cost(3 * 10**9, 8 * 10**6),
         name="early_project",
     )(meta, *pieces, gain, gates, w_key, w_value, w_query, w_down, *(before or ()))
@@ -338,7 +338,7 @@
             pltpu.SemaphoreType.DMA((2,)),
             pltpu.SemaphoreType.DMA((n,)),
         ],
-        compiler_params=params(54),
+        compiler_params=params(16),
         cost_estimate=cost(10 * 10**9, 14 * 10**6),
         name="block_maps",
     )(meta, *pieces, gain, rates, gates, w_key, w_value, acc_k, acc_v, acc_g, squares)
@@ -774,17 +774,23 @@
     ffn_scale = ffn_gain.astype(f32).reshape(1, features)
     taps = conv_taps.astype(f32)
 
+    gains = [ours(gain, d) for d in range(ys)]
+    gate_rows = [ours(gates, d) for d in range(ys)]
+    gains, gate_rows, rates, taps, ffn_scale, head_scale, meta = lax.optimization_barrier(
+        (gains, gate_rows, rates, taps, ffn_scale, head_gain.reshape(1, DK), meta)
+    )
+
     early = None
     for d in range(ys - 1):
         early = early_project(
-            meta, CHIP + d, groups[d], ours(gain, d), ours(gates, d), w_key, w_value, w_query, w_parts, early
+            meta, CHIP + d, groups[d], gains[d], gate_rows[d], w_key, w_value, w_query, w_parts, early
         )
         if d == 0:
             sent_w_down, early = early[5], early[:5]
         piece, _ = lax.optimization_barrier((shifted[d + 1], early[4]))
         groups.append(group_of(piece))
     scaled, scale_b, keys, erased, entry, own_maps, sent_maps, totals = block_maps(
-        meta, CHIP + ys - 1, groups[-1], ours(gain, -1), rates, ours(gates, -1), w_key, w_value, early
+        meta, CHIP + ys - 1, groups[-1], gains[-1], rates, gate_rows[-1], w_key, w_value, early
     )
 
     sent_w_out, sent_w_down, _ = lax.optimization_barrier((w_out_t, sent_w_down, groups[-1][-1]))
@@ -803,7 +809,7 @@
     kept_state, given_state = start_states(meta, first, pairs, out_done)
     other_state = pair_swap(given_state, seqs)
 
-    mixed = mixed_heads(meta, kept_state, other_state, shard_query, free, head_gain.reshape(1, DK))
+    mixed = mixed_heads(meta, kept_state, other_state, shard_query, free, head_scale)
     sums = []
     for own_mixed in mixed:
         summed = attend(meta, own_mixed, core_swap(own_mixed, n), w_out_t, other_w_out)

time: 228 us -> 128 us (0.56)
  Pallas kernels: 149 us -> 47.6 us
  local copies, waits for them, and re-layouts: 8.36 us -> 2.77 us
  waiting for transfers between devices: 45.2 us -> 49.9 us
    pallas_call x1, Pallas kernels: 99.2 us -> 6.32 us  [early_project(): pl.pallas_call(functools.partial(early_kernel, len(pieces), at), out_shap...]
    unnamed x52 -> x20, local copies, waits for them, and re-layouts: 5.24 us -> 0.05 us
    pallas_call x1, Pallas kernels: 17 us -> 12.3 us  [block_maps(): pl.pallas_call(functools.partial(maps_kernel, n, heads, at), out_shape=(s...]
    ppermute x5, waiting for transfers between devices: 28.1 us -> 32.3 us  [y_shift(): lax.ppermute(value, 'head', [(i, (i + 2 * step) % n) for i in range(n)])]
    pallas_call x2, Pallas kernels: 6.28 us -> 2.66 us  [attend(): pl.pallas_call(attend_kernel, out_shape=shape_of((weights.shape[0] // 2,...]
  transfers between devices with their start and end apart: 24 -> 24, of which waited for: 12 -> 13; matrix products, arithmetic and copies ran while one was open for 2% -> 3% of each run, Pallas kernels for 62% -> 32%
where the time goes in v5:
time: 128 us; the launch traced here: 127 us
  waiting for transfers between devices  49.9 us (39%)
  Pallas kernels  47.6 us (37%)
  starting transfers between devices  24.1 us (19%)
  local copies, waits for them, and re-layouts  2.77 us (2%)
  other arithmetic  2.48 us (2%)
    ppermute x5, waiting for transfers between devices, y_shift(): lax.ppermute(value, 'head', [(i, (i + 2 * step) % n) for i in range(n)])  32.3 us
    pallas_call x1, Pallas kernels, block_maps(): pl.pallas_call(functools.partial(maps_kernel, n, heads, at), out_shape=(s...  12.3 us
    pallas_call x2, Pallas kernels, up_project(): pl.pallas_call(functools.partial(up_kernel, len(own)), out_shape=(shape_o...  8.31 us
    ppermute x3, waiting for transfers between devices, later(): lax.ppermute(value, 'seq', [(i, i + 2 * step) for i in range(n - 2 * step)])  7.81 us
    ppermute x5, starting transfers between devices, y_shift(): lax.ppermute(value, 'head', [(i, (i + 2 * step) % n) for i in range(n)])  6.79 us
    pallas_call x1, Pallas kernels, early_project(): pl.pallas_call(functools.partial(early_kernel, len(pieces), at), out_shap...  6.32 us
    ppermute x3, starting transfers between devices, later(): lax.ppermute(value, 'seq', [(i, i + 2 * step) for i in range(n - 2 * step)])  6.26 us
    ppermute x2, waiting for transfers between devices, pair_swap(): return lax.ppermute(value, 'seq', [(i, i ^ 1) for i in range(n)])  4.97 us
  transfers between devices with their start and end apart: 24, of which 13 were waited for; matrix products, arithmetic and copies ran while one was open for 3% of the time, Pallas kernels for 32%

profile of v5, /device:TPU:16, one launch (start us, length us, event | category | flops | bytes accessed | tf_op | source)
XLA Modules:
  0.0 127.2 jit_solution(11564685899036367817)
XLA Ops:
  0.0 1.6 %collective-permute-start = (bf16[560,512]{1,0:T(8,128)(2,1)}, bf16[560,512]{1,0:T(8,128)(2,1)S(1)}, u32[]{:S(2)}, u32[]{:S(2)}) collective-permute-start(bf16[560,512]{1,0:T(8,128)(2,1)} %bitcast.37), channel_id=1, source_target_pairs={{0,2},{1,3},{2,0},{3,1},{4,6},{5,7},{6,4},{7,5},{8,10},{9,11},{10,... | collective-permute-start | bytes 1720328 | tf_op jit(solution)/shard_map/ppermute | solution.py:704
  1.6 0.8 fusion.3
  2.5 0.8 reshape.37
  3.3 0.7 convert_element_type.15.taps
  4.0 0.8 reshape.31
  4.7 0.7 reshape.39.refs_4_
  5.8 6.3 %early_project.1 = (f32[512,512]{1,0:T(8,128)S(1)}, f32[512,512]{1,0:T(8,128)S(1)}, f32[512,512]{1,0:T(8,128)S(1)}, f32[16,512]{1,0:T(8,128)S(1)}, f32[8,512]{1,0:T(8,128)S(1)}, /*index=5*/bf16[2,560,1400]{2,1,0:T(8,128)(2,1)}) custom-call(s32[6]{0:T(128)S(1)} %stack.24.meta, bf16[560,512]{1,0:T(8,128)(2,1)S(1)} %bitcast.38, ...), custom_call_target="tpu_custom_call" | custom-call | flops 3000000000 | bytes 8000000 | tf_op jit(solution)/shard_map/early_project/pallas_call | solution.py:149
  12.2 3.4 %collective-permute-done.refs_0_.refs_2_ = bf16[560,512]{1,0:T(8,128)(2,1)S(1)} collective-permute-done((bf16[560,512]{1,0:T(8,128)(2,1)}, bf16[560,512]{1,0:T(8,128)(2,1)S(1)}, u32[]{:S(2)}, u32[]{:S(2)}) %collective-permute-start) | collective-permute-done | bytes 573472 | tf_op jit(solution)/shard_map/ppermute | solution.py:704
  15.6 2.0 %collective-permute-done.2.refs_1_.refs_3_ = bf16[560,512]{1,0:T(8,128)(2,1)S(1)} collective-permute-done((bf16[560,512]{1,0:T(8,128)(2,1)S(1)}, bf16[560,512]{1,0:T(8,128)(2,1)S(1)}, u32[]{:S(2)}, u32[]{:S(2)}) %collective-permute-start.2) | collective-permute-done | bytes 573472 | tf_op jit(solution)/shard_map/ppermute | solution.py:700
  18.1 12.3 %block_maps.1 = (bf16[512,1120]{1,0:T(8,128)(2,1)S(1)}, f32[512,128]{1,0:T(8,128)S(1)}, bf16[512,512]{1,0:T(8,128)(2,1)S(1)}, bf16[512,1024]{1,0:T(8,128)(2,1)S(...) custom-call(s32[6]{0:T(128)S(1)} %stack.24.meta, ...), custom_call_target="tpu_custom_call" | custom-call | flops 10000000000 | bytes 14000000 | tf_op jit(solution)/shard_map/block_maps/pallas_call | solution.py:314
  30.4 1.6 %collective-permute-start.5 = (bf16[2,128,256]{2,1,0:T(8,128)(2,1)S(1)}, bf16[2,128,256]{2,1,0:T(8,128)(2,1)S(1)}, u32[]{:S(2)}, u32[]{:S(2)}) collective-permute-start(bf16[2,128,256]{2,1,0:T(8,128)(2,1)S(1)} %get-tuple-element.76), channel_id=1, source_target_pairs={{0,4},{4,0},{8,12},{12,8},{16,20},{20,16},{24,28},{28,24},{1,5},{5... | collective-permute-start | bytes 393224 | tf_op jit(solution)/shard_map/ppermute | solution.py:708
  32.0 1.9 %queries.1 = (bf16[512,512]{1,0:T(8,128)(2,1)S(1)}, bf16[2240,256]{1,0:T(8,128)(2,1)S(1)}, bf16[2240,256]{1,0:T(8,128)(2,1)S(1)}, f32[8,128]{1,0:T(8,128)S(1)}) custom-call(s32[6]{0:T(128)S(1)} %stack.24.meta, bf16[512,1120]{1,0:T(8,128)(2,1)S(1)} %get-tuple-element.67.scaled, f32[512,128]{1,0:T(8,128)S(1)} %get-tuple-element.68.scale_b, ...), custom_call_target="tpu_custom_call" | custom-call | flops 1000000000 | bytes 8000000 | tf_op jit(solution)/shard_map/queries/pallas_call | solution.py:378
  33.9 2.2 %collective-permute-done.5.other = bf16[2,128,256]{2,1,0:T(8,128)(2,1)S(1)} collective-permute-done((bf16[2,128,256]{2,1,0:T(8,128)(2,1)S(1)}, bf16[2,128,256]{2,1,0:T(8,128)(2,1)S(1)}, u32[]{:S(2)}, u32[]{:S(2)}) %collective-permute-start.5) | collective-permute-done | bytes 131104 | tf_op jit(solution)/shard_map/ppermute | solution.py:708
  36.0 0.7 pair_maps.1
  36.8 0.7 collective-permute-start.6
  37.5 1.3 %collective-permute-start.7 = (bf16[2,128,256]{2,1,0:T(8,128)(2,1)S(1)}, bf16[2,128,256]{2,1,0:T(8,128)(2,1)S(1)}, u32[]{:S(2)}, u32[]{:S(2)}) collective-permute-start(bf16[2,128,256]{2,1,0:T(8,128)(2,1)S(1)} %get-tuple-element.79), channel_id=1, source_target_pairs={{0,16},{4,20},{8,24},{12,28},{1,17},{5,21},{9,25},{13,29},{2,18},{... | collective-permute-start | bytes 393224 | tf_op jit(solution)/shard_map/ppermute | solution.py:712
  38.8 4.3 %collective-permute-start.8 = (bf16[2,128,256]{2,1,0:T(8,128)(2,1)S(1)}, bf16[2,128,256]{2,1,0:T(8,128)(2,1)S(1)}, u32[]{:S(2)}, u32[]{:S(2)}) collective-permute-start(bf16[2,128,256]{2,1,0:T(8,128)(2,1)S(1)} %get-tuple-element.79), channel_id=1, source_target_pairs={{0,8},{4,12},{8,16},{12,20},{16,24},{20,28},{1,9},{5,13},{9,17},{1... | collective-permute-start | bytes 393224 | tf_op jit(solution)/shard_map/ppermute | solution.py:712
  43.1 2.8 %block_outputs.1 = (bf16[512,512]{1,0:T(8,128)(2,1)S(1)}, f32[512,512]{1,0:T(8,128)S(1)}, f32[8,128]{1,0:T(8,128)S(1)}) custom-call(bf16[512,512]{1,0:T(8,128)(2,1)S(1)} %get-tuple-element.80.query, bf16[512,512]{1,0:T(8,128)(2,1)S(1)} %get-tuple-element.81.keys, bf16[512,1024]{1,0:T(8,128)(2,1)S(1)} %get-tuple-element.82.erased, ...), custom_call_target="tpu_custom_call" | custom-call | flops 3000000000 | bytes 4000000 | tf_op jit(solution)/shard_map/block_outputs/pallas_call | solution.py:429
  45.9 3.6 %collective-permute-done.7.refs_1_ = bf16[2,128,256]{2,1,0:T(8,128)(2,1)S(1)} collective-permute-done((bf16[2,128,256]{2,1,0:T(8,128)(2,1)S(1)}, bf16[2,128,256]{2,1,0:T(8,128)(2,1)S(1)}, u32[]{:S(2)}, u32[]{:S(2)}) %collective-permute-start.7) | collective-permute-done | bytes 131104 | tf_op jit(solution)/shard_map/ppermute | solution.py:712
  49.6 4.2 %collective-permute-done.8.refs_2_ = bf16[2,128,256]{2,1,0:T(8,128)(2,1)S(1)} collective-permute-done((bf16[2,128,256]{2,1,0:T(8,128)(2,1)S(1)}, bf16[2,128,256]{2,1,0:T(8,128)(2,1)S(1)}, u32[]{:S(2)}, u32[]{:S(2)}) %collective-permute-start.8) | collective-permute-done | bytes 131104 | tf_op jit(solution)/shard_map/ppermute | solution.py:712
  53.7 1.2 start_states.1
  55.0 1.5 %collective-permute-start.9 = (bf16[2,128,128]{2,1,0:T(8,128)(2,1)S(1)}, bf16[2,128,128]{2,1,0:T(8,128)(2,1)S(1)}, u32[]{:S(2)}, u32[]{:S(2)}) collective-permute-start(bf16[2,128,128]{2,1,0:T(8,128)(2,1)S(1)} %get-tuple-element.88), channel_id=1, source_target_pairs={{0,4},{4,0},{8,12},{12,8},{16,20},{20,16},{24,28},{28,24},{1,5},{5... | collective-permute-start | bytes 196616 | tf_op jit(solution)/shard_map/ppermute | solution.py:708
  56.5 2.8 %collective-permute-done.9.other = bf16[2,128,128]{2,1,0:T(8,128)(2,1)S(1)} collective-permute-done((bf16[2,128,128]{2,1,0:T(8,128)(2,1)S(1)}, bf16[2,128,128]{2,1,0:T(8,128)(2,1)S(1)}, u32[]{:S(2)}, u32[]{:S(2)}) %collective-permute-start.9) | collective-permute-done | bytes 65568 | tf_op jit(solution)/shard_map/ppermute | solution.py:708
  59.3 1.1 mixed_heads.1
  60.5 1.5 %collective-permute-done.10.other = bf16[256,512]{1,0:T(8,128)(2,1)S(1)} collective-permute-done((bf16[256,512]{1,0:T(8,128)(2,1)S(1)}, bf16[256,512]{1,0:T(8,128)(2,1)S(1)}, u32[]{:S(2)}, u32[]{:S(2)}) %collective-permute-start.10) | collective-permute-done | bytes 262176 | tf_op jit(solution)/shard_map/ppermute | solution.py:700
  62.0 1.3 %attend.2.refs_0_ = bf16[1120,256]{1,0:T(8,128)(2,1)S(1)} custom-call(s32[6]{0:T(128)S(1)} %stack.24.meta, bf16[256,512]{1,0:T(8,128)(2,1)S(1)} %get-tuple-element.92.own, bf16[256,512]{1,0:T(8,128)(2,1)S(1)} %collective-permute-done.10.other, bf16[2240,512]{1,0:T(8,128)(2,1)S(1)} %bitcast.34, bf16[2240,512]{1,0:T(8,128)(2,1)S(1)} %collective-permute-done.3.other_weights), custom_call_target="tpu_custom_call" | custom-call | flops 1000000000 | bytes 5000000 | tf_op jit(solution)/shard_map/attend/pallas_call | solution.py:540
  63.3 1.6 %collective-permute-start.11 = (bf16[1120,256]{1,0:T(8,128)(2,1)S(1)}, bf16[1120,256]{1,0:T(8,128)(2,1)S(1)}, u32[]{:S(2)}, u32[]{:S(2)}) collective-permute-start(bf16[1120,256]{1,0:T(8,128)(2,1)S(1)} %attend.2.refs_0_), channel_id=1, source_target_pairs={{0,2},{1,3},{2,0},{3,1},{4,6},{5,7},{6,4},{7,5},{8,10},{9,11},{10,... | collective-permute-start | bytes 1720328 | tf_op jit(solution)/shard_map/ppermute | solution.py:704
  64.9 0.5 collective-permute-start.13
  65.4 1.0 collective-permute-done.12.other
  66.4 1.3 %attend.3.refs_0_ = bf16[1120,256]{1,0:T(8,128)(2,1)S(1)} custom-call(s32[6]{0:T(128)S(1)} %stack.24.meta, bf16[256,512]{1,0:T(8,128)(2,1)S(1)} %get-tuple-element.94.own, bf16[256,512]{1,0:T(8,128)(2,1)S(1)} %collective-permute-done.12.other, bf16[2240,512]{1,0:T(8,128)(2,1)S(1)} %bitcast.35, bf16[2240,512]{1,0:T(8,128)(2,1)S(1)} %collective-permute-done.3.other_weights), custom_call_target="tpu_custom_call" | custom-call | flops 1000000000 | bytes 5000000 | tf_op jit(solution)/shard_map/attend/pallas_call | solution.py:540
  67.8 10.7 %collective-permute-done.11.refs_1_ = bf16[1120,256]{1,0:T(8,128)(2,1)S(1)} collective-permute-done((bf16[1120,256]{1,0:T(8,128)(2,1)S(1)}, bf16[1120,256]{1,0:T(8,128)(2,1)S(1)}, u32[]{:S(2)}, u32[]{:S(2)}) %collective-permute-start.11) | collective-permute-done | bytes 573472 | tf_op jit(solution)/shard_map/ppermute | solution.py:704
  78.4 1.5 %collective-permute-start.15 = (bf16[1120,256]{1,0:T(8,128)(2,1)S(1)}, bf16[1120,256]{1,0:T(8,128)(2,1)S(1)}, u32[]{:S(2)}, u32[]{:S(2)}) collective-permute-start(bf16[1120,256]{1,0:T(8,128)(2,1)S(1)} %attend.3.refs_0_), channel_id=1, source_target_pairs={{0,2},{1,3},{2,0},{3,1},{4,6},{5,7},{6,4},{7,5},{8,10},{9,11},{10,... | collective-permute-start | bytes 1720328 | tf_op jit(solution)/shard_map/ppermute | solution.py:704
  80.4 3.9 %up_project.2 = (bf16[256,1400]{1,0:T(8,128)(2,1)S(1)}, f32[560,256]{1,0:T(8,128)S(1)}, bf16[1,1400]{1,0:T(2,128)(2,1)S(1)}, bf16[1,1400]{1,0:T(2,128)(2,1)S(1)}) custom-call(s32[6]{0:T(128)S(1)} %stack.24.meta, bf16[2240,256]{1,0:T(8,128)(2,1)S(1)} %get-tuple-element.74.tokens, bf16[1120,256]{1,0:T(8,128)(2,1)S(1)} %attend.2.refs_0_, ...), custom_call_target="tpu_custom_call" | custom-call | flops 2000000000 | bytes 8000000 | tf_op jit(solution)/shard_map/up_project/pallas_call | solution.py:585
  84.3 9.5 %collective-permute-done.15.refs_1_ = bf16[1120,256]{1,0:T(8,128)(2,1)S(1)} collective-permute-done((bf16[1120,256]{1,0:T(8,128)(2,1)S(1)}, bf16[1120,256]{1,0:T(8,128)(2,1)S(1)}, u32[]{:S(2)}, u32[]{:S(2)}) %collective-permute-start.15) | collective-permute-done | bytes 573472 | tf_op jit(solution)/shard_map/ppermute | solution.py:704
  93.8 2.3 %collective-permute-start.19 = (bf16[1,1400]{1,0:T(2,128)(2,1)S(1)}, bf16[1,1400]{1,0:T(2,128)(2,1)S(1)}, u32[]{:S(2)}, u32[]{:S(2)}) collective-permute-start(bf16[1,1400]{1,0:T(2,128)(2,1)S(1)} %get-tuple-element.99), channel_id=1, source_target_pairs={{4,0},{8,4},{12,8},{16,12},{20,16},{24,20},{28,24},{5,1},{9,5},{13... | collective-permute-start | bytes 8408 | tf_op jit(solution)/shard_map/ppermute | solution.py:825
  96.2 3.7 %collective-permute-start.18 = (bf16[1,1400]{1,0:T(2,128)(2,1)S(1)}, bf16[1,1400]{1,0:T(2,128)(2,1)S(1)}, u32[]{:S(2)}, u32[]{:S(2)}) collective-permute-start(bf16[1,1400]{1,0:T(2,128)(2,1)S(1)} %get-tuple-element.102), channel_id=1, source_target_pairs={{0,4},{4,8},{8,12},{12,16},{16,20},{20,24},{24,28},{1,5},{5,9},{9,... | collective-permute-start | bytes 8408 | tf_op jit(solution)/shard_map/ppermute | solution.py:824
  99.9 4.4 %up_project.3 = (bf16[256,1400]{1,0:T(8,128)(2,1)S(1)}, f32[560,256]{1,0:T(8,128)S(1)}, bf16[1,1400]{1,0:T(2,128)(2,1)}, bf16[1,1400]{1,0:T(2,128)(2,1)}) custom-call(s32[6]{0:T(128)S(1)} %stack.24.meta, bf16[2240,256]{1,0:T(8,128)(2,1)S(1)} %get-tuple-element.98.tokens, bf16[1120,256]{1,0:T(8,128)(2,1)S(1)} %attend.3.refs_0_, ...), custom_call_target="tpu_custom_call" | custom-call | flops 2000000000 | bytes 8000000 | tf_op jit(solution)/shard_map/up_project/pallas_call | solution.py:585
  104.4 2.3 %activate.2.own_a.own = bf16[1400,256]{1,0:T(8,128)(2,1)S(1)} custom-call(s32[6]{0:T(128)S(1)} %stack.24.meta, bf16[256,1400]{1,0:T(8,128)(2,1)S(1)} %get-tuple-element.97.outer, bf16[256,1400]{1,0:T(8,128)(2,1)S(1)} %get-tuple-element.101.inside, bf16[1,1400]{1,0:T(2,128)(2,1)S(1)} %collective-permute-done.18.before, ...), custom_call_target="tpu_custom_call" | custom-call | flops 1000000000 | bytes 2000000 | tf_op jit(solution)/shard_map/activate/pallas_call | solution.py:641
  106.7 2.3 %activate.3.own.own_b = bf16[1400,256]{1,0:T(8,128)(2,1)S(1)} custom-call(s32[6]{0:T(128)S(1)} %stack.24.meta, bf16[256,1400]{1,0:T(8,128)(2,1)S(1)} %get-tuple-element.97.outer, bf16[256,1400]{1,0:T(8,128)(2,1)S(1)} %get-tuple-element.101.inside, bf16[1,1400]{1,0:T(2,128)(2,1)S(1)} %collective-permute-done.18.before, ...), custom_call_target="tpu_custom_call" | custom-call | flops 1000000000 | bytes 2000000 | tf_op jit(solution)/shard_map/activate/pallas_call | solution.py:641
  109.0 0.6 collective-permute-start.21
  109.6 1.6 %far_project.3 = bf16[560,256]{1,0:T(8,128)(2,1)S(1)} custom-call(s32[6]{0:T(128)S(1)} %stack.24.meta, bf16[1400,256]{1,0:T(8,128)(2,1)S(1)} %activate.2.own_a.own, bf16[1400,256]{1,0:T(8,128)(2,1)S(1)} %collective-permute-done.20.other_a.other, bf16[4,560,1400]{2,1,0:T(8,128)(2,1)S(1)} %bitcast.28, ...), custom_call_target="tpu_custom_call" | custom-call | flops 1000000000 | bytes 4000000 | tf_op jit(solution)/shard_map/far_project/pallas_call | solution.py:663
  111.2 1.6 %collective-permute-start.22 = (bf16[560,256]{1,0:T(8,128)(2,1)S(1)}, bf16[560,256]{1,0:T(8,128)(2,1)S(1)}, u32[]{:S(2)}, u32[]{:S(2)}) collective-permute-start(bf16[560,256]{1,0:T(8,128)(2,1)S(1)} %far_project.3), channel_id=1, source_target_pairs={{0,2},{1,3},{2,0},{3,1},{4,6},{5,7},{6,4},{7,5},{8,10},{9,11},{10,... | collective-permute-start | bytes 860168 | tf_op jit(solution)/shard_map/ppermute | solution.py:704
  112.8 1.6 %far_project.2.after = bf16[560,256]{1,0:T(8,128)(2,1)S(1)} custom-call(s32[6]{0:T(128)S(1)} %stack.24.meta, bf16[1400,256]{1,0:T(8,128)(2,1)S(1)} %activate.3.own.own_b, bf16[1400,256]{1,0:T(8,128)(2,1)S(1)} %collective-permute-done.21.other.other_b, bf16[4,560,1400]{2,1,0:T(8,128)(2,1)S(1)} %bitcast.29, ...), custom_call_target="tpu_custom_call" | custom-call | flops 1000000000 | bytes 4000000 | tf_op jit(solution)/shard_map/far_project/pallas_call | solution.py:663
  114.4 0.6 collective-permute-start.23
  115.0 2.5 %near_project.1 = f32[560,512]{1,0:T(8,128)S(1)} custom-call(s32[6]{0:T(128)S(1)} %stack.24.meta, bf16[1400,256]{1,0:T(8,128)(2,1)S(1)} %activate.2.own_a.own, bf16[1400,256]{1,0:T(8,128)(2,1)S(1)} %collective-permute-done.20.other_a.other, bf16[1400,256]{1,0:T(8,128)(2,1)S(1)} %activate.3.own.own_b, ...), custom_call_target="tpu_custom_call" | custom-call | flops 2000000000 | bytes 6000000 | tf_op jit(solution)/shard_map/near_project/pallas_call | solution.py:688
  117.5 3.5 %collective-permute-done.22 = bf16[560,256]{1,0:T(8,128)(2,1)S(1)} collective-permute-done((bf16[560,256]{1,0:T(8,128)(2,1)S(1)}, bf16[560,256]{1,0:T(8,128)(2,1)S(1)}, u32[]{:S(2)}, u32[]{:S(2)}) %collective-permute-start.22) | collective-permute-done | bytes 286752 | tf_op jit(solution)/shard_map/ppermute | solution.py:704
  121.0 5.2 %collective-permute-done.23 = bf16[560,256]{1,0:T(8,128)(2,1)S(1)} collective-permute-done((bf16[560,256]{1,0:T(8,128)(2,1)S(1)}, bf16[560,256]{1,0:T(8,128)(2,1)S(1)}, u32[]{:S(2)}, u32[]{:S(2)}) %collective-permute-start.23) | collective-permute-done | bytes 286752 | tf_op jit(solution)/shard_map/ppermute | solution.py:704
  126.2 1.0 fusion
  (51 shorter events, 1.7 us)
Async XLA Ops:
  0.0 5.8 %copy-start.4 = (bf16[512,560]{0,1:T(8,128)(2,1)S(1)}, bf16[512,560]{0,1:T(8,128)(2,1)}, u32[]{:S(2)}) copy-start(bf16[512,560]{0,1:T(8,128)(2,1)} %param.14) | copy-start | bytes 1720324
  0.0 5.8 %collective-permute-start.1 = (bf16[560,512]{1,0:T(8,128)(2,1)}, bf16[560,512]{1,0:T(8,128)(2,1)S(1)}, u32[]{:S(2)}, u32[]{:S(2)}) collective-permute-start(bf16[560,512]{1,0:T(8,128)(2,1)} %bitcast.36), channel_id=1, source_target_pairs={{0,1},{1,0},{2,3},{3,2},{4,5},{5,4},{6,7},{7,6},{8,9},{9,8},{10,11... | collective-permute-start | bytes 1720328 | tf_op jit(solution)/shard_map/ppermute | solution.py:700
  0.0 15.6 %collective-permute-start = (bf16[560,512]{1,0:T(8,128)(2,1)}, bf16[560,512]{1,0:T(8,128)(2,1)S(1)}, u32[]{:S(2)}, u32[]{:S(2)}) collective-permute-start(bf16[560,512]{1,0:T(8,128)(2,1)} %bitcast.37), channel_id=1, source_target_pairs={{0,2},{1,3},{2,0},{3,1},{4,6},{5,7},{6,4},{7,5},{8,10},{9,11},{10,... | collective-permute-start | bytes 1720328 | tf_op jit(solution)/shard_map/ppermute | solution.py:704
  5.8 11.9 %copy-start = (bf16[512,2240]{0,1:T(8,128)(2,1)S(1)}, bf16[512,2240]{0,1:T(8,128)(2,1)}, u32[]{:S(2)}) copy-start(bf16[512,2240]{0,1:T(8,128)(2,1)} %param.23) | copy-start | bytes 6881284
  5.8 12.3 %copy-start.2 = (bf16[2240,512]{1,0:T(8,128)(2,1)S(1)}, bf16[2240,512]{1,0:T(8,128)(2,1)}, u32[]{:S(2)}) copy-start(bf16[2240,512]{1,0:T(8,128)(2,1)} %refs_5_.5) | copy-start | bytes 6881284
  5.8 12.3 %copy-start.3 = (bf16[2240,512]{1,0:T(8,128)(2,1)S(1)}, bf16[2240,512]{1,0:T(8,128)(2,1)}, u32[]{:S(2)}) copy-start(bf16[2240,512]{1,0:T(8,128)(2,1)} %refs_6_.3) | copy-start | bytes 6881284
  15.6 2.0 %collective-permute-start.2 = (bf16[560,512]{1,0:T(8,128)(2,1)S(1)}, bf16[560,512]{1,0:T(8,128)(2,1)S(1)}, u32[]{:S(2)}, u32[]{:S(2)}) collective-permute-start(bf16[560,512]{1,0:T(8,128)(2,1)S(1)} %collective-permute-done.refs_0_.refs_2_), channel_id=1, source_target_pairs={{0,1},{1,0},{2,3},{3,2},{4,5},{5,4},{6,7},{7,6},{8,9},{9,8},{10,11... | collective-permute-start | bytes 1720328 | tf_op jit(solution)/shard_map/ppermute | solution.py:700
  17.6 14.4 %collective-permute-start.4 = (bf16[2,560,1400]{2,1,0:T(8,128)(2,1)}, bf16[2,560,1400]{2,1,0:T(8,128)(2,1)S(1)}, u32[]{:S(2)}, u32[]{:S(2)}) collective-permute-start(bf16[2,560,1400]{2,1,0:T(8,128)(2,1)} %get-tuple-element.72), channel_id=1, source_target_pairs={{0,1},{1,0},{2,3},{3,2},{4,5},{5,4},{6,7},{7,6},{8,9},{9,8},{10,11... | collective-permute-start | bytes 9408008 | tf_op jit(solution)/shard_map/ppermute | solution.py:700
  17.7 14.3 %collective-permute-start.3 = (bf16[2240,512]{1,0:T(8,128)(2,1)S(1)}, bf16[2240,512]{1,0:T(8,128)(2,1)S(1)}, u32[]{:S(2)}, u32[]{:S(2)}) collective-permute-start(bf16[2240,512]{1,0:T(8,128)(2,1)S(1)} %bitcast.33), channel_id=1, source_target_pairs={{0,1},{1,0},{2,3},{3,2},{4,5},{5,4},{6,7},{7,6},{8,9},{9,8},{10,11... | collective-permute-start | bytes 6881288 | tf_op jit(solution)/shard_map/ppermute | solution.py:700
  18.1 13.9 %copy-start.1 = (bf16[2240,512]{1,0:T(8,128)(2,1)S(1)}, bf16[2240,512]{1,0:T(8,128)(2,1)}, u32[]{:S(2)}) copy-start(bf16[2240,512]{1,0:T(8,128)(2,1)} %weights.1) | copy-start | bytes 6881284
  30.4 5.6 %collective-permute-start.5 = (bf16[2,128,256]{2,1,0:T(8,128)(2,1)S(1)}, bf16[2,128,256]{2,1,0:T(8,128)(2,1)S(1)}, u32[]{:S(2)}, u32[]{:S(2)}) collective-permute-start(bf16[2,128,256]{2,1,0:T(8,128)(2,1)S(1)} %get-tuple-element.76), channel_id=1, source_target_pairs={{0,4},{4,0},{8,12},{12,8},{16,20},{20,16},{24,28},{28,24},{1,5},{5... | collective-permute-start | bytes 393224 | tf_op jit(solution)/shard_map/ppermute | solution.py:708
  36.8 9.2 %collective-permute-start.6 = (bf16[2,128,256]{2,1,0:T(8,128)(2,1)S(1)}, bf16[2,128,256]{2,1,0:T(8,128)(2,1)S(1)}, u32[]{:S(2)}, u32[]{:S(2)}) collective-permute-start(bf16[2,128,256]{2,1,0:T(8,128)(2,1)S(1)} %get-tuple-element.79), channel_id=1, source_target_pairs={{0,24},{4,28},{1,25},{5,29},{2,26},{6,30},{3,27},{7,31}} | collective-permute-start | bytes 393224 | tf_op jit(solution)/shard_map/ppermute | solution.py:712
  37.5 12.1 %collective-permute-start.7 = (bf16[2,128,256]{2,1,0:T(8,128)(2,1)S(1)}, bf16[2,128,256]{2,1,0:T(8,128)(2,1)S(1)}, u32[]{:S(2)}, u32[]{:S(2)}) collective-permute-start(bf16[2,128,256]{2,1,0:T(8,128)(2,1)S(1)} %get-tuple-element.79), channel_id=1, source_target_pairs={{0,16},{4,20},{8,24},{12,28},{1,17},{5,21},{9,25},{13,29},{2,18},{... | collective-permute-start | bytes 393224 | tf_op jit(solution)/shard_map/ppermute | solution.py:712
  38.8 15.0 %collective-permute-start.8 = (bf16[2,128,256]{2,1,0:T(8,128)(2,1)S(1)}, bf16[2,128,256]{2,1,0:T(8,128)(2,1)S(1)}, u32[]{:S(2)}, u32[]{:S(2)}) collective-permute-start(bf16[2,128,256]{2,1,0:T(8,128)(2,1)S(1)} %get-tuple-element.79), channel_id=1, source_target_pairs={{0,8},{4,12},{8,16},{12,20},{16,24},{20,28},{1,9},{5,13},{9,17},{1... | collective-permute-start | bytes 393224 | tf_op jit(solution)/shard_map/ppermute | solution.py:712
  43.1 16.2 %copy-start.5 = (bf16[128]{0:T(256)(128)(2,1)S(1)}, bf16[128]{0:T(256)(128)(2,1)}, u32[]{:S(2)}) copy-start(bf16[128]{0:T(256)(128)(2,1)} %param.22) | copy-start | bytes 772
  55.0 4.3 %collective-permute-start.9 = (bf16[2,128,128]{2,1,0:T(8,128)(2,1)S(1)}, bf16[2,128,128]{2,1,0:T(8,128)(2,1)S(1)}, u32[]{:S(2)}, u32[]{:S(2)}) collective-permute-start(bf16[2,128,128]{2,1,0:T(8,128)(2,1)S(1)} %get-tuple-element.88), channel_id=1, source_target_pairs={{0,4},{4,0},{8,12},{12,8},{16,20},{20,16},{24,28},{28,24},{1,5},{5... | collective-permute-start | bytes 196616 | tf_op jit(solution)/shard_map/ppermute | solution.py:708
  59.3 21.1 %slice-start.2 = ((s8[6307840]{0:T(1024)(128)(4,1)}), s8[4194304]{0:T(1024)(128)(4,1)S(1)}, s32[]{:S(2)}) async-start(s8[6307840]{0:T(1024)(128)(4,1)} %bitcast.31), calls=%async_computation.2 | async-start | bytes 8388608
  60.4 20.0 %slice-start.3 = ((s8[6307840]{0:T(1024)(128)(4,1)}), s8[2113536]{0:T(1024)(128)(4,1)S(1)}, s32[]{:S(2)}) async-start(s8[6307840]{0:T(1024)(128)(4,1)} %bitcast.31), calls=%async_computation.3 | async-start | bytes 4227072
  60.4 1.6 %collective-permute-start.10 = (bf16[256,512]{1,0:T(8,128)(2,1)S(1)}, bf16[256,512]{1,0:T(8,128)(2,1)S(1)}, u32[]{:S(2)}, u32[]{:S(2)}) collective-permute-start(bf16[256,512]{1,0:T(8,128)(2,1)S(1)} %get-tuple-element.92.own), channel_id=1, source_target_pairs={{0,1},{1,0},{2,3},{3,2},{4,5},{5,4},{6,7},{7,6},{8,9},{9,8},{10,11... | collective-permute-start | bytes 786440 | tf_op jit(solution)/shard_map/ppermute | solution.py:700
  63.3 15.1 %collective-permute-start.11 = (bf16[1120,256]{1,0:T(8,128)(2,1)S(1)}, bf16[1120,256]{1,0:T(8,128)(2,1)S(1)}, u32[]{:S(2)}, u32[]{:S(2)}) collective-permute-start(bf16[1120,256]{1,0:T(8,128)(2,1)S(1)} %attend.2.refs_0_), channel_id=1, source_target_pairs={{0,2},{1,3},{2,0},{3,1},{4,6},{5,7},{6,4},{7,5},{8,10},{9,11},{10,... | collective-permute-start | bytes 1720328 | tf_op jit(solution)/shard_map/ppermute | solution.py:704
  64.9 1.5 %collective-permute-start.12 = (bf16[256,512]{1,0:T(8,128)(2,1)S(1)}, bf16[256,512]{1,0:T(8,128)(2,1)S(1)}, u32[]{:S(2)}, u32[]{:S(2)}) collective-permute-start(bf16[256,512]{1,0:T(8,128)(2,1)S(1)} %get-tuple-element.94.own), channel_id=1, source_target_pairs={{0,1},{1,0},{2,3},{3,2},{4,5},{5,4},{6,7},{7,6},{8,9},{9,8},{10,11... | collective-permute-start | bytes 786440 | tf_op jit(solution)/shard_map/ppermute | solution.py:700
  64.9 15.2 %collective-permute-start.13 = (bf16[1120,256]{1,0:T(8,128)(2,1)S(1)}, bf16[1120,256]{1,0:T(8,128)(2,1)S(1)}, u32[]{:S(2)}, u32[]{:S(2)}) collective-permute-start(bf16[1120,256]{1,0:T(8,128)(2,1)S(1)} %attend.2.refs_0_), channel_id=1, source_target_pairs={{0,1},{1,0},{2,3},{3,2},{4,5},{5,4},{6,7},{7,6},{8,9},{9,8},{10,11... | collective-permute-start | bytes 1720328 | tf_op jit(solution)/shard_map/ppermute | solution.py:700
  78.4 2.0 %collective-permute-start.14 = (bf16[1120,256]{1,0:T(8,128)(2,1)S(1)}, bf16[1120,256]{1,0:T(8,128)(2,1)S(1)}, u32[]{:S(2)}, u32[]{:S(2)}) collective-permute-start(bf16[1120,256]{1,0:T(8,128)(2,1)S(1)} %collective-permute-done.11.refs_1_), channel_id=1, source_target_pairs={{0,1},{1,0},{2,3},{3,2},{4,5},{5,4},{6,7},{7,6},{8,9},{9,8},{10,11... | collective-permute-start | bytes 1720328 | tf_op jit(solution)/shard_map/ppermute | solution.py:700
  78.4 15.4 %collective-permute-start.15 = (bf16[1120,256]{1,0:T(8,128)(2,1)S(1)}, bf16[1120,256]{1,0:T(8,128)(2,1)S(1)}, u32[]{:S(2)}, u32[]{:S(2)}) collective-permute-start(bf16[1120,256]{1,0:T(8,128)(2,1)S(1)} %attend.3.refs_0_), channel_id=1, source_target_pairs={{0,2},{1,3},{2,0},{3,1},{4,6},{5,7},{6,4},{7,5},{8,10},{9,11},{10,... | collective-permute-start | bytes 1720328 | tf_op jit(solution)/shard_map/ppermute | solution.py:704
  79.9 20.0 %collective-permute-start.16 = (bf16[1120,256]{1,0:T(8,128)(2,1)S(1)}, bf16[1120,256]{1,0:T(8,128)(2,1)S(1)}, u32[]{:S(2)}, u32[]{:S(2)}) collective-permute-start(bf16[1120,256]{1,0:T(8,128)(2,1)S(1)} %attend.3.refs_0_), channel_id=1, source_target_pairs={{0,1},{1,0},{2,3},{3,2},{4,5},{5,4},{6,7},{7,6},{8,9},{9,8},{10,11... | collective-permute-start | bytes 1720328 | tf_op jit(solution)/shard_map/ppermute | solution.py:700
  80.4 29.2 %slice-start = ((s8[6307840]{0:T(1024)(128)(4,1)}), s8[4194304]{0:T(1024)(128)(4,1)S(1)}, s32[]{:S(2)}) async-start(s8[6307840]{0:T(1024)(128)(4,1)} %bitcast.26), calls=%async_computation | async-start | bytes 8388608
  93.8 6.1 %collective-permute-start.17 = (bf16[1120,256]{1,0:T(8,128)(2,1)S(1)}, bf16[1120,256]{1,0:T(8,128)(2,1)S(1)}, u32[]{:S(2)}, u32[]{:S(2)}) collective-permute-start(bf16[1120,256]{1,0:T(8,128)(2,1)S(1)} %collective-permute-done.15.refs_1_), channel_id=1, source_target_pairs={{0,1},{1,0},{2,3},{3,2},{4,5},{5,4},{6,7},{7,6},{8,9},{9,8},{10,11... | collective-permute-start | bytes 1720328 | tf_op jit(solution)/shard_map/ppermute | solution.py:700
  93.8 10.6 %collective-permute-start.19 = (bf16[1,1400]{1,0:T(2,128)(2,1)S(1)}, bf16[1,1400]{1,0:T(2,128)(2,1)S(1)}, u32[]{:S(2)}, u32[]{:S(2)}) collective-permute-start(bf16[1,1400]{1,0:T(2,128)(2,1)S(1)} %get-tuple-element.99), channel_id=1, source_target_pairs={{4,0},{8,4},{12,8},{16,12},{20,16},{24,20},{28,24},{5,1},{9,5},{13... | collective-permute-start | bytes 8408 | tf_op jit(solution)/shard_map/ppermute | solution.py:825
  96.2 8.2 %collective-permute-start.18 = (bf16[1,1400]{1,0:T(2,128)(2,1)S(1)}, bf16[1,1400]{1,0:T(2,128)(2,1)S(1)}, u32[]{:S(2)}, u32[]{:S(2)}) collective-permute-start(bf16[1,1400]{1,0:T(2,128)(2,1)S(1)} %get-tuple-element.102), channel_id=1, source_target_pairs={{0,4},{4,8},{8,12},{12,16},{16,20},{20,24},{24,28},{1,5},{5,9},{9,... | collective-permute-start | bytes 8408 | tf_op jit(solution)/shard_map/ppermute | solution.py:824
  99.9 9.7 %slice-start.1 = ((s8[6307840]{0:T(1024)(128)(4,1)}), s8[2113536]{0:T(1024)(128)(4,1)S(1)}, s32[]{:S(2)}) async-start(s8[6307840]{0:T(1024)(128)(4,1)} %bitcast.26), calls=%async_computation.1 | async-start | bytes 4227072
  106.7 2.9 %collective-permute-start.20 = (bf16[1400,256]{1,0:T(8,128)(2,1)S(1)}, bf16[1400,256]{1,0:T(8,128)(2,1)S(1)}, u32[]{:S(2)}, u32[]{:S(2)}) collective-permute-start(bf16[1400,256]{1,0:T(8,128)(2,1)S(1)} %activate.2.own_a.own), channel_id=1, source_target_pairs={{0,1},{1,0},{2,3},{3,2},{4,5},{5,4},{6,7},{7,6},{8,9},{9,8},{10,11... | collective-permute-start | bytes 2150408 | tf_op jit(solution)/shard_map/ppermute | solution.py:700
  109.0 3.7 %collective-permute-start.21 = (bf16[1400,256]{1,0:T(8,128)(2,1)S(1)}, bf16[1400,256]{1,0:T(8,128)(2,1)S(1)}, u32[]{:S(2)}, u32[]{:S(2)}) collective-permute-start(bf16[1400,256]{1,0:T(8,128)(2,1)S(1)} %activate.3.own.own_b), channel_id=1, source_target_pairs={{0,1},{1,0},{2,3},{3,2},{4,5},{5,4},{6,7},{7,6},{8,9},{9,8},{10,11... | collective-permute-start | bytes 2150408 | tf_op jit(solution)/shard_map/ppermute | solution.py:700
  111.2 9.8 %collective-permute-start.22 = (bf16[560,256]{1,0:T(8,128)(2,1)S(1)}, bf16[560,256]{1,0:T(8,128)(2,1)S(1)}, u32[]{:S(2)}, u32[]{:S(2)}) collective-permute-start(bf16[560,256]{1,0:T(8,128)(2,1)S(1)} %far_project.3), channel_id=1, source_target_pairs={{0,2},{1,3},{2,0},{3,1},{4,6},{5,7},{6,4},{7,5},{8,10},{9,11},{10,... | collective-permute-start | bytes 860168 | tf_op jit(solution)/shard_map/ppermute | solution.py:704
  114.4 11.8 %collective-permute-start.23 = (bf16[560,256]{1,0:T(8,128)(2,1)S(1)}, bf16[560,256]{1,0:T(8,128)(2,1)S(1)}, u32[]{:S(2)}, u32[]{:S(2)}) collective-permute-start(bf16[560,256]{1,0:T(8,128)(2,1)S(1)} %far_project.2.after), channel_id=1, source_target_pairs={{0,2},{1,3},{2,0},{3,1},{4,6},{5,7},{6,4},{7,5},{8,10},{9,11},{10,... | collective-permute-start | bytes 860168 | tf_op jit(solution)/shard_map/ppermute | solution.py:704

commit v6 on v5

--- a/solution.py
+++ b/solution.py
@@ -112,18 +112,32 @@
 def early_kernel(count_in, at, meta, *refs):
     first = at == CHIP
     pieces = refs[:count_in]
-    gain, gates, w_key, w_value, w_query, w_down = refs[count_in : count_in + 6]
-    refs = refs[count_in + 6 :]
+    gain, gates, w_key, w_value, w_query, w_down, w_out = refs[count_in : count_in + 7]
+    refs = refs[count_in + 7 :]
     before, refs = (None, refs) if first else (refs[:5], refs[5:])
     acc_k, acc_v, acc_q, acc_g, squares = refs[:5]
-    partner_w, whole, scaled, held, held_sem, sem = refs[5:] if first else (None, *refs[5:])
+    sent, (whole, scaled, held, held_sem, sem) = (refs[5:8], refs[8:]) if first else ((), refs[5:])
     rows_copies = held_rows(meta, at, (w_key, w_value, w_query), held, held_sem)
-    copies = [
-        pltpu.make_async_copy(
-            w_down.at[2 * y + 1 - meta[CORE]], partner_w.at[y], sem.at[count_in + y]
-        )
-        for y in range(partner_w.shape[0] if first else 0)
-    ]
+    copies = []
+    if first:
+        partner_w, their_rows, my_rows = sent
+        ys = partner_w.shape[0]
+        copies = [
+            pltpu.make_async_copy(
+                w_down.at[2 * y + 1 - meta[CORE]], partner_w.at[y], sem.at[count_in + y]
+            )
+            for y in range(ys)
+        ]
+        for i, (start, target) in enumerate(
+            (
+                ((1 - meta[CORE]) * 2 * my_rows.shape[0], their_rows),
+                ((2 * meta[CORE] + meta[PARITY]) * my_rows.shape[0], my_rows),
+            )
+        ):
+            rows = pl.ds(pl.multiple_of(start, 16), target.shape[0])
+            copies.append(
+                pltpu.make_async_copy(w_out.at[rows], target, sem.at[count_in + ys + i])
+            )
     for copy in copies:
         copy.start()
     load_pair(meta, pieces, whole, sem)
@@ -139,31 +153,36 @@
         copy.wait()
 
 
-def early_project(meta, at, pieces, gain, gates, w_key, w_value, w_query, w_down, before):
+def early_project(meta, at, pieces, gain, gates, w_key, w_value, w_query, w_down, w_out, before):
     first = before is None
     blocks, part, hidden = w_down.shape
     ys = blocks // 2
     span = gain.shape[1]
     count = pieces[0].shape[1]
-    inner = w_key.shape[1]
+    features, inner = w_key.shape
     return pl.pallas_call(
         functools.partial(early_kernel, len(pieces), at),
         out_shape=[shape_of((count, inner), f32)] * 3
         + [shape_of((16, count), f32), shape_of((8, count), f32)]
-        + [shape_of((ys, part, hidden))] * first,
-        in_specs=[SM] + [ANY] * len(pieces) + [VM] * 2 + [ANY] * 4 + [VM] * (0 if first else 5),
-        out_specs=[VM] * (5 + first),
+        + [
+            shape_of((ys, part, hidden)),
+            shape_of((features // 2, inner)),
+            shape_of((features // 4, inner)),
+        ]
+        * first,
+        in_specs=[SM] + [ANY] * len(pieces) + [VM] * 2 + [ANY] * 5 + [VM] * (0 if first else 5),
+        out_specs=[VM] * (8 if first else 5),
         scratch_shapes=[
             pltpu.VMEM((span, count), bf16),
             pltpu.VMEM((count, span), bf16),
             pltpu.VMEM((3, span, inner), bf16),
             pltpu.SemaphoreType.DMA((3,)),
-            pltpu.SemaphoreType.DMA((len(pieces) + ys,)),
+            pltpu.SemaphoreType.DMA((len(pieces) + ys + 2,)),
         ],
         compiler_params=params(48),
         cost_estimate=cost(3 * 10**9, 8 * 10**6),
         name="early_project",
-    )(meta, *pieces, gain, gates, w_key, w_value, w_query, w_down, *(before or ()))
+    )(meta, *pieces, gain, gates, w_key, w_value, w_query, w_down, w_out, *(before or ()))
 
 
 def maps_kernel(n, heads, at, meta, *refs):
@@ -530,40 +549,48 @@
     )(meta, own, other, shard_query, free, gain)
 
 
-def attend_kernel(meta, own, other, weights, other_weights, chip):
-    rows = pl.ds(pl.multiple_of(meta[CORE] * chip.shape[0], 16), chip.shape[0])
-    total = dot_nt(weights[rows, :], own[...]) + dot_nt(other_weights[rows, :], other[...])
-    chip[...] = total.astype(bf16)
-
-
-def attend(meta, own, other, weights, other_weights):
-    return pl.pallas_call(
-        attend_kernel,
+def attend_kernel(ys, meta, tokens, own, partner, weights, partner_weights, *refs):
+    far, middle = refs[:-1], refs[-1]
+    half = middle.shape[0]
+    size = half // 2
+    for i in range(2):
+        quarter = meta[PARITY] if i == 0 else 1 - meta[PARITY]
+        base = meta[CORE] * half + quarter * size
+        here = pl.ds(pl.multiple_of(base, 16), size)
+        rows = pl.ds(pl.multiple_of(quarter * size, 16), size)
+        total = tokens[here, :].astype(f32)
+        total = total + dot_nt(weights[here, :], own[...])
+        total = total + dot_nt(partner_weights[rows, :], partner[...])
+        for d in range(ys - 1):
+            same, diagonal, fetched, swapped, far_weights = far[5 * d : 5 * d + 5]
+            total = total + dot_nt((fetched if i == 0 else swapped)[...], same[...])
+            total = total + dot_nt(far_weights[rows, :], diagonal[...])
+        middle[rows, :] = total.astype(bf16)
+
+
+def attend(meta, ys, tokens, own, partner, weights, partner_weights, far):
+    return pl.pallas_call(
+        functools.partial(attend_kernel, ys),
         out_shape=shape_of((weights.shape[0] // 2, own.shape[0])),
-        in_specs=[SM] + [VM] * 4,
+        in_specs=[SM] + [VM] * (5 + len(far)),
         out_specs=VM,
-        compiler_params=params(10),
-        cost_estimate=cost(10**9, 5 * 10**6),
+        compiler_params=params(12),
+        cost_estimate=cost(2 * 10**9, 7 * 10**6),
         name="attend",
-    )(meta, own, other, weights, other_weights)
-
-
-def up_kernel(adds, meta, tokens, *refs):
-    own, other = refs[:adds], refs[adds : 2 * adds]
-    gain, weights, lifted, middle_part, first, last, middle, hidden, scale_b = refs[2 * adds :]
+    )(meta, tokens, own, partner, weights, partner_weights, *far)
+
+
+def up_kernel(meta, own, other, gain, weights, lifted, middle_part, first, last, middle, hidden, scale_b):
     features, count = middle.shape
     half = features // 2
     step = 160
-    for side, parts in ((meta[CORE], own), (1 - meta[CORE], other)):
+    for side, source in ((meta[CORE], own), (1 - meta[CORE], other)):
 
         @pl.loop(0, half // step)
         def _(r):
             rows = pl.ds(pl.multiple_of(r * step, 32), step)
             target = pl.ds(pl.multiple_of(side * half + r * step, 32), step)
-            total = tokens[target, :].astype(f32)
-            for ref in parts:
-                total = total + ref[rows, :].astype(f32)
-            middle[target, :] = total.astype(bf16).astype(f32)
+            middle[target, :] = source[rows, :].astype(f32)
 
     squares = scale_pass(middle, lambda at, size: gain[:, at : at + size], hidden)
     fill_columns(inverse_of(squares, features), scale_b)
@@ -579,18 +606,18 @@
     last[...] = lifted[count - 1 : count, :]
 
 
-def up_project(meta, tokens, own, other, gain, weights, part):
+def up_project(meta, own, other, gain, weights, part):
     features, hidden = weights.shape
-    count = tokens.shape[1]
-    return pl.pallas_call(
-        functools.partial(up_kernel, len(own)),
+    count = own.shape[1]
+    return pl.pallas_call(
+        up_kernel,
         out_shape=(
             shape_of((count, hidden)),
             shape_of((part, count), f32),
             shape_of((1, hidden)),
             shape_of((1, hidden)),
         ),
-        in_specs=[SM] + [VM] * (3 + 2 * len(own)),
+        in_specs=[SM] + [VM] * 4,
         out_specs=[VM] * 4,
         scratch_shapes=[
             pltpu.VMEM((features, count), f32),
@@ -600,7 +627,7 @@
         compiler_params=params(16),
         cost_estimate=cost(2 * 10**9, 8 * 10**6),
         name="up_project",
-    )(meta, tokens, *own, *other, gain, weights)
+    )(meta, own, other, gain, weights)
 
 
 def gelu_of(x):
@@ -783,46 +810,66 @@
     early = None
     for d in range(ys - 1):
         early = early_project(
-            meta, CHIP + d, groups[d], gains[d], gate_rows[d], w_key, w_value, w_query, w_parts, early
+            meta, CHIP + d, groups[d], gains[d], gate_rows[d], w_key, w_value, w_query, w_parts, w_out_t, early
         )
         if d == 0:
-            sent_w_down, early = early[5], early[:5]
+            sent, early = early[5:], early[:5]
         piece, _ = lax.optimization_barrier((shifted[d + 1], early[4]))
         groups.append(group_of(piece))
     scaled, scale_b, keys, erased, entry, own_maps, sent_maps, totals = block_maps(
         meta, CHIP + ys - 1, groups[-1], gains[-1], rates, gate_rows[-1], w_key, w_value, early
     )
 
-    sent_w_out, sent_w_down, _ = lax.optimization_barrier((w_out_t, sent_w_down, groups[-1][-1]))
-    other_w_out, other_w_down = core_swap(sent_w_out, n), core_swap(sent_w_down, n)
-    acc_query, other_w_out, other_w_down = lax.optimization_barrier(
-        (early[2], other_w_out, other_w_down)
+    sent, _ = lax.optimization_barrier((sent, groups[-1][-1]))
+    sent_w_down, their_rows, my_rows = sent
+    other_w_down = core_swap(sent_w_down, n)
+    fetched = [y_shift(my_rows, n, d) for d in range(1, ys)]
+    partner_w_out = core_swap(their_rows, n)
+    acc_query, partner_w_out, other_w_down = lax.optimization_barrier(
+        (early[2], partner_w_out, other_w_down)
     )
+    their_rows, fetched, _ = lax.optimization_barrier((their_rows, fetched, totals))
+    diagonal = [
+        lax.ppermute(their_rows, "head", [(i, ((i + 2 * d) % n) ^ 1) for i in range(n)])
+        for d in range(1, ys)
+    ]
 
     other_maps = pair_swap(sent_maps, seqs)
     query, tokens_a, tokens_b, query_done = queries(
         meta, ys, scaled, scale_b, w_query, acc_query, sum(groups, [])
     )
     pair, first, done = pair_maps(meta, own_maps, other_maps, query_done)
+    fetched, _ = lax.optimization_barrier((fetched, done))
+    swapped = [pair_swap(value, seqs) for value in fetched]
     pairs = [later(pair, seqs, d) for d in range(seqs // 2 - 1, 0, -1)]
     shard_query, free, out_done = block_outputs(query, keys, erased, entry, totals, done)
     kept_state, given_state = start_states(meta, first, pairs, out_done)
     other_state = pair_swap(given_state, seqs)
 
+    other_state, swapped, diagonal = lax.optimization_barrier((other_state, swapped, diagonal))
     mixed = mixed_heads(meta, kept_state, other_state, shard_query, free, head_scale)
-    sums = []
-    for own_mixed in mixed:
-        summed = attend(meta, own_mixed, core_swap(own_mixed, n), w_out_t, other_w_out)
-        sums.append([summed] + [y_shift(summed, n, d) for d in range(1, ys)])
-    ups = []
-    for own, own_tokens in zip(sums, (tokens_a, tokens_b)):
-        ahead = ups[0][2] if ups else sums[1][0]
-        own = own[:1] + list(lax.optimization_barrier((tuple(own[1:]), ahead))[0])
-        other = [core_swap(value, n) for value in own]
-        ups.append(up_project(meta, own_tokens, own, other, ffn_scale, w_up, part))
-    (outer, middle_a, first_row, last_row), (inside, middle_b, _, _) = ups
+    far_mixed = [[y_shift(value, n, d) for d in range(1, ys)] for value in mixed]
+
+    def middle_of(i, far):
+        heads_far = [[value, core_swap(value, n)] for value in far]
+        operands = []
+        for pair_of, *weights in zip(heads_far, fetched, swapped, diagonal):
+            operands += pair_of + weights
+        own_tokens = (tokens_a, tokens_b)[i]
+        return attend(
+            meta, ys, own_tokens, mixed[i], core_swap(mixed[i], n), w_out_t, partner_w_out, operands
+        )
+
+    middle = middle_of(0, far_mixed[0])
+    outer, middle_a, first_row, last_row = up_project(
+        meta, middle, core_swap(middle, n), ffn_scale, w_up, part
+    )
     before = lax.ppermute(last_row, "seq", [(i, i + 1) for i in range(seqs - 1)])
     after = lax.ppermute(first_row, "seq", [(i + 1, i) for i in range(seqs - 1)])
+    middle = middle_of(1, far_mixed[1])
+    inside, middle_b, _, _ = up_project(
+        meta, middle, core_swap(middle, n), ffn_scale, w_up, part
+    )
 
     acts = [activate(meta, outer, inside, before, after, taps, late) for late in (False, True)]
     partner_acts = [core_swap(act, n) for act in acts]

time: 128 us -> 119 us (0.930)
  waiting for transfers between devices: 49.9 us -> 36.9 us
  starting transfers between devices: 24.1 us -> 26.4 us
    ppermute x5 -> x6, waiting for transfers between devices: 32.3 us -> 23.9 us  [y_shift(): lax.ppermute(value, 'head', [(i, (i + 2 * step) % n) for i in range(n)])]
    ppermute x0 -> x1, waiting for transfers between devices: none -> 3.62 us  [shards(): lax.ppermute(their_rows, 'head', [(i, (i + 2 * d) % n ^ 1) for i in range...]
    ppermute x3, waiting for transfers between devices: 7.81 us -> 4.22 us  [later(): lax.ppermute(value, 'seq', [(i, i + 2 * step) for i in range(n - 2 * step)])]
    ppermute x12, waiting for transfers between devices: 4.8 us -> 2.01 us  [core_swap(): return lax.ppermute(value, 'head', [(i, i ^ 1) for i in range(n)])]
    ppermute x2 -> x3, waiting for transfers between devices: 4.97 us -> 3.09 us  [pair_swap(): return lax.ppermute(value, 'seq', [(i, i ^ 1) for i in range(n)])]
    ppermute x1, starting transfers between devices: 2.33 us -> 3.76 us  [shards(): lax.ppermute(first_row, 'seq', [(i + 1, i) for i in range(seqs - 1)])]
    ppermute x5 -> x6, starting transfers between devices: 6.79 us -> 7.37 us  [y_shift(): lax.ppermute(value, 'head', [(i, (i + 2 * step) % n) for i in range(n)])]
    ppermute x2 -> x3, starting transfers between devices: 3.08 us -> 3.65 us  [pair_swap(): return lax.ppermute(value, 'seq', [(i, i ^ 1) for i in range(n)])]
  transfers between devices with their start and end apart: 24 -> 27, of which waited for: 13 -> 11; matrix products, arithmetic and copies ran while one was open for 3% -> 4% of each run, Pallas kernels for 32% -> 39%
where the time goes in v6:
time: 119 us; the launch traced here: 118 us
  Pallas kernels  48.8 us (41%)
  waiting for transfers between devices  36.9 us (31%)
  starting transfers between devices  26.4 us (22%)
  local copies, waits for them, and re-layouts  2.78 us (2%)
  other arithmetic  2.48 us (2%)
    ppermute x6, waiting for transfers between devices, y_shift(): lax.ppermute(value, 'head', [(i, (i + 2 * step) % n) for i in range(n)])  23.9 us
    pallas_call x1, Pallas kernels, block_maps(): pl.pallas_call(functools.partial(maps_kernel, n, heads, at), out_shape=(s...  12.3 us
    pallas_call x2, Pallas kernels, up_project(): pl.pallas_call(up_kernel, out_shape=(shape_of((count, hidden)), shape_of(...  7.42 us
    ppermute x6, starting transfers between devices, y_shift(): lax.ppermute(value, 'head', [(i, (i + 2 * step) % n) for i in range(n)])  7.37 us
    pallas_call x1, Pallas kernels, early_project(): pl.pallas_call(functools.partial(early_kernel, len(pieces), at), out_shap...  7.15 us
    ppermute x3, starting transfers between devices, later(): lax.ppermute(value, 'seq', [(i, i + 2 * step) for i in range(n - 2 * step)])  5.61 us
    pallas_call x2, Pallas kernels, activate(): pl.pallas_call(functools.partial(act_kernel, late), out_shape=shape_of((h...  4.62 us
    ppermute x3, waiting for transfers between devices, later(): lax.ppermute(value, 'seq', [(i, i + 2 * step) for i in range(n - 2 * step)])  4.22 us
  transfers between devices with their start and end apart: 27, of which 11 were waited for; matrix products, arithmetic and copies ran while one was open for 4% of the time, Pallas kernels for 39%

profile of v6, /device:TPU:16, one launch (start us, length us, event | category | flops | bytes accessed | tf_op | source)
XLA Modules:
  0.0 117.7 jit_solution(16733304030795668012)
XLA Ops:
  0.0 1.6 %collective-permute-start = (bf16[560,512]{1,0:T(8,128)(2,1)}, bf16[560,512]{1,0:T(8,128)(2,1)S(1)}, u32[]{:S(2)}, u32[]{:S(2)}) collective-permute-start(bf16[560,512]{1,0:T(8,128)(2,1)} %bitcast.37), channel_id=1, source_target_pairs={{0,2},{1,3},{2,0},{3,1},{4,6},{5,7},{6,4},{7,5},{8,10},{9,11},{10,... | collective-permute-start | bytes 1720328 | tf_op jit(solution)/shard_map/ppermute | solution.py:731
  1.6 0.8 reshape.31
  2.3 0.8 reshape.37
  3.1 0.7 reshape.39.gain
  3.8 0.7 convert_element_type.15.taps
  4.5 0.8 fusion.3
  5.9 7.2 %early_project.1 = (f32[512,512]{1,0:T(8,128)S(1)}, f32[512,512]{1,0:T(8,128)S(1)}, f32[512,512]{1,0:T(8,128)S(1)}, f32[16,512]{1,0:T(8,128)S(1)}, f32[8,512]{1,...) custom-call(s32[6]{0:T(128)S(1)} %stack.24.meta, ...), custom_call_target="tpu_custom_call" | custom-call | flops 3000000000 | bytes 8000000 | tf_op jit(solution)/shard_map/early_project/pallas_call | solution.py:163
  13.0 2.6 %collective-permute-done.refs_0_.refs_2_ = bf16[560,512]{1,0:T(8,128)(2,1)S(1)} collective-permute-done((bf16[560,512]{1,0:T(8,128)(2,1)}, bf16[560,512]{1,0:T(8,128)(2,1)S(1)}, u32[]{:S(2)}, u32[]{:S(2)}) %collective-permute-start) | collective-permute-done | bytes 573472 | tf_op jit(solution)/shard_map/ppermute | solution.py:731
  15.6 2.0 %collective-permute-done.2.refs_1_.refs_3_ = bf16[560,512]{1,0:T(8,128)(2,1)S(1)} collective-permute-done((bf16[560,512]{1,0:T(8,128)(2,1)S(1)}, bf16[560,512]{1,0:T(8,128)(2,1)S(1)}, u32[]{:S(2)}, u32[]{:S(2)}) %collective-permute-start.2) | collective-permute-done | bytes 573472 | tf_op jit(solution)/shard_map/ppermute | solution.py:727
  17.7 1.5 %collective-permute-start.10 = (bf16[560,512]{1,0:T(8,128)(2,1)S(1)}, bf16[560,512]{1,0:T(8,128)(2,1)S(1)}, u32[]{:S(2)}, u32[]{:S(2)}) collective-permute-start(bf16[560,512]{1,0:T(8,128)(2,1)S(1)} %get-tuple-element.98), channel_id=1, source_target_pairs={{0,2},{1,3},{2,0},{3,1},{4,6},{5,7},{6,4},{7,5},{8,10},{9,11},{10,... | collective-permute-start | bytes 1720328 | tf_op jit(solution)/shard_map/ppermute | solution.py:731
  19.3 12.3 %block_maps.1 = (bf16[512,1120]{1,0:T(8,128)(2,1)S(1)}, f32[512,128]{1,0:T(8,128)S(1)}, bf16[512,512]{1,0:T(8,128)(2,1)S(1)}, bf16[512,1024]{1,0:T(8,128)(2,1)S(...) custom-call(s32[6]{0:T(128)S(1)} %stack.24.meta, ...), custom_call_target="tpu_custom_call" | custom-call | flops 10000000000 | bytes 14000000 | tf_op jit(solution)/shard_map/block_maps/pallas_call | solution.py:333
  31.7 1.3 %collective-permute-done.10.refs_2_ = bf16[560,512]{1,0:T(8,128)(2,1)S(1)} collective-permute-done((bf16[560,512]{1,0:T(8,128)(2,1)S(1)}, bf16[560,512]{1,0:T(8,128)(2,1)S(1)}, u32[]{:S(2)}, u32[]{:S(2)}) %collective-permute-start.10) | collective-permute-done | bytes 573472 | tf_op jit(solution)/shard_map/ppermute | solution.py:731
  33.0 0.7 collective-permute-start.12
  33.7 1.5 %collective-permute-start.5 = (bf16[2,128,256]{2,1,0:T(8,128)(2,1)S(1)}, bf16[2,128,256]{2,1,0:T(8,128)(2,1)S(1)}, u32[]{:S(2)}, u32[]{:S(2)}) collective-permute-start(bf16[2,128,256]{2,1,0:T(8,128)(2,1)S(1)} %get-tuple-element.85), channel_id=1, source_target_pairs={{0,4},{4,0},{8,12},{12,8},{16,20},{20,16},{24,28},{28,24},{1,5},{5... | collective-permute-start | bytes 393224 | tf_op jit(solution)/shard_map/ppermute | solution.py:735
  35.2 1.9 %queries.1 = (bf16[512,512]{1,0:T(8,128)(2,1)S(1)}, bf16[2240,256]{1,0:T(8,128)(2,1)S(1)}, bf16[2240,256]{1,0:T(8,128)(2,1)S(1)}, f32[8,128]{1,0:T(8,128)S(1)}) custom-call(s32[6]{0:T(128)S(1)} %stack.24.meta, bf16[512,1120]{1,0:T(8,128)(2,1)S(1)} %get-tuple-element.74.scaled, f32[512,128]{1,0:T(8,128)S(1)} %get-tuple-element.75.scale_b, ...), custom_call_target="tpu_custom_call" | custom-call | flops 1000000000 | bytes 8000000 | tf_op jit(solution)/shard_map/queries/pallas_call | solution.py:397
  37.0 3.0 %collective-permute-done.5.other = bf16[2,128,256]{2,1,0:T(8,128)(2,1)S(1)} collective-permute-done((bf16[2,128,256]{2,1,0:T(8,128)(2,1)S(1)}, bf16[2,128,256]{2,1,0:T(8,128)(2,1)S(1)}, u32[]{:S(2)}, u32[]{:S(2)}) %collective-permute-start.5) | collective-permute-done | bytes 131104 | tf_op jit(solution)/shard_map/ppermute | solution.py:735
  40.0 0.7 pair_maps.1
  40.8 1.6 %collective-permute-start.11 = (bf16[560,512]{1,0:T(8,128)(2,1)S(1)}, bf16[560,512]{1,0:T(8,128)(2,1)S(1)}, u32[]{:S(2)}, u32[]{:S(2)}) collective-permute-start(bf16[560,512]{1,0:T(8,128)(2,1)S(1)} %collective-permute-done.10.refs_2_), channel_id=1, source_target_pairs={{0,4},{4,0},{8,12},{12,8},{16,20},{20,16},{24,28},{28,24},{1,5},{5... | collective-permute-start | bytes 1720328 | tf_op jit(solution)/shard_map/ppermute | solution.py:735
  42.3 3.5 %collective-permute-start.8 = (bf16[2,128,256]{2,1,0:T(8,128)(2,1)S(1)}, bf16[2,128,256]{2,1,0:T(8,128)(2,1)S(1)}, u32[]{:S(2)}, u32[]{:S(2)}) collective-permute-start(bf16[2,128,256]{2,1,0:T(8,128)(2,1)S(1)} %get-tuple-element.88), channel_id=1, source_target_pairs={{0,8},{4,12},{8,16},{12,20},{16,24},{20,28},{1,9},{5,13},{9,17},{1... | collective-permute-start | bytes 393224 | tf_op jit(solution)/shard_map/ppermute | solution.py:739
  45.8 1.3 %collective-permute-start.7 = (bf16[2,128,256]{2,1,0:T(8,128)(2,1)S(1)}, bf16[2,128,256]{2,1,0:T(8,128)(2,1)S(1)}, u32[]{:S(2)}, u32[]{:S(2)}) collective-permute-start(bf16[2,128,256]{2,1,0:T(8,128)(2,1)S(1)} %get-tuple-element.88), channel_id=1, source_target_pairs={{0,16},{4,20},{8,24},{12,28},{1,17},{5,21},{9,25},{13,29},{2,18},{... | collective-permute-start | bytes 393224 | tf_op jit(solution)/shard_map/ppermute | solution.py:739
  47.1 0.8 collective-permute-start.6
  48.0 2.8 %block_outputs.1 = (bf16[512,512]{1,0:T(8,128)(2,1)S(1)}, f32[512,512]{1,0:T(8,128)S(1)}, f32[8,128]{1,0:T(8,128)S(1)}) custom-call(bf16[512,512]{1,0:T(8,128)(2,1)S(1)} %get-tuple-element.89.query, bf16[512,512]{1,0:T(8,128)(2,1)S(1)} %get-tuple-element.90.keys, bf16[512,1024]{1,0:T(8,128)(2,1)S(1)} %get-tuple-element.91.erased, ...), custom_call_target="tpu_custom_call" | custom-call | flops 3000000000 | bytes 4000000 | tf_op jit(solution)/shard_map/block_outputs/pallas_call | solution.py:448
  50.8 4.2 %collective-permute-done.7.refs_1_ = bf16[2,128,256]{2,1,0:T(8,128)(2,1)S(1)} collective-permute-done((bf16[2,128,256]{2,1,0:T(8,128)(2,1)S(1)}, bf16[2,128,256]{2,1,0:T(8,128)(2,1)S(1)}, u32[]{:S(2)}, u32[]{:S(2)}) %collective-permute-start.7) | collective-permute-done | bytes 131104 | tf_op jit(solution)/shard_map/ppermute | solution.py:739
  55.0 1.2 %start_states.1 = (bf16[2,128,128]{2,1,0:T(8,128)(2,1)S(1)}, bf16[2,128,128]{2,1,0:T(8,128)(2,1)S(1)}) custom-call(s32[6]{0:T(128)S(1)} %stack.24.meta, bf16[2,128,256]{2,1,0:T(8,128)(2,1)S(1)} %get-tuple-element.87.first, bf16[2,128,256]{2,1,0:T(8,128)(2,1)S(1)} %collective-permute-done.6.refs_0_, bf16[2,128,256]{2,1,0:T(8,128)(2,1)S(1)} %collective-permute-done.7.refs_1_, ...), custom_call_target="tpu_custom_call" | custom-call | tf_op jit(solution)/shard_map/start_states/pallas_call | solution.py:506
  56.2 0.6 collective-permute-start.9
  56.8 3.6 %collective-permute-done.12.refs_4_ = bf16[1120,512]{1,0:T(8,128)(2,1)S(1)} collective-permute-done((bf16[1120,512]{1,0:T(8,128)(2,1)S(1)}, bf16[1120,512]{1,0:T(8,128)(2,1)S(1)}, u32[]{:S(2)}, u32[]{:S(2)}) %collective-permute-start.12) | collective-permute-done | bytes 1146912 | tf_op jit(solution)/shard_map/ppermute | solution.py:833
  60.6 1.1 mixed_heads.1
  61.7 1.3 %collective-permute-start.14 = (bf16[256,512]{1,0:T(8,128)(2,1)S(1)}, bf16[256,512]{1,0:T(8,128)(2,1)S(1)}, u32[]{:S(2)}, u32[]{:S(2)}) collective-permute-start(bf16[256,512]{1,0:T(8,128)(2,1)S(1)} %get-tuple-element.106.own), channel_id=1, source_target_pairs={{0,2},{1,3},{2,0},{3,1},{4,6},{5,7},{6,4},{7,5},{8,10},{9,11},{10,... | collective-permute-start | bytes 786440 | tf_op jit(solution)/shard_map/ppermute | solution.py:731
  63.0 0.8 collective-permute-start.18
  63.8 7.1 %collective-permute-done.14.refs_0_ = bf16[256,512]{1,0:T(8,128)(2,1)S(1)} collective-permute-done((bf16[256,512]{1,0:T(8,128)(2,1)S(1)}, bf16[256,512]{1,0:T(8,128)(2,1)S(1)}, u32[]{:S(2)}, u32[]{:S(2)}) %collective-permute-start.14) | collective-permute-done | bytes 262176 | tf_op jit(solution)/shard_map/ppermute | solution.py:731
  71.4 4.3 %collective-permute-done.18.refs_0_ = bf16[256,512]{1,0:T(8,128)(2,1)S(1)} collective-permute-done((bf16[256,512]{1,0:T(8,128)(2,1)S(1)}, bf16[256,512]{1,0:T(8,128)(2,1)S(1)}, u32[]{:S(2)}, u32[]{:S(2)}) %collective-permute-start.18) | collective-permute-done | bytes 262176 | tf_op jit(solution)/shard_map/ppermute | solution.py:731
  75.7 1.9 %attend.2.own = bf16[1120,256]{1,0:T(8,128)(2,1)S(1)} custom-call(s32[6]{0:T(128)S(1)} %stack.24.meta, bf16[2240,256]{1,0:T(8,128)(2,1)S(1)} %get-tuple-element.83.tokens, bf16[256,512]{1,0:T(8,128)(2,1)S(1)} %get-tuple-element.106.own, bf16[256,512]{1,0:T(8,128)(2,1)S(1)} %collective-permute-done.13.partner, bf16[2240,512]{1,0:T(8,128)(2,1)S(1)} %bitcast.34, ...), custom_call_target="tpu_custom_call" | custom-call | flops 2000000000 | bytes 7000000 | tf_op jit(solution)/shard_map/attend/pallas_call | solution.py:572
  78.2 1.9 %attend.3.own = bf16[1120,256]{1,0:T(8,128)(2,1)S(1)} custom-call(s32[6]{0:T(128)S(1)} %stack.24.meta, bf16[2240,256]{1,0:T(8,128)(2,1)S(1)} %get-tuple-element.112.tokens, bf16[256,512]{1,0:T(8,128)(2,1)S(1)} %get-tuple-element.113.own, bf16[256,512]{1,0:T(8,128)(2,1)S(1)} %collective-permute-done.17.partner, bf16[2240,512]{1,0:T(8,128)(2,1)S(1)} %bitcast.35, ...), custom_call_target="tpu_custom_call" | custom-call | flops 2000000000 | bytes 7000000 | tf_op jit(solution)/shard_map/attend/pallas_call | solution.py:572
  80.3 3.4 %up_project.2 = (bf16[256,1400]{1,0:T(8,128)(2,1)S(1)}, f32[560,256]{1,0:T(8,128)S(1)}, bf16[1,1400]{1,0:T(2,128)(2,1)S(1)}, bf16[1,1400]{1,0:T(2,128)(2,1)S(1)}) custom-call(s32[6]{0:T(128)S(1)} %stack.24.meta, bf16[1120,256]{1,0:T(8,128)(2,1)S(1)} %attend.2.own, bf16[1120,256]{1,0:T(8,128)(2,1)S(1)} %collective-permute-done.16.other, ...), custom_call_target="tpu_custom_call" | custom-call | flops 2000000000 | bytes 8000000 | tf_op jit(solution)/shard_map/up_project/pallas_call | solution.py:612
  83.7 3.3 %collective-permute-start.21 = (bf16[1,1400]{1,0:T(2,128)(2,1)S(1)}, bf16[1,1400]{1,0:T(2,128)(2,1)S(1)}, u32[]{:S(2)}, u32[]{:S(2)}) collective-permute-start(bf16[1,1400]{1,0:T(2,128)(2,1)S(1)} %get-tuple-element.115), channel_id=1, source_target_pairs={{0,4},{4,8},{8,12},{12,16},{16,20},{20,24},{24,28},{1,5},{5,9},{9,... | collective-permute-start | bytes 8408 | tf_op jit(solution)/shard_map/ppermute | solution.py:867
  87.1 3.8 %collective-permute-start.22 = (bf16[1,1400]{1,0:T(2,128)(2,1)S(1)}, bf16[1,1400]{1,0:T(2,128)(2,1)S(1)}, u32[]{:S(2)}, u32[]{:S(2)}) collective-permute-start(bf16[1,1400]{1,0:T(2,128)(2,1)S(1)} %get-tuple-element.116), channel_id=1, source_target_pairs={{4,0},{8,4},{12,8},{16,12},{20,16},{24,20},{28,24},{5,1},{9,5},{13... | collective-permute-start | bytes 8408 | tf_op jit(solution)/shard_map/ppermute | solution.py:868
  90.8 4.0 %up_project.3 = (bf16[256,1400]{1,0:T(8,128)(2,1)S(1)}, f32[560,256]{1,0:T(8,128)S(1)}, bf16[1,1400]{1,0:T(2,128)(2,1)}, bf16[1,1400]{1,0:T(2,128)(2,1)}) custom-call(s32[6]{0:T(128)S(1)} %stack.24.meta, bf16[1120,256]{1,0:T(8,128)(2,1)S(1)} %attend.3.own, bf16[1120,256]{1,0:T(8,128)(2,1)S(1)} %collective-permute-done.20.other, f32[1,2240]{1,0:T(1,128)S(1)} %reshape.39.gain, ...), custom_call_target="tpu_custom_call" | custom-call | flops 2000000000 | bytes 8000000 | tf_op jit(solution)/shard_map/up_project/pallas_call | solution.py:612
  94.9 2.3 %activate.2.own_a.own = bf16[1400,256]{1,0:T(8,128)(2,1)S(1)} custom-call(s32[6]{0:T(128)S(1)} %stack.24.meta, bf16[256,1400]{1,0:T(8,128)(2,1)S(1)} %get-tuple-element.111.outer, bf16[256,1400]{1,0:T(8,128)(2,1)S(1)} %get-tuple-element.114.inside, bf16[1,1400]{1,0:T(2,128)(2,1)S(1)} %collective-permute-done.21.before, ...), custom_call_target="tpu_custom_call" | custom-call | flops 1000000000 | bytes 2000000 | tf_op jit(solution)/shard_map/activate/pallas_call | solution.py:668
  97.3 2.3 %activate.3.own.own_b = bf16[1400,256]{1,0:T(8,128)(2,1)S(1)} custom-call(s32[6]{0:T(128)S(1)} %stack.24.meta, bf16[256,1400]{1,0:T(8,128)(2,1)S(1)} %get-tuple-element.111.outer, bf16[256,1400]{1,0:T(8,128)(2,1)S(1)} %get-tuple-element.114.inside, bf16[1,1400]{1,0:T(2,128)(2,1)S(1)} %collective-permute-done.21.before, ...), custom_call_target="tpu_custom_call" | custom-call | flops 1000000000 | bytes 2000000 | tf_op jit(solution)/shard_map/activate/pallas_call | solution.py:668
  99.6 0.6 collective-permute-start.24
  100.2 1.6 %far_project.3 = bf16[560,256]{1,0:T(8,128)(2,1)S(1)} custom-call(s32[6]{0:T(128)S(1)} %stack.24.meta, bf16[1400,256]{1,0:T(8,128)(2,1)S(1)} %activate.2.own_a.own, bf16[1400,256]{1,0:T(8,128)(2,1)S(1)} %collective-permute-done.23.other_a.other, bf16[4,560,1400]{2,1,0:T(8,128)(2,1)S(1)} %bitcast.28, ...), custom_call_target="tpu_custom_call" | custom-call | flops 1000000000 | bytes 4000000 | tf_op jit(solution)/shard_map/far_project/pallas_call | solution.py:690
  101.8 1.0 collective-permute-start.25
  102.8 1.6 %far_project.2.after = bf16[560,256]{1,0:T(8,128)(2,1)S(1)} custom-call(s32[6]{0:T(128)S(1)} %stack.24.meta, bf16[1400,256]{1,0:T(8,128)(2,1)S(1)} %activate.3.own.own_b, bf16[1400,256]{1,0:T(8,128)(2,1)S(1)} %collective-permute-done.24.other.other_b, bf16[4,560,1400]{2,1,0:T(8,128)(2,1)S(1)} %bitcast.29, ...), custom_call_target="tpu_custom_call" | custom-call | flops 1000000000 | bytes 4000000 | tf_op jit(solution)/shard_map/far_project/pallas_call | solution.py:690
  104.4 1.1 collective-permute-start.26
  105.5 2.5 %near_project.1 = f32[560,512]{1,0:T(8,128)S(1)} custom-call(s32[6]{0:T(128)S(1)} %stack.24.meta, bf16[1400,256]{1,0:T(8,128)(2,1)S(1)} %activate.2.own_a.own, bf16[1400,256]{1,0:T(8,128)(2,1)S(1)} %collective-permute-done.23.other_a.other, bf16[1400,256]{1,0:T(8,128)(2,1)S(1)} %activate.3.own.own_b, ...), custom_call_target="tpu_custom_call" | custom-call | flops 2000000000 | bytes 6000000 | tf_op jit(solution)/shard_map/near_project/pallas_call | solution.py:715
  108.1 3.5 %collective-permute-done.25 = bf16[560,256]{1,0:T(8,128)(2,1)S(1)} collective-permute-done((bf16[560,256]{1,0:T(8,128)(2,1)S(1)}, bf16[560,256]{1,0:T(8,128)(2,1)S(1)}, u32[]{:S(2)}, u32[]{:S(2)}) %collective-permute-start.25) | collective-permute-done | bytes 286752 | tf_op jit(solution)/shard_map/ppermute | solution.py:731
  111.5 5.2 %collective-permute-done.26 = bf16[560,256]{1,0:T(8,128)(2,1)S(1)} collective-permute-done((bf16[560,256]{1,0:T(8,128)(2,1)S(1)}, bf16[560,256]{1,0:T(8,128)(2,1)S(1)}, u32[]{:S(2)}, u32[]{:S(2)}) %collective-permute-start.26) | collective-permute-done | bytes 286752 | tf_op jit(solution)/shard_map/ppermute | solution.py:731
  116.7 1.0 fusion
  (57 shorter events, 2.1 us)
Async XLA Ops:
  0.0 5.8 %copy-start.4 = (bf16[512,560]{0,1:T(8,128)(2,1)S(1)}, bf16[512,560]{0,1:T(8,128)(2,1)}, u32[]{:S(2)}) copy-start(bf16[512,560]{0,1:T(8,128)(2,1)} %param.14) | copy-start | bytes 1720324
  0.0 5.8 %collective-permute-start.1 = (bf16[560,512]{1,0:T(8,128)(2,1)}, bf16[560,512]{1,0:T(8,128)(2,1)S(1)}, u32[]{:S(2)}, u32[]{:S(2)}) collective-permute-start(bf16[560,512]{1,0:T(8,128)(2,1)} %bitcast.36), channel_id=1, source_target_pairs={{0,1},{1,0},{2,3},{3,2},{4,5},{5,4},{6,7},{7,6},{8,9},{9,8},{10,11... | collective-permute-start | bytes 1720328 | tf_op jit(solution)/shard_map/ppermute | solution.py:727
  0.0 15.6 %collective-permute-start = (bf16[560,512]{1,0:T(8,128)(2,1)}, bf16[560,512]{1,0:T(8,128)(2,1)S(1)}, u32[]{:S(2)}, u32[]{:S(2)}) collective-permute-start(bf16[560,512]{1,0:T(8,128)(2,1)} %bitcast.37), channel_id=1, source_target_pairs={{0,2},{1,3},{2,0},{3,1},{4,6},{5,7},{6,4},{7,5},{8,10},{9,11},{10,... | collective-permute-start | bytes 1720328 | tf_op jit(solution)/shard_map/ppermute | solution.py:731
  5.8 13.5 %copy-start.2 = (bf16[2240,512]{1,0:T(8,128)(2,1)S(1)}, bf16[2240,512]{1,0:T(8,128)(2,1)}, u32[]{:S(2)}) copy-start(bf16[2240,512]{1,0:T(8,128)(2,1)} %refs_5_.3) | copy-start | bytes 6881284
  5.8 13.5 %copy-start.3 = (bf16[2240,512]{1,0:T(8,128)(2,1)S(1)}, bf16[2240,512]{1,0:T(8,128)(2,1)}, u32[]{:S(2)}) copy-start(bf16[2240,512]{1,0:T(8,128)(2,1)} %refs_6_.3) | copy-start | bytes 6881284
  15.6 2.0 %collective-permute-start.2 = (bf16[560,512]{1,0:T(8,128)(2,1)S(1)}, bf16[560,512]{1,0:T(8,128)(2,1)S(1)}, u32[]{:S(2)}, u32[]{:S(2)}) collective-permute-start(bf16[560,512]{1,0:T(8,128)(2,1)S(1)} %collective-permute-done.refs_0_.refs_2_), channel_id=1, source_target_pairs={{0,1},{1,0},{2,3},{3,2},{4,5},{5,4},{6,7},{7,6},{8,9},{9,8},{10,11... | collective-permute-start | bytes 1720328 | tf_op jit(solution)/shard_map/ppermute | solution.py:727
  17.6 17.6 %collective-permute-start.4 = (bf16[2,560,1400]{2,1,0:T(8,128)(2,1)}, bf16[2,560,1400]{2,1,0:T(8,128)(2,1)S(1)}, u32[]{:S(2)}, u32[]{:S(2)}) collective-permute-start(bf16[2,560,1400]{2,1,0:T(8,128)(2,1)} %get-tuple-element.81), channel_id=1, source_target_pairs={{0,1},{1,0},{2,3},{3,2},{4,5},{5,4},{6,7},{7,6},{8,9},{9,8},{10,11... | collective-permute-start | bytes 9408008 | tf_op jit(solution)/shard_map/ppermute | solution.py:727
  17.7 15.3 %collective-permute-start.10 = (bf16[560,512]{1,0:T(8,128)(2,1)S(1)}, bf16[560,512]{1,0:T(8,128)(2,1)S(1)}, u32[]{:S(2)}, u32[]{:S(2)}) collective-permute-start(bf16[560,512]{1,0:T(8,128)(2,1)S(1)} %get-tuple-element.98), channel_id=1, source_target_pairs={{0,2},{1,3},{2,0},{3,1},{4,6},{5,7},{6,4},{7,5},{8,10},{9,11},{10,... | collective-permute-start | bytes 1720328 | tf_op jit(solution)/shard_map/ppermute | solution.py:731
  19.3 15.9 %collective-permute-start.3 = (bf16[1120,512]{1,0:T(8,128)(2,1)S(1)}, bf16[1120,512]{1,0:T(8,128)(2,1)S(1)}, u32[]{:S(2)}, u32[]{:S(2)}) collective-permute-start(bf16[1120,512]{1,0:T(8,128)(2,1)S(1)} %get-tuple-element.101), channel_id=1, source_target_pairs={{0,1},{1,0},{2,3},{3,2},{4,5},{5,4},{6,7},{7,6},{8,9},{9,8},{10,11... | collective-permute-start | bytes 3440648 | tf_op jit(solution)/shard_map/ppermute | solution.py:727
  19.3 15.8 %copy-start.1 = (bf16[2240,512]{1,0:T(8,128)(2,1)S(1)}, bf16[2240,512]{1,0:T(8,128)(2,1)}, u32[]{:S(2)}) copy-start(bf16[2240,512]{1,0:T(8,128)(2,1)} %weights.3) | copy-start | bytes 6881284
  33.0 27.5 %collective-permute-start.12 = (bf16[1120,512]{1,0:T(8,128)(2,1)S(1)}, bf16[1120,512]{1,0:T(8,128)(2,1)S(1)}, u32[]{:S(2)}, u32[]{:S(2)}) collective-permute-start(bf16[1120,512]{1,0:T(8,128)(2,1)S(1)} %get-tuple-element.101), channel_id=1, source_target_pairs={{0,3},{1,2},{2,1},{3,0},{4,7},{5,6},{6,5},{7,4},{8,11},{9,10},{10,... | collective-permute-start | bytes 3440648 | tf_op jit(solution)/shard_map/ppermute | solution.py:833
  33.7 6.4 %collective-permute-start.5 = (bf16[2,128,256]{2,1,0:T(8,128)(2,1)S(1)}, bf16[2,128,256]{2,1,0:T(8,128)(2,1)S(1)}, u32[]{:S(2)}, u32[]{:S(2)}) collective-permute-start(bf16[2,128,256]{2,1,0:T(8,128)(2,1)S(1)} %get-tuple-element.85), channel_id=1, source_target_pairs={{0,4},{4,0},{8,12},{12,8},{16,20},{20,16},{24,28},{28,24},{1,5},{5... | collective-permute-start | bytes 393224 | tf_op jit(solution)/shard_map/ppermute | solution.py:735
  40.8 19.8 %collective-permute-start.11 = (bf16[560,512]{1,0:T(8,128)(2,1)S(1)}, bf16[560,512]{1,0:T(8,128)(2,1)S(1)}, u32[]{:S(2)}, u32[]{:S(2)}) collective-permute-start(bf16[560,512]{1,0:T(8,128)(2,1)S(1)} %collective-permute-done.10.refs_2_), channel_id=1, source_target_pairs={{0,4},{4,0},{8,12},{12,8},{16,20},{20,16},{24,28},{28,24},{1,5},{5... | collective-permute-start | bytes 1720328 | tf_op jit(solution)/shard_map/ppermute | solution.py:735
  42.3 8.5 %collective-permute-start.8 = (bf16[2,128,256]{2,1,0:T(8,128)(2,1)S(1)}, bf16[2,128,256]{2,1,0:T(8,128)(2,1)S(1)}, u32[]{:S(2)}, u32[]{:S(2)}) collective-permute-start(bf16[2,128,256]{2,1,0:T(8,128)(2,1)S(1)} %get-tuple-element.88), channel_id=1, source_target_pairs={{0,8},{4,12},{8,16},{12,20},{16,24},{20,28},{1,9},{5,13},{9,17},{1... | collective-permute-start | bytes 393224 | tf_op jit(solution)/shard_map/ppermute | solution.py:739
  45.8 9.2 %collective-permute-start.7 = (bf16[2,128,256]{2,1,0:T(8,128)(2,1)S(1)}, bf16[2,128,256]{2,1,0:T(8,128)(2,1)S(1)}, u32[]{:S(2)}, u32[]{:S(2)}) collective-permute-start(bf16[2,128,256]{2,1,0:T(8,128)(2,1)S(1)} %get-tuple-element.88), channel_id=1, source_target_pairs={{0,16},{4,20},{8,24},{12,28},{1,17},{5,21},{9,25},{13,29},{2,18},{... | collective-permute-start | bytes 393224 | tf_op jit(solution)/shard_map/ppermute | solution.py:739
  47.1 7.9 %collective-permute-start.6 = (bf16[2,128,256]{2,1,0:T(8,128)(2,1)S(1)}, bf16[2,128,256]{2,1,0:T(8,128)(2,1)S(1)}, u32[]{:S(2)}, u32[]{:S(2)}) collective-permute-start(bf16[2,128,256]{2,1,0:T(8,128)(2,1)S(1)} %get-tuple-element.88), channel_id=1, source_target_pairs={{0,24},{4,28},{1,25},{5,29},{2,26},{6,30},{3,27},{7,31}} | collective-permute-start | bytes 393224 | tf_op jit(solution)/shard_map/ppermute | solution.py:739
  47.9 12.6 %copy-start.5 = (bf16[128]{0:T(256)(128)(2,1)S(1)}, bf16[128]{0:T(256)(128)(2,1)}, u32[]{:S(2)}) copy-start(bf16[128]{0:T(256)(128)(2,1)} %param.22) | copy-start | bytes 772
  56.2 4.3 %collective-permute-start.9 = (bf16[2,128,128]{2,1,0:T(8,128)(2,1)S(1)}, bf16[2,128,128]{2,1,0:T(8,128)(2,1)S(1)}, u32[]{:S(2)}, u32[]{:S(2)}) collective-permute-start(bf16[2,128,128]{2,1,0:T(8,128)(2,1)S(1)} %get-tuple-element.97), channel_id=1, source_target_pairs={{0,4},{4,0},{8,12},{12,8},{16,20},{20,16},{24,28},{28,24},{1,5},{5... | collective-permute-start | bytes 196616 | tf_op jit(solution)/shard_map/ppermute | solution.py:735
  60.6 15.1 %copy-start = (bf16[512,2240]{0,1:T(8,128)(2,1)S(1)}, bf16[512,2240]{0,1:T(8,128)(2,1)}, u32[]{:S(2)}) copy-start(bf16[512,2240]{0,1:T(8,128)(2,1)} %param.23) | copy-start | bytes 6881284
  61.7 9.2 %collective-permute-start.14 = (bf16[256,512]{1,0:T(8,128)(2,1)S(1)}, bf16[256,512]{1,0:T(8,128)(2,1)S(1)}, u32[]{:S(2)}, u32[]{:S(2)}) collective-permute-start(bf16[256,512]{1,0:T(8,128)(2,1)S(1)} %get-tuple-element.106.own), channel_id=1, source_target_pairs={{0,2},{1,3},{2,0},{3,1},{4,6},{5,7},{6,4},{7,5},{8,10},{9,11},{10,... | collective-permute-start | bytes 786440 | tf_op jit(solution)/shard_map/ppermute | solution.py:731
  63.0 12.7 %collective-permute-start.18 = (bf16[256,512]{1,0:T(8,128)(2,1)S(1)}, bf16[256,512]{1,0:T(8,128)(2,1)S(1)}, u32[]{:S(2)}, u32[]{:S(2)}) collective-permute-start(bf16[256,512]{1,0:T(8,128)(2,1)S(1)} %get-tuple-element.113.own), channel_id=1, source_target_pairs={{0,2},{1,3},{2,0},{3,1},{4,6},{5,7},{6,4},{7,5},{8,10},{9,11},{10,... | collective-permute-start | bytes 786440 | tf_op jit(solution)/shard_map/ppermute | solution.py:731
  63.7 11.9 %collective-permute-start.13 = (bf16[256,512]{1,0:T(8,128)(2,1)S(1)}, bf16[256,512]{1,0:T(8,128)(2,1)S(1)}, u32[]{:S(2)}, u32[]{:S(2)}) collective-permute-start(bf16[256,512]{1,0:T(8,128)(2,1)S(1)} %get-tuple-element.106.own), channel_id=1, source_target_pairs={{0,1},{1,0},{2,3},{3,2},{4,5},{5,4},{6,7},{7,6},{8,9},{9,8},{10,11... | collective-permute-start | bytes 786440 | tf_op jit(solution)/shard_map/ppermute | solution.py:727
  70.9 4.8 %collective-permute-start.15 = (bf16[256,512]{1,0:T(8,128)(2,1)S(1)}, bf16[256,512]{1,0:T(8,128)(2,1)S(1)}, u32[]{:S(2)}, u32[]{:S(2)}) collective-permute-start(bf16[256,512]{1,0:T(8,128)(2,1)S(1)} %collective-permute-done.14.refs_0_), channel_id=1, source_target_pairs={{0,1},{1,0},{2,3},{3,2},{4,5},{5,4},{6,7},{7,6},{8,9},{9,8},{10,11... | collective-permute-start | bytes 786440 | tf_op jit(solution)/shard_map/ppermute | solution.py:727
  70.9 7.3 %collective-permute-start.17 = (bf16[256,512]{1,0:T(8,128)(2,1)S(1)}, bf16[256,512]{1,0:T(8,128)(2,1)S(1)}, u32[]{:S(2)}, u32[]{:S(2)}) collective-permute-start(bf16[256,512]{1,0:T(8,128)(2,1)S(1)} %get-tuple-element.113.own), channel_id=1, source_target_pairs={{0,1},{1,0},{2,3},{3,2},{4,5},{5,4},{6,7},{7,6},{8,9},{9,8},{10,11... | collective-permute-start | bytes 786440 | tf_op jit(solution)/shard_map/ppermute | solution.py:727
  75.7 2.6 %collective-permute-start.19 = (bf16[256,512]{1,0:T(8,128)(2,1)S(1)}, bf16[256,512]{1,0:T(8,128)(2,1)S(1)}, u32[]{:S(2)}, u32[]{:S(2)}) collective-permute-start(bf16[256,512]{1,0:T(8,128)(2,1)S(1)} %collective-permute-done.18.refs_0_), channel_id=1, source_target_pairs={{0,1},{1,0},{2,3},{3,2},{4,5},{5,4},{6,7},{7,6},{8,9},{9,8},{10,11... | collective-permute-start | bytes 786440 | tf_op jit(solution)/shard_map/ppermute | solution.py:727
  75.7 4.6 %slice-start.2 = ((s8[6307840]{0:T(1024)(128)(4,1)}), s8[4194304]{0:T(1024)(128)(4,1)S(1)}, s32[]{:S(2)}) async-start(s8[6307840]{0:T(1024)(128)(4,1)} %bitcast.31), calls=%async_computation.2 | async-start | bytes 8388608
  77.6 2.6 %slice-start.3 = ((s8[6307840]{0:T(1024)(128)(4,1)}), s8[2113536]{0:T(1024)(128)(4,1)S(1)}, s32[]{:S(2)}) async-start(s8[6307840]{0:T(1024)(128)(4,1)} %bitcast.31), calls=%async_computation.3 | async-start | bytes 4227072
  77.7 2.6 %collective-permute-start.16 = (bf16[1120,256]{1,0:T(8,128)(2,1)S(1)}, bf16[1120,256]{1,0:T(8,128)(2,1)S(1)}, u32[]{:S(2)}, u32[]{:S(2)}) collective-permute-start(bf16[1120,256]{1,0:T(8,128)(2,1)S(1)} %attend.2.own), channel_id=1, source_target_pairs={{0,1},{1,0},{2,3},{3,2},{4,5},{5,4},{6,7},{7,6},{8,9},{9,8},{10,11... | collective-permute-start | bytes 1720328 | tf_op jit(solution)/shard_map/ppermute | solution.py:727
  80.2 10.7 %collective-permute-start.20 = (bf16[1120,256]{1,0:T(8,128)(2,1)S(1)}, bf16[1120,256]{1,0:T(8,128)(2,1)S(1)}, u32[]{:S(2)}, u32[]{:S(2)}) collective-permute-start(bf16[1120,256]{1,0:T(8,128)(2,1)S(1)} %attend.3.own), channel_id=1, source_target_pairs={{0,1},{1,0},{2,3},{3,2},{4,5},{5,4},{6,7},{7,6},{8,9},{9,8},{10,11... | collective-permute-start | bytes 1720328 | tf_op jit(solution)/shard_map/ppermute | solution.py:727
  80.3 19.8 %slice-start = ((s8[6307840]{0:T(1024)(128)(4,1)}), s8[4194304]{0:T(1024)(128)(4,1)S(1)}, s32[]{:S(2)}) async-start(s8[6307840]{0:T(1024)(128)(4,1)} %bitcast.26), calls=%async_computation | async-start | bytes 8388608
  83.7 11.1 %collective-permute-start.21 = (bf16[1,1400]{1,0:T(2,128)(2,1)S(1)}, bf16[1,1400]{1,0:T(2,128)(2,1)S(1)}, u32[]{:S(2)}, u32[]{:S(2)}) collective-permute-start(bf16[1,1400]{1,0:T(2,128)(2,1)S(1)} %get-tuple-element.115), channel_id=1, source_target_pairs={{0,4},{4,8},{8,12},{12,16},{16,20},{20,24},{24,28},{1,5},{5,9},{9,... | collective-permute-start | bytes 8408 | tf_op jit(solution)/shard_map/ppermute | solution.py:867
  87.0 13.1 %slice-start.1 = ((s8[6307840]{0:T(1024)(128)(4,1)}), s8[2113536]{0:T(1024)(128)(4,1)S(1)}, s32[]{:S(2)}) async-start(s8[6307840]{0:T(1024)(128)(4,1)} %bitcast.26), calls=%async_computation.1 | async-start | bytes 4227072
  87.1 7.8 %collective-permute-start.22 = (bf16[1,1400]{1,0:T(2,128)(2,1)S(1)}, bf16[1,1400]{1,0:T(2,128)(2,1)S(1)}, u32[]{:S(2)}, u32[]{:S(2)}) collective-permute-start(bf16[1,1400]{1,0:T(2,128)(2,1)S(1)} %get-tuple-element.116), channel_id=1, source_target_pairs={{4,0},{8,4},{12,8},{16,12},{20,16},{24,20},{28,24},{5,1},{9,5},{13... | collective-permute-start | bytes 8408 | tf_op jit(solution)/shard_map/ppermute | solution.py:868
  97.2 3.0 %collective-permute-start.23 = (bf16[1400,256]{1,0:T(8,128)(2,1)S(1)}, bf16[1400,256]{1,0:T(8,128)(2,1)S(1)}, u32[]{:S(2)}, u32[]{:S(2)}) collective-permute-start(bf16[1400,256]{1,0:T(8,128)(2,1)S(1)} %activate.2.own_a.own), channel_id=1, source_target_pairs={{0,1},{1,0},{2,3},{3,2},{4,5},{5,4},{6,7},{7,6},{8,9},{9,8},{10,11... | collective-permute-start | bytes 2150408 | tf_op jit(solution)/shard_map/ppermute | solution.py:727
  99.6 3.2 %collective-permute-start.24 = (bf16[1400,256]{1,0:T(8,128)(2,1)S(1)}, bf16[1400,256]{1,0:T(8,128)(2,1)S(1)}, u32[]{:S(2)}, u32[]{:S(2)}) collective-permute-start(bf16[1400,256]{1,0:T(8,128)(2,1)S(1)} %activate.3.own.own_b), channel_id=1, source_target_pairs={{0,1},{1,0},{2,3},{3,2},{4,5},{5,4},{6,7},{7,6},{8,9},{9,8},{10,11... | collective-permute-start | bytes 2150408 | tf_op jit(solution)/shard_map/ppermute | solution.py:727
  101.8 9.8 %collective-permute-start.25 = (bf16[560,256]{1,0:T(8,128)(2,1)S(1)}, bf16[560,256]{1,0:T(8,128)(2,1)S(1)}, u32[]{:S(2)}, u32[]{:S(2)}) collective-permute-start(bf16[560,256]{1,0:T(8,128)(2,1)S(1)} %far_project.3), channel_id=1, source_target_pairs={{0,2},{1,3},{2,0},{3,1},{4,6},{5,7},{6,4},{7,5},{8,10},{9,11},{10,... | collective-permute-start | bytes 860168 | tf_op jit(solution)/shard_map/ppermute | solution.py:731
  104.4 12.3 %collective-permute-start.26 = (bf16[560,256]{1,0:T(8,128)(2,1)S(1)}, bf16[560,256]{1,0:T(8,128)(2,1)S(1)}, u32[]{:S(2)}, u32[]{:S(2)}) collective-permute-start(bf16[560,256]{1,0:T(8,128)(2,1)S(1)} %far_project.2.after), channel_id=1, source_target_pairs={{0,2},{1,3},{2,0},{3,1},{4,6},{5,7},{6,4},{7,5},{8,10},{9,11},{10,... | collective-permute-start | bytes 860168 | tf_op jit(solution)/shard_map/ppermute | solution.py:731

commit v7 on v6

--- a/solution.py
+++ b/solution.py
@@ -457,7 +457,7 @@
     )(query, keys, erased, entry, totals, after)
 
 
-def pair_kernel(meta, own, other, after, pair, first, done):
+def pair_kernel(meta, own, other, pair, first, done):
     even = meta[PARITY] == 0
     for h in range(own.shape[0]):
         mine, theirs = own[h], other[h]
@@ -470,15 +470,15 @@
     done[...] = jnp.zeros_like(done)
 
 
-def pair_maps(meta, own, other, after):
+def pair_maps(meta, own, other):
     return pl.pallas_call(
         pair_kernel,
         out_shape=(shape_of(own.shape), shape_of(own.shape), shape_of((8, 128), f32)),
-        in_specs=[SM, VM, VM, ANY],
+        in_specs=[SM, VM, VM],
         out_specs=[VM] * 3,
         compiler_params=params(4),
         name="pair_maps",
-    )(meta, own, other, after)
+    )(meta, own, other)
 
 
 def apply_map(whole, state):
@@ -635,19 +635,7 @@
     return 0.5 * x * (1.0 + jnp.tanh(inner))
 
 
-def act_kernel(late, meta, outer, inside, before, after, taps, act_t, padded, act):
-    count = act.shape[0]
-    if late:
-        padded[7:8, :] = inside[BLOCK - 1 : BLOCK, :].astype(f32)
-        padded[8 : 8 + BLOCK, :] = inside[BLOCK:, :].astype(f32)
-        padded[8 + BLOCK : 8 + count, :] = outer[BLOCK:, :].astype(f32)
-        padded[8 + count : 9 + count, :] = after[...].astype(f32)
-    else:
-        padded[7:8, :] = before[...].astype(f32)
-        padded[8 : 8 + BLOCK, :] = outer[:BLOCK, :].astype(f32)
-        padded[8 + BLOCK : 8 + count, :] = inside[:BLOCK, :].astype(f32)
-        padded[8 + count : 9 + count, :] = inside[BLOCK : BLOCK + 1, :].astype(f32)
-
+def act_rows(taps, act, padded, start, count):
     @pl.loop(0, count // 32)
     def _(r):
         base = pl.multiple_of(r * 32, 32)
@@ -657,24 +645,46 @@
             + taps[1:2, :] * window[8:40, :]
             + taps[2:3, :] * window[9:41, :]
         )
-        act[pl.ds(base, 32), :] = gelu_of(value).astype(bf16)
-
+        act[pl.ds(start + base, 32), :] = gelu_of(value).astype(bf16)
+
+
+def inner_kernel(meta, outer, inside, taps, act_t, padded, act):
+    count = act.shape[0]
+    padded[7:8, :] = outer[BLOCK - 1 : BLOCK, :].astype(f32)
+    padded[8 : 8 + count, :] = inside[...].astype(f32)
+    padded[8 + count : 9 + count, :] = outer[BLOCK : BLOCK + 1, :].astype(f32)
+    act_rows(taps, act, padded, 0, count)
     act_t[...] = act[...].T
 
 
-def activate(meta, outer, inside, before, after, taps, late):
+def outer_kernel(meta, outer, inside, before, after, taps, act_t, padded_a, padded_b, act):
+    count = inside.shape[0]
+    padded_a[7:8, :] = before[...].astype(f32)
+    padded_a[8 : 8 + BLOCK, :] = outer[:BLOCK, :].astype(f32)
+    padded_a[8 + BLOCK : 9 + BLOCK, :] = inside[0:1, :].astype(f32)
+    padded_b[7:8, :] = inside[count - 1 : count, :].astype(f32)
+    padded_b[8 : 8 + BLOCK, :] = outer[BLOCK:, :].astype(f32)
+    padded_b[8 + BLOCK : 9 + BLOCK, :] = after[...].astype(f32)
+    act_rows(taps, act, padded_a, 0, BLOCK)
+    act_rows(taps, act, padded_b, BLOCK, BLOCK)
+    act_t[...] = act[...].T
+
+
+def activate(meta, outer, inside, taps, halo):
     hidden = outer.shape[1]
-    count = (outer.shape[0] + inside.shape[0]) // 2
-    return pl.pallas_call(
-        functools.partial(act_kernel, late),
+    count = outer.shape[0] if halo else inside.shape[0]
+    padded = [BLOCK, BLOCK] if halo else [count]
+    return pl.pallas_call(
+        outer_kernel if halo else inner_kernel,
         out_shape=shape_of((hidden, count)),
-        in_specs=[SM] + [VM] * 5,
+        in_specs=[SM] + [VM] * (3 + len(halo)),
         out_specs=VM,
-        scratch_shapes=[pltpu.VMEM((count + 16, hidden), f32), pltpu.VMEM((count, hidden), bf16)],
+        scratch_shapes=[pltpu.VMEM((rows + 16, hidden), f32) for rows in padded]
+        + [pltpu.VMEM((count, hidden), bf16)],
         compiler_params=params(8),
         cost_estimate=cost(10**9, 2 * 10**6),
         name="activate",
-    )(meta, outer, inside, before, after, taps)
+    )(meta, outer, inside, *halo, taps)
 
 
 def far_kernel(ys, meta, own, other, weights, other_weights, *outs):
@@ -699,28 +709,53 @@
 
 
 def near_kernel(meta, own_a, other_a, own_b, other_b, middle_a, middle_b, weights, other_weights, after, base):
-    size = own_a.shape[1]
-    middle = (
-        jnp.concatenate([middle_a[:, :BLOCK], middle_b[:, :BLOCK]], axis=1),
-        jnp.concatenate([middle_b[:, BLOCK:], middle_a[:, BLOCK:]], axis=1),
-    )
-    for i, (own, other) in enumerate(((own_a, other_a), (own_b, other_b))):
+    inside = own_b.shape[1]
+    for own, other, middle, spans in (
+        (own_b, other_b, middle_b, ((0, BLOCK, inside),)),
+        (own_a, other_a, middle_a, ((0, 0, BLOCK), (BLOCK, BLOCK + inside, BLOCK))),
+    ):
         total = dot(weights[meta[ME]], own[...])
-        total = total + dot(other_weights[meta[CHIP]], other[...])
-        base[:, i * size : (i + 1) * size] = total + middle[i]
+        total = total + dot(other_weights[meta[CHIP]], other[...]) + middle[...]
+        for source, target, size in spans:
+            base[:, target : target + size] = total[:, source : source + size]
 
 
 def near_project(meta, own, other, middle_a, middle_b, weights, other_weights, after):
     part = weights.shape[1]
     return pl.pallas_call(
         near_kernel,
-        out_shape=shape_of((part, 2 * own[0].shape[1]), f32),
+        out_shape=shape_of((part, own[0].shape[1] + own[1].shape[1]), f32),
         in_specs=[SM] + [VM] * 8 + [ANY],
         out_specs=VM,
         compiler_params=params(10),
         cost_estimate=cost(2 * 10**9, 6 * 10**6),
         name="near_project",
     )(meta, own[0], other[0], own[1], other[1], middle_a, middle_b, weights, other_weights, after)
+
+
+def finish_kernel(count, base, *refs):
+    ends, inner, out = refs[:count], refs[count : 2 * count], refs[2 * count]
+    inside = inner[0].shape[1]
+    for target, size, refs_of, source in (
+        (0, BLOCK, ends, 0),
+        (BLOCK, inside, inner, 0),
+        (BLOCK + inside, BLOCK, ends, BLOCK),
+    ):
+        total = base[:, target : target + size]
+        for ref in refs_of:
+            total = total + ref[:, source : source + size].astype(f32)
+        out[:, target : target + size] = total.astype(bf16)
+
+
+def finish(base, ends, inner):
+    return pl.pallas_call(
+        functools.partial(finish_kernel, len(ends)),
+        out_shape=shape_of(base.shape),
+        in_specs=[VM] * (1 + 2 * len(ends)),
+        out_specs=VM,
+        compiler_params=params(8),
+        name="finish",
+    )(base, *ends, *inner)
 
 
 def core_swap(value, n):
@@ -825,23 +860,22 @@
     other_w_down = core_swap(sent_w_down, n)
     fetched = [y_shift(my_rows, n, d) for d in range(1, ys)]
     partner_w_out = core_swap(their_rows, n)
-    acc_query, partner_w_out, other_w_down = lax.optimization_barrier(
-        (early[2], partner_w_out, other_w_down)
-    )
-    their_rows, fetched, _ = lax.optimization_barrier((their_rows, fetched, totals))
+    other_maps = pair_swap(sent_maps, seqs)
+    their_rows, fetched, _ = lax.optimization_barrier((their_rows, fetched, other_maps))
     diagonal = [
         lax.ppermute(their_rows, "head", [(i, ((i + 2 * d) % n) ^ 1) for i in range(n)])
         for d in range(1, ys)
     ]
-
-    other_maps = pair_swap(sent_maps, seqs)
-    query, tokens_a, tokens_b, query_done = queries(
-        meta, ys, scaled, scale_b, w_query, acc_query, sum(groups, [])
-    )
-    pair, first, done = pair_maps(meta, own_maps, other_maps, query_done)
+    pair, first, done = pair_maps(meta, own_maps, other_maps)
     fetched, _ = lax.optimization_barrier((fetched, done))
     swapped = [pair_swap(value, seqs) for value in fetched]
     pairs = [later(pair, seqs, d) for d in range(seqs // 2 - 1, 0, -1)]
+    acc_query, partner_w_out, other_w_down, _ = lax.optimization_barrier(
+        (early[2], partner_w_out, other_w_down, done)
+    )
+    query, tokens_a, tokens_b, _ = queries(
+        meta, ys, scaled, scale_b, w_query, acc_query, sum(groups, [])
+    )
     shard_query, free, out_done = block_outputs(query, keys, erased, entry, totals, done)
     kept_state, given_state = start_states(meta, first, pairs, out_done)
     other_state = pair_swap(given_state, seqs)
@@ -864,26 +898,34 @@
     outer, middle_a, first_row, last_row = up_project(
         meta, middle, core_swap(middle, n), ffn_scale, w_up, part
     )
-    before = lax.ppermute(last_row, "seq", [(i, i + 1) for i in range(seqs - 1)])
-    after = lax.ppermute(first_row, "seq", [(i + 1, i) for i in range(seqs - 1)])
     middle = middle_of(1, far_mixed[1])
     inside, middle_b, _, _ = up_project(
         meta, middle, core_swap(middle, n), ffn_scale, w_up, part
     )
 
-    acts = [activate(meta, outer, inside, before, after, taps, late) for late in (False, True)]
-    partner_acts = [core_swap(act, n) for act in acts]
-    fars = [
-        far_project(meta, ys, act, partner, w_parts, other_w_down)
-        for act, partner in zip(acts, partner_acts)
-    ]
+    act_b = activate(meta, outer, inside, taps, ())
+    partner_b = core_swap(act_b, n)
+    far_b = far_project(meta, ys, act_b, partner_b, w_parts, other_w_down)
+    arrived_b = [y_shift(value, n, d + 1) for d, value in enumerate(far_b)]
+    first_row, last_row, _ = lax.optimization_barrier((first_row, last_row, far_b))
+    before = lax.ppermute(last_row, "seq", [(i, i + 1) for i in range(seqs - 1)])
+    after = lax.ppermute(first_row, "seq", [(i + 1, i) for i in range(seqs - 1)])
+    before, after, arrived_b = lax.optimization_barrier((before, after, arrived_b))
+    act_a = activate(meta, outer, inside, taps, (before, after))
+    partner_a = core_swap(act_a, n)
+    far_a = far_project(meta, ys, act_a, partner_a, w_parts, other_w_down)
+    arrived_a = [y_shift(value, n, d + 1) for d, value in enumerate(far_a)]
     total = near_project(
-        meta, acts, partner_acts, middle_a, middle_b, w_parts, other_w_down, fars[1][0]
+        meta,
+        (act_a, act_b),
+        (partner_a, partner_b),
+        middle_a,
+        middle_b,
+        w_parts,
+        other_w_down,
+        far_a[0],
     )
-    for d in range(1, ys):
-        halves = [y_shift(far[d - 1], n, d) for far in fars]
-        total = total + jnp.concatenate(halves, axis=1).astype(f32)
-    return total.astype(bf16).T
+    return finish(total, arrived_a, arrived_b).T
 
 
 def solution(mesh):

time: 119 us -> 125 us (1.050)
  waiting for transfers between devices: 36.9 us -> 41.2 us
    ppermute x6, waiting for transfers between devices: 23.9 us -> 18 us  [y_shift(): lax.ppermute(value, 'head', [(i, (i + 2 * step) % n) for i in range(n)])]
    ppermute x12, waiting for transfers between devices: 2.01 us -> 5.99 us  [core_swap(): return lax.ppermute(value, 'head', [(i, i ^ 1) for i in range(n)])]
    ppermute x3, waiting for transfers between devices: 4.22 us -> 6.91 us  [later(): lax.ppermute(value, 'seq', [(i, i + 2 * step) for i in range(n - 2 * step)])]
    ppermute x1, waiting for transfers between devices: 0.01 us -> 1.93 us  [shards(): lax.ppermute(first_row, 'seq', [(i + 1, i) for i in range(seqs - 1)])]
    pallas_call x3 -> x4, Pallas kernels: 7.13 us -> 8.05 us  [the longest x2 4.58 us: activate(): pl.pallas_call(outer_kernel if halo else inner_kernel, out_shape=shape_of...]
  transfers between devices with their start and end apart: 27 -> 27, of which waited for: 11 -> 12; matrix products, arithmetic and copies ran while one was open for 4% -> 3% of each run, Pallas kernels for 39% -> 29%
where the time goes in v7:
time: 125 us; the launch traced here: 123 us
  Pallas kernels  49.8 us (40%)
  waiting for transfers between devices  41.2 us (33%)
  starting transfers between devices  26.5 us (21%)
  local copies, waits for them, and re-layouts  3.84 us (3%)
  other arithmetic  1.47 us (1%)
    ppermute x6, waiting for transfers between devices, y_shift(): lax.ppermute(value, 'head', [(i, (i + 2 * step) % n) for i in range(n)])  18 us
    pallas_call x1, Pallas kernels, block_maps(): pl.pallas_call(functools.partial(maps_kernel, n, heads, at), out_shape=(s...  12.3 us
    pallas_call x2, Pallas kernels, up_project(): pl.pallas_call(up_kernel, out_shape=(shape_of((count, hidden)), shape_of(...  7.55 us
    ppermute x6, starting transfers between devices, y_shift(): lax.ppermute(value, 'head', [(i, (i + 2 * step) % n) for i in range(n)])  7.3 us
    pallas_call x1, Pallas kernels, early_project(): pl.pallas_call(functools.partial(early_kernel, len(pieces), at), out_shap...  7.14 us
    ppermute x3, waiting for transfers between devices, later(): lax.ppermute(value, 'seq', [(i, i + 2 * step) for i in range(n - 2 * step)])  6.91 us
    ppermute x3, starting transfers between devices, later(): lax.ppermute(value, 'seq', [(i, i + 2 * step) for i in range(n - 2 * step)])  6.24 us
    ppermute x12, waiting for transfers between devices, core_swap(): return lax.ppermute(value, 'head', [(i, i ^ 1) for i in range(n)])  5.99 us
  transfers between devices with their start and end apart: 27, of which 12 were waited for; matrix products, arithmetic and copies ran while one was open for 3% of the time, Pallas kernels for 29%

profile of v7, /device:TPU:16, one launch (start us, length us, event | category | flops | bytes accessed | tf_op | source)
XLA Modules:
  0.0 123.3 jit_solution(5029580129564873711)
XLA Ops:
  0.0 1.5 %collective-permute-start = (bf16[560,512]{1,0:T(8,128)(2,1)}, bf16[560,512]{1,0:T(8,128)(2,1)S(1)}, u32[]{:S(2)}, u32[]{:S(2)}) collective-permute-start(bf16[560,512]{1,0:T(8,128)(2,1)} %bitcast.35), channel_id=1, source_target_pairs={{0,2},{1,3},{2,0},{3,1},{4,6},{5,7},{6,4},{7,5},{8,10},{9,11},{10,... | collective-permute-start | bytes 1720328 | tf_op jit(solution)/shard_map/ppermute | solution.py:766
  1.5 0.8 reshape.37
  2.3 0.8 fusion.2
  3.2 0.8 reshape.31
  4.0 0.7 convert_element_type.6.taps
  4.7 0.7 reshape.39.gain
  5.8 1.1 copy-done.4
  6.8 7.1 %early_project.1 = (f32[512,512]{1,0:T(8,128)S(1)}, f32[512,512]{1,0:T(8,128)S(1)}, f32[512,512]{1,0:T(8,128)S(1)}, f32[16,512]{1,0:T(8,128)S(1)}, f32[8,512]{1,...) custom-call(s32[6]{0:T(128)S(1)} %stack.24.meta, ...), custom_call_target="tpu_custom_call" | custom-call | flops 3000000000 | bytes 8000000 | tf_op jit(solution)/shard_map/early_project/pallas_call | solution.py:163
  14.0 1.0 collective-permute-done.refs_0_.refs_2_
  14.9 2.0 %collective-permute-done.2.refs_1_.refs_3_ = bf16[560,512]{1,0:T(8,128)(2,1)S(1)} collective-permute-done((bf16[560,512]{1,0:T(8,128)(2,1)S(1)}, bf16[560,512]{1,0:T(8,128)(2,1)S(1)}, u32[]{:S(2)}, u32[]{:S(2)}) %collective-permute-start.2) | collective-permute-done | bytes 573472 | tf_op jit(solution)/shard_map/ppermute | solution.py:762
  17.4 1.5 %collective-permute-start.10 = (bf16[560,512]{1,0:T(8,128)(2,1)S(1)}, bf16[560,512]{1,0:T(8,128)(2,1)S(1)}, u32[]{:S(2)}, u32[]{:S(2)}) collective-permute-start(bf16[560,512]{1,0:T(8,128)(2,1)S(1)} %get-tuple-element.101), channel_id=1, source_target_pairs={{0,2},{1,3},{2,0},{3,1},{4,6},{5,7},{6,4},{7,5},{8,10},{9,11},{10,... | collective-permute-start | bytes 1720328 | tf_op jit(solution)/shard_map/ppermute | solution.py:766
  18.9 12.3 %block_maps.1 = (bf16[512,1120]{1,0:T(8,128)(2,1)S(1)}, f32[512,128]{1,0:T(8,128)S(1)}, bf16[512,512]{1,0:T(8,128)(2,1)S(1)}, bf16[512,1024]{1,0:T(8,128)(2,1)S(...) custom-call(s32[6]{0:T(128)S(1)} %stack.24.meta, ...), custom_call_target="tpu_custom_call" | custom-call | flops 10000000000 | bytes 14000000 | tf_op jit(solution)/shard_map/block_maps/pallas_call | solution.py:333
  31.3 1.6 %collective-permute-start.5 = (bf16[2,128,256]{2,1,0:T(8,128)(2,1)S(1)}, bf16[2,128,256]{2,1,0:T(8,128)(2,1)S(1)}, u32[]{:S(2)}, u32[]{:S(2)}) collective-permute-start(bf16[2,128,256]{2,1,0:T(8,128)(2,1)S(1)} %get-tuple-element.87), channel_id=1, source_target_pairs={{0,4},{4,0},{8,12},{12,8},{16,20},{20,16},{24,28},{28,24},{1,5},{5... | collective-permute-start | bytes 393224 | tf_op jit(solution)/shard_map/ppermute | solution.py:770
  32.8 3.8 %collective-permute-done.5.other = bf16[2,128,256]{2,1,0:T(8,128)(2,1)S(1)} collective-permute-done((bf16[2,128,256]{2,1,0:T(8,128)(2,1)S(1)}, bf16[2,128,256]{2,1,0:T(8,128)(2,1)S(1)}, u32[]{:S(2)}, u32[]{:S(2)}) %collective-permute-start.5) | collective-permute-done | bytes 131104 | tf_op jit(solution)/shard_map/ppermute | solution.py:770
  36.6 0.7 pair_maps.1
  37.3 1.6 %collective-permute-start.11 = (bf16[560,512]{1,0:T(8,128)(2,1)S(1)}, bf16[560,512]{1,0:T(8,128)(2,1)S(1)}, u32[]{:S(2)}, u32[]{:S(2)}) collective-permute-start(bf16[560,512]{1,0:T(8,128)(2,1)S(1)} %collective-permute-done.10.refs_2_), channel_id=1, source_target_pairs={{0,4},{4,0},{8,12},{12,8},{16,20},{20,16},{24,28},{28,24},{1,5},{5... | collective-permute-start | bytes 1720328 | tf_op jit(solution)/shard_map/ppermute | solution.py:770
  38.9 0.7 collective-permute-start.6
  39.6 1.3 %collective-permute-start.7 = (bf16[2,128,256]{2,1,0:T(8,128)(2,1)S(1)}, bf16[2,128,256]{2,1,0:T(8,128)(2,1)S(1)}, u32[]{:S(2)}, u32[]{:S(2)}) collective-permute-start(bf16[2,128,256]{2,1,0:T(8,128)(2,1)S(1)} %get-tuple-element.92), channel_id=1, source_target_pairs={{0,16},{4,20},{8,24},{12,28},{1,17},{5,21},{9,25},{13,29},{2,18},{... | collective-permute-start | bytes 393224 | tf_op jit(solution)/shard_map/ppermute | solution.py:774
  40.9 4.3 %collective-permute-start.8 = (bf16[2,128,256]{2,1,0:T(8,128)(2,1)S(1)}, bf16[2,128,256]{2,1,0:T(8,128)(2,1)S(1)}, u32[]{:S(2)}, u32[]{:S(2)}) collective-permute-start(bf16[2,128,256]{2,1,0:T(8,128)(2,1)S(1)} %get-tuple-element.92), channel_id=1, source_target_pairs={{0,8},{4,12},{8,16},{12,20},{16,24},{20,28},{1,9},{5,13},{9,17},{1... | collective-permute-start | bytes 393224 | tf_op jit(solution)/shard_map/ppermute | solution.py:774
  45.2 1.9 %queries.1 = (bf16[512,512]{1,0:T(8,128)(2,1)S(1)}, bf16[2240,256]{1,0:T(8,128)(2,1)S(1)}, bf16[2240,256]{1,0:T(8,128)(2,1)S(1)}, f32[8,128]{1,0:T(8,128)}) custom-call(s32[6]{0:T(128)S(1)} %stack.24.meta, bf16[512,1120]{1,0:T(8,128)(2,1)S(1)} %get-tuple-element.78.scaled, f32[512,128]{1,0:T(8,128)S(1)} %get-tuple-element.79.scale_b, ...), custom_call_target="tpu_custom_call" | custom-call | flops 1000000000 | bytes 8000000 | tf_op jit(solution)/shard_map/queries/pallas_call | solution.py:397
  47.1 2.8 %block_outputs.1 = (bf16[512,512]{1,0:T(8,128)(2,1)S(1)}, f32[512,512]{1,0:T(8,128)S(1)}, f32[8,128]{1,0:T(8,128)S(1)}) custom-call(bf16[512,512]{1,0:T(8,128)(2,1)S(1)} %get-tuple-element.93.query, bf16[512,512]{1,0:T(8,128)(2,1)S(1)} %get-tuple-element.94.keys, bf16[512,1024]{1,0:T(8,128)(2,1)S(1)} %get-tuple-element.95.erased, ...), custom_call_target="tpu_custom_call" | custom-call | flops 3000000000 | bytes 4000000 | tf_op jit(solution)/shard_map/block_outputs/pallas_call | solution.py:448
  49.9 1.9 %collective-permute-done.7.refs_1_ = bf16[2,128,256]{2,1,0:T(8,128)(2,1)S(1)} collective-permute-done((bf16[2,128,256]{2,1,0:T(8,128)(2,1)S(1)}, bf16[2,128,256]{2,1,0:T(8,128)(2,1)S(1)}, u32[]{:S(2)}, u32[]{:S(2)}) %collective-permute-start.7) | collective-permute-done | bytes 131104 | tf_op jit(solution)/shard_map/ppermute | solution.py:774
  51.8 5.0 %collective-permute-done.8.refs_2_ = bf16[2,128,256]{2,1,0:T(8,128)(2,1)S(1)} collective-permute-done((bf16[2,128,256]{2,1,0:T(8,128)(2,1)S(1)}, bf16[2,128,256]{2,1,0:T(8,128)(2,1)S(1)}, u32[]{:S(2)}, u32[]{:S(2)}) %collective-permute-start.8) | collective-permute-done | bytes 131104 | tf_op jit(solution)/shard_map/ppermute | solution.py:774
  56.8 1.2 start_states.1
  58.0 0.6 collective-permute-start.9
  58.7 4.6 %collective-permute-done.12.refs_4_ = bf16[1120,512]{1,0:T(8,128)(2,1)S(1)} collective-permute-done((bf16[1120,512]{1,0:T(8,128)(2,1)S(1)}, bf16[1120,512]{1,0:T(8,128)(2,1)S(1)}, u32[]{:S(2)}, u32[]{:S(2)}) %collective-permute-start.12) | collective-permute-done | bytes 1146912 | tf_op jit(solution)/shard_map/ppermute | solution.py:866
  63.3 1.1 mixed_heads.1
  64.4 1.4 %collective-permute-start.14 = (bf16[256,512]{1,0:T(8,128)(2,1)S(1)}, bf16[256,512]{1,0:T(8,128)(2,1)S(1)}, u32[]{:S(2)}, u32[]{:S(2)}) collective-permute-start(bf16[256,512]{1,0:T(8,128)(2,1)S(1)} %get-tuple-element.109.own), channel_id=1, source_target_pairs={{0,2},{1,3},{2,0},{3,1},{4,6},{5,7},{6,4},{7,5},{8,10},{9,11},{10,... | collective-permute-start | bytes 786440 | tf_op jit(solution)/shard_map/ppermute | solution.py:766
  65.8 0.7 collective-permute-start.18
  66.5 7.2 %collective-permute-done.14.refs_0_ = bf16[256,512]{1,0:T(8,128)(2,1)S(1)} collective-permute-done((bf16[256,512]{1,0:T(8,128)(2,1)S(1)}, bf16[256,512]{1,0:T(8,128)(2,1)S(1)}, u32[]{:S(2)}, u32[]{:S(2)}) %collective-permute-start.14) | collective-permute-done | bytes 262176 | tf_op jit(solution)/shard_map/ppermute | solution.py:766
  74.2 3.8 %collective-permute-done.18.refs_0_ = bf16[256,512]{1,0:T(8,128)(2,1)S(1)} collective-permute-done((bf16[256,512]{1,0:T(8,128)(2,1)S(1)}, bf16[256,512]{1,0:T(8,128)(2,1)S(1)}, u32[]{:S(2)}, u32[]{:S(2)}) %collective-permute-start.18) | collective-permute-done | bytes 262176 | tf_op jit(solution)/shard_map/ppermute | solution.py:766
  78.0 1.9 %attend.2.own = bf16[1120,256]{1,0:T(8,128)(2,1)S(1)} custom-call(s32[6]{0:T(128)S(1)} %stack.24.meta, bf16[2240,256]{1,0:T(8,128)(2,1)S(1)} %get-tuple-element.90.tokens, bf16[256,512]{1,0:T(8,128)(2,1)S(1)} %get-tuple-element.109.own, bf16[256,512]{1,0:T(8,128)(2,1)S(1)} %collective-permute-done.13.partner, bf16[2240,512]{1,0:T(8,128)(2,1)S(1)} %bitcast.33, ...), custom_call_target="tpu_custom_call" | custom-call | flops 2000000000 | bytes 7000000 | tf_op jit(solution)/shard_map/attend/pallas_call | solution.py:572
  80.5 1.9 %attend.3.own = bf16[1120,256]{1,0:T(8,128)(2,1)S(1)} custom-call(s32[6]{0:T(128)S(1)} %stack.24.meta, bf16[2240,256]{1,0:T(8,128)(2,1)S(1)} %get-tuple-element.115.tokens, bf16[256,512]{1,0:T(8,128)(2,1)S(1)} %get-tuple-element.116.own, bf16[256,512]{1,0:T(8,128)(2,1)S(1)} %collective-permute-done.17.partner, bf16[2240,512]{1,0:T(8,128)(2,1)S(1)} %bitcast.34, ...), custom_call_target="tpu_custom_call" | custom-call | flops 2000000000 | bytes 7000000 | tf_op jit(solution)/shard_map/attend/pallas_call | solution.py:572
  82.6 3.5 %up_project.2 = (bf16[256,1400]{1,0:T(8,128)(2,1)S(1)}, f32[560,256]{1,0:T(8,128)S(1)}, bf16[1,1400]{1,0:T(2,128)(2,1)S(1)}, bf16[1,1400]{1,0:T(2,128)(2,1)S(1)}) custom-call(s32[6]{0:T(128)S(1)} %stack.24.meta, bf16[1120,256]{1,0:T(8,128)(2,1)S(1)} %attend.2.own, bf16[1120,256]{1,0:T(8,128)(2,1)S(1)} %collective-permute-done.16.other, ...), custom_call_target="tpu_custom_call" | custom-call | flops 2000000000 | bytes 8000000 | tf_op jit(solution)/shard_map/up_project/pallas_call | solution.py:612
  86.1 4.1 %up_project.3 = (bf16[256,1400]{1,0:T(8,128)(2,1)S(1)}, f32[560,256]{1,0:T(8,128)S(1)}, bf16[1,1400]{1,0:T(2,128)(2,1)}, bf16[1,1400]{1,0:T(2,128)(2,1)}) custom-call(s32[6]{0:T(128)S(1)} %stack.24.meta, bf16[1120,256]{1,0:T(8,128)(2,1)S(1)} %attend.3.own, bf16[1120,256]{1,0:T(8,128)(2,1)S(1)} %collective-permute-done.20.other, f32[1,2240]{1,0:T(1,128)S(1)} %reshape.39.gain, ...), custom_call_target="tpu_custom_call" | custom-call | flops 2000000000 | bytes 8000000 | tf_op jit(solution)/shard_map/up_project/pallas_call | solution.py:612
  90.2 2.3 %activate.2.own.own_b = bf16[1400,256]{1,0:T(8,128)(2,1)S(1)} custom-call(s32[6]{0:T(128)S(1)} %stack.24.meta, bf16[256,1400]{1,0:T(8,128)(2,1)S(1)} %get-tuple-element.114.outer, bf16[256,1400]{1,0:T(8,128)(2,1)S(1)} %get-tuple-element.117.inside, f32[3,1400]{1,0:T(4,128)S(1)} %convert_element_type.6.taps), custom_call_target="tpu_custom_call" | custom-call | flops 1000000000 | bytes 2000000 | tf_op jit(solution)/shard_map/activate/pallas_call | solution.py:677
  93.0 1.8 %collective-permute-done.21.other.other_b = bf16[1400,256]{1,0:T(8,128)(2,1)S(1)} collective-permute-done((bf16[1400,256]{1,0:T(8,128)(2,1)S(1)}, bf16[1400,256]{1,0:T(8,128)(2,1)S(1)}, u32[]{:S(2)}, u32[]{:S(2)}) %collective-permute-start.21) | collective-permute-done | bytes 716832 | tf_op jit(solution)/shard_map/ppermute | solution.py:762
  94.9 1.6 %far_project.2 = bf16[560,256]{1,0:T(8,128)(2,1)S(1)} custom-call(s32[6]{0:T(128)S(1)} %stack.24.meta, bf16[1400,256]{1,0:T(8,128)(2,1)S(1)} %activate.2.own.own_b, bf16[1400,256]{1,0:T(8,128)(2,1)S(1)} %collective-permute-done.21.other.other_b, bf16[4,560,1400]{2,1,0:T(8,128)(2,1)S(1)} %bitcast.27, ...), custom_call_target="tpu_custom_call" | custom-call | flops 1000000000 | bytes 4000000 | tf_op jit(solution)/shard_map/far_project/pallas_call | solution.py:700
  96.5 1.8 %collective-permute-start.24 = (bf16[560,256]{1,0:T(8,128)(2,1)S(1)}, bf16[560,256]{1,0:T(8,128)(2,1)S(1)}, u32[]{:S(2)}, u32[]{:S(2)}) collective-permute-start(bf16[560,256]{1,0:T(8,128)(2,1)S(1)} %far_project.2), channel_id=1, source_target_pairs={{0,2},{1,3},{2,0},{3,1},{4,6},{5,7},{6,4},{7,5},{8,10},{9,11},{10,... | collective-permute-start | bytes 860168 | tf_op jit(solution)/shard_map/ppermute | solution.py:766
  98.3 3.4 %collective-permute-start.22 = (bf16[1,1400]{1,0:T(2,128)(2,1)S(1)}, bf16[1,1400]{1,0:T(2,128)(2,1)S(1)}, u32[]{:S(2)}, u32[]{:S(2)}) collective-permute-start(bf16[1,1400]{1,0:T(2,128)(2,1)S(1)} %get-tuple-element.122), channel_id=1, source_target_pairs={{0,4},{4,8},{8,12},{12,16},{16,20},{20,24},{24,28},{1,5},{5,9},{9,... | collective-permute-start | bytes 8408 | tf_op jit(solution)/shard_map/ppermute | solution.py:911
  101.7 3.6 %collective-permute-start.23 = (bf16[1,1400]{1,0:T(2,128)(2,1)S(1)}, bf16[1,1400]{1,0:T(2,128)(2,1)S(1)}, u32[]{:S(2)}, u32[]{:S(2)}) collective-permute-start(bf16[1,1400]{1,0:T(2,128)(2,1)S(1)} %get-tuple-element.123), channel_id=1, source_target_pairs={{4,0},{8,4},{12,8},{16,12},{20,16},{24,20},{28,24},{5,1},{9,5},{13... | collective-permute-start | bytes 8408 | tf_op jit(solution)/shard_map/ppermute | solution.py:912
  105.3 1.9 %collective-permute-done.23.after = bf16[1,1400]{1,0:T(2,128)(2,1)S(1)} collective-permute-done((bf16[1,1400]{1,0:T(2,128)(2,1)S(1)}, bf16[1,1400]{1,0:T(2,128)(2,1)S(1)}, u32[]{:S(2)}, u32[]{:S(2)}) %collective-permute-start.23) | collective-permute-done | bytes 2832 | tf_op jit(solution)/shard_map/ppermute | solution.py:912
  107.2 2.3 %activate.3.own.own_a = bf16[1400,256]{1,0:T(8,128)(2,1)S(1)} custom-call(s32[6]{0:T(128)S(1)} %stack.24.meta, bf16[256,1400]{1,0:T(8,128)(2,1)S(1)} %get-tuple-element.114.outer, bf16[256,1400]{1,0:T(8,128)(2,1)S(1)} %get-tuple-element.117.inside, bf16[1,1400]{1,0:T(2,128)(2,1)S(1)} %collective-permute-done.22.before, ...), custom_call_target="tpu_custom_call" | custom-call | flops 1000000000 | bytes 2000000 | tf_op jit(solution)/shard_map/activate/pallas_call | solution.py:677
  109.6 2.2 %collective-permute-done.25.other.other_a = bf16[1400,256]{1,0:T(8,128)(2,1)S(1)} collective-permute-done((bf16[1400,256]{1,0:T(8,128)(2,1)S(1)}, bf16[1400,256]{1,0:T(8,128)(2,1)S(1)}, u32[]{:S(2)}, u32[]{:S(2)}) %collective-permute-start.25) | collective-permute-done | bytes 716832 | tf_op jit(solution)/shard_map/ppermute | solution.py:762
  111.7 1.6 %far_project.3.after = bf16[560,256]{1,0:T(8,128)(2,1)S(1)} custom-call(s32[6]{0:T(128)S(1)} %stack.24.meta, bf16[1400,256]{1,0:T(8,128)(2,1)S(1)} %activate.3.own.own_a, bf16[1400,256]{1,0:T(8,128)(2,1)S(1)} %collective-permute-done.25.other.other_a, bf16[4,560,1400]{2,1,0:T(8,128)(2,1)S(1)} %bitcast.28, ...), custom_call_target="tpu_custom_call" | custom-call | flops 1000000000 | bytes 4000000 | tf_op jit(solution)/shard_map/far_project/pallas_call | solution.py:700
  113.7 2.5 %near_project.1.base = f32[560,512]{1,0:T(8,128)S(1)} custom-call(s32[6]{0:T(128)S(1)} %stack.24.meta, bf16[1400,256]{1,0:T(8,128)(2,1)S(1)} %activate.3.own.own_a, bf16[1400,256]{1,0:T(8,128)(2,1)S(1)} %collective-permute-done.25.other.other_a, bf16[1400,256]{1,0:T(8,128)(2,1)S(1)} %activate.2.own.own_b, ...), custom_call_target="tpu_custom_call" | custom-call | flops 2000000000 | bytes 6000000 | tf_op jit(solution)/shard_map/near_project/pallas_call | solution.py:725
  116.2 6.1 %collective-permute-done.26.refs_0_ = bf16[560,256]{1,0:T(8,128)(2,1)S(1)} collective-permute-done((bf16[560,256]{1,0:T(8,128)(2,1)S(1)}, bf16[560,256]{1,0:T(8,128)(2,1)S(1)}, u32[]{:S(2)}, u32[]{:S(2)}) %collective-permute-start.26) | collective-permute-done | bytes 286752 | tf_op jit(solution)/shard_map/ppermute | solution.py:766
  122.3 1.0 finish.1
  (57 shorter events, 3.2 us)
Async XLA Ops:
  0.0 14.9 %collective-permute-start = (bf16[560,512]{1,0:T(8,128)(2,1)}, bf16[560,512]{1,0:T(8,128)(2,1)S(1)}, u32[]{:S(2)}, u32[]{:S(2)}) collective-permute-start(bf16[560,512]{1,0:T(8,128)(2,1)} %bitcast.35), channel_id=1, source_target_pairs={{0,2},{1,3},{2,0},{3,1},{4,6},{5,7},{6,4},{7,5},{8,10},{9,11},{10,... | collective-permute-start | bytes 1720328 | tf_op jit(solution)/shard_map/ppermute | solution.py:766
  1.5 4.2 %collective-permute-start.1 = (bf16[560,512]{1,0:T(8,128)(2,1)}, bf16[560,512]{1,0:T(8,128)(2,1)S(1)}, u32[]{:S(2)}, u32[]{:S(2)}) collective-permute-start(bf16[560,512]{1,0:T(8,128)(2,1)} %bitcast.36), channel_id=1, source_target_pairs={{0,1},{1,0},{2,3},{3,2},{4,5},{5,4},{6,7},{7,6},{8,9},{9,8},{10,11... | collective-permute-start | bytes 1720328 | tf_op jit(solution)/shard_map/ppermute | solution.py:762
  5.7 1.1 copy-start.4
  6.8 12.1 %copy-start.2 = (bf16[2240,512]{1,0:T(8,128)(2,1)S(1)}, bf16[2240,512]{1,0:T(8,128)(2,1)}, u32[]{:S(2)}) copy-start(bf16[2240,512]{1,0:T(8,128)(2,1)} %refs_5_.3) | copy-start | bytes 6881284
  6.8 12.1 %copy-start.3 = (bf16[2240,512]{1,0:T(8,128)(2,1)S(1)}, bf16[2240,512]{1,0:T(8,128)(2,1)}, u32[]{:S(2)}) copy-start(bf16[2240,512]{1,0:T(8,128)(2,1)} %refs_6_.3) | copy-start | bytes 6881284
  14.9 2.0 %collective-permute-start.2 = (bf16[560,512]{1,0:T(8,128)(2,1)S(1)}, bf16[560,512]{1,0:T(8,128)(2,1)S(1)}, u32[]{:S(2)}, u32[]{:S(2)}) collective-permute-start(bf16[560,512]{1,0:T(8,128)(2,1)S(1)} %collective-permute-done.refs_0_.refs_2_), channel_id=1, source_target_pairs={{0,1},{1,0},{2,3},{3,2},{4,5},{5,4},{6,7},{7,6},{8,9},{9,8},{10,11... | collective-permute-start | bytes 1720328 | tf_op jit(solution)/shard_map/ppermute | solution.py:762
  16.9 23.9 %collective-permute-start.4 = (bf16[2,560,1400]{2,1,0:T(8,128)(2,1)}, bf16[2,560,1400]{2,1,0:T(8,128)(2,1)S(1)}, u32[]{:S(2)}, u32[]{:S(2)}) collective-permute-start(bf16[2,560,1400]{2,1,0:T(8,128)(2,1)} %get-tuple-element.85), channel_id=1, source_target_pairs={{0,1},{1,0},{2,3},{3,2},{4,5},{5,4},{6,7},{7,6},{8,9},{9,8},{10,11... | collective-permute-start | bytes 9408008 | tf_op jit(solution)/shard_map/ppermute | solution.py:762
  17.0 22.5 %collective-permute-start.3 = (bf16[1120,512]{1,0:T(8,128)(2,1)S(1)}, bf16[1120,512]{1,0:T(8,128)(2,1)S(1)}, u32[]{:S(2)}, u32[]{:S(2)}) collective-permute-start(bf16[1120,512]{1,0:T(8,128)(2,1)S(1)} %get-tuple-element.104), channel_id=1, source_target_pairs={{0,1},{1,0},{2,3},{3,2},{4,5},{5,4},{6,7},{7,6},{8,9},{9,8},{10,11... | collective-permute-start | bytes 3440648 | tf_op jit(solution)/shard_map/ppermute | solution.py:762
  17.4 19.2 %collective-permute-start.10 = (bf16[560,512]{1,0:T(8,128)(2,1)S(1)}, bf16[560,512]{1,0:T(8,128)(2,1)S(1)}, u32[]{:S(2)}, u32[]{:S(2)}) collective-permute-start(bf16[560,512]{1,0:T(8,128)(2,1)S(1)} %get-tuple-element.101), channel_id=1, source_target_pairs={{0,2},{1,3},{2,0},{3,1},{4,6},{5,7},{6,4},{7,5},{8,10},{9,11},{10,... | collective-permute-start | bytes 1720328 | tf_op jit(solution)/shard_map/ppermute | solution.py:766
  18.9 26.2 %copy-start.1 = (bf16[2240,512]{1,0:T(8,128)(2,1)S(1)}, bf16[2240,512]{1,0:T(8,128)(2,1)}, u32[]{:S(2)}) copy-start(bf16[2240,512]{1,0:T(8,128)(2,1)} %weights.3) | copy-start | bytes 6881284
  31.3 5.3 %collective-permute-start.5 = (bf16[2,128,256]{2,1,0:T(8,128)(2,1)S(1)}, bf16[2,128,256]{2,1,0:T(8,128)(2,1)S(1)}, u32[]{:S(2)}, u32[]{:S(2)}) collective-permute-start(bf16[2,128,256]{2,1,0:T(8,128)(2,1)S(1)} %get-tuple-element.87), channel_id=1, source_target_pairs={{0,4},{4,0},{8,12},{12,8},{16,20},{20,16},{24,28},{28,24},{1,5},{5... | collective-permute-start | bytes 393224 | tf_op jit(solution)/shard_map/ppermute | solution.py:770
  36.6 26.7 %collective-permute-start.12 = (bf16[1120,512]{1,0:T(8,128)(2,1)S(1)}, bf16[1120,512]{1,0:T(8,128)(2,1)S(1)}, u32[]{:S(2)}, u32[]{:S(2)}) collective-permute-start(bf16[1120,512]{1,0:T(8,128)(2,1)S(1)} %get-tuple-element.104), channel_id=1, source_target_pairs={{0,3},{1,2},{2,1},{3,0},{4,7},{5,6},{6,5},{7,4},{8,11},{9,10},{10,... | collective-permute-start | bytes 3440648 | tf_op jit(solution)/shard_map/ppermute | solution.py:866
  37.3 21.3 %collective-permute-start.11 = (bf16[560,512]{1,0:T(8,128)(2,1)S(1)}, bf16[560,512]{1,0:T(8,128)(2,1)S(1)}, u32[]{:S(2)}, u32[]{:S(2)}) collective-permute-start(bf16[560,512]{1,0:T(8,128)(2,1)S(1)} %collective-permute-done.10.refs_2_), channel_id=1, source_target_pairs={{0,4},{4,0},{8,12},{12,8},{16,20},{20,16},{24,28},{28,24},{1,5},{5... | collective-permute-start | bytes 1720328 | tf_op jit(solution)/shard_map/ppermute | solution.py:770
  38.9 11.0 %collective-permute-start.6 = (bf16[2,128,256]{2,1,0:T(8,128)(2,1)S(1)}, bf16[2,128,256]{2,1,0:T(8,128)(2,1)S(1)}, u32[]{:S(2)}, u32[]{:S(2)}) collective-permute-start(bf16[2,128,256]{2,1,0:T(8,128)(2,1)S(1)} %get-tuple-element.92), channel_id=1, source_target_pairs={{0,24},{4,28},{1,25},{5,29},{2,26},{6,30},{3,27},{7,31}} | collective-permute-start | bytes 393224 | tf_op jit(solution)/shard_map/ppermute | solution.py:774
  39.6 12.3 %collective-permute-start.7 = (bf16[2,128,256]{2,1,0:T(8,128)(2,1)S(1)}, bf16[2,128,256]{2,1,0:T(8,128)(2,1)S(1)}, u32[]{:S(2)}, u32[]{:S(2)}) collective-permute-start(bf16[2,128,256]{2,1,0:T(8,128)(2,1)S(1)} %get-tuple-element.92), channel_id=1, source_target_pairs={{0,16},{4,20},{8,24},{12,28},{1,17},{5,21},{9,25},{13,29},{2,18},{... | collective-permute-start | bytes 393224 | tf_op jit(solution)/shard_map/ppermute | solution.py:774
  40.9 16.0 %collective-permute-start.8 = (bf16[2,128,256]{2,1,0:T(8,128)(2,1)S(1)}, bf16[2,128,256]{2,1,0:T(8,128)(2,1)S(1)}, u32[]{:S(2)}, u32[]{:S(2)}) collective-permute-start(bf16[2,128,256]{2,1,0:T(8,128)(2,1)S(1)} %get-tuple-element.92), channel_id=1, source_target_pairs={{0,8},{4,12},{8,16},{12,20},{16,24},{20,28},{1,9},{5,13},{9,17},{1... | collective-permute-start | bytes 393224 | tf_op jit(solution)/shard_map/ppermute | solution.py:774
  47.0 16.3 %copy-start.5 = (bf16[128]{0:T(256)(128)(2,1)S(1)}, bf16[128]{0:T(256)(128)(2,1)}, u32[]{:S(2)}) copy-start(bf16[128]{0:T(256)(128)(2,1)} %param.22) | copy-start | bytes 772
  49.9 28.1 %copy-start = (bf16[512,2240]{0,1:T(8,128)(2,1)S(1)}, bf16[512,2240]{0,1:T(8,128)(2,1)}, u32[]{:S(2)}) copy-start(bf16[512,2240]{0,1:T(8,128)(2,1)} %param.23) | copy-start | bytes 6881284
  58.0 5.3 %collective-permute-start.9 = (bf16[2,128,128]{2,1,0:T(8,128)(2,1)S(1)}, bf16[2,128,128]{2,1,0:T(8,128)(2,1)S(1)}, u32[]{:S(2)}, u32[]{:S(2)}) collective-permute-start(bf16[2,128,128]{2,1,0:T(8,128)(2,1)S(1)} %get-tuple-element.100), channel_id=1, source_target_pairs={{0,4},{4,0},{8,12},{12,8},{16,20},{20,16},{24,28},{28,24},{1,5},{5... | collective-permute-start | bytes 196616 | tf_op jit(solution)/shard_map/ppermute | solution.py:770
  64.4 9.3 %collective-permute-start.14 = (bf16[256,512]{1,0:T(8,128)(2,1)S(1)}, bf16[256,512]{1,0:T(8,128)(2,1)S(1)}, u32[]{:S(2)}, u32[]{:S(2)}) collective-permute-start(bf16[256,512]{1,0:T(8,128)(2,1)S(1)} %get-tuple-element.109.own), channel_id=1, source_target_pairs={{0,2},{1,3},{2,0},{3,1},{4,6},{5,7},{6,4},{7,5},{8,10},{9,11},{10,... | collective-permute-start | bytes 786440 | tf_op jit(solution)/shard_map/ppermute | solution.py:766
  65.8 12.2 %collective-permute-start.18 = (bf16[256,512]{1,0:T(8,128)(2,1)S(1)}, bf16[256,512]{1,0:T(8,128)(2,1)S(1)}, u32[]{:S(2)}, u32[]{:S(2)}) collective-permute-start(bf16[256,512]{1,0:T(8,128)(2,1)S(1)} %get-tuple-element.116.own), channel_id=1, source_target_pairs={{0,2},{1,3},{2,0},{3,1},{4,6},{5,7},{6,4},{7,5},{8,10},{9,11},{10,... | collective-permute-start | bytes 786440 | tf_op jit(solution)/shard_map/ppermute | solution.py:766
  66.5 11.5 %collective-permute-start.13 = (bf16[256,512]{1,0:T(8,128)(2,1)S(1)}, bf16[256,512]{1,0:T(8,128)(2,1)S(1)}, u32[]{:S(2)}, u32[]{:S(2)}) collective-permute-start(bf16[256,512]{1,0:T(8,128)(2,1)S(1)} %get-tuple-element.109.own), channel_id=1, source_target_pairs={{0,1},{1,0},{2,3},{3,2},{4,5},{5,4},{6,7},{7,6},{8,9},{9,8},{10,11... | collective-permute-start | bytes 786440 | tf_op jit(solution)/shard_map/ppermute | solution.py:762
  73.7 4.3 %collective-permute-start.15 = (bf16[256,512]{1,0:T(8,128)(2,1)S(1)}, bf16[256,512]{1,0:T(8,128)(2,1)S(1)}, u32[]{:S(2)}, u32[]{:S(2)}) collective-permute-start(bf16[256,512]{1,0:T(8,128)(2,1)S(1)} %collective-permute-done.14.refs_0_), channel_id=1, source_target_pairs={{0,1},{1,0},{2,3},{3,2},{4,5},{5,4},{6,7},{7,6},{8,9},{9,8},{10,11... | collective-permute-start | bytes 786440 | tf_op jit(solution)/shard_map/ppermute | solution.py:762
  73.7 6.8 %collective-permute-start.17 = (bf16[256,512]{1,0:T(8,128)(2,1)S(1)}, bf16[256,512]{1,0:T(8,128)(2,1)S(1)}, u32[]{:S(2)}, u32[]{:S(2)}) collective-permute-start(bf16[256,512]{1,0:T(8,128)(2,1)S(1)} %get-tuple-element.116.own), channel_id=1, source_target_pairs={{0,1},{1,0},{2,3},{3,2},{4,5},{5,4},{6,7},{7,6},{8,9},{9,8},{10,11... | collective-permute-start | bytes 786440 | tf_op jit(solution)/shard_map/ppermute | solution.py:762
  78.0 2.6 %collective-permute-start.19 = (bf16[256,512]{1,0:T(8,128)(2,1)S(1)}, bf16[256,512]{1,0:T(8,128)(2,1)S(1)}, u32[]{:S(2)}, u32[]{:S(2)}) collective-permute-start(bf16[256,512]{1,0:T(8,128)(2,1)S(1)} %collective-permute-done.18.refs_0_), channel_id=1, source_target_pairs={{0,1},{1,0},{2,3},{3,2},{4,5},{5,4},{6,7},{7,6},{8,9},{9,8},{10,11... | collective-permute-start | bytes 786440 | tf_op jit(solution)/shard_map/ppermute | solution.py:762
  78.0 4.6 %slice-start.2 = ((s8[6307840]{0:T(1024)(128)(4,1)}), s8[4194304]{0:T(1024)(128)(4,1)S(1)}, s32[]{:S(2)}) async-start(s8[6307840]{0:T(1024)(128)(4,1)} %bitcast.30), calls=%async_computation.2 | async-start | bytes 8388608
  80.0 2.6 %slice-start.3 = ((s8[6307840]{0:T(1024)(128)(4,1)}), s8[2113536]{0:T(1024)(128)(4,1)S(1)}, s32[]{:S(2)}) async-start(s8[6307840]{0:T(1024)(128)(4,1)} %bitcast.30), calls=%async_computation.3 | async-start | bytes 4227072
  80.0 2.6 %collective-permute-start.16 = (bf16[1120,256]{1,0:T(8,128)(2,1)S(1)}, bf16[1120,256]{1,0:T(8,128)(2,1)S(1)}, u32[]{:S(2)}, u32[]{:S(2)}) collective-permute-start(bf16[1120,256]{1,0:T(8,128)(2,1)S(1)} %attend.2.own), channel_id=1, source_target_pairs={{0,1},{1,0},{2,3},{3,2},{4,5},{5,4},{6,7},{7,6},{8,9},{9,8},{10,11... | collective-permute-start | bytes 1720328 | tf_op jit(solution)/shard_map/ppermute | solution.py:762
  82.5 3.6 %collective-permute-start.20 = (bf16[1120,256]{1,0:T(8,128)(2,1)S(1)}, bf16[1120,256]{1,0:T(8,128)(2,1)S(1)}, u32[]{:S(2)}, u32[]{:S(2)}) collective-permute-start(bf16[1120,256]{1,0:T(8,128)(2,1)S(1)} %attend.3.own), channel_id=1, source_target_pairs={{0,1},{1,0},{2,3},{3,2},{4,5},{5,4},{6,7},{7,6},{8,9},{9,8},{10,11... | collective-permute-start | bytes 1720328 | tf_op jit(solution)/shard_map/ppermute | solution.py:762
  82.6 12.2 %slice-start = ((s8[6307840]{0:T(1024)(128)(4,1)}), s8[4194304]{0:T(1024)(128)(4,1)S(1)}, s32[]{:S(2)}) async-start(s8[6307840]{0:T(1024)(128)(4,1)} %bitcast.25), calls=%async_computation | async-start | bytes 8388608
  86.1 8.8 %slice-start.1 = ((s8[6307840]{0:T(1024)(128)(4,1)}), s8[2113536]{0:T(1024)(128)(4,1)S(1)}, s32[]{:S(2)}) async-start(s8[6307840]{0:T(1024)(128)(4,1)} %bitcast.25), calls=%async_computation.1 | async-start | bytes 4227072
  92.5 2.4 %collective-permute-start.21 = (bf16[1400,256]{1,0:T(8,128)(2,1)S(1)}, bf16[1400,256]{1,0:T(8,128)(2,1)S(1)}, u32[]{:S(2)}, u32[]{:S(2)}) collective-permute-start(bf16[1400,256]{1,0:T(8,128)(2,1)S(1)} %activate.2.own.own_b), channel_id=1, source_target_pairs={{0,1},{1,0},{2,3},{3,2},{4,5},{5,4},{6,7},{7,6},{8,9},{9,8},{10,11... | collective-permute-start | bytes 2150408 | tf_op jit(solution)/shard_map/ppermute | solution.py:762
  96.5 10.7 %collective-permute-start.24 = (bf16[560,256]{1,0:T(8,128)(2,1)S(1)}, bf16[560,256]{1,0:T(8,128)(2,1)S(1)}, u32[]{:S(2)}, u32[]{:S(2)}) collective-permute-start(bf16[560,256]{1,0:T(8,128)(2,1)S(1)} %far_project.2), channel_id=1, source_target_pairs={{0,2},{1,3},{2,0},{3,1},{4,6},{5,7},{6,4},{7,5},{8,10},{9,11},{10,... | collective-permute-start | bytes 860168 | tf_op jit(solution)/shard_map/ppermute | solution.py:766
  98.3 7.0 %collective-permute-start.22 = (bf16[1,1400]{1,0:T(2,128)(2,1)S(1)}, bf16[1,1400]{1,0:T(2,128)(2,1)S(1)}, u32[]{:S(2)}, u32[]{:S(2)}) collective-permute-start(bf16[1,1400]{1,0:T(2,128)(2,1)S(1)} %get-tuple-element.122), channel_id=1, source_target_pairs={{0,4},{4,8},{8,12},{12,16},{16,20},{20,24},{24,28},{1,5},{5,9},{9,... | collective-permute-start | bytes 8408 | tf_op jit(solution)/shard_map/ppermute | solution.py:911
  101.7 5.5 %collective-permute-start.23 = (bf16[1,1400]{1,0:T(2,128)(2,1)S(1)}, bf16[1,1400]{1,0:T(2,128)(2,1)S(1)}, u32[]{:S(2)}, u32[]{:S(2)}) collective-permute-start(bf16[1,1400]{1,0:T(2,128)(2,1)S(1)} %get-tuple-element.123), channel_id=1, source_target_pairs={{4,0},{8,4},{12,8},{16,12},{20,16},{24,20},{28,24},{5,1},{9,5},{13... | collective-permute-start | bytes 8408 | tf_op jit(solution)/shard_map/ppermute | solution.py:912
  109.5 2.3 %collective-permute-start.25 = (bf16[1400,256]{1,0:T(8,128)(2,1)S(1)}, bf16[1400,256]{1,0:T(8,128)(2,1)S(1)}, u32[]{:S(2)}, u32[]{:S(2)}) collective-permute-start(bf16[1400,256]{1,0:T(8,128)(2,1)S(1)} %activate.3.own.own_a), channel_id=1, source_target_pairs={{0,1},{1,0},{2,3},{3,2},{4,5},{5,4},{6,7},{7,6},{8,9},{9,8},{10,11... | collective-permute-start | bytes 2150408 | tf_op jit(solution)/shard_map/ppermute | solution.py:762
  113.3 8.9 %collective-permute-start.26 = (bf16[560,256]{1,0:T(8,128)(2,1)S(1)}, bf16[560,256]{1,0:T(8,128)(2,1)S(1)}, u32[]{:S(2)}, u32[]{:S(2)}) collective-permute-start(bf16[560,256]{1,0:T(8,128)(2,1)S(1)} %far_project.3.after), channel_id=1, source_target_pairs={{0,2},{1,3},{2,0},{3,1},{4,6},{5,7},{6,4},{7,5},{8,10},{9,11},{10,... | collective-permute-start | bytes 860168 | tf_op jit(solution)/shard_map/ppermute | solution.py:766

commit v8 on v6

--- a/solution.py
+++ b/solution.py
@@ -457,7 +457,7 @@
     )(query, keys, erased, entry, totals, after)
 
 
-def pair_kernel(meta, own, other, after, pair, first, done):
+def pair_kernel(meta, own, other, pair, first, done):
     even = meta[PARITY] == 0
     for h in range(own.shape[0]):
         mine, theirs = own[h], other[h]
@@ -470,15 +470,15 @@
     done[...] = jnp.zeros_like(done)
 
 
-def pair_maps(meta, own, other, after):
+def pair_maps(meta, own, other):
     return pl.pallas_call(
         pair_kernel,
         out_shape=(shape_of(own.shape), shape_of(own.shape), shape_of((8, 128), f32)),
-        in_specs=[SM, VM, VM, ANY],
+        in_specs=[SM, VM, VM],
         out_specs=[VM] * 3,
         compiler_params=params(4),
         name="pair_maps",
-    )(meta, own, other, after)
+    )(meta, own, other)
 
 
 def apply_map(whole, state):
@@ -580,7 +580,9 @@
     )(meta, tokens, own, partner, weights, partner_weights, *far)
 
 
-def up_kernel(meta, own, other, gain, weights, lifted, middle_part, first, last, middle, hidden, scale_b):
+def up_kernel(
+    meta, own, other, gain, weights, lifted, middle_part, near_row, next_row, middle, hidden, scale_b
+):
     features, count = middle.shape
     half = features // 2
     step = 160
@@ -602,8 +604,10 @@
         cols = slice(start, start + size)
         scale = doubled(scale_b[...])[:, :size]
         lifted[:, cols] = (dot(hidden[...], weights[:, cols]) * scale).astype(bf16)
-    first[...] = lifted[0:1, :]
-    last[...] = lifted[count - 1 : count, :]
+    even = meta[PARITY] == 0
+    first, last = lifted[0:1, :], lifted[count - 1 : count, :]
+    near_row[...] = jnp.where(even, last, first)
+    next_row[...] = jnp.where(even, first, last)
 
 
 def up_project(meta, own, other, gain, weights, part):
@@ -635,15 +639,16 @@
     return 0.5 * x * (1.0 + jnp.tanh(inner))
 
 
-def act_kernel(late, meta, outer, inside, before, after, taps, act_t, padded, act):
+def act_kernel(late, meta, outer, inside, near_row, next_row, taps, act_t, padded, act):
     count = act.shape[0]
+    even = meta[PARITY] == 0
     if late:
         padded[7:8, :] = inside[BLOCK - 1 : BLOCK, :].astype(f32)
         padded[8 : 8 + BLOCK, :] = inside[BLOCK:, :].astype(f32)
         padded[8 + BLOCK : 8 + count, :] = outer[BLOCK:, :].astype(f32)
-        padded[8 + count : 9 + count, :] = after[...].astype(f32)
+        padded[8 + count : 9 + count, :] = jnp.where(even, near_row[...], next_row[...]).astype(f32)
     else:
-        padded[7:8, :] = before[...].astype(f32)
+        padded[7:8, :] = jnp.where(even, next_row[...], near_row[...]).astype(f32)
         padded[8 : 8 + BLOCK, :] = outer[:BLOCK, :].astype(f32)
         padded[8 + BLOCK : 8 + count, :] = inside[:BLOCK, :].astype(f32)
         padded[8 + count : 9 + count, :] = inside[BLOCK : BLOCK + 1, :].astype(f32)
@@ -662,7 +667,7 @@
     act_t[...] = act[...].T
 
 
-def activate(meta, outer, inside, before, after, taps, late):
+def activate(meta, outer, inside, near_row, next_row, taps, late):
     hidden = outer.shape[1]
     count = (outer.shape[0] + inside.shape[0]) // 2
     return pl.pallas_call(
@@ -674,7 +679,7 @@
         compiler_params=params(8),
         cost_estimate=cost(10**9, 2 * 10**6),
         name="activate",
-    )(meta, outer, inside, before, after, taps)
+    )(meta, outer, inside, near_row, next_row, taps)
 
 
 def far_kernel(ys, meta, own, other, weights, other_weights, *outs):
@@ -824,31 +829,29 @@
     sent_w_down, their_rows, my_rows = sent
     other_w_down = core_swap(sent_w_down, n)
     fetched = [y_shift(my_rows, n, d) for d in range(1, ys)]
-    partner_w_out = core_swap(their_rows, n)
-    acc_query, partner_w_out, other_w_down = lax.optimization_barrier(
-        (early[2], partner_w_out, other_w_down)
-    )
-    their_rows, fetched, _ = lax.optimization_barrier((their_rows, fetched, totals))
     diagonal = [
         lax.ppermute(their_rows, "head", [(i, ((i + 2 * d) % n) ^ 1) for i in range(n)])
         for d in range(1, ys)
     ]
-
+    partner_w_out = core_swap(their_rows, n)
     other_maps = pair_swap(sent_maps, seqs)
-    query, tokens_a, tokens_b, query_done = queries(
+    pair, first, done = pair_maps(meta, own_maps, other_maps)
+    pairs = [later(pair, seqs, d) for d in range(seqs // 2 - 1, 0, -1)]
+    acc_query, partner_w_out, other_w_down, _ = lax.optimization_barrier(
+        (early[2], partner_w_out, other_w_down, done)
+    )
+    query, tokens_a, tokens_b, _ = queries(
         meta, ys, scaled, scale_b, w_query, acc_query, sum(groups, [])
     )
-    pair, first, done = pair_maps(meta, own_maps, other_maps, query_done)
-    fetched, _ = lax.optimization_barrier((fetched, done))
-    swapped = [pair_swap(value, seqs) for value in fetched]
-    pairs = [later(pair, seqs, d) for d in range(seqs // 2 - 1, 0, -1)]
     shard_query, free, out_done = block_outputs(query, keys, erased, entry, totals, done)
     kept_state, given_state = start_states(meta, first, pairs, out_done)
     other_state = pair_swap(given_state, seqs)
 
-    other_state, swapped, diagonal = lax.optimization_barrier((other_state, swapped, diagonal))
     mixed = mixed_heads(meta, kept_state, other_state, shard_query, free, head_scale)
     far_mixed = [[y_shift(value, n, d) for d in range(1, ys)] for value in mixed]
+
+    fetched, _ = lax.optimization_barrier((fetched, mixed))
+    swapped = [pair_swap(value, seqs) for value in fetched]
 
     def middle_of(i, far):
         heads_far = [[value, core_swap(value, n)] for value in far]
@@ -861,17 +864,19 @@
         )
 
     middle = middle_of(0, far_mixed[0])
-    outer, middle_a, first_row, last_row = up_project(
+    outer, middle_a, near_row, next_row = up_project(
         meta, middle, core_swap(middle, n), ffn_scale, w_up, part
     )
-    before = lax.ppermute(last_row, "seq", [(i, i + 1) for i in range(seqs - 1)])
-    after = lax.ppermute(first_row, "seq", [(i + 1, i) for i in range(seqs - 1)])
+    near_row = lax.ppermute(near_row, "seq", [(i, i ^ 1) for i in range(seqs)])
+    next_row = lax.ppermute(
+        next_row, "seq", [(i, ((i + 1) ^ 1) - 1) for i in range(1, seqs - 1)]
+    )
     middle = middle_of(1, far_mixed[1])
     inside, middle_b, _, _ = up_project(
         meta, middle, core_swap(middle, n), ffn_scale, w_up, part
     )
 
-    acts = [activate(meta, outer, inside, before, after, taps, late) for late in (False, True)]
+    acts = [activate(meta, outer, inside, near_row, next_row, taps, late) for late in (False, True)]
     partner_acts = [core_swap(act, n) for act in acts]
     fars = [
         far_project(meta, ys, act, partner, w_parts, other_w_down)

time: 119 us -> 127 us (1.067)
  waiting for transfers between devices: 36.9 us -> 47.8 us
  starting transfers between devices: 26.4 us -> 23.8 us
    ppermute x6, waiting for transfers between devices: 23.9 us -> 33.8 us  [y_shift(): lax.ppermute(value, 'head', [(i, (i + 2 * step) % n) for i in range(n)])]
    ppermute x1, waiting for transfers between devices: 3.62 us -> 0.01 us  [shards(): lax.ppermute(their_rows, 'head', [(i, (i + 2 * d) % n ^ 1) for i in range...]
    ppermute x3, waiting for transfers between devices: 3.09 us -> 6.01 us  [pair_swap(): return lax.ppermute(value, 'seq', [(i, i ^ 1) for i in range(n)])]
    ppermute x2, starting transfers between devices: 7.09 us -> 4.26 us  [the longest x1 3.44 us: shards(): lax.ppermute(next_row, 'seq', [(i, (i + 1 ^ 1) - 1) for i in range(1, seq...]
    ppermute x3, waiting for transfers between devices: 4.22 us -> 5.89 us  [later(): lax.ppermute(value, 'seq', [(i, i + 2 * step) for i in range(n - 2 * step)])]
  transfers between devices with their start and end apart: 27 -> 27, of which waited for: 11 -> 12; matrix products, arithmetic and copies ran while one was open for 4% -> 3% of each run, Pallas kernels for 39% -> 37%
where the time goes in v8:
time: 127 us; the launch traced here: 126 us
  Pallas kernels  48.9 us (39%)
  waiting for transfers between devices  47.8 us (38%)
  starting transfers between devices  23.8 us (19%)
  local copies, waits for them, and re-layouts  2.77 us (2%)
  other arithmetic  2.48 us (2%)
    ppermute x6, waiting for transfers between devices, y_shift(): lax.ppermute(value, 'head', [(i, (i + 2 * step) % n) for i in range(n)])  33.8 us
    pallas_call x1, Pallas kernels, block_maps(): pl.pallas_call(functools.partial(maps_kernel, n, heads, at), out_shape=(s...  12.3 us
    pallas_call x2, Pallas kernels, up_project(): pl.pallas_call(up_kernel, out_shape=(shape_of((count, hidden)), shape_of(...  7.55 us
    pallas_call x1, Pallas kernels, early_project(): pl.pallas_call(functools.partial(early_kernel, len(pieces), at), out_shap...  7.16 us
    ppermute x6, starting transfers between devices, y_shift(): lax.ppermute(value, 'head', [(i, (i + 2 * step) % n) for i in range(n)])  6.35 us
    ppermute x3, starting transfers between devices, later(): lax.ppermute(value, 'seq', [(i, i + 2 * step) for i in range(n - 2 * step)])  6.26 us
    ppermute x3, waiting for transfers between devices, pair_swap(): return lax.ppermute(value, 'seq', [(i, i ^ 1) for i in range(n)])  6.01 us
    ppermute x3, waiting for transfers between devices, later(): lax.ppermute(value, 'seq', [(i, i + 2 * step) for i in range(n - 2 * step)])  5.89 us
  transfers between devices with their start and end apart: 27, of which 12 were waited for; matrix products, arithmetic and copies ran while one was open for 3% of the time, Pallas kernels for 37%

profile of v8, /device:TPU:16, one launch (start us, length us, event | category | flops | bytes accessed | tf_op | source)
XLA Modules:
  0.0 126.0 jit_solution(14629660450173032556)
XLA Ops:
  0.0 1.6 %collective-permute-start = (bf16[560,512]{1,0:T(8,128)(2,1)}, bf16[560,512]{1,0:T(8,128)(2,1)S(1)}, u32[]{:S(2)}, u32[]{:S(2)}) collective-permute-start(bf16[560,512]{1,0:T(8,128)(2,1)} %bitcast.37), channel_id=1, source_target_pairs={{0,2},{1,3},{2,0},{3,1},{4,6},{5,7},{6,4},{7,5},{8,10},{9,11},{10,... | collective-permute-start | bytes 1720328 | tf_op jit(solution)/shard_map/ppermute | solution.py:736
  1.6 0.8 fusion.3
  2.5 0.8 reshape.37
  3.3 0.7 convert_element_type.15.taps
  4.0 0.8 reshape.31
  4.7 0.7 reshape.39.gain
  5.8 7.2 %early_project.1 = (f32[512,512]{1,0:T(8,128)S(1)}, f32[512,512]{1,0:T(8,128)S(1)}, f32[512,512]{1,0:T(8,128)S(1)}, f32[16,512]{1,0:T(8,128)S(1)}, f32[8,512]{1,...) custom-call(s32[6]{0:T(128)S(1)} %stack.24.meta, ...), custom_call_target="tpu_custom_call" | custom-call | flops 3000000000 | bytes 8000000 | tf_op jit(solution)/shard_map/early_project/pallas_call | solution.py:163
  13.0 2.6 %collective-permute-done.refs_0_.refs_2_ = bf16[560,512]{1,0:T(8,128)(2,1)S(1)} collective-permute-done((bf16[560,512]{1,0:T(8,128)(2,1)}, bf16[560,512]{1,0:T(8,128)(2,1)S(1)}, u32[]{:S(2)}, u32[]{:S(2)}) %collective-permute-start) | collective-permute-done | bytes 573472 | tf_op jit(solution)/shard_map/ppermute | solution.py:736
  15.6 2.0 %collective-permute-done.2.refs_1_.refs_3_ = bf16[560,512]{1,0:T(8,128)(2,1)S(1)} collective-permute-done((bf16[560,512]{1,0:T(8,128)(2,1)S(1)}, bf16[560,512]{1,0:T(8,128)(2,1)S(1)}, u32[]{:S(2)}, u32[]{:S(2)}) %collective-permute-start.2) | collective-permute-done | bytes 573472 | tf_op jit(solution)/shard_map/ppermute | solution.py:732
  18.1 12.3 %block_maps.1 = (bf16[512,1120]{1,0:T(8,128)(2,1)S(1)}, f32[512,128]{1,0:T(8,128)S(1)}, bf16[512,512]{1,0:T(8,128)(2,1)S(1)}, bf16[512,1024]{1,0:T(8,128)(2,1)S(...) custom-call(s32[6]{0:T(128)S(1)} %stack.24.meta, ...), custom_call_target="tpu_custom_call" | custom-call | flops 10000000000 | bytes 14000000 | tf_op jit(solution)/shard_map/block_maps/pallas_call | solution.py:333
  30.4 1.6 %collective-permute-start.5 = (bf16[2,128,256]{2,1,0:T(8,128)(2,1)S(1)}, bf16[2,128,256]{2,1,0:T(8,128)(2,1)S(1)}, u32[]{:S(2)}, u32[]{:S(2)}) collective-permute-start(bf16[2,128,256]{2,1,0:T(8,128)(2,1)S(1)} %get-tuple-element.77), channel_id=1, source_target_pairs={{0,4},{4,0},{8,12},{12,8},{16,20},{20,16},{24,28},{28,24},{1,5},{5... | collective-permute-start | bytes 393224 | tf_op jit(solution)/shard_map/ppermute | solution.py:740
  32.0 1.0 collective-permute-start.15
  33.0 0.6 collective-permute-start.13
  33.6 2.5 %collective-permute-done.5.other = bf16[2,128,256]{2,1,0:T(8,128)(2,1)S(1)} collective-permute-done((bf16[2,128,256]{2,1,0:T(8,128)(2,1)S(1)}, bf16[2,128,256]{2,1,0:T(8,128)(2,1)S(1)}, u32[]{:S(2)}, u32[]{:S(2)}) %collective-permute-start.5) | collective-permute-done | bytes 131104 | tf_op jit(solution)/shard_map/ppermute | solution.py:740
  36.0 0.7 pair_maps.1
  36.8 0.7 collective-permute-start.6
  37.5 1.3 %collective-permute-start.7 = (bf16[2,128,256]{2,1,0:T(8,128)(2,1)S(1)}, bf16[2,128,256]{2,1,0:T(8,128)(2,1)S(1)}, u32[]{:S(2)}, u32[]{:S(2)}) collective-permute-start(bf16[2,128,256]{2,1,0:T(8,128)(2,1)S(1)} %get-tuple-element.82), channel_id=1, source_target_pairs={{0,16},{4,20},{8,24},{12,28},{1,17},{5,21},{9,25},{13,29},{2,18},{... | collective-permute-start | bytes 393224 | tf_op jit(solution)/shard_map/ppermute | solution.py:744
  38.8 4.3 %collective-permute-start.8 = (bf16[2,128,256]{2,1,0:T(8,128)(2,1)S(1)}, bf16[2,128,256]{2,1,0:T(8,128)(2,1)S(1)}, u32[]{:S(2)}, u32[]{:S(2)}) collective-permute-start(bf16[2,128,256]{2,1,0:T(8,128)(2,1)S(1)} %get-tuple-element.82), channel_id=1, source_target_pairs={{0,8},{4,12},{8,16},{12,20},{16,24},{20,28},{1,9},{5,13},{9,17},{1... | collective-permute-start | bytes 393224 | tf_op jit(solution)/shard_map/ppermute | solution.py:744
  43.1 1.9 %queries.1 = (bf16[512,512]{1,0:T(8,128)(2,1)S(1)}, bf16[2240,256]{1,0:T(8,128)(2,1)S(1)}, bf16[2240,256]{1,0:T(8,128)(2,1)S(1)}, f32[8,128]{1,0:T(8,128)}) custom-call(s32[6]{0:T(128)S(1)} %stack.24.meta, bf16[512,1120]{1,0:T(8,128)(2,1)S(1)} %get-tuple-element.68.scaled, f32[512,128]{1,0:T(8,128)S(1)} %get-tuple-element.69.scale_b, ...), custom_call_target="tpu_custom_call" | custom-call | flops 1000000000 | bytes 8000000 | tf_op jit(solution)/shard_map/queries/pallas_call | solution.py:397
  45.0 2.8 %block_outputs.1 = (bf16[512,512]{1,0:T(8,128)(2,1)S(1)}, f32[512,512]{1,0:T(8,128)S(1)}, f32[8,128]{1,0:T(8,128)S(1)}) custom-call(bf16[512,512]{1,0:T(8,128)(2,1)S(1)} %get-tuple-element.83.query, bf16[512,512]{1,0:T(8,128)(2,1)S(1)} %get-tuple-element.84.keys, bf16[512,1024]{1,0:T(8,128)(2,1)S(1)} %get-tuple-element.85.erased, ...), custom_call_target="tpu_custom_call" | custom-call | flops 3000000000 | bytes 4000000 | tf_op jit(solution)/shard_map/block_outputs/pallas_call | solution.py:448
  47.8 1.7 %collective-permute-done.7.refs_1_ = bf16[2,128,256]{2,1,0:T(8,128)(2,1)S(1)} collective-permute-done((bf16[2,128,256]{2,1,0:T(8,128)(2,1)S(1)}, bf16[2,128,256]{2,1,0:T(8,128)(2,1)S(1)}, u32[]{:S(2)}, u32[]{:S(2)}) %collective-permute-start.7) | collective-permute-done | bytes 131104 | tf_op jit(solution)/shard_map/ppermute | solution.py:744
  49.6 4.2 %collective-permute-done.8.refs_2_ = bf16[2,128,256]{2,1,0:T(8,128)(2,1)S(1)} collective-permute-done((bf16[2,128,256]{2,1,0:T(8,128)(2,1)S(1)}, bf16[2,128,256]{2,1,0:T(8,128)(2,1)S(1)}, u32[]{:S(2)}, u32[]{:S(2)}) %collective-permute-start.8) | collective-permute-done | bytes 131104 | tf_op jit(solution)/shard_map/ppermute | solution.py:744
  53.7 1.2 start_states.1
  54.9 1.6 %collective-permute-start.9 = (bf16[2,128,128]{2,1,0:T(8,128)(2,1)S(1)}, bf16[2,128,128]{2,1,0:T(8,128)(2,1)S(1)}, u32[]{:S(2)}, u32[]{:S(2)}) collective-permute-start(bf16[2,128,128]{2,1,0:T(8,128)(2,1)S(1)} %get-tuple-element.90), channel_id=1, source_target_pairs={{0,4},{4,0},{8,12},{12,8},{16,20},{20,16},{24,28},{28,24},{1,5},{5... | collective-permute-start | bytes 196616 | tf_op jit(solution)/shard_map/ppermute | solution.py:740
  56.5 2.8 %collective-permute-done.9.other = bf16[2,128,128]{2,1,0:T(8,128)(2,1)S(1)} collective-permute-done((bf16[2,128,128]{2,1,0:T(8,128)(2,1)S(1)}, bf16[2,128,128]{2,1,0:T(8,128)(2,1)S(1)}, u32[]{:S(2)}, u32[]{:S(2)}) %collective-permute-start.9) | collective-permute-done | bytes 65568 | tf_op jit(solution)/shard_map/ppermute | solution.py:740
  59.3 1.1 mixed_heads.1
  60.4 11.5 %collective-permute-done.13.refs_2_ = bf16[560,512]{1,0:T(8,128)(2,1)S(1)} collective-permute-done((bf16[560,512]{1,0:T(8,128)(2,1)S(1)}, bf16[560,512]{1,0:T(8,128)(2,1)S(1)}, u32[]{:S(2)}, u32[]{:S(2)}) %collective-permute-start.13) | collective-permute-done | bytes 573472 | tf_op jit(solution)/shard_map/ppermute | solution.py:736
  72.4 1.5 %collective-permute-start.11 = (bf16[256,512]{1,0:T(8,128)(2,1)S(1)}, bf16[256,512]{1,0:T(8,128)(2,1)S(1)}, u32[]{:S(2)}, u32[]{:S(2)}) collective-permute-start(bf16[256,512]{1,0:T(8,128)(2,1)S(1)} %get-tuple-element.94.own), channel_id=1, source_target_pairs={{0,2},{1,3},{2,0},{3,1},{4,6},{5,7},{6,4},{7,5},{8,10},{9,11},{10,... | collective-permute-start | bytes 786440 | tf_op jit(solution)/shard_map/ppermute | solution.py:736
  74.4 7.2 %collective-permute-done.11.refs_0_ = bf16[256,512]{1,0:T(8,128)(2,1)S(1)} collective-permute-done((bf16[256,512]{1,0:T(8,128)(2,1)S(1)}, bf16[256,512]{1,0:T(8,128)(2,1)S(1)}, u32[]{:S(2)}, u32[]{:S(2)}) %collective-permute-start.11) | collective-permute-done | bytes 262176 | tf_op jit(solution)/shard_map/ppermute | solution.py:736
  82.1 3.9 %collective-permute-done.18.refs_0_ = bf16[256,512]{1,0:T(8,128)(2,1)S(1)} collective-permute-done((bf16[256,512]{1,0:T(8,128)(2,1)S(1)}, bf16[256,512]{1,0:T(8,128)(2,1)S(1)}, u32[]{:S(2)}, u32[]{:S(2)}) %collective-permute-start.18) | collective-permute-done | bytes 262176 | tf_op jit(solution)/shard_map/ppermute | solution.py:736
  86.0 0.8 collective-permute-done.14.refs_3_
  86.8 1.9 %attend.2.own = bf16[1120,256]{1,0:T(8,128)(2,1)S(1)} custom-call(s32[6]{0:T(128)S(1)} %stack.24.meta, bf16[2240,256]{1,0:T(8,128)(2,1)S(1)} %get-tuple-element.80.tokens, bf16[256,512]{1,0:T(8,128)(2,1)S(1)} %get-tuple-element.94.own, bf16[256,512]{1,0:T(8,128)(2,1)S(1)} %collective-permute-done.10.partner, bf16[2240,512]{1,0:T(8,128)(2,1)S(1)} %bitcast.34, ...), custom_call_target="tpu_custom_call" | custom-call | flops 2000000000 | bytes 7000000 | tf_op jit(solution)/shard_map/attend/pallas_call | solution.py:572
  88.8 1.9 %attend.3.own = bf16[1120,256]{1,0:T(8,128)(2,1)S(1)} custom-call(s32[6]{0:T(128)S(1)} %stack.24.meta, bf16[2240,256]{1,0:T(8,128)(2,1)S(1)} %get-tuple-element.101.tokens, bf16[256,512]{1,0:T(8,128)(2,1)S(1)} %get-tuple-element.97.own, bf16[256,512]{1,0:T(8,128)(2,1)S(1)} %collective-permute-done.17.partner, bf16[2240,512]{1,0:T(8,128)(2,1)S(1)} %bitcast.35, ...), custom_call_target="tpu_custom_call" | custom-call | flops 2000000000 | bytes 7000000 | tf_op jit(solution)/shard_map/attend/pallas_call | solution.py:572
  90.8 0.5 collective-permute-start.20
  91.3 3.5 %up_project.2 = (bf16[256,1400]{1,0:T(8,128)(2,1)S(1)}, f32[560,256]{1,0:T(8,128)S(1)}, bf16[1,1400]{1,0:T(2,128)(2,1)S(1)}, bf16[1,1400]{1,0:T(2,128)(2,1)S(1)}) custom-call(s32[6]{0:T(128)S(1)} %stack.24.meta, bf16[1120,256]{1,0:T(8,128)(2,1)S(1)} %attend.2.own, bf16[1120,256]{1,0:T(8,128)(2,1)S(1)} %collective-permute-done.16.other, ...), custom_call_target="tpu_custom_call" | custom-call | flops 2000000000 | bytes 8000000 | tf_op jit(solution)/shard_map/up_project/pallas_call | solution.py:616
  94.8 0.8 collective-permute-start.21
  95.6 3.4 %collective-permute-start.22 = (bf16[1,1400]{1,0:T(2,128)(2,1)S(1)}, bf16[1,1400]{1,0:T(2,128)(2,1)S(1)}, u32[]{:S(2)}, u32[]{:S(2)}) collective-permute-start(bf16[1,1400]{1,0:T(2,128)(2,1)S(1)} %get-tuple-element.104), channel_id=1, source_target_pairs={{4,8},{8,4},{12,16},{16,12},{20,24},{24,20},{5,9},{9,5},{13,17},{1... | collective-permute-start | bytes 8408 | tf_op jit(solution)/shard_map/ppermute | solution.py:871
  99.1 4.1 %up_project.3 = (bf16[256,1400]{1,0:T(8,128)(2,1)S(1)}, f32[560,256]{1,0:T(8,128)S(1)}, bf16[1,1400]{1,0:T(2,128)(2,1)}, bf16[1,1400]{1,0:T(2,128)(2,1)}) custom-call(s32[6]{0:T(128)S(1)} %stack.24.meta, bf16[1120,256]{1,0:T(8,128)(2,1)S(1)} %attend.3.own, bf16[1120,256]{1,0:T(8,128)(2,1)S(1)} %collective-permute-done.20.other, f32[1,2240]{1,0:T(1,128)S(1)} %reshape.39.gain, ...), custom_call_target="tpu_custom_call" | custom-call | flops 2000000000 | bytes 8000000 | tf_op jit(solution)/shard_map/up_project/pallas_call | solution.py:616
  103.2 2.3 %activate.2.own_a.own = bf16[1400,256]{1,0:T(8,128)(2,1)S(1)} custom-call(s32[6]{0:T(128)S(1)} %stack.24.meta, bf16[256,1400]{1,0:T(8,128)(2,1)S(1)} %get-tuple-element.100.outer, bf16[256,1400]{1,0:T(8,128)(2,1)S(1)} %get-tuple-element.102.inside, bf16[1,1400]{1,0:T(2,128)(2,1)S(1)} %collective-permute-done.21.near_row, ...), custom_call_target="tpu_custom_call" | custom-call | flops 1000000000 | bytes 2000000 | tf_op jit(solution)/shard_map/activate/pallas_call | solution.py:673
  105.6 2.3 %activate.3.own.own_b = bf16[1400,256]{1,0:T(8,128)(2,1)S(1)} custom-call(s32[6]{0:T(128)S(1)} %stack.24.meta, bf16[256,1400]{1,0:T(8,128)(2,1)S(1)} %get-tuple-element.100.outer, bf16[256,1400]{1,0:T(8,128)(2,1)S(1)} %get-tuple-element.102.inside, bf16[1,1400]{1,0:T(2,128)(2,1)S(1)} %collective-permute-done.21.near_row, ...), custom_call_target="tpu_custom_call" | custom-call | flops 1000000000 | bytes 2000000 | tf_op jit(solution)/shard_map/activate/pallas_call | solution.py:673
  107.9 0.6 collective-permute-start.24
  108.4 1.6 %far_project.3 = bf16[560,256]{1,0:T(8,128)(2,1)S(1)} custom-call(s32[6]{0:T(128)S(1)} %stack.24.meta, bf16[1400,256]{1,0:T(8,128)(2,1)S(1)} %activate.2.own_a.own, bf16[1400,256]{1,0:T(8,128)(2,1)S(1)} %collective-permute-done.23.other_a.other, bf16[4,560,1400]{2,1,0:T(8,128)(2,1)S(1)} %bitcast.28, ...), custom_call_target="tpu_custom_call" | custom-call | flops 1000000000 | bytes 4000000 | tf_op jit(solution)/shard_map/far_project/pallas_call | solution.py:695
  110.0 1.6 %collective-permute-start.25 = (bf16[560,256]{1,0:T(8,128)(2,1)S(1)}, bf16[560,256]{1,0:T(8,128)(2,1)S(1)}, u32[]{:S(2)}, u32[]{:S(2)}) collective-permute-start(bf16[560,256]{1,0:T(8,128)(2,1)S(1)} %far_project.3), channel_id=1, source_target_pairs={{0,2},{1,3},{2,0},{3,1},{4,6},{5,7},{6,4},{7,5},{8,10},{9,11},{10,... | collective-permute-start | bytes 860168 | tf_op jit(solution)/shard_map/ppermute | solution.py:736
  111.7 1.6 %far_project.2.after = bf16[560,256]{1,0:T(8,128)(2,1)S(1)} custom-call(s32[6]{0:T(128)S(1)} %stack.24.meta, bf16[1400,256]{1,0:T(8,128)(2,1)S(1)} %activate.3.own.own_b, bf16[1400,256]{1,0:T(8,128)(2,1)S(1)} %collective-permute-done.24.other.other_b, bf16[4,560,1400]{2,1,0:T(8,128)(2,1)S(1)} %bitcast.29, ...), custom_call_target="tpu_custom_call" | custom-call | flops 1000000000 | bytes 4000000 | tf_op jit(solution)/shard_map/far_project/pallas_call | solution.py:695
  113.8 2.5 %near_project.1 = f32[560,512]{1,0:T(8,128)S(1)} custom-call(s32[6]{0:T(128)S(1)} %stack.24.meta, bf16[1400,256]{1,0:T(8,128)(2,1)S(1)} %activate.2.own_a.own, bf16[1400,256]{1,0:T(8,128)(2,1)S(1)} %collective-permute-done.23.other_a.other, bf16[1400,256]{1,0:T(8,128)(2,1)S(1)} %activate.3.own.own_b, ...), custom_call_target="tpu_custom_call" | custom-call | flops 2000000000 | bytes 6000000 | tf_op jit(solution)/shard_map/near_project/pallas_call | solution.py:720
  116.3 3.5 %collective-permute-done.25 = bf16[560,256]{1,0:T(8,128)(2,1)S(1)} collective-permute-done((bf16[560,256]{1,0:T(8,128)(2,1)S(1)}, bf16[560,256]{1,0:T(8,128)(2,1)S(1)}, u32[]{:S(2)}, u32[]{:S(2)}) %collective-permute-start.25) | collective-permute-done | bytes 286752 | tf_op jit(solution)/shard_map/ppermute | solution.py:736
  119.8 5.2 %collective-permute-done.26 = bf16[560,256]{1,0:T(8,128)(2,1)S(1)} collective-permute-done((bf16[560,256]{1,0:T(8,128)(2,1)S(1)}, bf16[560,256]{1,0:T(8,128)(2,1)S(1)}, u32[]{:S(2)}, u32[]{:S(2)}) %collective-permute-start.26) | collective-permute-done | bytes 286752 | tf_op jit(solution)/shard_map/ppermute | solution.py:736
  125.0 1.0 fusion
  (57 shorter events, 3.3 us)
Async XLA Ops:
  0.0 5.8 %copy-start.4 = (bf16[512,560]{0,1:T(8,128)(2,1)S(1)}, bf16[512,560]{0,1:T(8,128)(2,1)}, u32[]{:S(2)}) copy-start(bf16[512,560]{0,1:T(8,128)(2,1)} %param.14) | copy-start | bytes 1720324
  0.0 5.8 %collective-permute-start.1 = (bf16[560,512]{1,0:T(8,128)(2,1)}, bf16[560,512]{1,0:T(8,128)(2,1)S(1)}, u32[]{:S(2)}, u32[]{:S(2)}) collective-permute-start(bf16[560,512]{1,0:T(8,128)(2,1)} %bitcast.36), channel_id=1, source_target_pairs={{0,1},{1,0},{2,3},{3,2},{4,5},{5,4},{6,7},{7,6},{8,9},{9,8},{10,11... | collective-permute-start | bytes 1720328 | tf_op jit(solution)/shard_map/ppermute | solution.py:732
  0.0 15.6 %collective-permute-start = (bf16[560,512]{1,0:T(8,128)(2,1)}, bf16[560,512]{1,0:T(8,128)(2,1)S(1)}, u32[]{:S(2)}, u32[]{:S(2)}) collective-permute-start(bf16[560,512]{1,0:T(8,128)(2,1)} %bitcast.37), channel_id=1, source_target_pairs={{0,2},{1,3},{2,0},{3,1},{4,6},{5,7},{6,4},{7,5},{8,10},{9,11},{10,... | collective-permute-start | bytes 1720328 | tf_op jit(solution)/shard_map/ppermute | solution.py:736
  5.8 12.3 %copy-start.2 = (bf16[2240,512]{1,0:T(8,128)(2,1)S(1)}, bf16[2240,512]{1,0:T(8,128)(2,1)}, u32[]{:S(2)}) copy-start(bf16[2240,512]{1,0:T(8,128)(2,1)} %refs_5_.3) | copy-start | bytes 6881284
  5.8 12.3 %copy-start.3 = (bf16[2240,512]{1,0:T(8,128)(2,1)S(1)}, bf16[2240,512]{1,0:T(8,128)(2,1)}, u32[]{:S(2)}) copy-start(bf16[2240,512]{1,0:T(8,128)(2,1)} %refs_6_.3) | copy-start | bytes 6881284
  15.6 2.0 %collective-permute-start.2 = (bf16[560,512]{1,0:T(8,128)(2,1)S(1)}, bf16[560,512]{1,0:T(8,128)(2,1)S(1)}, u32[]{:S(2)}, u32[]{:S(2)}) collective-permute-start(bf16[560,512]{1,0:T(8,128)(2,1)S(1)} %collective-permute-done.refs_0_.refs_2_), channel_id=1, source_target_pairs={{0,1},{1,0},{2,3},{3,2},{4,5},{5,4},{6,7},{7,6},{8,9},{9,8},{10,11... | collective-permute-start | bytes 1720328 | tf_op jit(solution)/shard_map/ppermute | solution.py:732
  17.6 21.2 %collective-permute-start.4 = (bf16[2,560,1400]{2,1,0:T(8,128)(2,1)}, bf16[2,560,1400]{2,1,0:T(8,128)(2,1)S(1)}, u32[]{:S(2)}, u32[]{:S(2)}) collective-permute-start(bf16[2,560,1400]{2,1,0:T(8,128)(2,1)} %get-tuple-element.75), channel_id=1, source_target_pairs={{0,1},{1,0},{2,3},{3,2},{4,5},{5,4},{6,7},{7,6},{8,9},{9,8},{10,11... | collective-permute-start | bytes 9408008 | tf_op jit(solution)/shard_map/ppermute | solution.py:732
  17.7 19.7 %collective-permute-start.3 = (bf16[1120,512]{1,0:T(8,128)(2,1)S(1)}, bf16[1120,512]{1,0:T(8,128)(2,1)S(1)}, u32[]{:S(2)}, u32[]{:S(2)}) collective-permute-start(bf16[1120,512]{1,0:T(8,128)(2,1)S(1)} %get-tuple-element.74), channel_id=1, source_target_pairs={{0,1},{1,0},{2,3},{3,2},{4,5},{5,4},{6,7},{7,6},{8,9},{9,8},{10,11... | collective-permute-start | bytes 3440648 | tf_op jit(solution)/shard_map/ppermute | solution.py:732
  18.1 25.0 %copy-start.1 = (bf16[2240,512]{1,0:T(8,128)(2,1)S(1)}, bf16[2240,512]{1,0:T(8,128)(2,1)}, u32[]{:S(2)}) copy-start(bf16[2240,512]{1,0:T(8,128)(2,1)} %weights.3) | copy-start | bytes 6881284
  30.4 5.6 %collective-permute-start.5 = (bf16[2,128,256]{2,1,0:T(8,128)(2,1)S(1)}, bf16[2,128,256]{2,1,0:T(8,128)(2,1)S(1)}, u32[]{:S(2)}, u32[]{:S(2)}) collective-permute-start(bf16[2,128,256]{2,1,0:T(8,128)(2,1)S(1)} %get-tuple-element.77), channel_id=1, source_target_pairs={{0,4},{4,0},{8,12},{12,8},{16,20},{20,16},{24,28},{28,24},{1,5},{5... | collective-permute-start | bytes 393224 | tf_op jit(solution)/shard_map/ppermute | solution.py:740
  32.0 49.6 %collective-permute-start.15 = (bf16[1120,512]{1,0:T(8,128)(2,1)S(1)}, bf16[1120,512]{1,0:T(8,128)(2,1)S(1)}, u32[]{:S(2)}, u32[]{:S(2)}) collective-permute-start(bf16[1120,512]{1,0:T(8,128)(2,1)S(1)} %get-tuple-element.74), channel_id=1, source_target_pairs={{0,3},{1,2},{2,1},{3,0},{4,7},{5,6},{6,5},{7,4},{8,11},{9,10},{10,... | collective-permute-start | bytes 3440648 | tf_op jit(solution)/shard_map/ppermute | solution.py:833
  33.0 38.9 %collective-permute-start.13 = (bf16[560,512]{1,0:T(8,128)(2,1)S(1)}, bf16[560,512]{1,0:T(8,128)(2,1)S(1)}, u32[]{:S(2)}, u32[]{:S(2)}) collective-permute-start(bf16[560,512]{1,0:T(8,128)(2,1)S(1)} %get-tuple-element.96), channel_id=1, source_target_pairs={{0,2},{1,3},{2,0},{3,1},{4,6},{5,7},{6,4},{7,5},{8,10},{9,11},{10,... | collective-permute-start | bytes 1720328 | tf_op jit(solution)/shard_map/ppermute | solution.py:736
  36.8 11.1 %collective-permute-start.6 = (bf16[2,128,256]{2,1,0:T(8,128)(2,1)S(1)}, bf16[2,128,256]{2,1,0:T(8,128)(2,1)S(1)}, u32[]{:S(2)}, u32[]{:S(2)}) collective-permute-start(bf16[2,128,256]{2,1,0:T(8,128)(2,1)S(1)} %get-tuple-element.82), channel_id=1, source_target_pairs={{0,24},{4,28},{1,25},{5,29},{2,26},{6,30},{3,27},{7,31}} | collective-permute-start | bytes 393224 | tf_op jit(solution)/shard_map/ppermute | solution.py:744
  37.5 12.1 %collective-permute-start.7 = (bf16[2,128,256]{2,1,0:T(8,128)(2,1)S(1)}, bf16[2,128,256]{2,1,0:T(8,128)(2,1)S(1)}, u32[]{:S(2)}, u32[]{:S(2)}) collective-permute-start(bf16[2,128,256]{2,1,0:T(8,128)(2,1)S(1)} %get-tuple-element.82), channel_id=1, source_target_pairs={{0,16},{4,20},{8,24},{12,28},{1,17},{5,21},{9,25},{13,29},{2,18},{... | collective-permute-start | bytes 393224 | tf_op jit(solution)/shard_map/ppermute | solution.py:744
  38.8 15.0 %collective-permute-start.8 = (bf16[2,128,256]{2,1,0:T(8,128)(2,1)S(1)}, bf16[2,128,256]{2,1,0:T(8,128)(2,1)S(1)}, u32[]{:S(2)}, u32[]{:S(2)}) collective-permute-start(bf16[2,128,256]{2,1,0:T(8,128)(2,1)S(1)} %get-tuple-element.82), channel_id=1, source_target_pairs={{0,8},{4,12},{8,16},{12,20},{16,24},{20,28},{1,9},{5,13},{9,17},{1... | collective-permute-start | bytes 393224 | tf_op jit(solution)/shard_map/ppermute | solution.py:744
  45.0 14.3 %copy-start.5 = (bf16[128]{0:T(256)(128)(2,1)S(1)}, bf16[128]{0:T(256)(128)(2,1)}, u32[]{:S(2)}) copy-start(bf16[128]{0:T(256)(128)(2,1)} %param.22) | copy-start | bytes 772
  54.9 4.3 %collective-permute-start.9 = (bf16[2,128,128]{2,1,0:T(8,128)(2,1)S(1)}, bf16[2,128,128]{2,1,0:T(8,128)(2,1)S(1)}, u32[]{:S(2)}, u32[]{:S(2)}) collective-permute-start(bf16[2,128,128]{2,1,0:T(8,128)(2,1)S(1)} %get-tuple-element.90), channel_id=1, source_target_pairs={{0,4},{4,0},{8,12},{12,8},{16,20},{20,16},{24,28},{28,24},{1,5},{5... | collective-permute-start | bytes 196616 | tf_op jit(solution)/shard_map/ppermute | solution.py:740
  59.3 27.5 %copy-start = (bf16[512,2240]{0,1:T(8,128)(2,1)S(1)}, bf16[512,2240]{0,1:T(8,128)(2,1)}, u32[]{:S(2)}) copy-start(bf16[512,2240]{0,1:T(8,128)(2,1)} %param.23) | copy-start | bytes 6881284
  71.8 14.9 %collective-permute-start.14 = (bf16[560,512]{1,0:T(8,128)(2,1)S(1)}, bf16[560,512]{1,0:T(8,128)(2,1)S(1)}, u32[]{:S(2)}, u32[]{:S(2)}) collective-permute-start(bf16[560,512]{1,0:T(8,128)(2,1)S(1)} %collective-permute-done.13.refs_2_), channel_id=1, source_target_pairs={{0,4},{4,0},{8,12},{12,8},{16,20},{20,16},{24,28},{28,24},{1,5},{5... | collective-permute-start | bytes 1720328 | tf_op jit(solution)/shard_map/ppermute | solution.py:740
  72.4 9.2 %collective-permute-start.11 = (bf16[256,512]{1,0:T(8,128)(2,1)S(1)}, bf16[256,512]{1,0:T(8,128)(2,1)S(1)}, u32[]{:S(2)}, u32[]{:S(2)}) collective-permute-start(bf16[256,512]{1,0:T(8,128)(2,1)S(1)} %get-tuple-element.94.own), channel_id=1, source_target_pairs={{0,2},{1,3},{2,0},{3,1},{4,6},{5,7},{6,4},{7,5},{8,10},{9,11},{10,... | collective-permute-start | bytes 786440 | tf_op jit(solution)/shard_map/ppermute | solution.py:736
  73.9 12.1 %collective-permute-start.18 = (bf16[256,512]{1,0:T(8,128)(2,1)S(1)}, bf16[256,512]{1,0:T(8,128)(2,1)S(1)}, u32[]{:S(2)}, u32[]{:S(2)}) collective-permute-start(bf16[256,512]{1,0:T(8,128)(2,1)S(1)} %get-tuple-element.97.own), channel_id=1, source_target_pairs={{0,2},{1,3},{2,0},{3,1},{4,6},{5,7},{6,4},{7,5},{8,10},{9,11},{10,... | collective-permute-start | bytes 786440 | tf_op jit(solution)/shard_map/ppermute | solution.py:736
  74.4 11.6 %collective-permute-start.10 = (bf16[256,512]{1,0:T(8,128)(2,1)S(1)}, bf16[256,512]{1,0:T(8,128)(2,1)S(1)}, u32[]{:S(2)}, u32[]{:S(2)}) collective-permute-start(bf16[256,512]{1,0:T(8,128)(2,1)S(1)} %get-tuple-element.94.own), channel_id=1, source_target_pairs={{0,1},{1,0},{2,3},{3,2},{4,5},{5,4},{6,7},{7,6},{8,9},{9,8},{10,11... | collective-permute-start | bytes 786440 | tf_op jit(solution)/shard_map/ppermute | solution.py:732
  81.6 4.4 %collective-permute-start.12 = (bf16[256,512]{1,0:T(8,128)(2,1)S(1)}, bf16[256,512]{1,0:T(8,128)(2,1)S(1)}, u32[]{:S(2)}, u32[]{:S(2)}) collective-permute-start(bf16[256,512]{1,0:T(8,128)(2,1)S(1)} %collective-permute-done.11.refs_0_), channel_id=1, source_target_pairs={{0,1},{1,0},{2,3},{3,2},{4,5},{5,4},{6,7},{7,6},{8,9},{9,8},{10,11... | collective-permute-start | bytes 786440 | tf_op jit(solution)/shard_map/ppermute | solution.py:732
  81.6 7.2 %collective-permute-start.17 = (bf16[256,512]{1,0:T(8,128)(2,1)S(1)}, bf16[256,512]{1,0:T(8,128)(2,1)S(1)}, u32[]{:S(2)}, u32[]{:S(2)}) collective-permute-start(bf16[256,512]{1,0:T(8,128)(2,1)S(1)} %get-tuple-element.97.own), channel_id=1, source_target_pairs={{0,1},{1,0},{2,3},{3,2},{4,5},{5,4},{6,7},{7,6},{8,9},{9,8},{10,11... | collective-permute-start | bytes 786440 | tf_op jit(solution)/shard_map/ppermute | solution.py:732
  86.0 2.8 %collective-permute-start.19 = (bf16[256,512]{1,0:T(8,128)(2,1)S(1)}, bf16[256,512]{1,0:T(8,128)(2,1)S(1)}, u32[]{:S(2)}, u32[]{:S(2)}) collective-permute-start(bf16[256,512]{1,0:T(8,128)(2,1)S(1)} %collective-permute-done.18.refs_0_), channel_id=1, source_target_pairs={{0,1},{1,0},{2,3},{3,2},{4,5},{5,4},{6,7},{7,6},{8,9},{9,8},{10,11... | collective-permute-start | bytes 786440 | tf_op jit(solution)/shard_map/ppermute | solution.py:732
  86.8 4.6 %slice-start.2 = ((s8[6307840]{0:T(1024)(128)(4,1)}), s8[4194304]{0:T(1024)(128)(4,1)S(1)}, s32[]{:S(2)}) async-start(s8[6307840]{0:T(1024)(128)(4,1)} %bitcast.31), calls=%async_computation.2 | async-start | bytes 8388608
  88.7 2.6 %slice-start.3 = ((s8[6307840]{0:T(1024)(128)(4,1)}), s8[2113536]{0:T(1024)(128)(4,1)S(1)}, s32[]{:S(2)}) async-start(s8[6307840]{0:T(1024)(128)(4,1)} %bitcast.31), calls=%async_computation.3 | async-start | bytes 4227072
  88.7 2.6 %collective-permute-start.16 = (bf16[1120,256]{1,0:T(8,128)(2,1)S(1)}, bf16[1120,256]{1,0:T(8,128)(2,1)S(1)}, u32[]{:S(2)}, u32[]{:S(2)}) collective-permute-start(bf16[1120,256]{1,0:T(8,128)(2,1)S(1)} %attend.2.own), channel_id=1, source_target_pairs={{0,1},{1,0},{2,3},{3,2},{4,5},{5,4},{6,7},{7,6},{8,9},{9,8},{10,11... | collective-permute-start | bytes 1720328 | tf_op jit(solution)/shard_map/ppermute | solution.py:732
  90.8 8.3 %collective-permute-start.20 = (bf16[1120,256]{1,0:T(8,128)(2,1)S(1)}, bf16[1120,256]{1,0:T(8,128)(2,1)S(1)}, u32[]{:S(2)}, u32[]{:S(2)}) collective-permute-start(bf16[1120,256]{1,0:T(8,128)(2,1)S(1)} %attend.3.own), channel_id=1, source_target_pairs={{0,1},{1,0},{2,3},{3,2},{4,5},{5,4},{6,7},{7,6},{8,9},{9,8},{10,11... | collective-permute-start | bytes 1720328 | tf_op jit(solution)/shard_map/ppermute | solution.py:732
  91.3 17.1 %slice-start = ((s8[6307840]{0:T(1024)(128)(4,1)}), s8[4194304]{0:T(1024)(128)(4,1)S(1)}, s32[]{:S(2)}) async-start(s8[6307840]{0:T(1024)(128)(4,1)} %bitcast.26), calls=%async_computation | async-start | bytes 8388608
  94.8 8.4 %collective-permute-start.21 = (bf16[1,1400]{1,0:T(2,128)(2,1)S(1)}, bf16[1,1400]{1,0:T(2,128)(2,1)S(1)}, u32[]{:S(2)}, u32[]{:S(2)}) collective-permute-start(bf16[1,1400]{1,0:T(2,128)(2,1)S(1)} %get-tuple-element.103), channel_id=1, source_target_pairs={{0,4},{4,0},{8,12},{12,8},{16,20},{20,16},{24,28},{28,24},{1,5},{5... | collective-permute-start | bytes 8408 | tf_op jit(solution)/shard_map/ppermute | solution.py:870
  95.6 12.8 %slice-start.1 = ((s8[6307840]{0:T(1024)(128)(4,1)}), s8[2113536]{0:T(1024)(128)(4,1)S(1)}, s32[]{:S(2)}) async-start(s8[6307840]{0:T(1024)(128)(4,1)} %bitcast.26), calls=%async_computation.1 | async-start | bytes 4227072
  95.6 7.5 %collective-permute-start.22 = (bf16[1,1400]{1,0:T(2,128)(2,1)S(1)}, bf16[1,1400]{1,0:T(2,128)(2,1)S(1)}, u32[]{:S(2)}, u32[]{:S(2)}) collective-permute-start(bf16[1,1400]{1,0:T(2,128)(2,1)S(1)} %get-tuple-element.104), channel_id=1, source_target_pairs={{4,8},{8,4},{12,16},{16,12},{20,24},{24,20},{5,9},{9,5},{13,17},{1... | collective-permute-start | bytes 8408 | tf_op jit(solution)/shard_map/ppermute | solution.py:871
  105.5 2.9 %collective-permute-start.23 = (bf16[1400,256]{1,0:T(8,128)(2,1)S(1)}, bf16[1400,256]{1,0:T(8,128)(2,1)S(1)}, u32[]{:S(2)}, u32[]{:S(2)}) collective-permute-start(bf16[1400,256]{1,0:T(8,128)(2,1)S(1)} %activate.2.own_a.own), channel_id=1, source_target_pairs={{0,1},{1,0},{2,3},{3,2},{4,5},{5,4},{6,7},{7,6},{8,9},{9,8},{10,11... | collective-permute-start | bytes 2150408 | tf_op jit(solution)/shard_map/ppermute | solution.py:732
  107.9 3.8 %collective-permute-start.24 = (bf16[1400,256]{1,0:T(8,128)(2,1)S(1)}, bf16[1400,256]{1,0:T(8,128)(2,1)S(1)}, u32[]{:S(2)}, u32[]{:S(2)}) collective-permute-start(bf16[1400,256]{1,0:T(8,128)(2,1)S(1)} %activate.3.own.own_b), channel_id=1, source_target_pairs={{0,1},{1,0},{2,3},{3,2},{4,5},{5,4},{6,7},{7,6},{8,9},{9,8},{10,11... | collective-permute-start | bytes 2150408 | tf_op jit(solution)/shard_map/ppermute | solution.py:732
  110.0 9.8 %collective-permute-start.25 = (bf16[560,256]{1,0:T(8,128)(2,1)S(1)}, bf16[560,256]{1,0:T(8,128)(2,1)S(1)}, u32[]{:S(2)}, u32[]{:S(2)}) collective-permute-start(bf16[560,256]{1,0:T(8,128)(2,1)S(1)} %far_project.3), channel_id=1, source_target_pairs={{0,2},{1,3},{2,0},{3,1},{4,6},{5,7},{6,4},{7,5},{8,10},{9,11},{10,... | collective-permute-start | bytes 860168 | tf_op jit(solution)/shard_map/ppermute | solution.py:736
  113.3 11.7 %collective-permute-start.26 = (bf16[560,256]{1,0:T(8,128)(2,1)S(1)}, bf16[560,256]{1,0:T(8,128)(2,1)S(1)}, u32[]{:S(2)}, u32[]{:S(2)}) collective-permute-start(bf16[560,256]{1,0:T(8,128)(2,1)S(1)} %far_project.2.after), channel_id=1, source_target_pairs={{0,2},{1,3},{2,0},{3,1},{4,6},{5,7},{6,4},{7,5},{8,10},{9,11},{10,... | collective-permute-start | bytes 860168 | tf_op jit(solution)/shard_map/ppermute | solution.py:736

commit v9 on v8

--- a/solution.py
+++ b/solution.py
@@ -836,6 +836,8 @@
     partner_w_out = core_swap(their_rows, n)
     other_maps = pair_swap(sent_maps, seqs)
     pair, first, done = pair_maps(meta, own_maps, other_maps)
+    fetched, _ = lax.optimization_barrier((fetched, done))
+    swapped = [pair_swap(value, seqs) for value in fetched]
     pairs = [later(pair, seqs, d) for d in range(seqs // 2 - 1, 0, -1)]
     acc_query, partner_w_out, other_w_down, _ = lax.optimization_barrier(
         (early[2], partner_w_out, other_w_down, done)
@@ -850,8 +852,6 @@
     mixed = mixed_heads(meta, kept_state, other_state, shard_query, free, head_scale)
     far_mixed = [[y_shift(value, n, d) for d in range(1, ys)] for value in mixed]
 
-    fetched, _ = lax.optimization_barrier((fetched, mixed))
-    swapped = [pair_swap(value, seqs) for value in fetched]
 
     def middle_of(i, far):
         heads_far = [[value, core_swap(value, n)] for value in far]

time: 127 us -> 115 us (0.906)
  waiting for transfers between devices: 47.8 us -> 35.5 us
    ppermute x6, waiting for transfers between devices: 33.8 us -> 19.8 us  [y_shift(): lax.ppermute(value, 'head', [(i, (i + 2 * step) % n) for i in range(n)])]
    ppermute x3, waiting for transfers between devices: 6.01 us -> 7.87 us  [pair_swap(): return lax.ppermute(value, 'seq', [(i, i ^ 1) for i in range(n)])]
  transfers between devices with their start and end apart: 27 -> 27, of which waited for: 12 -> 12; matrix products, arithmetic and copies ran while one was open for 3% -> 4% of each run, Pallas kernels for 37% -> 41%
where the time goes in v9:
time: 115 us; the launch traced here: 113 us
  Pallas kernels  48.9 us (43%)
  waiting for transfers between devices  35.5 us (31%)
  starting transfers between devices  22.8 us (20%)
  local copies, waits for them, and re-layouts  2.77 us (2%)
  other arithmetic  2.48 us (2%)
    ppermute x6, waiting for transfers between devices, y_shift(): lax.ppermute(value, 'head', [(i, (i + 2 * step) % n) for i in range(n)])  19.8 us
    pallas_call x1, Pallas kernels, block_maps(): pl.pallas_call(functools.partial(maps_kernel, n, heads, at), out_shape=(s...  12.3 us
    ppermute x3, waiting for transfers between devices, pair_swap(): return lax.ppermute(value, 'seq', [(i, i ^ 1) for i in range(n)])  7.87 us
    pallas_call x2, Pallas kernels, up_project(): pl.pallas_call(up_kernel, out_shape=(shape_of((count, hidden)), shape_of(...  7.55 us
    ppermute x6, starting transfers between devices, y_shift(): lax.ppermute(value, 'head', [(i, (i + 2 * step) % n) for i in range(n)])  7.27 us
    pallas_call x1, Pallas kernels, early_project(): pl.pallas_call(functools.partial(early_kernel, len(pieces), at), out_shap...  7.16 us
    ppermute x3, starting transfers between devices, later(): lax.ppermute(value, 'seq', [(i, i + 2 * step) for i in range(n - 2 * step)])  6.26 us
    ppermute x3, waiting for transfers between devices, later(): lax.ppermute(value, 'seq', [(i, i + 2 * step) for i in range(n - 2 * step)])  5.63 us
  transfers between devices with their start and end apart: 27, of which 12 were waited for; matrix products, arithmetic and copies ran while one was open for 4% of the time, Pallas kernels for 41%

profile of v9, /device:TPU:16, one launch (start us, length us, event | category | flops | bytes accessed | tf_op | source)
XLA Modules:
  0.0 112.8 jit_solution(5878710941954969027)
XLA Ops:
  0.0 1.5 %collective-permute-start = (bf16[560,512]{1,0:T(8,128)(2,1)}, bf16[560,512]{1,0:T(8,128)(2,1)S(1)}, u32[]{:S(2)}, u32[]{:S(2)}) collective-permute-start(bf16[560,512]{1,0:T(8,128)(2,1)} %bitcast.36), channel_id=1, source_target_pairs={{0,2},{1,3},{2,0},{3,1},{4,6},{5,7},{6,4},{7,5},{8,10},{9,11},{10,... | collective-permute-start | bytes 1720328 | tf_op jit(solution)/shard_map/ppermute | solution.py:736
  1.5 0.8 reshape.37
  2.3 0.8 fusion.3
  3.2 0.8 reshape.31
  4.0 0.7 convert_element_type.15.taps
  4.7 0.7 reshape.39.gain
  5.8 7.2 %early_project.1 = (f32[512,512]{1,0:T(8,128)S(1)}, f32[512,512]{1,0:T(8,128)S(1)}, f32[512,512]{1,0:T(8,128)S(1)}, f32[16,512]{1,0:T(8,128)S(1)}, f32[8,512]{1,...) custom-call(s32[6]{0:T(128)S(1)} %stack.24.meta, ...), custom_call_target="tpu_custom_call" | custom-call | flops 3000000000 | bytes 8000000 | tf_op jit(solution)/shard_map/early_project/pallas_call | solution.py:163
  12.9 2.0 %collective-permute-done.refs_0_.refs_2_ = bf16[560,512]{1,0:T(8,128)(2,1)S(1)} collective-permute-done((bf16[560,512]{1,0:T(8,128)(2,1)}, bf16[560,512]{1,0:T(8,128)(2,1)S(1)}, u32[]{:S(2)}, u32[]{:S(2)}) %collective-permute-start) | collective-permute-done | bytes 573472 | tf_op jit(solution)/shard_map/ppermute | solution.py:736
  14.9 2.0 %collective-permute-done.2.refs_1_.refs_3_ = bf16[560,512]{1,0:T(8,128)(2,1)S(1)} collective-permute-done((bf16[560,512]{1,0:T(8,128)(2,1)S(1)}, bf16[560,512]{1,0:T(8,128)(2,1)S(1)}, u32[]{:S(2)}, u32[]{:S(2)}) %collective-permute-start.2) | collective-permute-done | bytes 573472 | tf_op jit(solution)/shard_map/ppermute | solution.py:732
  17.4 1.5 %collective-permute-start.13 = (bf16[560,512]{1,0:T(8,128)(2,1)S(1)}, bf16[560,512]{1,0:T(8,128)(2,1)S(1)}, u32[]{:S(2)}, u32[]{:S(2)}) collective-permute-start(bf16[560,512]{1,0:T(8,128)(2,1)S(1)} %get-tuple-element.96), channel_id=1, source_target_pairs={{0,2},{1,3},{2,0},{3,1},{4,6},{5,7},{6,4},{7,5},{8,10},{9,11},{10,... | collective-permute-start | bytes 1720328 | tf_op jit(solution)/shard_map/ppermute | solution.py:736
  19.0 12.3 %block_maps.1 = (bf16[512,1120]{1,0:T(8,128)(2,1)S(1)}, f32[512,128]{1,0:T(8,128)S(1)}, bf16[512,512]{1,0:T(8,128)(2,1)S(1)}, bf16[512,1024]{1,0:T(8,128)(2,1)S(...) custom-call(s32[6]{0:T(128)S(1)} %stack.24.meta, ...), custom_call_target="tpu_custom_call" | custom-call | flops 10000000000 | bytes 14000000 | tf_op jit(solution)/shard_map/block_maps/pallas_call | solution.py:333
  31.3 1.6 %collective-permute-start.5 = (bf16[2,128,256]{2,1,0:T(8,128)(2,1)S(1)}, bf16[2,128,256]{2,1,0:T(8,128)(2,1)S(1)}, u32[]{:S(2)}, u32[]{:S(2)}) collective-permute-start(bf16[2,128,256]{2,1,0:T(8,128)(2,1)S(1)} %get-tuple-element.77), channel_id=1, source_target_pairs={{0,4},{4,0},{8,12},{12,8},{16,20},{20,16},{24,28},{28,24},{1,5},{5... | collective-permute-start | bytes 393224 | tf_op jit(solution)/shard_map/ppermute | solution.py:740
  32.9 3.8 %collective-permute-done.5.other = bf16[2,128,256]{2,1,0:T(8,128)(2,1)S(1)} collective-permute-done((bf16[2,128,256]{2,1,0:T(8,128)(2,1)S(1)}, bf16[2,128,256]{2,1,0:T(8,128)(2,1)S(1)}, u32[]{:S(2)}, u32[]{:S(2)}) %collective-permute-start.5) | collective-permute-done | bytes 131104 | tf_op jit(solution)/shard_map/ppermute | solution.py:740
  36.6 0.7 pair_maps.1
  37.3 0.7 collective-permute-start.6
  38.0 1.3 %collective-permute-start.7 = (bf16[2,128,256]{2,1,0:T(8,128)(2,1)S(1)}, bf16[2,128,256]{2,1,0:T(8,128)(2,1)S(1)}, u32[]{:S(2)}, u32[]{:S(2)}) collective-permute-start(bf16[2,128,256]{2,1,0:T(8,128)(2,1)S(1)} %get-tuple-element.82), channel_id=1, source_target_pairs={{0,16},{4,20},{8,24},{12,28},{1,17},{5,21},{9,25},{13,29},{2,18},{... | collective-permute-start | bytes 393224 | tf_op jit(solution)/shard_map/ppermute | solution.py:744
  39.3 4.3 %collective-permute-start.8 = (bf16[2,128,256]{2,1,0:T(8,128)(2,1)S(1)}, bf16[2,128,256]{2,1,0:T(8,128)(2,1)S(1)}, u32[]{:S(2)}, u32[]{:S(2)}) collective-permute-start(bf16[2,128,256]{2,1,0:T(8,128)(2,1)S(1)} %get-tuple-element.82), channel_id=1, source_target_pairs={{0,8},{4,12},{8,16},{12,20},{16,24},{20,28},{1,9},{5,13},{9,17},{1... | collective-permute-start | bytes 393224 | tf_op jit(solution)/shard_map/ppermute | solution.py:744
  43.7 1.9 %queries.1 = (bf16[512,512]{1,0:T(8,128)(2,1)S(1)}, bf16[2240,256]{1,0:T(8,128)(2,1)S(1)}, bf16[2240,256]{1,0:T(8,128)(2,1)S(1)}, f32[8,128]{1,0:T(8,128)}) custom-call(s32[6]{0:T(128)S(1)} %stack.24.meta, bf16[512,1120]{1,0:T(8,128)(2,1)S(1)} %get-tuple-element.68.scaled, f32[512,128]{1,0:T(8,128)S(1)} %get-tuple-element.69.scale_b, ...), custom_call_target="tpu_custom_call" | custom-call | flops 1000000000 | bytes 8000000 | tf_op jit(solution)/shard_map/queries/pallas_call | solution.py:397
  45.5 2.8 %block_outputs.1 = (bf16[512,512]{1,0:T(8,128)(2,1)S(1)}, f32[512,512]{1,0:T(8,128)S(1)}, f32[8,128]{1,0:T(8,128)S(1)}) custom-call(bf16[512,512]{1,0:T(8,128)(2,1)S(1)} %get-tuple-element.83.query, bf16[512,512]{1,0:T(8,128)(2,1)S(1)} %get-tuple-element.84.keys, bf16[512,1024]{1,0:T(8,128)(2,1)S(1)} %get-tuple-element.85.erased, ...), custom_call_target="tpu_custom_call" | custom-call | flops 3000000000 | bytes 4000000 | tf_op jit(solution)/shard_map/block_outputs/pallas_call | solution.py:448
  48.4 1.4 %collective-permute-done.7.refs_1_ = bf16[2,128,256]{2,1,0:T(8,128)(2,1)S(1)} collective-permute-done((bf16[2,128,256]{2,1,0:T(8,128)(2,1)S(1)}, bf16[2,128,256]{2,1,0:T(8,128)(2,1)S(1)}, u32[]{:S(2)}, u32[]{:S(2)}) %collective-permute-start.7) | collective-permute-done | bytes 131104 | tf_op jit(solution)/shard_map/ppermute | solution.py:744
  49.8 4.2 %collective-permute-done.8.refs_2_ = bf16[2,128,256]{2,1,0:T(8,128)(2,1)S(1)} collective-permute-done((bf16[2,128,256]{2,1,0:T(8,128)(2,1)S(1)}, bf16[2,128,256]{2,1,0:T(8,128)(2,1)S(1)}, u32[]{:S(2)}, u32[]{:S(2)}) %collective-permute-start.8) | collective-permute-done | bytes 131104 | tf_op jit(solution)/shard_map/ppermute | solution.py:744
  54.0 1.2 %start_states.1 = (bf16[2,128,128]{2,1,0:T(8,128)(2,1)S(1)}, bf16[2,128,128]{2,1,0:T(8,128)(2,1)S(1)}) custom-call(s32[6]{0:T(128)S(1)} %stack.24.meta, bf16[2,128,256]{2,1,0:T(8,128)(2,1)S(1)} %get-tuple-element.81.first, bf16[2,128,256]{2,1,0:T(8,128)(2,1)S(1)} %collective-permute-done.6.refs_0_, bf16[2,128,256]{2,1,0:T(8,128)(2,1)S(1)} %collective-permute-done.7.refs_1_, ...), custom_call_target="tpu_custom_call" | custom-call | tf_op jit(solution)/shard_map/start_states/pallas_call | solution.py:506
  55.2 1.5 %collective-permute-start.9 = (bf16[2,128,128]{2,1,0:T(8,128)(2,1)S(1)}, bf16[2,128,128]{2,1,0:T(8,128)(2,1)S(1)}, u32[]{:S(2)}, u32[]{:S(2)}) collective-permute-start(bf16[2,128,128]{2,1,0:T(8,128)(2,1)S(1)} %get-tuple-element.90), channel_id=1, source_target_pairs={{0,4},{4,0},{8,12},{12,8},{16,20},{20,16},{24,28},{28,24},{1,5},{5... | collective-permute-start | bytes 196616 | tf_op jit(solution)/shard_map/ppermute | solution.py:740
  56.8 0.6 collective-permute-start.14
  57.3 2.7 %collective-permute-done.9.other = bf16[2,128,128]{2,1,0:T(8,128)(2,1)S(1)} collective-permute-done((bf16[2,128,128]{2,1,0:T(8,128)(2,1)S(1)}, bf16[2,128,128]{2,1,0:T(8,128)(2,1)S(1)}, u32[]{:S(2)}, u32[]{:S(2)}) %collective-permute-start.9) | collective-permute-done | bytes 65568 | tf_op jit(solution)/shard_map/ppermute | solution.py:740
  60.0 1.1 mixed_heads.1
  61.7 1.5 %collective-permute-start.18 = (bf16[256,512]{1,0:T(8,128)(2,1)S(1)}, bf16[256,512]{1,0:T(8,128)(2,1)S(1)}, u32[]{:S(2)}, u32[]{:S(2)}) collective-permute-start(bf16[256,512]{1,0:T(8,128)(2,1)S(1)} %get-tuple-element.101.own), channel_id=1, source_target_pairs={{0,2},{1,3},{2,0},{3,1},{4,6},{5,7},{6,4},{7,5},{8,10},{9,11},{10,... | collective-permute-start | bytes 786440 | tf_op jit(solution)/shard_map/ppermute | solution.py:736
  63.2 7.2 %collective-permute-done.11.refs_0_ = bf16[256,512]{1,0:T(8,128)(2,1)S(1)} collective-permute-done((bf16[256,512]{1,0:T(8,128)(2,1)S(1)}, bf16[256,512]{1,0:T(8,128)(2,1)S(1)}, u32[]{:S(2)}, u32[]{:S(2)}) %collective-permute-start.11) | collective-permute-done | bytes 262176 | tf_op jit(solution)/shard_map/ppermute | solution.py:736
  70.4 1.4 %collective-permute-done.14.refs_3_ = bf16[560,512]{1,0:T(8,128)(2,1)S(1)} collective-permute-done((bf16[560,512]{1,0:T(8,128)(2,1)S(1)}, bf16[560,512]{1,0:T(8,128)(2,1)S(1)}, u32[]{:S(2)}, u32[]{:S(2)}) %collective-permute-start.14) | collective-permute-done | bytes 573472 | tf_op jit(solution)/shard_map/ppermute | solution.py:740
  71.9 1.9 %collective-permute-done.18.refs_0_ = bf16[256,512]{1,0:T(8,128)(2,1)S(1)} collective-permute-done((bf16[256,512]{1,0:T(8,128)(2,1)S(1)}, bf16[256,512]{1,0:T(8,128)(2,1)S(1)}, u32[]{:S(2)}, u32[]{:S(2)}) %collective-permute-start.18) | collective-permute-done | bytes 262176 | tf_op jit(solution)/shard_map/ppermute | solution.py:736
  73.8 1.9 %attend.2.own = bf16[1120,256]{1,0:T(8,128)(2,1)S(1)} custom-call(s32[6]{0:T(128)S(1)} %stack.24.meta, bf16[2240,256]{1,0:T(8,128)(2,1)S(1)} %get-tuple-element.80.tokens, bf16[256,512]{1,0:T(8,128)(2,1)S(1)} %get-tuple-element.94.own, bf16[256,512]{1,0:T(8,128)(2,1)S(1)} %collective-permute-done.10.partner, bf16[2240,512]{1,0:T(8,128)(2,1)S(1)} %bitcast.34, ...), custom_call_target="tpu_custom_call" | custom-call | flops 2000000000 | bytes 7000000 | tf_op jit(solution)/shard_map/attend/pallas_call | solution.py:572
  75.7 0.6 collective-permute-start.16
  76.3 1.9 %attend.3.own = bf16[1120,256]{1,0:T(8,128)(2,1)S(1)} custom-call(s32[6]{0:T(128)S(1)} %stack.24.meta, bf16[2240,256]{1,0:T(8,128)(2,1)S(1)} %get-tuple-element.100.tokens, bf16[256,512]{1,0:T(8,128)(2,1)S(1)} %get-tuple-element.101.own, bf16[256,512]{1,0:T(8,128)(2,1)S(1)} %collective-permute-done.17.partner, bf16[2240,512]{1,0:T(8,128)(2,1)S(1)} %bitcast.35, ...), custom_call_target="tpu_custom_call" | custom-call | flops 2000000000 | bytes 7000000 | tf_op jit(solution)/shard_map/attend/pallas_call | solution.py:572
  78.4 3.5 %up_project.2 = (bf16[256,1400]{1,0:T(8,128)(2,1)S(1)}, f32[560,256]{1,0:T(8,128)S(1)}, bf16[1,1400]{1,0:T(2,128)(2,1)S(1)}, bf16[1,1400]{1,0:T(2,128)(2,1)S(1)}) custom-call(s32[6]{0:T(128)S(1)} %stack.24.meta, bf16[1120,256]{1,0:T(8,128)(2,1)S(1)} %attend.2.own, bf16[1120,256]{1,0:T(8,128)(2,1)S(1)} %collective-permute-done.16.other, ...), custom_call_target="tpu_custom_call" | custom-call | flops 2000000000 | bytes 8000000 | tf_op jit(solution)/shard_map/up_project/pallas_call | solution.py:616
  81.9 1.5 %collective-permute-start.21 = (bf16[1,1400]{1,0:T(2,128)(2,1)S(1)}, bf16[1,1400]{1,0:T(2,128)(2,1)S(1)}, u32[]{:S(2)}, u32[]{:S(2)}) collective-permute-start(bf16[1,1400]{1,0:T(2,128)(2,1)S(1)} %get-tuple-element.103), channel_id=1, source_target_pairs={{0,4},{4,0},{8,12},{12,8},{16,20},{20,16},{24,28},{28,24},{1,5},{5... | collective-permute-start | bytes 8408 | tf_op jit(solution)/shard_map/ppermute | solution.py:870
  83.4 2.3 %collective-permute-start.22 = (bf16[1,1400]{1,0:T(2,128)(2,1)S(1)}, bf16[1,1400]{1,0:T(2,128)(2,1)S(1)}, u32[]{:S(2)}, u32[]{:S(2)}) collective-permute-start(bf16[1,1400]{1,0:T(2,128)(2,1)S(1)} %get-tuple-element.104), channel_id=1, source_target_pairs={{4,8},{8,4},{12,16},{16,12},{20,24},{24,20},{5,9},{9,5},{13,17},{1... | collective-permute-start | bytes 8408 | tf_op jit(solution)/shard_map/ppermute | solution.py:871
  85.7 4.1 %up_project.3 = (bf16[256,1400]{1,0:T(8,128)(2,1)S(1)}, f32[560,256]{1,0:T(8,128)S(1)}, bf16[1,1400]{1,0:T(2,128)(2,1)}, bf16[1,1400]{1,0:T(2,128)(2,1)}) custom-call(s32[6]{0:T(128)S(1)} %stack.24.meta, bf16[1120,256]{1,0:T(8,128)(2,1)S(1)} %attend.3.own, bf16[1120,256]{1,0:T(8,128)(2,1)S(1)} %collective-permute-done.20.other, f32[1,2240]{1,0:T(1,128)S(1)} %reshape.39.gain, ...), custom_call_target="tpu_custom_call" | custom-call | flops 2000000000 | bytes 8000000 | tf_op jit(solution)/shard_map/up_project/pallas_call | solution.py:616
  89.9 2.3 %activate.3.own.own_b = bf16[1400,256]{1,0:T(8,128)(2,1)S(1)} custom-call(s32[6]{0:T(128)S(1)} %stack.24.meta, bf16[256,1400]{1,0:T(8,128)(2,1)S(1)} %get-tuple-element.99.outer, bf16[256,1400]{1,0:T(8,128)(2,1)S(1)} %get-tuple-element.102.inside, bf16[1,1400]{1,0:T(2,128)(2,1)S(1)} %collective-permute-done.21.near_row, ...), custom_call_target="tpu_custom_call" | custom-call | flops 1000000000 | bytes 2000000 | tf_op jit(solution)/shard_map/activate/pallas_call | solution.py:673
  92.3 2.3 %activate.2.own_a.own = bf16[1400,256]{1,0:T(8,128)(2,1)S(1)} custom-call(s32[6]{0:T(128)S(1)} %stack.24.meta, bf16[256,1400]{1,0:T(8,128)(2,1)S(1)} %get-tuple-element.99.outer, bf16[256,1400]{1,0:T(8,128)(2,1)S(1)} %get-tuple-element.102.inside, bf16[1,1400]{1,0:T(2,128)(2,1)S(1)} %collective-permute-done.21.near_row, ...), custom_call_target="tpu_custom_call" | custom-call | flops 1000000000 | bytes 2000000 | tf_op jit(solution)/shard_map/activate/pallas_call | solution.py:673
  94.6 0.6 collective-permute-start.23
  95.2 1.6 %far_project.2.after = bf16[560,256]{1,0:T(8,128)(2,1)S(1)} custom-call(s32[6]{0:T(128)S(1)} %stack.24.meta, bf16[1400,256]{1,0:T(8,128)(2,1)S(1)} %activate.3.own.own_b, bf16[1400,256]{1,0:T(8,128)(2,1)S(1)} %collective-permute-done.24.other.other_b, bf16[4,560,1400]{2,1,0:T(8,128)(2,1)S(1)} %bitcast.28, ...), custom_call_target="tpu_custom_call" | custom-call | flops 1000000000 | bytes 4000000 | tf_op jit(solution)/shard_map/far_project/pallas_call | solution.py:695
  96.8 0.6 collective-permute-start.26
  97.4 1.6 %far_project.3 = bf16[560,256]{1,0:T(8,128)(2,1)S(1)} custom-call(s32[6]{0:T(128)S(1)} %stack.24.meta, bf16[1400,256]{1,0:T(8,128)(2,1)S(1)} %activate.2.own_a.own, bf16[1400,256]{1,0:T(8,128)(2,1)S(1)} %collective-permute-done.23.other_a.other, bf16[4,560,1400]{2,1,0:T(8,128)(2,1)S(1)} %bitcast.29, ...), custom_call_target="tpu_custom_call" | custom-call | flops 1000000000 | bytes 4000000 | tf_op jit(solution)/shard_map/far_project/pallas_call | solution.py:695
  99.0 1.6 %collective-permute-start.25 = (bf16[560,256]{1,0:T(8,128)(2,1)S(1)}, bf16[560,256]{1,0:T(8,128)(2,1)S(1)}, u32[]{:S(2)}, u32[]{:S(2)}) collective-permute-start(bf16[560,256]{1,0:T(8,128)(2,1)S(1)} %far_project.3), channel_id=1, source_target_pairs={{0,2},{1,3},{2,0},{3,1},{4,6},{5,7},{6,4},{7,5},{8,10},{9,11},{10,... | collective-permute-start | bytes 860168 | tf_op jit(solution)/shard_map/ppermute | solution.py:736
  100.5 2.5 %near_project.1 = f32[560,512]{1,0:T(8,128)S(1)} custom-call(s32[6]{0:T(128)S(1)} %stack.24.meta, bf16[1400,256]{1,0:T(8,128)(2,1)S(1)} %activate.2.own_a.own, bf16[1400,256]{1,0:T(8,128)(2,1)S(1)} %collective-permute-done.23.other_a.other, bf16[1400,256]{1,0:T(8,128)(2,1)S(1)} %activate.3.own.own_b, ...), custom_call_target="tpu_custom_call" | custom-call | flops 2000000000 | bytes 6000000 | tf_op jit(solution)/shard_map/near_project/pallas_call | solution.py:720
  103.1 3.5 %collective-permute-done.26 = bf16[560,256]{1,0:T(8,128)(2,1)S(1)} collective-permute-done((bf16[560,256]{1,0:T(8,128)(2,1)S(1)}, bf16[560,256]{1,0:T(8,128)(2,1)S(1)}, u32[]{:S(2)}, u32[]{:S(2)}) %collective-permute-start.26) | collective-permute-done | bytes 286752 | tf_op jit(solution)/shard_map/ppermute | solution.py:736
  106.6 5.2 %collective-permute-done.25 = bf16[560,256]{1,0:T(8,128)(2,1)S(1)} collective-permute-done((bf16[560,256]{1,0:T(8,128)(2,1)S(1)}, bf16[560,256]{1,0:T(8,128)(2,1)S(1)}, u32[]{:S(2)}, u32[]{:S(2)}) %collective-permute-start.25) | collective-permute-done | bytes 286752 | tf_op jit(solution)/shard_map/ppermute | solution.py:736
  111.8 1.0 fusion
  (57 shorter events, 2.0 us)
Async XLA Ops:
  0.0 5.8 %copy-start.4 = (bf16[512,560]{0,1:T(8,128)(2,1)S(1)}, bf16[512,560]{0,1:T(8,128)(2,1)}, u32[]{:S(2)}) copy-start(bf16[512,560]{0,1:T(8,128)(2,1)} %param.14) | copy-start | bytes 1720324
  0.0 14.9 %collective-permute-start = (bf16[560,512]{1,0:T(8,128)(2,1)}, bf16[560,512]{1,0:T(8,128)(2,1)S(1)}, u32[]{:S(2)}, u32[]{:S(2)}) collective-permute-start(bf16[560,512]{1,0:T(8,128)(2,1)} %bitcast.36), channel_id=1, source_target_pairs={{0,2},{1,3},{2,0},{3,1},{4,6},{5,7},{6,4},{7,5},{8,10},{9,11},{10,... | collective-permute-start | bytes 1720328 | tf_op jit(solution)/shard_map/ppermute | solution.py:736
  1.5 4.2 %collective-permute-start.1 = (bf16[560,512]{1,0:T(8,128)(2,1)}, bf16[560,512]{1,0:T(8,128)(2,1)S(1)}, u32[]{:S(2)}, u32[]{:S(2)}) collective-permute-start(bf16[560,512]{1,0:T(8,128)(2,1)} %bitcast.37), channel_id=1, source_target_pairs={{0,1},{1,0},{2,3},{3,2},{4,5},{5,4},{6,7},{7,6},{8,9},{9,8},{10,11... | collective-permute-start | bytes 1720328 | tf_op jit(solution)/shard_map/ppermute | solution.py:732
  5.8 13.2 %copy-start.2 = (bf16[2240,512]{1,0:T(8,128)(2,1)S(1)}, bf16[2240,512]{1,0:T(8,128)(2,1)}, u32[]{:S(2)}) copy-start(bf16[2240,512]{1,0:T(8,128)(2,1)} %refs_5_.3) | copy-start | bytes 6881284
  5.8 13.2 %copy-start.3 = (bf16[2240,512]{1,0:T(8,128)(2,1)S(1)}, bf16[2240,512]{1,0:T(8,128)(2,1)}, u32[]{:S(2)}) copy-start(bf16[2240,512]{1,0:T(8,128)(2,1)} %refs_6_.3) | copy-start | bytes 6881284
  14.9 2.0 %collective-permute-start.2 = (bf16[560,512]{1,0:T(8,128)(2,1)S(1)}, bf16[560,512]{1,0:T(8,128)(2,1)S(1)}, u32[]{:S(2)}, u32[]{:S(2)}) collective-permute-start(bf16[560,512]{1,0:T(8,128)(2,1)S(1)} %collective-permute-done.refs_0_.refs_2_), channel_id=1, source_target_pairs={{0,1},{1,0},{2,3},{3,2},{4,5},{5,4},{6,7},{7,6},{8,9},{9,8},{10,11... | collective-permute-start | bytes 1720328 | tf_op jit(solution)/shard_map/ppermute | solution.py:732
  16.9 22.4 %collective-permute-start.4 = (bf16[2,560,1400]{2,1,0:T(8,128)(2,1)}, bf16[2,560,1400]{2,1,0:T(8,128)(2,1)S(1)}, u32[]{:S(2)}, u32[]{:S(2)}) collective-permute-start(bf16[2,560,1400]{2,1,0:T(8,128)(2,1)} %get-tuple-element.75), channel_id=1, source_target_pairs={{0,1},{1,0},{2,3},{3,2},{4,5},{5,4},{6,7},{7,6},{8,9},{9,8},{10,11... | collective-permute-start | bytes 9408008 | tf_op jit(solution)/shard_map/ppermute | solution.py:732
  17.0 21.0 %collective-permute-start.3 = (bf16[1120,512]{1,0:T(8,128)(2,1)S(1)}, bf16[1120,512]{1,0:T(8,128)(2,1)S(1)}, u32[]{:S(2)}, u32[]{:S(2)}) collective-permute-start(bf16[1120,512]{1,0:T(8,128)(2,1)S(1)} %get-tuple-element.74), channel_id=1, source_target_pairs={{0,1},{1,0},{2,3},{3,2},{4,5},{5,4},{6,7},{7,6},{8,9},{9,8},{10,11... | collective-permute-start | bytes 3440648 | tf_op jit(solution)/shard_map/ppermute | solution.py:732
  17.4 39.4 %collective-permute-start.13 = (bf16[560,512]{1,0:T(8,128)(2,1)S(1)}, bf16[560,512]{1,0:T(8,128)(2,1)S(1)}, u32[]{:S(2)}, u32[]{:S(2)}) collective-permute-start(bf16[560,512]{1,0:T(8,128)(2,1)S(1)} %get-tuple-element.96), channel_id=1, source_target_pairs={{0,2},{1,3},{2,0},{3,1},{4,6},{5,7},{6,4},{7,5},{8,10},{9,11},{10,... | collective-permute-start | bytes 1720328 | tf_op jit(solution)/shard_map/ppermute | solution.py:736
  18.9 24.7 %copy-start.1 = (bf16[2240,512]{1,0:T(8,128)(2,1)S(1)}, bf16[2240,512]{1,0:T(8,128)(2,1)}, u32[]{:S(2)}) copy-start(bf16[2240,512]{1,0:T(8,128)(2,1)} %weights.3) | copy-start | bytes 6881284
  31.3 5.3 %collective-permute-start.5 = (bf16[2,128,256]{2,1,0:T(8,128)(2,1)S(1)}, bf16[2,128,256]{2,1,0:T(8,128)(2,1)S(1)}, u32[]{:S(2)}, u32[]{:S(2)}) collective-permute-start(bf16[2,128,256]{2,1,0:T(8,128)(2,1)S(1)} %get-tuple-element.77), channel_id=1, source_target_pairs={{0,4},{4,0},{8,12},{12,8},{16,20},{20,16},{24,28},{28,24},{1,5},{5... | collective-permute-start | bytes 393224 | tf_op jit(solution)/shard_map/ppermute | solution.py:740
  32.9 40.9 %collective-permute-start.15 = (bf16[1120,512]{1,0:T(8,128)(2,1)S(1)}, bf16[1120,512]{1,0:T(8,128)(2,1)S(1)}, u32[]{:S(2)}, u32[]{:S(2)}) collective-permute-start(bf16[1120,512]{1,0:T(8,128)(2,1)S(1)} %get-tuple-element.74), channel_id=1, source_target_pairs={{0,3},{1,2},{2,1},{3,0},{4,7},{5,6},{6,5},{7,4},{8,11},{9,10},{10,... | collective-permute-start | bytes 3440648 | tf_op jit(solution)/shard_map/ppermute | solution.py:833
  37.3 11.1 %collective-permute-start.6 = (bf16[2,128,256]{2,1,0:T(8,128)(2,1)S(1)}, bf16[2,128,256]{2,1,0:T(8,128)(2,1)S(1)}, u32[]{:S(2)}, u32[]{:S(2)}) collective-permute-start(bf16[2,128,256]{2,1,0:T(8,128)(2,1)S(1)} %get-tuple-element.82), channel_id=1, source_target_pairs={{0,24},{4,28},{1,25},{5,29},{2,26},{6,30},{3,27},{7,31}} | collective-permute-start | bytes 393224 | tf_op jit(solution)/shard_map/ppermute | solution.py:744
  38.0 11.8 %collective-permute-start.7 = (bf16[2,128,256]{2,1,0:T(8,128)(2,1)S(1)}, bf16[2,128,256]{2,1,0:T(8,128)(2,1)S(1)}, u32[]{:S(2)}, u32[]{:S(2)}) collective-permute-start(bf16[2,128,256]{2,1,0:T(8,128)(2,1)S(1)} %get-tuple-element.82), channel_id=1, source_target_pairs={{0,16},{4,20},{8,24},{12,28},{1,17},{5,21},{9,25},{13,29},{2,18},{... | collective-permute-start | bytes 393224 | tf_op jit(solution)/shard_map/ppermute | solution.py:744
  39.3 14.7 %collective-permute-start.8 = (bf16[2,128,256]{2,1,0:T(8,128)(2,1)S(1)}, bf16[2,128,256]{2,1,0:T(8,128)(2,1)S(1)}, u32[]{:S(2)}, u32[]{:S(2)}) collective-permute-start(bf16[2,128,256]{2,1,0:T(8,128)(2,1)S(1)} %get-tuple-element.82), channel_id=1, source_target_pairs={{0,8},{4,12},{8,16},{12,20},{16,24},{20,28},{1,9},{5,13},{9,17},{1... | collective-permute-start | bytes 393224 | tf_op jit(solution)/shard_map/ppermute | solution.py:744
  45.5 14.5 %copy-start.5 = (bf16[128]{0:T(256)(128)(2,1)S(1)}, bf16[128]{0:T(256)(128)(2,1)}, u32[]{:S(2)}) copy-start(bf16[128]{0:T(256)(128)(2,1)} %param.22) | copy-start | bytes 772
  55.2 4.8 %collective-permute-start.9 = (bf16[2,128,128]{2,1,0:T(8,128)(2,1)S(1)}, bf16[2,128,128]{2,1,0:T(8,128)(2,1)S(1)}, u32[]{:S(2)}, u32[]{:S(2)}) collective-permute-start(bf16[2,128,128]{2,1,0:T(8,128)(2,1)S(1)} %get-tuple-element.90), channel_id=1, source_target_pairs={{0,4},{4,0},{8,12},{12,8},{16,20},{20,16},{24,28},{28,24},{1,5},{5... | collective-permute-start | bytes 196616 | tf_op jit(solution)/shard_map/ppermute | solution.py:740
  56.8 15.1 %collective-permute-start.14 = (bf16[560,512]{1,0:T(8,128)(2,1)S(1)}, bf16[560,512]{1,0:T(8,128)(2,1)S(1)}, u32[]{:S(2)}, u32[]{:S(2)}) collective-permute-start(bf16[560,512]{1,0:T(8,128)(2,1)S(1)} %collective-permute-done.13.refs_2_), channel_id=1, source_target_pairs={{0,4},{4,0},{8,12},{12,8},{16,20},{20,16},{24,28},{28,24},{1,5},{5... | collective-permute-start | bytes 1720328 | tf_op jit(solution)/shard_map/ppermute | solution.py:740
  60.0 13.7 %copy-start = (bf16[512,2240]{0,1:T(8,128)(2,1)S(1)}, bf16[512,2240]{0,1:T(8,128)(2,1)}, u32[]{:S(2)}) copy-start(bf16[512,2240]{0,1:T(8,128)(2,1)} %param.23) | copy-start | bytes 6881284
  61.1 9.3 %collective-permute-start.11 = (bf16[256,512]{1,0:T(8,128)(2,1)S(1)}, bf16[256,512]{1,0:T(8,128)(2,1)S(1)}, u32[]{:S(2)}, u32[]{:S(2)}) collective-permute-start(bf16[256,512]{1,0:T(8,128)(2,1)S(1)} %get-tuple-element.94.own), channel_id=1, source_target_pairs={{0,2},{1,3},{2,0},{3,1},{4,6},{5,7},{6,4},{7,5},{8,10},{9,11},{10,... | collective-permute-start | bytes 786440 | tf_op jit(solution)/shard_map/ppermute | solution.py:736
  61.7 12.0 %collective-permute-start.18 = (bf16[256,512]{1,0:T(8,128)(2,1)S(1)}, bf16[256,512]{1,0:T(8,128)(2,1)S(1)}, u32[]{:S(2)}, u32[]{:S(2)}) collective-permute-start(bf16[256,512]{1,0:T(8,128)(2,1)S(1)} %get-tuple-element.101.own), channel_id=1, source_target_pairs={{0,2},{1,3},{2,0},{3,1},{4,6},{5,7},{6,4},{7,5},{8,10},{9,11},{10,... | collective-permute-start | bytes 786440 | tf_op jit(solution)/shard_map/ppermute | solution.py:736
  63.2 10.5 %collective-permute-start.10 = (bf16[256,512]{1,0:T(8,128)(2,1)S(1)}, bf16[256,512]{1,0:T(8,128)(2,1)S(1)}, u32[]{:S(2)}, u32[]{:S(2)}) collective-permute-start(bf16[256,512]{1,0:T(8,128)(2,1)S(1)} %get-tuple-element.94.own), channel_id=1, source_target_pairs={{0,1},{1,0},{2,3},{3,2},{4,5},{5,4},{6,7},{7,6},{8,9},{9,8},{10,11... | collective-permute-start | bytes 786440 | tf_op jit(solution)/shard_map/ppermute | solution.py:732
  70.4 3.3 %collective-permute-start.12 = (bf16[256,512]{1,0:T(8,128)(2,1)S(1)}, bf16[256,512]{1,0:T(8,128)(2,1)S(1)}, u32[]{:S(2)}, u32[]{:S(2)}) collective-permute-start(bf16[256,512]{1,0:T(8,128)(2,1)S(1)} %collective-permute-done.11.refs_0_), channel_id=1, source_target_pairs={{0,1},{1,0},{2,3},{3,2},{4,5},{5,4},{6,7},{7,6},{8,9},{9,8},{10,11... | collective-permute-start | bytes 786440 | tf_op jit(solution)/shard_map/ppermute | solution.py:732
  71.9 4.4 %collective-permute-start.17 = (bf16[256,512]{1,0:T(8,128)(2,1)S(1)}, bf16[256,512]{1,0:T(8,128)(2,1)S(1)}, u32[]{:S(2)}, u32[]{:S(2)}) collective-permute-start(bf16[256,512]{1,0:T(8,128)(2,1)S(1)} %get-tuple-element.101.own), channel_id=1, source_target_pairs={{0,1},{1,0},{2,3},{3,2},{4,5},{5,4},{6,7},{7,6},{8,9},{9,8},{10,11... | collective-permute-start | bytes 786440 | tf_op jit(solution)/shard_map/ppermute | solution.py:732
  73.7 2.6 %collective-permute-start.19 = (bf16[256,512]{1,0:T(8,128)(2,1)S(1)}, bf16[256,512]{1,0:T(8,128)(2,1)S(1)}, u32[]{:S(2)}, u32[]{:S(2)}) collective-permute-start(bf16[256,512]{1,0:T(8,128)(2,1)S(1)} %collective-permute-done.18.refs_0_), channel_id=1, source_target_pairs={{0,1},{1,0},{2,3},{3,2},{4,5},{5,4},{6,7},{7,6},{8,9},{9,8},{10,11... | collective-permute-start | bytes 786440 | tf_op jit(solution)/shard_map/ppermute | solution.py:732
  73.8 4.6 %slice-start.2 = ((s8[6307840]{0:T(1024)(128)(4,1)}), s8[4194304]{0:T(1024)(128)(4,1)S(1)}, s32[]{:S(2)}) async-start(s8[6307840]{0:T(1024)(128)(4,1)} %bitcast.31), calls=%async_computation.2 | async-start | bytes 8388608
  75.7 2.6 %slice-start.3 = ((s8[6307840]{0:T(1024)(128)(4,1)}), s8[2113536]{0:T(1024)(128)(4,1)S(1)}, s32[]{:S(2)}) async-start(s8[6307840]{0:T(1024)(128)(4,1)} %bitcast.31), calls=%async_computation.3 | async-start | bytes 4227072
  75.7 2.6 %collective-permute-start.16 = (bf16[1120,256]{1,0:T(8,128)(2,1)S(1)}, bf16[1120,256]{1,0:T(8,128)(2,1)S(1)}, u32[]{:S(2)}, u32[]{:S(2)}) collective-permute-start(bf16[1120,256]{1,0:T(8,128)(2,1)S(1)} %attend.2.own), channel_id=1, source_target_pairs={{0,1},{1,0},{2,3},{3,2},{4,5},{5,4},{6,7},{7,6},{8,9},{9,8},{10,11... | collective-permute-start | bytes 1720328 | tf_op jit(solution)/shard_map/ppermute | solution.py:732
  78.2 7.4 %collective-permute-start.20 = (bf16[1120,256]{1,0:T(8,128)(2,1)S(1)}, bf16[1120,256]{1,0:T(8,128)(2,1)S(1)}, u32[]{:S(2)}, u32[]{:S(2)}) collective-permute-start(bf16[1120,256]{1,0:T(8,128)(2,1)S(1)} %attend.3.own), channel_id=1, source_target_pairs={{0,1},{1,0},{2,3},{3,2},{4,5},{5,4},{6,7},{7,6},{8,9},{9,8},{10,11... | collective-permute-start | bytes 1720328 | tf_op jit(solution)/shard_map/ppermute | solution.py:732
  78.4 16.8 %slice-start = ((s8[6307840]{0:T(1024)(128)(4,1)}), s8[4194304]{0:T(1024)(128)(4,1)S(1)}, s32[]{:S(2)}) async-start(s8[6307840]{0:T(1024)(128)(4,1)} %bitcast.26), calls=%async_computation | async-start | bytes 8388608
  81.9 7.9 %collective-permute-start.21 = (bf16[1,1400]{1,0:T(2,128)(2,1)S(1)}, bf16[1,1400]{1,0:T(2,128)(2,1)S(1)}, u32[]{:S(2)}, u32[]{:S(2)}) collective-permute-start(bf16[1,1400]{1,0:T(2,128)(2,1)S(1)} %get-tuple-element.103), channel_id=1, source_target_pairs={{0,4},{4,0},{8,12},{12,8},{16,20},{20,16},{24,28},{28,24},{1,5},{5... | collective-permute-start | bytes 8408 | tf_op jit(solution)/shard_map/ppermute | solution.py:870
  83.4 11.8 %slice-start.1 = ((s8[6307840]{0:T(1024)(128)(4,1)}), s8[2113536]{0:T(1024)(128)(4,1)S(1)}, s32[]{:S(2)}) async-start(s8[6307840]{0:T(1024)(128)(4,1)} %bitcast.26), calls=%async_computation.1 | async-start | bytes 4227072
  83.4 6.5 %collective-permute-start.22 = (bf16[1,1400]{1,0:T(2,128)(2,1)S(1)}, bf16[1,1400]{1,0:T(2,128)(2,1)S(1)}, u32[]{:S(2)}, u32[]{:S(2)}) collective-permute-start(bf16[1,1400]{1,0:T(2,128)(2,1)S(1)} %get-tuple-element.104), channel_id=1, source_target_pairs={{4,8},{8,4},{12,16},{16,12},{20,24},{24,20},{5,9},{9,5},{13,17},{1... | collective-permute-start | bytes 8408 | tf_op jit(solution)/shard_map/ppermute | solution.py:871
  92.2 2.9 %collective-permute-start.24 = (bf16[1400,256]{1,0:T(8,128)(2,1)S(1)}, bf16[1400,256]{1,0:T(8,128)(2,1)S(1)}, u32[]{:S(2)}, u32[]{:S(2)}) collective-permute-start(bf16[1400,256]{1,0:T(8,128)(2,1)S(1)} %activate.3.own.own_b), channel_id=1, source_target_pairs={{0,1},{1,0},{2,3},{3,2},{4,5},{5,4},{6,7},{7,6},{8,9},{9,8},{10,11... | collective-permute-start | bytes 2150408 | tf_op jit(solution)/shard_map/ppermute | solution.py:732
  94.6 2.8 %collective-permute-start.23 = (bf16[1400,256]{1,0:T(8,128)(2,1)S(1)}, bf16[1400,256]{1,0:T(8,128)(2,1)S(1)}, u32[]{:S(2)}, u32[]{:S(2)}) collective-permute-start(bf16[1400,256]{1,0:T(8,128)(2,1)S(1)} %activate.2.own_a.own), channel_id=1, source_target_pairs={{0,1},{1,0},{2,3},{3,2},{4,5},{5,4},{6,7},{7,6},{8,9},{9,8},{10,11... | collective-permute-start | bytes 2150408 | tf_op jit(solution)/shard_map/ppermute | solution.py:732
  96.8 9.8 %collective-permute-start.26 = (bf16[560,256]{1,0:T(8,128)(2,1)S(1)}, bf16[560,256]{1,0:T(8,128)(2,1)S(1)}, u32[]{:S(2)}, u32[]{:S(2)}) collective-permute-start(bf16[560,256]{1,0:T(8,128)(2,1)S(1)} %far_project.2.after), channel_id=1, source_target_pairs={{0,2},{1,3},{2,0},{3,1},{4,6},{5,7},{6,4},{7,5},{8,10},{9,11},{10,... | collective-permute-start | bytes 860168 | tf_op jit(solution)/shard_map/ppermute | solution.py:736
  99.0 12.8 %collective-permute-start.25 = (bf16[560,256]{1,0:T(8,128)(2,1)S(1)}, bf16[560,256]{1,0:T(8,128)(2,1)S(1)}, u32[]{:S(2)}, u32[]{:S(2)}) collective-permute-start(bf16[560,256]{1,0:T(8,128)(2,1)S(1)} %far_project.3), channel_id=1, source_target_pairs={{0,2},{1,3},{2,0},{3,1},{4,6},{5,7},{6,4},{7,5},{8,10},{9,11},{10,... | collective-permute-start | bytes 860168 | tf_op jit(solution)/shard_map/ppermute | solution.py:736

commit v10 on v9

--- a/solution.py
+++ b/solution.py
@@ -457,7 +457,7 @@
     )(query, keys, erased, entry, totals, after)
 
 
-def pair_kernel(meta, own, other, pair, first, done):
+def pair_kernel(meta, own, other, pair_map, pair_shift, first, done):
     even = meta[PARITY] == 0
     for h in range(own.shape[0]):
         mine, theirs = own[h], other[h]
@@ -465,52 +465,54 @@
         late = jnp.where(even, theirs, mine)
         product = dot(late[:, :DK], early)
         shift = late[:, DK:].astype(f32)
-        pair[h] = (product + jnp.concatenate([jnp.zeros_like(shift), shift], axis=1)).astype(bf16)
+        pair_map[h] = product[:, :DK].astype(bf16)
+        pair_shift[h] = (product[:, DK:] + shift).astype(bf16)
         first[h] = early
     done[...] = jnp.zeros_like(done)
 
 
 def pair_maps(meta, own, other):
+    half = shape_of((own.shape[0], DK, DK))
     return pl.pallas_call(
         pair_kernel,
-        out_shape=(shape_of(own.shape), shape_of(own.shape), shape_of((8, 128), f32)),
+        out_shape=(half, half, shape_of(own.shape), shape_of((8, 128), f32)),
         in_specs=[SM, VM, VM],
-        out_specs=[VM] * 3,
+        out_specs=[VM] * 4,
         compiler_params=params(4),
         name="pair_maps",
     )(meta, own, other)
 
 
-def apply_map(whole, state):
+def apply_map(matrix, shift, state):
     high = state.astype(bf16)
     low = (state - high.astype(f32)).astype(bf16)
-    product = dot(whole[:, :DK], jnp.concatenate([high, low], axis=1))
-    return product[:, :DK] + product[:, DK:] + whole[:, DK:].astype(f32)
+    product = dot(matrix, jnp.concatenate([high, low], axis=1))
+    return product[:, :DK] + product[:, DK:] + shift.astype(f32)
 
 
 def start_kernel(steps, meta, first, *refs):
-    pairs, (after, keep, give) = refs[:steps], refs[steps:]
+    maps, shifts, (after, keep, give) = refs[: steps - 1], refs[steps - 1 : -3], refs[-3:]
     even = meta[PARITY] == 0
     for h in range(first.shape[0]):
-        state = pairs[0][h][:, DK:].astype(f32)
-        for pair in pairs[1:]:
-            state = apply_map(pair[h], state)
-        later = apply_map(first[h], state)
+        state = shifts[0][h].astype(f32)
+        for matrix, shift in zip(maps, shifts[1:]):
+            state = apply_map(matrix[h], shift[h], state)
+        later = apply_map(first[h][:, :DK], first[h][:, DK:], state)
         keep[h] = jnp.where(even, state, later).astype(bf16)
         give[h] = jnp.where(even, later, state).astype(bf16)
 
 
-def start_states(meta, first, pairs, after):
+def start_states(meta, first, maps, shifts, after):
     heads = first.shape[0]
     shape = shape_of((heads, DK, DK))
     return pl.pallas_call(
-        functools.partial(start_kernel, len(pairs)),
+        functools.partial(start_kernel, len(shifts)),
         out_shape=(shape, shape),
-        in_specs=[SM] + [VM] * (1 + len(pairs)) + [ANY],
+        in_specs=[SM] + [VM] * (1 + len(maps) + len(shifts)) + [ANY],
         out_specs=[VM] * 2,
         compiler_params=params(4),
         name="start_states",
-    )(meta, first, *pairs, after)
+    )(meta, first, *maps, *shifts, after)
 
 
 def mixed_kernel(heads, meta, own, other, shard_query, free, gain, mixed_a, mixed_b):
@@ -740,8 +742,8 @@
     return lax.ppermute(value, "seq", [(i, i ^ 1) for i in range(n)])
 
 
-def later(value, n, step):
-    return lax.ppermute(value, "seq", [(i, i + 2 * step) for i in range(n - 2 * step)])
+def later(value, n, step, start=0):
+    return lax.ppermute(value, "seq", [(i, i + 2 * step) for i in range(start, n - 2 * step)])
 
 
 def shards(
@@ -835,10 +837,11 @@
     ]
     partner_w_out = core_swap(their_rows, n)
     other_maps = pair_swap(sent_maps, seqs)
-    pair, first, done = pair_maps(meta, own_maps, other_maps)
+    pair_map, pair_shift, first, done = pair_maps(meta, own_maps, other_maps)
     fetched, _ = lax.optimization_barrier((fetched, done))
     swapped = [pair_swap(value, seqs) for value in fetched]
-    pairs = [later(pair, seqs, d) for d in range(seqs // 2 - 1, 0, -1)]
+    shifts = [later(pair_shift, seqs, d) for d in range(seqs // 2 - 1, 0, -1)]
+    maps = [later(pair_map, seqs, d, 2) for d in range(seqs // 2 - 2, 0, -1)]
     acc_query, partner_w_out, other_w_down, _ = lax.optimization_barrier(
         (early[2], partner_w_out, other_w_down, done)
     )
@@ -846,7 +849,7 @@
         meta, ys, scaled, scale_b, w_query, acc_query, sum(groups, [])
     )
     shard_query, free, out_done = block_outputs(query, keys, erased, entry, totals, done)
-    kept_state, given_state = start_states(meta, first, pairs, out_done)
+    kept_state, given_state = start_states(meta, first, maps, shifts, out_done)
     other_state = pair_swap(given_state, seqs)
 
     mixed = mixed_heads(meta, kept_state, other_state, shard_query, free, head_scale)

time: 115 us -> 113 us (0.983)
  waiting for transfers between devices: 35.5 us -> 29.1 us
  starting transfers between devices: 22.8 us -> 27.7 us
    ppermute x3 -> x5, waiting for transfers between devices: 5.63 us -> 1.76 us  [later(): lax.ppermute(value, 'seq', [(i, i + 2 * step) for i in range(start, n - 2...]
    ppermute x3 -> x5, starting transfers between devices: 6.26 us -> 9.66 us  [later(): lax.ppermute(value, 'seq', [(i, i + 2 * step) for i in range(start, n - 2...]
    ppermute x1, starting transfers between devices: 2.26 us -> 4.22 us  [shards(): lax.ppermute(next_row, 'seq', [(i, (i + 1 ^ 1) - 1) for i in range(1, seq...]
    ppermute x6, waiting for transfers between devices: 19.8 us -> 18.5 us  [y_shift(): lax.ppermute(value, 'head', [(i, (i + 2 * step) % n) for i in range(n)])]
  transfers between devices with their start and end apart: 27 -> 29, of which waited for: 12 -> 10; matrix products, arithmetic and copies ran while one was open for 4% -> 4% of each run, Pallas kernels for 41% -> 42%
where the time goes in v10:
time: 113 us; the launch traced here: 111 us
  Pallas kernels  48.9 us (43%)
  waiting for transfers between devices  29.1 us (26%)
  starting transfers between devices  27.7 us (25%)
  local copies, waits for them, and re-layouts  2.77 us (2%)
  other arithmetic  2.48 us (2%)
    ppermute x6, waiting for transfers between devices, y_shift(): lax.ppermute(value, 'head', [(i, (i + 2 * step) % n) for i in range(n)])  18.5 us
    pallas_call x1, Pallas kernels, block_maps(): pl.pallas_call(functools.partial(maps_kernel, n, heads, at), out_shape=(s...  12.3 us
    ppermute x5, starting transfers between devices, later(): lax.ppermute(value, 'seq', [(i, i + 2 * step) for i in range(start, n - 2...  9.66 us
    pallas_call x2, Pallas kernels, up_project(): pl.pallas_call(up_kernel, out_shape=(shape_of((count, hidden)), shape_of(...  7.56 us
    ppermute x6, starting transfers between devices, y_shift(): lax.ppermute(value, 'head', [(i, (i + 2 * step) % n) for i in range(n)])  7.27 us
    pallas_call x1, Pallas kernels, early_project(): pl.pallas_call(functools.partial(early_kernel, len(pieces), at), out_shap...  7.16 us
    ppermute x3, waiting for transfers between devices, pair_swap(): return lax.ppermute(value, 'seq', [(i, i ^ 1) for i in range(n)])  6.76 us
    pallas_call x2, Pallas kernels, activate(): pl.pallas_call(functools.partial(act_kernel, late), out_shape=shape_of((h...  4.58 us
  transfers between devices with their start and end apart: 29, of which 10 were waited for; matrix products, arithmetic and copies ran while one was open for 4% of the time, Pallas kernels for 42%

profile of v10, /device:TPU:16, one launch (start us, length us, event | category | flops | bytes accessed | tf_op | source)
XLA Modules:
  0.0 111.3 jit_solution(173959813833555492)
XLA Ops:
  0.0 1.5 %collective-permute-start = (bf16[560,512]{1,0:T(8,128)(2,1)}, bf16[560,512]{1,0:T(8,128)(2,1)S(1)}, u32[]{:S(2)}, u32[]{:S(2)}) collective-permute-start(bf16[560,512]{1,0:T(8,128)(2,1)} %bitcast.36), channel_id=1, source_target_pairs={{0,2},{1,3},{2,0},{3,1},{4,6},{5,7},{6,4},{7,5},{8,10},{9,11},{10,... | collective-permute-start | bytes 1720328 | tf_op jit(solution)/shard_map/ppermute | solution.py:738
  1.5 0.8 reshape.37
  2.3 0.8 fusion.3
  3.2 0.8 reshape.31
  4.0 0.7 convert_element_type.15.taps
  4.7 0.7 reshape.39.gain
  5.8 7.2 %early_project.1 = (f32[512,512]{1,0:T(8,128)S(1)}, f32[512,512]{1,0:T(8,128)S(1)}, f32[512,512]{1,0:T(8,128)S(1)}, f32[16,512]{1,0:T(8,128)S(1)}, f32[8,512]{1,...) custom-call(s32[6]{0:T(128)S(1)} %stack.24.meta, ...), custom_call_target="tpu_custom_call" | custom-call | flops 3000000000 | bytes 8000000 | tf_op jit(solution)/shard_map/early_project/pallas_call | solution.py:163
  12.9 2.0 %collective-permute-done.refs_0_.refs_2_ = bf16[560,512]{1,0:T(8,128)(2,1)S(1)} collective-permute-done((bf16[560,512]{1,0:T(8,128)(2,1)}, bf16[560,512]{1,0:T(8,128)(2,1)S(1)}, u32[]{:S(2)}, u32[]{:S(2)}) %collective-permute-start) | collective-permute-done | bytes 573472 | tf_op jit(solution)/shard_map/ppermute | solution.py:738
  14.9 2.0 %collective-permute-done.2.refs_1_.refs_3_ = bf16[560,512]{1,0:T(8,128)(2,1)S(1)} collective-permute-done((bf16[560,512]{1,0:T(8,128)(2,1)S(1)}, bf16[560,512]{1,0:T(8,128)(2,1)S(1)}, u32[]{:S(2)}, u32[]{:S(2)}) %collective-permute-start.2) | collective-permute-done | bytes 573472 | tf_op jit(solution)/shard_map/ppermute | solution.py:734
  17.4 1.5 %collective-permute-start.15 = (bf16[560,512]{1,0:T(8,128)(2,1)S(1)}, bf16[560,512]{1,0:T(8,128)(2,1)S(1)}, u32[]{:S(2)}, u32[]{:S(2)}) collective-permute-start(bf16[560,512]{1,0:T(8,128)(2,1)S(1)} %get-tuple-element.98), channel_id=1, source_target_pairs={{0,2},{1,3},{2,0},{3,1},{4,6},{5,7},{6,4},{7,5},{8,10},{9,11},{10,... | collective-permute-start | bytes 1720328 | tf_op jit(solution)/shard_map/ppermute | solution.py:738
  19.0 12.3 %block_maps.1 = (bf16[512,1120]{1,0:T(8,128)(2,1)S(1)}, f32[512,128]{1,0:T(8,128)S(1)}, bf16[512,512]{1,0:T(8,128)(2,1)S(1)}, bf16[512,1024]{1,0:T(8,128)(2,1)S(...) custom-call(s32[6]{0:T(128)S(1)} %stack.24.meta, ...), custom_call_target="tpu_custom_call" | custom-call | flops 10000000000 | bytes 14000000 | tf_op jit(solution)/shard_map/block_maps/pallas_call | solution.py:333
  31.3 1.6 %collective-permute-start.5 = (bf16[2,128,256]{2,1,0:T(8,128)(2,1)S(1)}, bf16[2,128,256]{2,1,0:T(8,128)(2,1)S(1)}, u32[]{:S(2)}, u32[]{:S(2)}) collective-permute-start(bf16[2,128,256]{2,1,0:T(8,128)(2,1)S(1)} %get-tuple-element.78), channel_id=1, source_target_pairs={{0,4},{4,0},{8,12},{12,8},{16,20},{20,16},{24,28},{28,24},{1,5},{5... | collective-permute-start | bytes 393224 | tf_op jit(solution)/shard_map/ppermute | solution.py:742
  32.9 3.8 %collective-permute-done.5.other = bf16[2,128,256]{2,1,0:T(8,128)(2,1)S(1)} collective-permute-done((bf16[2,128,256]{2,1,0:T(8,128)(2,1)S(1)}, bf16[2,128,256]{2,1,0:T(8,128)(2,1)S(1)}, u32[]{:S(2)}, u32[]{:S(2)}) %collective-permute-start.5) | collective-permute-done | bytes 131104 | tf_op jit(solution)/shard_map/ppermute | solution.py:742
  36.6 0.7 pair_maps.1
  37.3 0.7 collective-permute-start.6
  38.0 4.1 %collective-permute-start.7 = (bf16[2,128,128]{2,1,0:T(8,128)(2,1)S(1)}, bf16[2,128,128]{2,1,0:T(8,128)(2,1)S(1)}, u32[]{:S(2)}, u32[]{:S(2)}) collective-permute-start(bf16[2,128,128]{2,1,0:T(8,128)(2,1)S(1)} %get-tuple-element.83), channel_id=1, source_target_pairs={{8,16},{12,20},{16,24},{20,28},{9,17},{13,21},{17,25},{21,29},{10,... | collective-permute-start | bytes 196616 | tf_op jit(solution)/shard_map/ppermute | solution.py:746
  42.2 0.7 collective-permute-start.8
  42.8 1.9 %queries.1 = (bf16[512,512]{1,0:T(8,128)(2,1)S(1)}, bf16[2240,256]{1,0:T(8,128)(2,1)S(1)}, bf16[2240,256]{1,0:T(8,128)(2,1)S(1)}, f32[8,128]{1,0:T(8,128)}) custom-call(s32[6]{0:T(128)S(1)} %stack.24.meta, bf16[512,1120]{1,0:T(8,128)(2,1)S(1)} %get-tuple-element.69.scaled, f32[512,128]{1,0:T(8,128)S(1)} %get-tuple-element.70.scale_b, ...), custom_call_target="tpu_custom_call" | custom-call | flops 1000000000 | bytes 8000000 | tf_op jit(solution)/shard_map/queries/pallas_call | solution.py:397
  44.7 1.3 %collective-permute-start.9 = (bf16[2,128,128]{2,1,0:T(8,128)(2,1)S(1)}, bf16[2,128,128]{2,1,0:T(8,128)(2,1)S(1)}, u32[]{:S(2)}, u32[]{:S(2)}) collective-permute-start(bf16[2,128,128]{2,1,0:T(8,128)(2,1)S(1)} %get-tuple-element.84), channel_id=1, source_target_pairs={{0,16},{4,20},{8,24},{12,28},{1,17},{5,21},{9,25},{13,29},{2,18},{... | collective-permute-start | bytes 196616 | tf_op jit(solution)/shard_map/ppermute | solution.py:746
  46.5 2.9 %collective-permute-start.10 = (bf16[2,128,128]{2,1,0:T(8,128)(2,1)S(1)}, bf16[2,128,128]{2,1,0:T(8,128)(2,1)S(1)}, u32[]{:S(2)}, u32[]{:S(2)}) collective-permute-start(bf16[2,128,128]{2,1,0:T(8,128)(2,1)S(1)} %get-tuple-element.84), channel_id=1, source_target_pairs={{0,8},{4,12},{8,16},{12,20},{16,24},{20,28},{1,9},{5,13},{9,17},{1... | collective-permute-start | bytes 196616 | tf_op jit(solution)/shard_map/ppermute | solution.py:746
  49.5 2.8 %block_outputs.1 = (bf16[512,512]{1,0:T(8,128)(2,1)S(1)}, f32[512,512]{1,0:T(8,128)S(1)}, f32[8,128]{1,0:T(8,128)S(1)}) custom-call(bf16[512,512]{1,0:T(8,128)(2,1)S(1)} %get-tuple-element.85.query, bf16[512,512]{1,0:T(8,128)(2,1)S(1)} %get-tuple-element.86.keys, bf16[512,1024]{1,0:T(8,128)(2,1)S(1)} %get-tuple-element.87.erased, ...), custom_call_target="tpu_custom_call" | custom-call | flops 3000000000 | bytes 4000000 | tf_op jit(solution)/shard_map/block_outputs/pallas_call | solution.py:448
  52.4 1.2 %collective-permute-done.10.refs_4_ = bf16[2,128,128]{2,1,0:T(8,128)(2,1)S(1)} collective-permute-done((bf16[2,128,128]{2,1,0:T(8,128)(2,1)S(1)}, bf16[2,128,128]{2,1,0:T(8,128)(2,1)S(1)}, u32[]{:S(2)}, u32[]{:S(2)}) %collective-permute-start.10) | collective-permute-done | bytes 65568 | tf_op jit(solution)/shard_map/ppermute | solution.py:746
  53.6 1.2 %start_states.1 = (bf16[2,128,128]{2,1,0:T(8,128)(2,1)S(1)}, bf16[2,128,128]{2,1,0:T(8,128)(2,1)S(1)}) custom-call(s32[6]{0:T(128)S(1)} %stack.24.meta, bf16[2,128,256]{2,1,0:T(8,128)(2,1)S(1)} %get-tuple-element.82.first, bf16[2,128,128]{2,1,0:T(8,128)(2,1)S(1)} %collective-permute-done.6.refs_0_, bf16[2,128,128]{2,1,0:T(8,128)(2,1)S(1)} %collective-permute-done.7.refs_1_, ...), custom_call_target="tpu_custom_call" | custom-call | tf_op jit(solution)/shard_map/start_states/pallas_call | solution.py:508
  54.8 1.5 %collective-permute-start.11 = (bf16[2,128,128]{2,1,0:T(8,128)(2,1)S(1)}, bf16[2,128,128]{2,1,0:T(8,128)(2,1)S(1)}, u32[]{:S(2)}, u32[]{:S(2)}) collective-permute-start(bf16[2,128,128]{2,1,0:T(8,128)(2,1)S(1)} %get-tuple-element.92), channel_id=1, source_target_pairs={{0,4},{4,0},{8,12},{12,8},{16,20},{20,16},{24,28},{28,24},{1,5},{5... | collective-permute-start | bytes 196616 | tf_op jit(solution)/shard_map/ppermute | solution.py:742
  56.9 3.0 %collective-permute-done.11.other = bf16[2,128,128]{2,1,0:T(8,128)(2,1)S(1)} collective-permute-done((bf16[2,128,128]{2,1,0:T(8,128)(2,1)S(1)}, bf16[2,128,128]{2,1,0:T(8,128)(2,1)S(1)}, u32[]{:S(2)}, u32[]{:S(2)}) %collective-permute-start.11) | collective-permute-done | bytes 65568 | tf_op jit(solution)/shard_map/ppermute | solution.py:742
  59.9 1.1 mixed_heads.1
  61.0 0.6 collective-permute-start.13
  61.6 1.5 %collective-permute-start.20 = (bf16[256,512]{1,0:T(8,128)(2,1)S(1)}, bf16[256,512]{1,0:T(8,128)(2,1)S(1)}, u32[]{:S(2)}, u32[]{:S(2)}) collective-permute-start(bf16[256,512]{1,0:T(8,128)(2,1)S(1)} %get-tuple-element.103.own), channel_id=1, source_target_pairs={{0,2},{1,3},{2,0},{3,1},{4,6},{5,7},{6,4},{7,5},{8,10},{9,11},{10,... | collective-permute-start | bytes 786440 | tf_op jit(solution)/shard_map/ppermute | solution.py:738
  63.1 5.5 %collective-permute-done.13.refs_0_ = bf16[256,512]{1,0:T(8,128)(2,1)S(1)} collective-permute-done((bf16[256,512]{1,0:T(8,128)(2,1)S(1)}, bf16[256,512]{1,0:T(8,128)(2,1)S(1)}, u32[]{:S(2)}, u32[]{:S(2)}) %collective-permute-start.13) | collective-permute-done | bytes 262176 | tf_op jit(solution)/shard_map/ppermute | solution.py:738
  69.1 2.3 %collective-permute-done.20.refs_0_ = bf16[256,512]{1,0:T(8,128)(2,1)S(1)} collective-permute-done((bf16[256,512]{1,0:T(8,128)(2,1)S(1)}, bf16[256,512]{1,0:T(8,128)(2,1)S(1)}, u32[]{:S(2)}, u32[]{:S(2)}) %collective-permute-start.20) | collective-permute-done | bytes 262176 | tf_op jit(solution)/shard_map/ppermute | solution.py:738
  71.4 1.9 %attend.2.own = bf16[1120,256]{1,0:T(8,128)(2,1)S(1)} custom-call(s32[6]{0:T(128)S(1)} %stack.24.meta, bf16[2240,256]{1,0:T(8,128)(2,1)S(1)} %get-tuple-element.81.tokens, bf16[256,512]{1,0:T(8,128)(2,1)S(1)} %get-tuple-element.96.own, bf16[256,512]{1,0:T(8,128)(2,1)S(1)} %collective-permute-done.12.partner, bf16[2240,512]{1,0:T(8,128)(2,1)S(1)} %bitcast.34, ...), custom_call_target="tpu_custom_call" | custom-call | flops 2000000000 | bytes 7000000 | tf_op jit(solution)/shard_map/attend/pallas_call | solution.py:574
  73.4 0.6 collective-permute-start.18
  74.0 1.9 %attend.3.own = bf16[1120,256]{1,0:T(8,128)(2,1)S(1)} custom-call(s32[6]{0:T(128)S(1)} %stack.24.meta, bf16[2240,256]{1,0:T(8,128)(2,1)S(1)} %get-tuple-element.102.tokens, bf16[256,512]{1,0:T(8,128)(2,1)S(1)} %get-tuple-element.103.own, bf16[256,512]{1,0:T(8,128)(2,1)S(1)} %collective-permute-done.19.partner, bf16[2240,512]{1,0:T(8,128)(2,1)S(1)} %bitcast.35, ...), custom_call_target="tpu_custom_call" | custom-call | flops 2000000000 | bytes 7000000 | tf_op jit(solution)/shard_map/attend/pallas_call | solution.py:574
  76.1 3.5 %up_project.2 = (bf16[256,1400]{1,0:T(8,128)(2,1)S(1)}, f32[560,256]{1,0:T(8,128)S(1)}, bf16[1,1400]{1,0:T(2,128)(2,1)S(1)}, bf16[1,1400]{1,0:T(2,128)(2,1)S(1)}) custom-call(s32[6]{0:T(128)S(1)} %stack.24.meta, bf16[1120,256]{1,0:T(8,128)(2,1)S(1)} %attend.2.own, bf16[1120,256]{1,0:T(8,128)(2,1)S(1)} %collective-permute-done.18.other, ...), custom_call_target="tpu_custom_call" | custom-call | flops 2000000000 | bytes 8000000 | tf_op jit(solution)/shard_map/up_project/pallas_call | solution.py:618
  79.5 0.6 collective-permute-start.23
  80.2 4.2 %collective-permute-start.24 = (bf16[1,1400]{1,0:T(2,128)(2,1)S(1)}, bf16[1,1400]{1,0:T(2,128)(2,1)S(1)}, u32[]{:S(2)}, u32[]{:S(2)}) collective-permute-start(bf16[1,1400]{1,0:T(2,128)(2,1)S(1)} %get-tuple-element.106), channel_id=1, source_target_pairs={{4,8},{8,4},{12,16},{16,12},{20,24},{24,20},{5,9},{9,5},{13,17},{1... | collective-permute-start | bytes 8408 | tf_op jit(solution)/shard_map/ppermute | solution.py:874
  84.4 4.1 %up_project.3 = (bf16[256,1400]{1,0:T(8,128)(2,1)S(1)}, f32[560,256]{1,0:T(8,128)S(1)}, bf16[1,1400]{1,0:T(2,128)(2,1)}, bf16[1,1400]{1,0:T(2,128)(2,1)}) custom-call(s32[6]{0:T(128)S(1)} %stack.24.meta, bf16[1120,256]{1,0:T(8,128)(2,1)S(1)} %attend.3.own, bf16[1120,256]{1,0:T(8,128)(2,1)S(1)} %collective-permute-done.22.other, f32[1,2240]{1,0:T(1,128)S(1)} %reshape.39.gain, ...), custom_call_target="tpu_custom_call" | custom-call | flops 2000000000 | bytes 8000000 | tf_op jit(solution)/shard_map/up_project/pallas_call | solution.py:618
  88.5 2.3 %activate.3.own.own_b = bf16[1400,256]{1,0:T(8,128)(2,1)S(1)} custom-call(s32[6]{0:T(128)S(1)} %stack.24.meta, bf16[256,1400]{1,0:T(8,128)(2,1)S(1)} %get-tuple-element.101.outer, bf16[256,1400]{1,0:T(8,128)(2,1)S(1)} %get-tuple-element.104.inside, bf16[1,1400]{1,0:T(2,128)(2,1)S(1)} %collective-permute-done.23.near_row, ...), custom_call_target="tpu_custom_call" | custom-call | flops 1000000000 | bytes 2000000 | tf_op jit(solution)/shard_map/activate/pallas_call | solution.py:675
  90.9 2.3 %activate.2.own_a.own = bf16[1400,256]{1,0:T(8,128)(2,1)S(1)} custom-call(s32[6]{0:T(128)S(1)} %stack.24.meta, bf16[256,1400]{1,0:T(8,128)(2,1)S(1)} %get-tuple-element.101.outer, bf16[256,1400]{1,0:T(8,128)(2,1)S(1)} %get-tuple-element.104.inside, bf16[1,1400]{1,0:T(2,128)(2,1)S(1)} %collective-permute-done.23.near_row, ...), custom_call_target="tpu_custom_call" | custom-call | flops 1000000000 | bytes 2000000 | tf_op jit(solution)/shard_map/activate/pallas_call | solution.py:675
  93.1 0.6 collective-permute-start.25
  93.7 1.6 %far_project.2.after = bf16[560,256]{1,0:T(8,128)(2,1)S(1)} custom-call(s32[6]{0:T(128)S(1)} %stack.24.meta, bf16[1400,256]{1,0:T(8,128)(2,1)S(1)} %activate.3.own.own_b, bf16[1400,256]{1,0:T(8,128)(2,1)S(1)} %collective-permute-done.26.other.other_b, bf16[4,560,1400]{2,1,0:T(8,128)(2,1)S(1)} %bitcast.28, ...), custom_call_target="tpu_custom_call" | custom-call | flops 1000000000 | bytes 4000000 | tf_op jit(solution)/shard_map/far_project/pallas_call | solution.py:697
  95.3 0.6 collective-permute-start.28
  95.9 1.6 %far_project.3 = bf16[560,256]{1,0:T(8,128)(2,1)S(1)} custom-call(s32[6]{0:T(128)S(1)} %stack.24.meta, bf16[1400,256]{1,0:T(8,128)(2,1)S(1)} %activate.2.own_a.own, bf16[1400,256]{1,0:T(8,128)(2,1)S(1)} %collective-permute-done.25.other_a.other, bf16[4,560,1400]{2,1,0:T(8,128)(2,1)S(1)} %bitcast.29, ...), custom_call_target="tpu_custom_call" | custom-call | flops 1000000000 | bytes 4000000 | tf_op jit(solution)/shard_map/far_project/pallas_call | solution.py:697
  97.5 1.6 %collective-permute-start.27 = (bf16[560,256]{1,0:T(8,128)(2,1)S(1)}, bf16[560,256]{1,0:T(8,128)(2,1)S(1)}, u32[]{:S(2)}, u32[]{:S(2)}) collective-permute-start(bf16[560,256]{1,0:T(8,128)(2,1)S(1)} %far_project.3), channel_id=1, source_target_pairs={{0,2},{1,3},{2,0},{3,1},{4,6},{5,7},{6,4},{7,5},{8,10},{9,11},{10,... | collective-permute-start | bytes 860168 | tf_op jit(solution)/shard_map/ppermute | solution.py:738
  99.1 2.5 %near_project.1 = f32[560,512]{1,0:T(8,128)S(1)} custom-call(s32[6]{0:T(128)S(1)} %stack.24.meta, bf16[1400,256]{1,0:T(8,128)(2,1)S(1)} %activate.2.own_a.own, bf16[1400,256]{1,0:T(8,128)(2,1)S(1)} %collective-permute-done.25.other_a.other, bf16[1400,256]{1,0:T(8,128)(2,1)S(1)} %activate.3.own.own_b, ...), custom_call_target="tpu_custom_call" | custom-call | flops 2000000000 | bytes 6000000 | tf_op jit(solution)/shard_map/near_project/pallas_call | solution.py:722
  101.6 3.5 %collective-permute-done.28 = bf16[560,256]{1,0:T(8,128)(2,1)S(1)} collective-permute-done((bf16[560,256]{1,0:T(8,128)(2,1)S(1)}, bf16[560,256]{1,0:T(8,128)(2,1)S(1)}, u32[]{:S(2)}, u32[]{:S(2)}) %collective-permute-start.28) | collective-permute-done | bytes 286752 | tf_op jit(solution)/shard_map/ppermute | solution.py:738
  105.1 5.2 %collective-permute-done.27 = bf16[560,256]{1,0:T(8,128)(2,1)S(1)} collective-permute-done((bf16[560,256]{1,0:T(8,128)(2,1)S(1)}, bf16[560,256]{1,0:T(8,128)(2,1)S(1)}, u32[]{:S(2)}, u32[]{:S(2)}) %collective-permute-start.27) | collective-permute-done | bytes 286752 | tf_op jit(solution)/shard_map/ppermute | solution.py:738
  110.3 1.0 fusion
  (61 shorter events, 2.9 us)
Async XLA Ops:
  0.0 5.8 %copy-start.4 = (bf16[512,560]{0,1:T(8,128)(2,1)S(1)}, bf16[512,560]{0,1:T(8,128)(2,1)}, u32[]{:S(2)}) copy-start(bf16[512,560]{0,1:T(8,128)(2,1)} %param.14) | copy-start | bytes 1720324
  0.0 14.9 %collective-permute-start = (bf16[560,512]{1,0:T(8,128)(2,1)}, bf16[560,512]{1,0:T(8,128)(2,1)S(1)}, u32[]{:S(2)}, u32[]{:S(2)}) collective-permute-start(bf16[560,512]{1,0:T(8,128)(2,1)} %bitcast.36), channel_id=1, source_target_pairs={{0,2},{1,3},{2,0},{3,1},{4,6},{5,7},{6,4},{7,5},{8,10},{9,11},{10,... | collective-permute-start | bytes 1720328 | tf_op jit(solution)/shard_map/ppermute | solution.py:738
  1.5 4.2 %collective-permute-start.1 = (bf16[560,512]{1,0:T(8,128)(2,1)}, bf16[560,512]{1,0:T(8,128)(2,1)S(1)}, u32[]{:S(2)}, u32[]{:S(2)}) collective-permute-start(bf16[560,512]{1,0:T(8,128)(2,1)} %bitcast.37), channel_id=1, source_target_pairs={{0,1},{1,0},{2,3},{3,2},{4,5},{5,4},{6,7},{7,6},{8,9},{9,8},{10,11... | collective-permute-start | bytes 1720328 | tf_op jit(solution)/shard_map/ppermute | solution.py:734
  5.8 13.2 %copy-start.2 = (bf16[2240,512]{1,0:T(8,128)(2,1)S(1)}, bf16[2240,512]{1,0:T(8,128)(2,1)}, u32[]{:S(2)}) copy-start(bf16[2240,512]{1,0:T(8,128)(2,1)} %refs_5_.3) | copy-start | bytes 6881284
  5.8 13.2 %copy-start.3 = (bf16[2240,512]{1,0:T(8,128)(2,1)S(1)}, bf16[2240,512]{1,0:T(8,128)(2,1)}, u32[]{:S(2)}) copy-start(bf16[2240,512]{1,0:T(8,128)(2,1)} %refs_6_.3) | copy-start | bytes 6881284
  14.9 2.0 %collective-permute-start.2 = (bf16[560,512]{1,0:T(8,128)(2,1)S(1)}, bf16[560,512]{1,0:T(8,128)(2,1)S(1)}, u32[]{:S(2)}, u32[]{:S(2)}) collective-permute-start(bf16[560,512]{1,0:T(8,128)(2,1)S(1)} %collective-permute-done.refs_0_.refs_2_), channel_id=1, source_target_pairs={{0,1},{1,0},{2,3},{3,2},{4,5},{5,4},{6,7},{7,6},{8,9},{9,8},{10,11... | collective-permute-start | bytes 1720328 | tf_op jit(solution)/shard_map/ppermute | solution.py:734
  16.9 25.2 %collective-permute-start.4 = (bf16[2,560,1400]{2,1,0:T(8,128)(2,1)}, bf16[2,560,1400]{2,1,0:T(8,128)(2,1)S(1)}, u32[]{:S(2)}, u32[]{:S(2)}) collective-permute-start(bf16[2,560,1400]{2,1,0:T(8,128)(2,1)} %get-tuple-element.76), channel_id=1, source_target_pairs={{0,1},{1,0},{2,3},{3,2},{4,5},{5,4},{6,7},{7,6},{8,9},{9,8},{10,11... | collective-permute-start | bytes 9408008 | tf_op jit(solution)/shard_map/ppermute | solution.py:734
  17.0 21.0 %collective-permute-start.3 = (bf16[1120,512]{1,0:T(8,128)(2,1)S(1)}, bf16[1120,512]{1,0:T(8,128)(2,1)S(1)}, u32[]{:S(2)}, u32[]{:S(2)}) collective-permute-start(bf16[1120,512]{1,0:T(8,128)(2,1)S(1)} %get-tuple-element.75), channel_id=1, source_target_pairs={{0,1},{1,0},{2,3},{3,2},{4,5},{5,4},{6,7},{7,6},{8,9},{9,8},{10,11... | collective-permute-start | bytes 3440648 | tf_op jit(solution)/shard_map/ppermute | solution.py:734
  17.4 38.9 %collective-permute-start.15 = (bf16[560,512]{1,0:T(8,128)(2,1)S(1)}, bf16[560,512]{1,0:T(8,128)(2,1)S(1)}, u32[]{:S(2)}, u32[]{:S(2)}) collective-permute-start(bf16[560,512]{1,0:T(8,128)(2,1)S(1)} %get-tuple-element.98), channel_id=1, source_target_pairs={{0,2},{1,3},{2,0},{3,1},{4,6},{5,7},{6,4},{7,5},{8,10},{9,11},{10,... | collective-permute-start | bytes 1720328 | tf_op jit(solution)/shard_map/ppermute | solution.py:738
  18.9 23.9 %copy-start.1 = (bf16[2240,512]{1,0:T(8,128)(2,1)S(1)}, bf16[2240,512]{1,0:T(8,128)(2,1)}, u32[]{:S(2)}) copy-start(bf16[2240,512]{1,0:T(8,128)(2,1)} %weights.3) | copy-start | bytes 6881284
  31.3 5.3 %collective-permute-start.5 = (bf16[2,128,256]{2,1,0:T(8,128)(2,1)S(1)}, bf16[2,128,256]{2,1,0:T(8,128)(2,1)S(1)}, u32[]{:S(2)}, u32[]{:S(2)}) collective-permute-start(bf16[2,128,256]{2,1,0:T(8,128)(2,1)S(1)} %get-tuple-element.78), channel_id=1, source_target_pairs={{0,4},{4,0},{8,12},{12,8},{16,20},{20,16},{24,28},{28,24},{1,5},{5... | collective-permute-start | bytes 393224 | tf_op jit(solution)/shard_map/ppermute | solution.py:742
  32.9 38.6 %collective-permute-start.17 = (bf16[1120,512]{1,0:T(8,128)(2,1)S(1)}, bf16[1120,512]{1,0:T(8,128)(2,1)S(1)}, u32[]{:S(2)}, u32[]{:S(2)}) collective-permute-start(bf16[1120,512]{1,0:T(8,128)(2,1)S(1)} %get-tuple-element.75), channel_id=1, source_target_pairs={{0,3},{1,2},{2,1},{3,0},{4,7},{5,6},{6,5},{7,4},{8,11},{9,10},{10,... | collective-permute-start | bytes 3440648 | tf_op jit(solution)/shard_map/ppermute | solution.py:835
  37.3 7.4 %collective-permute-start.6 = (bf16[2,128,128]{2,1,0:T(8,128)(2,1)S(1)}, bf16[2,128,128]{2,1,0:T(8,128)(2,1)S(1)}, u32[]{:S(2)}, u32[]{:S(2)}) collective-permute-start(bf16[2,128,128]{2,1,0:T(8,128)(2,1)S(1)} %get-tuple-element.83), channel_id=1, source_target_pairs={{8,24},{12,28},{9,25},{13,29},{10,26},{14,30},{11,27},{15,31}} | collective-permute-start | bytes 196616 | tf_op jit(solution)/shard_map/ppermute | solution.py:746
  38.0 8.5 %collective-permute-start.7 = (bf16[2,128,128]{2,1,0:T(8,128)(2,1)S(1)}, bf16[2,128,128]{2,1,0:T(8,128)(2,1)S(1)}, u32[]{:S(2)}, u32[]{:S(2)}) collective-permute-start(bf16[2,128,128]{2,1,0:T(8,128)(2,1)S(1)} %get-tuple-element.83), channel_id=1, source_target_pairs={{8,16},{12,20},{16,24},{20,28},{9,17},{13,21},{17,25},{21,29},{10,... | collective-permute-start | bytes 196616 | tf_op jit(solution)/shard_map/ppermute | solution.py:746
  42.2 10.2 %collective-permute-start.8 = (bf16[2,128,128]{2,1,0:T(8,128)(2,1)S(1)}, bf16[2,128,128]{2,1,0:T(8,128)(2,1)S(1)}, u32[]{:S(2)}, u32[]{:S(2)}) collective-permute-start(bf16[2,128,128]{2,1,0:T(8,128)(2,1)S(1)} %get-tuple-element.84), channel_id=1, source_target_pairs={{0,24},{4,28},{1,25},{5,29},{2,26},{6,30},{3,27},{7,31}} | collective-permute-start | bytes 196616 | tf_op jit(solution)/shard_map/ppermute | solution.py:746
  44.7 7.6 %collective-permute-start.9 = (bf16[2,128,128]{2,1,0:T(8,128)(2,1)S(1)}, bf16[2,128,128]{2,1,0:T(8,128)(2,1)S(1)}, u32[]{:S(2)}, u32[]{:S(2)}) collective-permute-start(bf16[2,128,128]{2,1,0:T(8,128)(2,1)S(1)} %get-tuple-element.84), channel_id=1, source_target_pairs={{0,16},{4,20},{8,24},{12,28},{1,17},{5,21},{9,25},{13,29},{2,18},{... | collective-permute-start | bytes 196616 | tf_op jit(solution)/shard_map/ppermute | solution.py:746
  46.5 7.0 %collective-permute-start.10 = (bf16[2,128,128]{2,1,0:T(8,128)(2,1)S(1)}, bf16[2,128,128]{2,1,0:T(8,128)(2,1)S(1)}, u32[]{:S(2)}, u32[]{:S(2)}) collective-permute-start(bf16[2,128,128]{2,1,0:T(8,128)(2,1)S(1)} %get-tuple-element.84), channel_id=1, source_target_pairs={{0,8},{4,12},{8,16},{12,20},{16,24},{20,28},{1,9},{5,13},{9,17},{1... | collective-permute-start | bytes 196616 | tf_op jit(solution)/shard_map/ppermute | solution.py:746
  49.5 10.4 %copy-start.5 = (bf16[128]{0:T(256)(128)(2,1)S(1)}, bf16[128]{0:T(256)(128)(2,1)}, u32[]{:S(2)}) copy-start(bf16[128]{0:T(256)(128)(2,1)} %param.22) | copy-start | bytes 772
  54.8 5.1 %collective-permute-start.11 = (bf16[2,128,128]{2,1,0:T(8,128)(2,1)S(1)}, bf16[2,128,128]{2,1,0:T(8,128)(2,1)S(1)}, u32[]{:S(2)}, u32[]{:S(2)}) collective-permute-start(bf16[2,128,128]{2,1,0:T(8,128)(2,1)S(1)} %get-tuple-element.92), channel_id=1, source_target_pairs={{0,4},{4,0},{8,12},{12,8},{16,20},{20,16},{24,28},{28,24},{1,5},{5... | collective-permute-start | bytes 196616 | tf_op jit(solution)/shard_map/ppermute | solution.py:742
  56.3 12.3 %collective-permute-start.16 = (bf16[560,512]{1,0:T(8,128)(2,1)S(1)}, bf16[560,512]{1,0:T(8,128)(2,1)S(1)}, u32[]{:S(2)}, u32[]{:S(2)}) collective-permute-start(bf16[560,512]{1,0:T(8,128)(2,1)S(1)} %collective-permute-done.15.refs_2_), channel_id=1, source_target_pairs={{0,4},{4,0},{8,12},{12,8},{16,20},{20,16},{24,28},{28,24},{1,5},{5... | collective-permute-start | bytes 1720328 | tf_op jit(solution)/shard_map/ppermute | solution.py:742
  59.9 11.5 %copy-start = (bf16[512,2240]{0,1:T(8,128)(2,1)S(1)}, bf16[512,2240]{0,1:T(8,128)(2,1)}, u32[]{:S(2)}) copy-start(bf16[512,2240]{0,1:T(8,128)(2,1)} %param.23) | copy-start | bytes 6881284
  61.0 7.6 %collective-permute-start.13 = (bf16[256,512]{1,0:T(8,128)(2,1)S(1)}, bf16[256,512]{1,0:T(8,128)(2,1)S(1)}, u32[]{:S(2)}, u32[]{:S(2)}) collective-permute-start(bf16[256,512]{1,0:T(8,128)(2,1)S(1)} %get-tuple-element.96.own), channel_id=1, source_target_pairs={{0,2},{1,3},{2,0},{3,1},{4,6},{5,7},{6,4},{7,5},{8,10},{9,11},{10,... | collective-permute-start | bytes 786440 | tf_op jit(solution)/shard_map/ppermute | solution.py:738
  61.6 9.8 %collective-permute-start.20 = (bf16[256,512]{1,0:T(8,128)(2,1)S(1)}, bf16[256,512]{1,0:T(8,128)(2,1)S(1)}, u32[]{:S(2)}, u32[]{:S(2)}) collective-permute-start(bf16[256,512]{1,0:T(8,128)(2,1)S(1)} %get-tuple-element.103.own), channel_id=1, source_target_pairs={{0,2},{1,3},{2,0},{3,1},{4,6},{5,7},{6,4},{7,5},{8,10},{9,11},{10,... | collective-permute-start | bytes 786440 | tf_op jit(solution)/shard_map/ppermute | solution.py:738
  63.1 8.3 %collective-permute-start.12 = (bf16[256,512]{1,0:T(8,128)(2,1)S(1)}, bf16[256,512]{1,0:T(8,128)(2,1)S(1)}, u32[]{:S(2)}, u32[]{:S(2)}) collective-permute-start(bf16[256,512]{1,0:T(8,128)(2,1)S(1)} %get-tuple-element.96.own), channel_id=1, source_target_pairs={{0,1},{1,0},{2,3},{3,2},{4,5},{5,4},{6,7},{7,6},{8,9},{9,8},{10,11... | collective-permute-start | bytes 786440 | tf_op jit(solution)/shard_map/ppermute | solution.py:734
  68.6 2.8 %collective-permute-start.14 = (bf16[256,512]{1,0:T(8,128)(2,1)S(1)}, bf16[256,512]{1,0:T(8,128)(2,1)S(1)}, u32[]{:S(2)}, u32[]{:S(2)}) collective-permute-start(bf16[256,512]{1,0:T(8,128)(2,1)S(1)} %collective-permute-done.13.refs_0_), channel_id=1, source_target_pairs={{0,1},{1,0},{2,3},{3,2},{4,5},{5,4},{6,7},{7,6},{8,9},{9,8},{10,11... | collective-permute-start | bytes 786440 | tf_op jit(solution)/shard_map/ppermute | solution.py:734
  68.6 5.4 %collective-permute-start.19 = (bf16[256,512]{1,0:T(8,128)(2,1)S(1)}, bf16[256,512]{1,0:T(8,128)(2,1)S(1)}, u32[]{:S(2)}, u32[]{:S(2)}) collective-permute-start(bf16[256,512]{1,0:T(8,128)(2,1)S(1)} %get-tuple-element.103.own), channel_id=1, source_target_pairs={{0,1},{1,0},{2,3},{3,2},{4,5},{5,4},{6,7},{7,6},{8,9},{9,8},{10,11... | collective-permute-start | bytes 786440 | tf_op jit(solution)/shard_map/ppermute | solution.py:734
  71.4 2.6 %collective-permute-start.21 = (bf16[256,512]{1,0:T(8,128)(2,1)S(1)}, bf16[256,512]{1,0:T(8,128)(2,1)S(1)}, u32[]{:S(2)}, u32[]{:S(2)}) collective-permute-start(bf16[256,512]{1,0:T(8,128)(2,1)S(1)} %collective-permute-done.20.refs_0_), channel_id=1, source_target_pairs={{0,1},{1,0},{2,3},{3,2},{4,5},{5,4},{6,7},{7,6},{8,9},{9,8},{10,11... | collective-permute-start | bytes 786440 | tf_op jit(solution)/shard_map/ppermute | solution.py:734
  71.4 4.6 %slice-start.2 = ((s8[6307840]{0:T(1024)(128)(4,1)}), s8[4194304]{0:T(1024)(128)(4,1)S(1)}, s32[]{:S(2)}) async-start(s8[6307840]{0:T(1024)(128)(4,1)} %bitcast.31), calls=%async_computation.2 | async-start | bytes 8388608
  73.4 2.6 %slice-start.3 = ((s8[6307840]{0:T(1024)(128)(4,1)}), s8[2113536]{0:T(1024)(128)(4,1)S(1)}, s32[]{:S(2)}) async-start(s8[6307840]{0:T(1024)(128)(4,1)} %bitcast.31), calls=%async_computation.3 | async-start | bytes 4227072
  73.4 2.6 %collective-permute-start.18 = (bf16[1120,256]{1,0:T(8,128)(2,1)S(1)}, bf16[1120,256]{1,0:T(8,128)(2,1)S(1)}, u32[]{:S(2)}, u32[]{:S(2)}) collective-permute-start(bf16[1120,256]{1,0:T(8,128)(2,1)S(1)} %attend.2.own), channel_id=1, source_target_pairs={{0,1},{1,0},{2,3},{3,2},{4,5},{5,4},{6,7},{7,6},{8,9},{9,8},{10,11... | collective-permute-start | bytes 1720328 | tf_op jit(solution)/shard_map/ppermute | solution.py:734
  75.9 8.4 %collective-permute-start.22 = (bf16[1120,256]{1,0:T(8,128)(2,1)S(1)}, bf16[1120,256]{1,0:T(8,128)(2,1)S(1)}, u32[]{:S(2)}, u32[]{:S(2)}) collective-permute-start(bf16[1120,256]{1,0:T(8,128)(2,1)S(1)} %attend.3.own), channel_id=1, source_target_pairs={{0,1},{1,0},{2,3},{3,2},{4,5},{5,4},{6,7},{7,6},{8,9},{9,8},{10,11... | collective-permute-start | bytes 1720328 | tf_op jit(solution)/shard_map/ppermute | solution.py:734
  76.1 17.7 %slice-start = ((s8[6307840]{0:T(1024)(128)(4,1)}), s8[4194304]{0:T(1024)(128)(4,1)S(1)}, s32[]{:S(2)}) async-start(s8[6307840]{0:T(1024)(128)(4,1)} %bitcast.26), calls=%async_computation | async-start | bytes 8388608
  79.5 8.9 %collective-permute-start.23 = (bf16[1,1400]{1,0:T(2,128)(2,1)S(1)}, bf16[1,1400]{1,0:T(2,128)(2,1)S(1)}, u32[]{:S(2)}, u32[]{:S(2)}) collective-permute-start(bf16[1,1400]{1,0:T(2,128)(2,1)S(1)} %get-tuple-element.105), channel_id=1, source_target_pairs={{0,4},{4,0},{8,12},{12,8},{16,20},{20,16},{24,28},{28,24},{1,5},{5... | collective-permute-start | bytes 8408 | tf_op jit(solution)/shard_map/ppermute | solution.py:873
  80.1 13.6 %slice-start.1 = ((s8[6307840]{0:T(1024)(128)(4,1)}), s8[2113536]{0:T(1024)(128)(4,1)S(1)}, s32[]{:S(2)}) async-start(s8[6307840]{0:T(1024)(128)(4,1)} %bitcast.26), calls=%async_computation.1 | async-start | bytes 4227072
  80.2 8.3 %collective-permute-start.24 = (bf16[1,1400]{1,0:T(2,128)(2,1)S(1)}, bf16[1,1400]{1,0:T(2,128)(2,1)S(1)}, u32[]{:S(2)}, u32[]{:S(2)}) collective-permute-start(bf16[1,1400]{1,0:T(2,128)(2,1)S(1)} %get-tuple-element.106), channel_id=1, source_target_pairs={{4,8},{8,4},{12,16},{16,12},{20,24},{24,20},{5,9},{9,5},{13,17},{1... | collective-permute-start | bytes 8408 | tf_op jit(solution)/shard_map/ppermute | solution.py:874
  90.8 2.9 %collective-permute-start.26 = (bf16[1400,256]{1,0:T(8,128)(2,1)S(1)}, bf16[1400,256]{1,0:T(8,128)(2,1)S(1)}, u32[]{:S(2)}, u32[]{:S(2)}) collective-permute-start(bf16[1400,256]{1,0:T(8,128)(2,1)S(1)} %activate.3.own.own_b), channel_id=1, source_target_pairs={{0,1},{1,0},{2,3},{3,2},{4,5},{5,4},{6,7},{7,6},{8,9},{9,8},{10,11... | collective-permute-start | bytes 2150408 | tf_op jit(solution)/shard_map/ppermute | solution.py:734
  93.1 2.8 %collective-permute-start.25 = (bf16[1400,256]{1,0:T(8,128)(2,1)S(1)}, bf16[1400,256]{1,0:T(8,128)(2,1)S(1)}, u32[]{:S(2)}, u32[]{:S(2)}) collective-permute-start(bf16[1400,256]{1,0:T(8,128)(2,1)S(1)} %activate.2.own_a.own), channel_id=1, source_target_pairs={{0,1},{1,0},{2,3},{3,2},{4,5},{5,4},{6,7},{7,6},{8,9},{9,8},{10,11... | collective-permute-start | bytes 2150408 | tf_op jit(solution)/shard_map/ppermute | solution.py:734
  95.3 9.8 %collective-permute-start.28 = (bf16[560,256]{1,0:T(8,128)(2,1)S(1)}, bf16[560,256]{1,0:T(8,128)(2,1)S(1)}, u32[]{:S(2)}, u32[]{:S(2)}) collective-permute-start(bf16[560,256]{1,0:T(8,128)(2,1)S(1)} %far_project.2.after), channel_id=1, source_target_pairs={{0,2},{1,3},{2,0},{3,1},{4,6},{5,7},{6,4},{7,5},{8,10},{9,11},{10,... | collective-permute-start | bytes 860168 | tf_op jit(solution)/shard_map/ppermute | solution.py:738
  97.5 12.8 %collective-permute-start.27 = (bf16[560,256]{1,0:T(8,128)(2,1)S(1)}, bf16[560,256]{1,0:T(8,128)(2,1)S(1)}, u32[]{:S(2)}, u32[]{:S(2)}) collective-permute-start(bf16[560,256]{1,0:T(8,128)(2,1)S(1)} %far_project.3), channel_id=1, source_target_pairs={{0,2},{1,3},{2,0},{3,1},{4,6},{5,7},{6,4},{7,5},{8,10},{9,11},{10,... | collective-permute-start | bytes 860168 | tf_op jit(solution)/shard_map/ppermute | solution.py:738

commit v11 on v10

--- a/solution.py
+++ b/solution.py
@@ -74,6 +74,20 @@
 def fill_columns(row, target):
     for start in range(0, row.shape[1], 128):
         target[start : start + 128, :] = column_of(row[:, start : start + 128])
+
+
+def later_rows(tile, size):
+    return jnp.concatenate(
+        [tile[at + size : at + 2 * size] for at in range(0, tile.shape[0], 2 * size)], axis=0
+    )
+
+
+def spread_rows(tile, size):
+    empty = jnp.zeros((size, tile.shape[1]), tile.dtype)
+    parts = []
+    for at in range(0, tile.shape[0], size):
+        parts += [empty, tile[at : at + size]]
+    return jnp.concatenate(parts, axis=0)
 
 
 def doubled(tile):
@@ -262,7 +276,18 @@
             lows.append(low)
             solved.append(eye - jnp.where(xor == 1, low, 0.0))
         size = 2
+        steps = [None] * len(chains)
         while size < BLOCK:
+            if size >= 16:
+                mask = later_rows(xor, size) >= size
+                for i in range(len(chains)):
+                    link = jnp.where(mask & (later_rows(xor, size) < 2 * size), later_rows(lows[i], size), 0.0)
+                    whole_b = solved[i].astype(bf16)
+                    moved = dot(link.astype(bf16), whole_b).astype(bf16)
+                    steps[i] = dot(later_rows(whole_b, size), spread_rows(moved, size))
+                solved = [solved[i] - spread_rows(steps[i], size) for i in range(len(chains))]
+                size *= 2
+                continue
             mask = (xor >= size) & (xor < 2 * size)
             first = []
             for i in range(len(chains)):
@@ -637,8 +662,8 @@
 
 
 def gelu_of(x):
-    inner = 0.7978845608028654 * (x + 0.044715 * (x * x * x))
-    return 0.5 * x * (1.0 + jnp.tanh(inner))
+    half = 0.5 * x
+    return half + half * jnp.tanh(x * (0.7978845608028654 + 0.035677408136300125 * (x * x)))
 
 
 def act_kernel(late, meta, outer, inside, near_row, next_row, taps, act_t, padded, act):

time: 113 us -> 112 us (level)
  no operation moved by 1% of the time
where the time goes in v11:
time: 112 us; the launch traced here: 111 us
  Pallas kernels  48.3 us (43%)
  waiting for transfers between devices  29.1 us (26%)
  starting transfers between devices  27.7 us (25%)
  local copies, waits for them, and re-layouts  2.77 us (2%)
  other arithmetic  2.48 us (2%)
    ppermute x6, waiting for transfers between devices, y_shift(): lax.ppermute(value, 'head', [(i, (i + 2 * step) % n) for i in range(n)])  18.5 us
    pallas_call x1, Pallas kernels, block_maps(): pl.pallas_call(functools.partial(maps_kernel, n, heads, at), out_shape=(s...  11.8 us
    ppermute x5, starting transfers between devices, later(): lax.ppermute(value, 'seq', [(i, i + 2 * step) for i in range(start, n - 2...  9.66 us
    pallas_call x2, Pallas kernels, up_project(): pl.pallas_call(up_kernel, out_shape=(shape_of((count, hidden)), shape_of(...  7.56 us
    ppermute x6, starting transfers between devices, y_shift(): lax.ppermute(value, 'head', [(i, (i + 2 * step) % n) for i in range(n)])  7.27 us
    pallas_call x1, Pallas kernels, early_project(): pl.pallas_call(functools.partial(early_kernel, len(pieces), at), out_shap...  7.16 us
    ppermute x3, waiting for transfers between devices, pair_swap(): return lax.ppermute(value, 'seq', [(i, i ^ 1) for i in range(n)])  6.76 us
    pallas_call x2, Pallas kernels, activate(): pl.pallas_call(functools.partial(act_kernel, late), out_shape=shape_of((h...  4.5 us
  transfers between devices with their start and end apart: 29, of which 10 were waited for; matrix products, arithmetic and copies ran while one was open for 4% of the time, Pallas kernels for 42%

profile of v11, /device:TPU:16, one launch (start us, length us, event | category | flops | bytes accessed | tf_op | source)
XLA Modules:
  0.0 110.7 jit_solution(3748502305567281612)
XLA Ops:
  0.0 1.5 %collective-permute-start = (bf16[560,512]{1,0:T(8,128)(2,1)}, bf16[560,512]{1,0:T(8,128)(2,1)S(1)}, u32[]{:S(2)}, u32[]{:S(2)}) collective-permute-start(bf16[560,512]{1,0:T(8,128)(2,1)} %bitcast.36), channel_id=1, source_target_pairs={{0,2},{1,3},{2,0},{3,1},{4,6},{5,7},{6,4},{7,5},{8,10},{9,11},{10,... | collective-permute-start | bytes 1720328 | tf_op jit(solution)/shard_map/ppermute | solution.py:763
  1.5 0.8 reshape.37
  2.3 0.8 fusion.3
  3.2 0.8 reshape.31
  4.0 0.7 convert_element_type.15.taps
  4.7 0.7 reshape.39.gain
  5.8 7.2 %early_project.1 = (f32[512,512]{1,0:T(8,128)S(1)}, f32[512,512]{1,0:T(8,128)S(1)}, f32[512,512]{1,0:T(8,128)S(1)}, f32[16,512]{1,0:T(8,128)S(1)}, f32[8,512]{1,...) custom-call(s32[6]{0:T(128)S(1)} %stack.24.meta, ...), custom_call_target="tpu_custom_call" | custom-call | flops 3000000000 | bytes 8000000 | tf_op jit(solution)/shard_map/early_project/pallas_call | solution.py:177
  12.9 2.0 %collective-permute-done.refs_0_.refs_2_ = bf16[560,512]{1,0:T(8,128)(2,1)S(1)} collective-permute-done((bf16[560,512]{1,0:T(8,128)(2,1)}, bf16[560,512]{1,0:T(8,128)(2,1)S(1)}, u32[]{:S(2)}, u32[]{:S(2)}) %collective-permute-start) | collective-permute-done | bytes 573472 | tf_op jit(solution)/shard_map/ppermute | solution.py:763
  14.9 2.0 %collective-permute-done.2.refs_1_.refs_3_ = bf16[560,512]{1,0:T(8,128)(2,1)S(1)} collective-permute-done((bf16[560,512]{1,0:T(8,128)(2,1)S(1)}, bf16[560,512]{1,0:T(8,128)(2,1)S(1)}, u32[]{:S(2)}, u32[]{:S(2)}) %collective-permute-start.2) | collective-permute-done | bytes 573472 | tf_op jit(solution)/shard_map/ppermute | solution.py:759
  17.4 1.5 %collective-permute-start.15 = (bf16[560,512]{1,0:T(8,128)(2,1)S(1)}, bf16[560,512]{1,0:T(8,128)(2,1)S(1)}, u32[]{:S(2)}, u32[]{:S(2)}) collective-permute-start(bf16[560,512]{1,0:T(8,128)(2,1)S(1)} %get-tuple-element.98), channel_id=1, source_target_pairs={{0,2},{1,3},{2,0},{3,1},{4,6},{5,7},{6,4},{7,5},{8,10},{9,11},{10,... | collective-permute-start | bytes 1720328 | tf_op jit(solution)/shard_map/ppermute | solution.py:763
  19.0 11.8 %block_maps.1 = (bf16[512,1120]{1,0:T(8,128)(2,1)S(1)}, f32[512,128]{1,0:T(8,128)S(1)}, bf16[512,512]{1,0:T(8,128)(2,1)S(1)}, bf16[512,1024]{1,0:T(8,128)(2,1)S(...) custom-call(s32[6]{0:T(128)S(1)} %stack.24.meta, ...), custom_call_target="tpu_custom_call" | custom-call | flops 10000000000 | bytes 14000000 | tf_op jit(solution)/shard_map/block_maps/pallas_call | solution.py:358
  30.8 1.6 %collective-permute-start.5 = (bf16[2,128,256]{2,1,0:T(8,128)(2,1)S(1)}, bf16[2,128,256]{2,1,0:T(8,128)(2,1)S(1)}, u32[]{:S(2)}, u32[]{:S(2)}) collective-permute-start(bf16[2,128,256]{2,1,0:T(8,128)(2,1)S(1)} %get-tuple-element.78), channel_id=1, source_target_pairs={{0,4},{4,0},{8,12},{12,8},{16,20},{20,16},{24,28},{28,24},{1,5},{5... | collective-permute-start | bytes 393224 | tf_op jit(solution)/shard_map/ppermute | solution.py:767
  32.3 3.8 %collective-permute-done.5.other = bf16[2,128,256]{2,1,0:T(8,128)(2,1)S(1)} collective-permute-done((bf16[2,128,256]{2,1,0:T(8,128)(2,1)S(1)}, bf16[2,128,256]{2,1,0:T(8,128)(2,1)S(1)}, u32[]{:S(2)}, u32[]{:S(2)}) %collective-permute-start.5) | collective-permute-done | bytes 131104 | tf_op jit(solution)/shard_map/ppermute | solution.py:767
  36.1 0.7 pair_maps.1
  36.8 0.7 collective-permute-start.6
  37.5 4.1 %collective-permute-start.7 = (bf16[2,128,128]{2,1,0:T(8,128)(2,1)S(1)}, bf16[2,128,128]{2,1,0:T(8,128)(2,1)S(1)}, u32[]{:S(2)}, u32[]{:S(2)}) collective-permute-start(bf16[2,128,128]{2,1,0:T(8,128)(2,1)S(1)} %get-tuple-element.83), channel_id=1, source_target_pairs={{8,16},{12,20},{16,24},{20,28},{9,17},{13,21},{17,25},{21,29},{10,... | collective-permute-start | bytes 196616 | tf_op jit(solution)/shard_map/ppermute | solution.py:771
  41.6 0.7 collective-permute-start.8
  42.3 1.9 %queries.1 = (bf16[512,512]{1,0:T(8,128)(2,1)S(1)}, bf16[2240,256]{1,0:T(8,128)(2,1)S(1)}, bf16[2240,256]{1,0:T(8,128)(2,1)S(1)}, f32[8,128]{1,0:T(8,128)}) custom-call(s32[6]{0:T(128)S(1)} %stack.24.meta, bf16[512,1120]{1,0:T(8,128)(2,1)S(1)} %get-tuple-element.69.scaled, f32[512,128]{1,0:T(8,128)S(1)} %get-tuple-element.70.scale_b, ...), custom_call_target="tpu_custom_call" | custom-call | flops 1000000000 | bytes 8000000 | tf_op jit(solution)/shard_map/queries/pallas_call | solution.py:422
  44.2 1.3 %collective-permute-start.9 = (bf16[2,128,128]{2,1,0:T(8,128)(2,1)S(1)}, bf16[2,128,128]{2,1,0:T(8,128)(2,1)S(1)}, u32[]{:S(2)}, u32[]{:S(2)}) collective-permute-start(bf16[2,128,128]{2,1,0:T(8,128)(2,1)S(1)} %get-tuple-element.84), channel_id=1, source_target_pairs={{0,16},{4,20},{8,24},{12,28},{1,17},{5,21},{9,25},{13,29},{2,18},{... | collective-permute-start | bytes 196616 | tf_op jit(solution)/shard_map/ppermute | solution.py:771
  46.0 2.9 %collective-permute-start.10 = (bf16[2,128,128]{2,1,0:T(8,128)(2,1)S(1)}, bf16[2,128,128]{2,1,0:T(8,128)(2,1)S(1)}, u32[]{:S(2)}, u32[]{:S(2)}) collective-permute-start(bf16[2,128,128]{2,1,0:T(8,128)(2,1)S(1)} %get-tuple-element.84), channel_id=1, source_target_pairs={{0,8},{4,12},{8,16},{12,20},{16,24},{20,28},{1,9},{5,13},{9,17},{1... | collective-permute-start | bytes 196616 | tf_op jit(solution)/shard_map/ppermute | solution.py:771
  49.0 2.8 %block_outputs.1 = (bf16[512,512]{1,0:T(8,128)(2,1)S(1)}, f32[512,512]{1,0:T(8,128)S(1)}, f32[8,128]{1,0:T(8,128)S(1)}) custom-call(bf16[512,512]{1,0:T(8,128)(2,1)S(1)} %get-tuple-element.85.query, bf16[512,512]{1,0:T(8,128)(2,1)S(1)} %get-tuple-element.86.keys, bf16[512,1024]{1,0:T(8,128)(2,1)S(1)} %get-tuple-element.87.erased, ...), custom_call_target="tpu_custom_call" | custom-call | flops 3000000000 | bytes 4000000 | tf_op jit(solution)/shard_map/block_outputs/pallas_call | solution.py:473
  51.8 1.2 %collective-permute-done.10.refs_4_ = bf16[2,128,128]{2,1,0:T(8,128)(2,1)S(1)} collective-permute-done((bf16[2,128,128]{2,1,0:T(8,128)(2,1)S(1)}, bf16[2,128,128]{2,1,0:T(8,128)(2,1)S(1)}, u32[]{:S(2)}, u32[]{:S(2)}) %collective-permute-start.10) | collective-permute-done | bytes 65568 | tf_op jit(solution)/shard_map/ppermute | solution.py:771
  53.1 1.2 %start_states.1 = (bf16[2,128,128]{2,1,0:T(8,128)(2,1)S(1)}, bf16[2,128,128]{2,1,0:T(8,128)(2,1)S(1)}) custom-call(s32[6]{0:T(128)S(1)} %stack.24.meta, bf16[2,128,256]{2,1,0:T(8,128)(2,1)S(1)} %get-tuple-element.82.first, bf16[2,128,128]{2,1,0:T(8,128)(2,1)S(1)} %collective-permute-done.6.refs_0_, bf16[2,128,128]{2,1,0:T(8,128)(2,1)S(1)} %collective-permute-done.7.refs_1_, ...), custom_call_target="tpu_custom_call" | custom-call | tf_op jit(solution)/shard_map/start_states/pallas_call | solution.py:533
  54.3 1.5 %collective-permute-start.11 = (bf16[2,128,128]{2,1,0:T(8,128)(2,1)S(1)}, bf16[2,128,128]{2,1,0:T(8,128)(2,1)S(1)}, u32[]{:S(2)}, u32[]{:S(2)}) collective-permute-start(bf16[2,128,128]{2,1,0:T(8,128)(2,1)S(1)} %get-tuple-element.92), channel_id=1, source_target_pairs={{0,4},{4,0},{8,12},{12,8},{16,20},{20,16},{24,28},{28,24},{1,5},{5... | collective-permute-start | bytes 196616 | tf_op jit(solution)/shard_map/ppermute | solution.py:767
  55.8 0.6 collective-permute-start.16
  56.4 3.0 %collective-permute-done.11.other = bf16[2,128,128]{2,1,0:T(8,128)(2,1)S(1)} collective-permute-done((bf16[2,128,128]{2,1,0:T(8,128)(2,1)S(1)}, bf16[2,128,128]{2,1,0:T(8,128)(2,1)S(1)}, u32[]{:S(2)}, u32[]{:S(2)}) %collective-permute-start.11) | collective-permute-done | bytes 65568 | tf_op jit(solution)/shard_map/ppermute | solution.py:767
  59.4 1.1 mixed_heads.1
  60.5 0.6 collective-permute-start.13
  61.0 1.5 %collective-permute-start.20 = (bf16[256,512]{1,0:T(8,128)(2,1)S(1)}, bf16[256,512]{1,0:T(8,128)(2,1)S(1)}, u32[]{:S(2)}, u32[]{:S(2)}) collective-permute-start(bf16[256,512]{1,0:T(8,128)(2,1)S(1)} %get-tuple-element.103.own), channel_id=1, source_target_pairs={{0,2},{1,3},{2,0},{3,1},{4,6},{5,7},{6,4},{7,5},{8,10},{9,11},{10,... | collective-permute-start | bytes 786440 | tf_op jit(solution)/shard_map/ppermute | solution.py:763
  62.6 5.5 %collective-permute-done.13.refs_0_ = bf16[256,512]{1,0:T(8,128)(2,1)S(1)} collective-permute-done((bf16[256,512]{1,0:T(8,128)(2,1)S(1)}, bf16[256,512]{1,0:T(8,128)(2,1)S(1)}, u32[]{:S(2)}, u32[]{:S(2)}) %collective-permute-start.13) | collective-permute-done | bytes 262176 | tf_op jit(solution)/shard_map/ppermute | solution.py:763
  68.6 2.3 %collective-permute-done.20.refs_0_ = bf16[256,512]{1,0:T(8,128)(2,1)S(1)} collective-permute-done((bf16[256,512]{1,0:T(8,128)(2,1)S(1)}, bf16[256,512]{1,0:T(8,128)(2,1)S(1)}, u32[]{:S(2)}, u32[]{:S(2)}) %collective-permute-start.20) | collective-permute-done | bytes 262176 | tf_op jit(solution)/shard_map/ppermute | solution.py:763
  70.9 1.9 %attend.2.own = bf16[1120,256]{1,0:T(8,128)(2,1)S(1)} custom-call(s32[6]{0:T(128)S(1)} %stack.24.meta, bf16[2240,256]{1,0:T(8,128)(2,1)S(1)} %get-tuple-element.81.tokens, bf16[256,512]{1,0:T(8,128)(2,1)S(1)} %get-tuple-element.96.own, bf16[256,512]{1,0:T(8,128)(2,1)S(1)} %collective-permute-done.12.partner, bf16[2240,512]{1,0:T(8,128)(2,1)S(1)} %bitcast.34, ...), custom_call_target="tpu_custom_call" | custom-call | flops 2000000000 | bytes 7000000 | tf_op jit(solution)/shard_map/attend/pallas_call | solution.py:599
  72.9 0.6 collective-permute-start.18
  73.5 1.9 %attend.3.own = bf16[1120,256]{1,0:T(8,128)(2,1)S(1)} custom-call(s32[6]{0:T(128)S(1)} %stack.24.meta, bf16[2240,256]{1,0:T(8,128)(2,1)S(1)} %get-tuple-element.102.tokens, bf16[256,512]{1,0:T(8,128)(2,1)S(1)} %get-tuple-element.103.own, bf16[256,512]{1,0:T(8,128)(2,1)S(1)} %collective-permute-done.19.partner, bf16[2240,512]{1,0:T(8,128)(2,1)S(1)} %bitcast.35, ...), custom_call_target="tpu_custom_call" | custom-call | flops 2000000000 | bytes 7000000 | tf_op jit(solution)/shard_map/attend/pallas_call | solution.py:599
  75.5 3.5 %up_project.2 = (bf16[256,1400]{1,0:T(8,128)(2,1)S(1)}, f32[560,256]{1,0:T(8,128)S(1)}, bf16[1,1400]{1,0:T(2,128)(2,1)S(1)}, bf16[1,1400]{1,0:T(2,128)(2,1)S(1)}) custom-call(s32[6]{0:T(128)S(1)} %stack.24.meta, bf16[1120,256]{1,0:T(8,128)(2,1)S(1)} %attend.2.own, bf16[1120,256]{1,0:T(8,128)(2,1)S(1)} %collective-permute-done.18.other, ...), custom_call_target="tpu_custom_call" | custom-call | flops 2000000000 | bytes 8000000 | tf_op jit(solution)/shard_map/up_project/pallas_call | solution.py:643
  79.0 0.6 collective-permute-start.23
  79.6 4.2 %collective-permute-start.24 = (bf16[1,1400]{1,0:T(2,128)(2,1)S(1)}, bf16[1,1400]{1,0:T(2,128)(2,1)S(1)}, u32[]{:S(2)}, u32[]{:S(2)}) collective-permute-start(bf16[1,1400]{1,0:T(2,128)(2,1)S(1)} %get-tuple-element.106), channel_id=1, source_target_pairs={{4,8},{8,4},{12,16},{16,12},{20,24},{24,20},{5,9},{9,5},{13,17},{1... | collective-permute-start | bytes 8408 | tf_op jit(solution)/shard_map/ppermute | solution.py:899
  83.9 4.1 %up_project.3 = (bf16[256,1400]{1,0:T(8,128)(2,1)S(1)}, f32[560,256]{1,0:T(8,128)S(1)}, bf16[1,1400]{1,0:T(2,128)(2,1)}, bf16[1,1400]{1,0:T(2,128)(2,1)}) custom-call(s32[6]{0:T(128)S(1)} %stack.24.meta, bf16[1120,256]{1,0:T(8,128)(2,1)S(1)} %attend.3.own, bf16[1120,256]{1,0:T(8,128)(2,1)S(1)} %collective-permute-done.22.other, f32[1,2240]{1,0:T(1,128)S(1)} %reshape.39.gain, ...), custom_call_target="tpu_custom_call" | custom-call | flops 2000000000 | bytes 8000000 | tf_op jit(solution)/shard_map/up_project/pallas_call | solution.py:643
  88.0 2.2 %activate.3.own.own_b = bf16[1400,256]{1,0:T(8,128)(2,1)S(1)} custom-call(s32[6]{0:T(128)S(1)} %stack.24.meta, bf16[256,1400]{1,0:T(8,128)(2,1)S(1)} %get-tuple-element.101.outer, bf16[256,1400]{1,0:T(8,128)(2,1)S(1)} %get-tuple-element.104.inside, bf16[1,1400]{1,0:T(2,128)(2,1)S(1)} %collective-permute-done.23.near_row, ...), custom_call_target="tpu_custom_call" | custom-call | flops 1000000000 | bytes 2000000 | tf_op jit(solution)/shard_map/activate/pallas_call | solution.py:700
  90.3 2.2 %activate.2.own_a.own = bf16[1400,256]{1,0:T(8,128)(2,1)S(1)} custom-call(s32[6]{0:T(128)S(1)} %stack.24.meta, bf16[256,1400]{1,0:T(8,128)(2,1)S(1)} %get-tuple-element.101.outer, bf16[256,1400]{1,0:T(8,128)(2,1)S(1)} %get-tuple-element.104.inside, bf16[1,1400]{1,0:T(2,128)(2,1)S(1)} %collective-permute-done.23.near_row, ...), custom_call_target="tpu_custom_call" | custom-call | flops 1000000000 | bytes 2000000 | tf_op jit(solution)/shard_map/activate/pallas_call | solution.py:700
  93.1 1.6 %far_project.2.after = bf16[560,256]{1,0:T(8,128)(2,1)S(1)} custom-call(s32[6]{0:T(128)S(1)} %stack.24.meta, bf16[1400,256]{1,0:T(8,128)(2,1)S(1)} %activate.3.own.own_b, bf16[1400,256]{1,0:T(8,128)(2,1)S(1)} %collective-permute-done.26.other.other_b, bf16[4,560,1400]{2,1,0:T(8,128)(2,1)S(1)} %bitcast.28, ...), custom_call_target="tpu_custom_call" | custom-call | flops 1000000000 | bytes 4000000 | tf_op jit(solution)/shard_map/far_project/pallas_call | solution.py:722
  94.7 0.6 collective-permute-start.28
  95.3 1.6 %far_project.3 = bf16[560,256]{1,0:T(8,128)(2,1)S(1)} custom-call(s32[6]{0:T(128)S(1)} %stack.24.meta, bf16[1400,256]{1,0:T(8,128)(2,1)S(1)} %activate.2.own_a.own, bf16[1400,256]{1,0:T(8,128)(2,1)S(1)} %collective-permute-done.25.other_a.other, bf16[4,560,1400]{2,1,0:T(8,128)(2,1)S(1)} %bitcast.29, ...), custom_call_target="tpu_custom_call" | custom-call | flops 1000000000 | bytes 4000000 | tf_op jit(solution)/shard_map/far_project/pallas_call | solution.py:722
  96.9 1.6 %collective-permute-start.27 = (bf16[560,256]{1,0:T(8,128)(2,1)S(1)}, bf16[560,256]{1,0:T(8,128)(2,1)S(1)}, u32[]{:S(2)}, u32[]{:S(2)}) collective-permute-start(bf16[560,256]{1,0:T(8,128)(2,1)S(1)} %far_project.3), channel_id=1, source_target_pairs={{0,2},{1,3},{2,0},{3,1},{4,6},{5,7},{6,4},{7,5},{8,10},{9,11},{10,... | collective-permute-start | bytes 860168 | tf_op jit(solution)/shard_map/ppermute | solution.py:763
  98.5 2.5 %near_project.1 = f32[560,512]{1,0:T(8,128)S(1)} custom-call(s32[6]{0:T(128)S(1)} %stack.24.meta, bf16[1400,256]{1,0:T(8,128)(2,1)S(1)} %activate.2.own_a.own, bf16[1400,256]{1,0:T(8,128)(2,1)S(1)} %collective-permute-done.25.other_a.other, bf16[1400,256]{1,0:T(8,128)(2,1)S(1)} %activate.3.own.own_b, ...), custom_call_target="tpu_custom_call" | custom-call | flops 2000000000 | bytes 6000000 | tf_op jit(solution)/shard_map/near_project/pallas_call | solution.py:747
  101.0 3.5 %collective-permute-done.28 = bf16[560,256]{1,0:T(8,128)(2,1)S(1)} collective-permute-done((bf16[560,256]{1,0:T(8,128)(2,1)S(1)}, bf16[560,256]{1,0:T(8,128)(2,1)S(1)}, u32[]{:S(2)}, u32[]{:S(2)}) %collective-permute-start.28) | collective-permute-done | bytes 286752 | tf_op jit(solution)/shard_map/ppermute | solution.py:763
  104.5 5.2 %collective-permute-done.27 = bf16[560,256]{1,0:T(8,128)(2,1)S(1)} collective-permute-done((bf16[560,256]{1,0:T(8,128)(2,1)S(1)}, bf16[560,256]{1,0:T(8,128)(2,1)S(1)}, u32[]{:S(2)}, u32[]{:S(2)}) %collective-permute-start.27) | collective-permute-done | bytes 286752 | tf_op jit(solution)/shard_map/ppermute | solution.py:763
  109.7 1.0 fusion
  (61 shorter events, 2.9 us)
Async XLA Ops:
  0.0 5.8 %copy-start.4 = (bf16[512,560]{0,1:T(8,128)(2,1)S(1)}, bf16[512,560]{0,1:T(8,128)(2,1)}, u32[]{:S(2)}) copy-start(bf16[512,560]{0,1:T(8,128)(2,1)} %param.14) | copy-start | bytes 1720324
  0.0 14.9 %collective-permute-start = (bf16[560,512]{1,0:T(8,128)(2,1)}, bf16[560,512]{1,0:T(8,128)(2,1)S(1)}, u32[]{:S(2)}, u32[]{:S(2)}) collective-permute-start(bf16[560,512]{1,0:T(8,128)(2,1)} %bitcast.36), channel_id=1, source_target_pairs={{0,2},{1,3},{2,0},{3,1},{4,6},{5,7},{6,4},{7,5},{8,10},{9,11},{10,... | collective-permute-start | bytes 1720328 | tf_op jit(solution)/shard_map/ppermute | solution.py:763
  1.5 4.2 %collective-permute-start.1 = (bf16[560,512]{1,0:T(8,128)(2,1)}, bf16[560,512]{1,0:T(8,128)(2,1)S(1)}, u32[]{:S(2)}, u32[]{:S(2)}) collective-permute-start(bf16[560,512]{1,0:T(8,128)(2,1)} %bitcast.37), channel_id=1, source_target_pairs={{0,1},{1,0},{2,3},{3,2},{4,5},{5,4},{6,7},{7,6},{8,9},{9,8},{10,11... | collective-permute-start | bytes 1720328 | tf_op jit(solution)/shard_map/ppermute | solution.py:759
  5.8 13.2 %copy-start.2 = (bf16[2240,512]{1,0:T(8,128)(2,1)S(1)}, bf16[2240,512]{1,0:T(8,128)(2,1)}, u32[]{:S(2)}) copy-start(bf16[2240,512]{1,0:T(8,128)(2,1)} %refs_5_.3) | copy-start | bytes 6881284
  5.8 13.2 %copy-start.3 = (bf16[2240,512]{1,0:T(8,128)(2,1)S(1)}, bf16[2240,512]{1,0:T(8,128)(2,1)}, u32[]{:S(2)}) copy-start(bf16[2240,512]{1,0:T(8,128)(2,1)} %refs_6_.3) | copy-start | bytes 6881284
  14.9 2.0 %collective-permute-start.2 = (bf16[560,512]{1,0:T(8,128)(2,1)S(1)}, bf16[560,512]{1,0:T(8,128)(2,1)S(1)}, u32[]{:S(2)}, u32[]{:S(2)}) collective-permute-start(bf16[560,512]{1,0:T(8,128)(2,1)S(1)} %collective-permute-done.refs_0_.refs_2_), channel_id=1, source_target_pairs={{0,1},{1,0},{2,3},{3,2},{4,5},{5,4},{6,7},{7,6},{8,9},{9,8},{10,11... | collective-permute-start | bytes 1720328 | tf_op jit(solution)/shard_map/ppermute | solution.py:759
  16.9 24.7 %collective-permute-start.4 = (bf16[2,560,1400]{2,1,0:T(8,128)(2,1)}, bf16[2,560,1400]{2,1,0:T(8,128)(2,1)S(1)}, u32[]{:S(2)}, u32[]{:S(2)}) collective-permute-start(bf16[2,560,1400]{2,1,0:T(8,128)(2,1)} %get-tuple-element.76), channel_id=1, source_target_pairs={{0,1},{1,0},{2,3},{3,2},{4,5},{5,4},{6,7},{7,6},{8,9},{9,8},{10,11... | collective-permute-start | bytes 9408008 | tf_op jit(solution)/shard_map/ppermute | solution.py:759
  17.0 20.4 %collective-permute-start.3 = (bf16[1120,512]{1,0:T(8,128)(2,1)S(1)}, bf16[1120,512]{1,0:T(8,128)(2,1)S(1)}, u32[]{:S(2)}, u32[]{:S(2)}) collective-permute-start(bf16[1120,512]{1,0:T(8,128)(2,1)S(1)} %get-tuple-element.75), channel_id=1, source_target_pairs={{0,1},{1,0},{2,3},{3,2},{4,5},{5,4},{6,7},{7,6},{8,9},{9,8},{10,11... | collective-permute-start | bytes 3440648 | tf_op jit(solution)/shard_map/ppermute | solution.py:759
  17.4 38.4 %collective-permute-start.15 = (bf16[560,512]{1,0:T(8,128)(2,1)S(1)}, bf16[560,512]{1,0:T(8,128)(2,1)S(1)}, u32[]{:S(2)}, u32[]{:S(2)}) collective-permute-start(bf16[560,512]{1,0:T(8,128)(2,1)S(1)} %get-tuple-element.98), channel_id=1, source_target_pairs={{0,2},{1,3},{2,0},{3,1},{4,6},{5,7},{6,4},{7,5},{8,10},{9,11},{10,... | collective-permute-start | bytes 1720328 | tf_op jit(solution)/shard_map/ppermute | solution.py:763
  18.9 23.4 %copy-start.1 = (bf16[2240,512]{1,0:T(8,128)(2,1)S(1)}, bf16[2240,512]{1,0:T(8,128)(2,1)}, u32[]{:S(2)}) copy-start(bf16[2240,512]{1,0:T(8,128)(2,1)} %weights.3) | copy-start | bytes 6881284
  30.8 5.3 %collective-permute-start.5 = (bf16[2,128,256]{2,1,0:T(8,128)(2,1)S(1)}, bf16[2,128,256]{2,1,0:T(8,128)(2,1)S(1)}, u32[]{:S(2)}, u32[]{:S(2)}) collective-permute-start(bf16[2,128,256]{2,1,0:T(8,128)(2,1)S(1)} %get-tuple-element.78), channel_id=1, source_target_pairs={{0,4},{4,0},{8,12},{12,8},{16,20},{20,16},{24,28},{28,24},{1,5},{5... | collective-permute-start | bytes 393224 | tf_op jit(solution)/shard_map/ppermute | solution.py:767
  32.3 38.6 %collective-permute-start.17 = (bf16[1120,512]{1,0:T(8,128)(2,1)S(1)}, bf16[1120,512]{1,0:T(8,128)(2,1)S(1)}, u32[]{:S(2)}, u32[]{:S(2)}) collective-permute-start(bf16[1120,512]{1,0:T(8,128)(2,1)S(1)} %get-tuple-element.75), channel_id=1, source_target_pairs={{0,3},{1,2},{2,1},{3,0},{4,7},{5,6},{6,5},{7,4},{8,11},{9,10},{10,... | collective-permute-start | bytes 3440648 | tf_op jit(solution)/shard_map/ppermute | solution.py:860
  36.8 7.4 %collective-permute-start.6 = (bf16[2,128,128]{2,1,0:T(8,128)(2,1)S(1)}, bf16[2,128,128]{2,1,0:T(8,128)(2,1)S(1)}, u32[]{:S(2)}, u32[]{:S(2)}) collective-permute-start(bf16[2,128,128]{2,1,0:T(8,128)(2,1)S(1)} %get-tuple-element.83), channel_id=1, source_target_pairs={{8,24},{12,28},{9,25},{13,29},{10,26},{14,30},{11,27},{15,31}} | collective-permute-start | bytes 196616 | tf_op jit(solution)/shard_map/ppermute | solution.py:771
  37.5 8.5 %collective-permute-start.7 = (bf16[2,128,128]{2,1,0:T(8,128)(2,1)S(1)}, bf16[2,128,128]{2,1,0:T(8,128)(2,1)S(1)}, u32[]{:S(2)}, u32[]{:S(2)}) collective-permute-start(bf16[2,128,128]{2,1,0:T(8,128)(2,1)S(1)} %get-tuple-element.83), channel_id=1, source_target_pairs={{8,16},{12,20},{16,24},{20,28},{9,17},{13,21},{17,25},{21,29},{10,... | collective-permute-start | bytes 196616 | tf_op jit(solution)/shard_map/ppermute | solution.py:771
  41.6 10.2 %collective-permute-start.8 = (bf16[2,128,128]{2,1,0:T(8,128)(2,1)S(1)}, bf16[2,128,128]{2,1,0:T(8,128)(2,1)S(1)}, u32[]{:S(2)}, u32[]{:S(2)}) collective-permute-start(bf16[2,128,128]{2,1,0:T(8,128)(2,1)S(1)} %get-tuple-element.84), channel_id=1, source_target_pairs={{0,24},{4,28},{1,25},{5,29},{2,26},{6,30},{3,27},{7,31}} | collective-permute-start | bytes 196616 | tf_op jit(solution)/shard_map/ppermute | solution.py:771
  44.2 7.6 %collective-permute-start.9 = (bf16[2,128,128]{2,1,0:T(8,128)(2,1)S(1)}, bf16[2,128,128]{2,1,0:T(8,128)(2,1)S(1)}, u32[]{:S(2)}, u32[]{:S(2)}) collective-permute-start(bf16[2,128,128]{2,1,0:T(8,128)(2,1)S(1)} %get-tuple-element.84), channel_id=1, source_target_pairs={{0,16},{4,20},{8,24},{12,28},{1,17},{5,21},{9,25},{13,29},{2,18},{... | collective-permute-start | bytes 196616 | tf_op jit(solution)/shard_map/ppermute | solution.py:771
  46.0 7.0 %collective-permute-start.10 = (bf16[2,128,128]{2,1,0:T(8,128)(2,1)S(1)}, bf16[2,128,128]{2,1,0:T(8,128)(2,1)S(1)}, u32[]{:S(2)}, u32[]{:S(2)}) collective-permute-start(bf16[2,128,128]{2,1,0:T(8,128)(2,1)S(1)} %get-tuple-element.84), channel_id=1, source_target_pairs={{0,8},{4,12},{8,16},{12,20},{16,24},{20,28},{1,9},{5,13},{9,17},{1... | collective-permute-start | bytes 196616 | tf_op jit(solution)/shard_map/ppermute | solution.py:771
  48.9 10.4 %copy-start.5 = (bf16[128]{0:T(256)(128)(2,1)S(1)}, bf16[128]{0:T(256)(128)(2,1)}, u32[]{:S(2)}) copy-start(bf16[128]{0:T(256)(128)(2,1)} %param.22) | copy-start | bytes 772
  54.3 5.1 %collective-permute-start.11 = (bf16[2,128,128]{2,1,0:T(8,128)(2,1)S(1)}, bf16[2,128,128]{2,1,0:T(8,128)(2,1)S(1)}, u32[]{:S(2)}, u32[]{:S(2)}) collective-permute-start(bf16[2,128,128]{2,1,0:T(8,128)(2,1)S(1)} %get-tuple-element.92), channel_id=1, source_target_pairs={{0,4},{4,0},{8,12},{12,8},{16,20},{20,16},{24,28},{28,24},{1,5},{5... | collective-permute-start | bytes 196616 | tf_op jit(solution)/shard_map/ppermute | solution.py:767
  55.8 12.3 %collective-permute-start.16 = (bf16[560,512]{1,0:T(8,128)(2,1)S(1)}, bf16[560,512]{1,0:T(8,128)(2,1)S(1)}, u32[]{:S(2)}, u32[]{:S(2)}) collective-permute-start(bf16[560,512]{1,0:T(8,128)(2,1)S(1)} %collective-permute-done.15.refs_2_), channel_id=1, source_target_pairs={{0,4},{4,0},{8,12},{12,8},{16,20},{20,16},{24,28},{28,24},{1,5},{5... | collective-permute-start | bytes 1720328 | tf_op jit(solution)/shard_map/ppermute | solution.py:767
  59.4 11.5 %copy-start = (bf16[512,2240]{0,1:T(8,128)(2,1)S(1)}, bf16[512,2240]{0,1:T(8,128)(2,1)}, u32[]{:S(2)}) copy-start(bf16[512,2240]{0,1:T(8,128)(2,1)} %param.23) | copy-start | bytes 6881284
  60.5 7.6 %collective-permute-start.13 = (bf16[256,512]{1,0:T(8,128)(2,1)S(1)}, bf16[256,512]{1,0:T(8,128)(2,1)S(1)}, u32[]{:S(2)}, u32[]{:S(2)}) collective-permute-start(bf16[256,512]{1,0:T(8,128)(2,1)S(1)} %get-tuple-element.96.own), channel_id=1, source_target_pairs={{0,2},{1,3},{2,0},{3,1},{4,6},{5,7},{6,4},{7,5},{8,10},{9,11},{10,... | collective-permute-start | bytes 786440 | tf_op jit(solution)/shard_map/ppermute | solution.py:763
  61.0 9.8 %collective-permute-start.20 = (bf16[256,512]{1,0:T(8,128)(2,1)S(1)}, bf16[256,512]{1,0:T(8,128)(2,1)S(1)}, u32[]{:S(2)}, u32[]{:S(2)}) collective-permute-start(bf16[256,512]{1,0:T(8,128)(2,1)S(1)} %get-tuple-element.103.own), channel_id=1, source_target_pairs={{0,2},{1,3},{2,0},{3,1},{4,6},{5,7},{6,4},{7,5},{8,10},{9,11},{10,... | collective-permute-start | bytes 786440 | tf_op jit(solution)/shard_map/ppermute | solution.py:763
  62.6 8.3 %collective-permute-start.12 = (bf16[256,512]{1,0:T(8,128)(2,1)S(1)}, bf16[256,512]{1,0:T(8,128)(2,1)S(1)}, u32[]{:S(2)}, u32[]{:S(2)}) collective-permute-start(bf16[256,512]{1,0:T(8,128)(2,1)S(1)} %get-tuple-element.96.own), channel_id=1, source_target_pairs={{0,1},{1,0},{2,3},{3,2},{4,5},{5,4},{6,7},{7,6},{8,9},{9,8},{10,11... | collective-permute-start | bytes 786440 | tf_op jit(solution)/shard_map/ppermute | solution.py:759
  68.1 2.8 %collective-permute-start.14 = (bf16[256,512]{1,0:T(8,128)(2,1)S(1)}, bf16[256,512]{1,0:T(8,128)(2,1)S(1)}, u32[]{:S(2)}, u32[]{:S(2)}) collective-permute-start(bf16[256,512]{1,0:T(8,128)(2,1)S(1)} %collective-permute-done.13.refs_0_), channel_id=1, source_target_pairs={{0,1},{1,0},{2,3},{3,2},{4,5},{5,4},{6,7},{7,6},{8,9},{9,8},{10,11... | collective-permute-start | bytes 786440 | tf_op jit(solution)/shard_map/ppermute | solution.py:759
  68.1 5.4 %collective-permute-start.19 = (bf16[256,512]{1,0:T(8,128)(2,1)S(1)}, bf16[256,512]{1,0:T(8,128)(2,1)S(1)}, u32[]{:S(2)}, u32[]{:S(2)}) collective-permute-start(bf16[256,512]{1,0:T(8,128)(2,1)S(1)} %get-tuple-element.103.own), channel_id=1, source_target_pairs={{0,1},{1,0},{2,3},{3,2},{4,5},{5,4},{6,7},{7,6},{8,9},{9,8},{10,11... | collective-permute-start | bytes 786440 | tf_op jit(solution)/shard_map/ppermute | solution.py:759
  70.9 2.6 %collective-permute-start.21 = (bf16[256,512]{1,0:T(8,128)(2,1)S(1)}, bf16[256,512]{1,0:T(8,128)(2,1)S(1)}, u32[]{:S(2)}, u32[]{:S(2)}) collective-permute-start(bf16[256,512]{1,0:T(8,128)(2,1)S(1)} %collective-permute-done.20.refs_0_), channel_id=1, source_target_pairs={{0,1},{1,0},{2,3},{3,2},{4,5},{5,4},{6,7},{7,6},{8,9},{9,8},{10,11... | collective-permute-start | bytes 786440 | tf_op jit(solution)/shard_map/ppermute | solution.py:759
  70.9 4.6 %slice-start.2 = ((s8[6307840]{0:T(1024)(128)(4,1)}), s8[4194304]{0:T(1024)(128)(4,1)S(1)}, s32[]{:S(2)}) async-start(s8[6307840]{0:T(1024)(128)(4,1)} %bitcast.31), calls=%async_computation.2 | async-start | bytes 8388608
  72.9 2.6 %slice-start.3 = ((s8[6307840]{0:T(1024)(128)(4,1)}), s8[2113536]{0:T(1024)(128)(4,1)S(1)}, s32[]{:S(2)}) async-start(s8[6307840]{0:T(1024)(128)(4,1)} %bitcast.31), calls=%async_computation.3 | async-start | bytes 4227072
  72.9 2.6 %collective-permute-start.18 = (bf16[1120,256]{1,0:T(8,128)(2,1)S(1)}, bf16[1120,256]{1,0:T(8,128)(2,1)S(1)}, u32[]{:S(2)}, u32[]{:S(2)}) collective-permute-start(bf16[1120,256]{1,0:T(8,128)(2,1)S(1)} %attend.2.own), channel_id=1, source_target_pairs={{0,1},{1,0},{2,3},{3,2},{4,5},{5,4},{6,7},{7,6},{8,9},{9,8},{10,11... | collective-permute-start | bytes 1720328 | tf_op jit(solution)/shard_map/ppermute | solution.py:759
  75.4 8.4 %collective-permute-start.22 = (bf16[1120,256]{1,0:T(8,128)(2,1)S(1)}, bf16[1120,256]{1,0:T(8,128)(2,1)S(1)}, u32[]{:S(2)}, u32[]{:S(2)}) collective-permute-start(bf16[1120,256]{1,0:T(8,128)(2,1)S(1)} %attend.3.own), channel_id=1, source_target_pairs={{0,1},{1,0},{2,3},{3,2},{4,5},{5,4},{6,7},{7,6},{8,9},{9,8},{10,11... | collective-permute-start | bytes 1720328 | tf_op jit(solution)/shard_map/ppermute | solution.py:759
  75.5 17.6 %slice-start = ((s8[6307840]{0:T(1024)(128)(4,1)}), s8[4194304]{0:T(1024)(128)(4,1)S(1)}, s32[]{:S(2)}) async-start(s8[6307840]{0:T(1024)(128)(4,1)} %bitcast.26), calls=%async_computation | async-start | bytes 8388608
  79.0 8.9 %collective-permute-start.23 = (bf16[1,1400]{1,0:T(2,128)(2,1)S(1)}, bf16[1,1400]{1,0:T(2,128)(2,1)S(1)}, u32[]{:S(2)}, u32[]{:S(2)}) collective-permute-start(bf16[1,1400]{1,0:T(2,128)(2,1)S(1)} %get-tuple-element.105), channel_id=1, source_target_pairs={{0,4},{4,0},{8,12},{12,8},{16,20},{20,16},{24,28},{28,24},{1,5},{5... | collective-permute-start | bytes 8408 | tf_op jit(solution)/shard_map/ppermute | solution.py:898
  79.6 13.5 %slice-start.1 = ((s8[6307840]{0:T(1024)(128)(4,1)}), s8[2113536]{0:T(1024)(128)(4,1)S(1)}, s32[]{:S(2)}) async-start(s8[6307840]{0:T(1024)(128)(4,1)} %bitcast.26), calls=%async_computation.1 | async-start | bytes 4227072
  79.6 8.3 %collective-permute-start.24 = (bf16[1,1400]{1,0:T(2,128)(2,1)S(1)}, bf16[1,1400]{1,0:T(2,128)(2,1)S(1)}, u32[]{:S(2)}, u32[]{:S(2)}) collective-permute-start(bf16[1,1400]{1,0:T(2,128)(2,1)S(1)} %get-tuple-element.106), channel_id=1, source_target_pairs={{4,8},{8,4},{12,16},{16,12},{20,24},{24,20},{5,9},{9,5},{13,17},{1... | collective-permute-start | bytes 8408 | tf_op jit(solution)/shard_map/ppermute | solution.py:899
  90.2 2.9 %collective-permute-start.26 = (bf16[1400,256]{1,0:T(8,128)(2,1)S(1)}, bf16[1400,256]{1,0:T(8,128)(2,1)S(1)}, u32[]{:S(2)}, u32[]{:S(2)}) collective-permute-start(bf16[1400,256]{1,0:T(8,128)(2,1)S(1)} %activate.3.own.own_b), channel_id=1, source_target_pairs={{0,1},{1,0},{2,3},{3,2},{4,5},{5,4},{6,7},{7,6},{8,9},{9,8},{10,11... | collective-permute-start | bytes 2150408 | tf_op jit(solution)/shard_map/ppermute | solution.py:759
  92.5 2.8 %collective-permute-start.25 = (bf16[1400,256]{1,0:T(8,128)(2,1)S(1)}, bf16[1400,256]{1,0:T(8,128)(2,1)S(1)}, u32[]{:S(2)}, u32[]{:S(2)}) collective-permute-start(bf16[1400,256]{1,0:T(8,128)(2,1)S(1)} %activate.2.own_a.own), channel_id=1, source_target_pairs={{0,1},{1,0},{2,3},{3,2},{4,5},{5,4},{6,7},{7,6},{8,9},{9,8},{10,11... | collective-permute-start | bytes 2150408 | tf_op jit(solution)/shard_map/ppermute | solution.py:759
  94.7 9.8 %collective-permute-start.28 = (bf16[560,256]{1,0:T(8,128)(2,1)S(1)}, bf16[560,256]{1,0:T(8,128)(2,1)S(1)}, u32[]{:S(2)}, u32[]{:S(2)}) collective-permute-start(bf16[560,256]{1,0:T(8,128)(2,1)S(1)} %far_project.2.after), channel_id=1, source_target_pairs={{0,2},{1,3},{2,0},{3,1},{4,6},{5,7},{6,4},{7,5},{8,10},{9,11},{10,... | collective-permute-start | bytes 860168 | tf_op jit(solution)/shard_map/ppermute | solution.py:763
  96.9 12.8 %collective-permute-start.27 = (bf16[560,256]{1,0:T(8,128)(2,1)S(1)}, bf16[560,256]{1,0:T(8,128)(2,1)S(1)}, u32[]{:S(2)}, u32[]{:S(2)}) collective-permute-start(bf16[560,256]{1,0:T(8,128)(2,1)S(1)} %far_project.3), channel_id=1, source_target_pairs={{0,2},{1,3},{2,0},{3,1},{4,6},{5,7},{6,4},{7,5},{8,10},{9,11},{10,... | collective-permute-start | bytes 860168 | tf_op jit(solution)/shard_map/ppermute | solution.py:763
